TPU v7x, 32 devices: a whole 2x2x4 slice. The times are simulated.
32 devices in a mesh: lon: 8 (over z, y), lat: 4 (over x, core).
Axes of the slice: x: 2, y: 2, z: 4, core: 2. Of those that a mesh axis runs over, the one named last changes fastest.
Arguments:
- spectrum: float32 [1296, 64, 512], P(None, 'lon', 'lat'), may hold values from -6 to 6
- sea_mask: int32 [64, 512], P('lon', 'lat'), may hold values 0 or 1
- transfer: bfloat16 [1296, 1296], replicated, may hold values from -0.15625 to 0.15625
- bulk_weight: float32 [5, 1296], replicated, may hold values from -0.15625 to 0.15625
- remap_cell: int32 [192, 1536, 4], P('lon', 'lat'), may hold values from 0 to 8703, as said below
- remap_weight: float32 [192, 1536, 4], P('lon', 'lat'), may hold values from 0.1 to 0.5
- ocean_u: float32 [8, 192, 1536], P(None, 'lon', 'lat'), may hold values from -6 to 6
- ocean_v: float32 [8, 192, 1536], P(None, 'lon', 'lat'), may hold values from -6 to 6
- ocean_mask: int32 [192, 1536], P('lon', 'lat'), may hold values 0 or 1
- coriolis: float32 [1536], P('lat'), may hold values from -1 to 1
Outputs:
- spectrum_out: float32 [1296, 64, 512], P(None, 'lon', 'lat')
- ocean_u_out: float32 [8, 192, 1536], P(None, 'lon', 'lat')
- ocean_v_out: float32 [8, 192, 1536], P(None, 'lon', 'lat')
Inputs may be any that keep to these rules, and one draw needn't show every extreme that they name: `remap_cell`: for ocean cell (i, j) each entry c has c // 512 between 0 and 16, and its wave latitude c % 512 lies in the same block of 128 latitude cells as j // 3.
All inputs are finite; a program needn't handle non-finite values. No bound on the sum of `sea_mask` or of `ocean_mask` on one device may be relied on, other than what follows from the above.
Results may differ from a plain program's by a relative error of at most 0.0016.
Values sent between devices are 32-bit elements; how exact they have to be, the bound alone decides.
No kernel may reach another device: no remote copies, remote signals or barrier semaphores. Data moves between devices by JAX's collectives and lax.ppermute only.
A program may use at most 128 MiB of HBM per device.

v0:
```python
import jax
import jax.numpy as jnp
from jax import lax
from jax.sharding import PartitionSpec as P

NFREQ = 36


def passed_along(value, axis, steps):
    count = lax.axis_size(axis)
    first, last = (max(0, -steps), min(count, count - steps))
    return lax.ppermute(value, axis, [(source, source + steps) for source in range(first, last)])


def with_halo(array, sides, width, wrap):
    for axis, dim in sides:
        count, length = (lax.axis_size(axis), array.shape[dim])
        up = [(i, (i + 1) % count) for i in range(count if wrap else count - 1)]
        down = [(j, i) for i, j in up]
        last = lax.slice_in_dim(array, length - width, length, axis=dim)
        first = lax.slice_in_dim(array, 0, width, axis=dim)
        before = lax.ppermute(last, axis, up)
        after = lax.ppermute(first, axis, down)
        array = jnp.concatenate([before, array, after], axis=dim)
    return array


def courant(components, freqs):
    index = jnp.arange(components, dtype=jnp.int32)
    direction = (index // freqs).astype(jnp.float32)
    level = (index % freqs).astype(jnp.float32)
    theta = 2.0 * jnp.pi * (direction + 0.5) / (components // freqs)
    speed = jnp.power(jnp.float32(1.1), -level)
    return (
        (0.45 * speed * jnp.cos(theta))[:, None, None],
        (0.45 * speed * jnp.sin(theta))[:, None, None],
    )


def lat_sides(centre):
    below = passed_along(centre[:, :, -1:], "lat", 1)
    above = passed_along(centre[:, :, :1], "lat", -1)
    return (below, above)


def advect(lon_wide, below, above, east, north):
    centre = lon_wide[:, 1:-1, :]
    south_side = jnp.concatenate([below, centre[:, :, :-1]], axis=2)
    north_side = jnp.concatenate([centre[:, :, 1:], above], axis=2)
    result = (1.0 - jnp.abs(east) - jnp.abs(north)) * centre
    result = (
        result
        + jnp.maximum(east, 0.0) * lon_wide[:, :-2, :]
        + jnp.maximum(-east, 0.0) * lon_wide[:, 2:, :]
    )
    result = result + jnp.maximum(north, 0.0) * south_side + jnp.maximum(-north, 0.0) * north_side
    return result


def source(advected, transfer, maskf):
    flat = advected.reshape(advected.shape[0], -1).astype(jnp.bfloat16)
    added = jnp.dot(transfer, flat, preferred_element_type=jnp.float32).reshape(advected.shape)
    return maskf * (advected + 0.5 * added)


def ocean_update(padded, ocean_u, ocean_v, drift_u, drift_v, maskf, coriolis):
    levels = ocean_u.shape[0]

    def dxx(q):
        return 0.5 * (q[2:, 1:-1] - q[:-2, 1:-1])

    def dyy(q):
        return 0.5 * (q[1:-1, 2:] - q[1:-1, :-2])

    sxx = padded[2 * levels]
    sxy = padded[2 * levels + 1]
    syy = padded[2 * levels + 2]
    force_x = -(dxx(sxx) + dyy(sxy))
    force_y = -(dxx(sxy) + dyy(syy))

    def laplace(q):
        return (
            q[:, 2:, 1:-1]
            + q[:, :-2, 1:-1]
            + q[:, 1:-1, 2:]
            + q[:, 1:-1, :-2]
            - 4.0 * q[:, 1:-1, 1:-1]
        )

    decay = jnp.exp(-jnp.arange(levels, dtype=jnp.float32) / 3.0)[:, None, None]
    lap_u = laplace(padded[:levels])
    lap_v = laplace(padded[levels : 2 * levels])
    fcor = coriolis[None, None, :]
    new_u = maskf * (
        ocean_u + 0.5 * fcor * (ocean_v + decay * drift_v) + 0.5 * decay * force_x + 0.1 * lap_u
    )
    new_v = maskf * (
        ocean_v - 0.5 * fcor * (ocean_u + decay * drift_u) + 0.5 * decay * force_y + 0.1 * lap_v
    )
    return (new_u, new_v)


def local(
    spectrum,
    sea_mask,
    transfer,
    bulk_weight,
    remap_cell,
    remap_weight,
    ocean_u,
    ocean_v,
    ocean_mask,
    coriolis,
):
    components, width_x, width_y = spectrum.shape
    east, north = courant(components, NFREQ)
    maskf = sea_mask.astype(jnp.float32)[None]
    state = spectrum * maskf
    for step in range(2):
        extended = with_halo(state, (("lon", 1),), 1, True)
        below, above = lat_sides(state)
        state = source(advect(extended, below, above, east, north), transfer, maskf)
    flat = state.reshape(components, -1)
    bulk = jnp.dot(
        bulk_weight, flat, precision=lax.Precision.HIGHEST, preferred_element_type=jnp.float32
    )
    bulk = bulk.reshape(5, width_x, width_y)
    near = with_halo(bulk, (("lon", 1),), width_x, True).reshape(5, -1)
    lat_index = lax.axis_index("lat")
    total_y = width_y * lax.axis_size("lat")
    ocean_rows = jnp.arange(remap_cell.shape[0], dtype=jnp.int32)[:, None, None]
    local_lon = ocean_rows // 3 + remap_cell // total_y
    local_lat = remap_cell % total_y - lat_index * width_y
    position = local_lon * width_y + local_lat
    taken = jnp.take(near, position.reshape(-1), axis=1).reshape((5,) + remap_cell.shape)
    forcing = jnp.sum(taken * remap_weight[None], axis=-1)
    stacked = jnp.concatenate([ocean_u, ocean_v, forcing[:3]], axis=0)
    padded = with_halo(stacked, (("lon", 1),), 1, True)
    padded = with_halo(padded, (("lat", 2),), 1, False)
    new_u, new_v = ocean_update(
        padded,
        ocean_u,
        ocean_v,
        forcing[3],
        forcing[4],
        ocean_mask.astype(jnp.float32)[None],
        coriolis,
    )
    return (state, new_u, new_v)


def solution(mesh):
    placed = (
        P(None, "lon", "lat"),
        P("lon", "lat"),
        P(),
        P(),
        P("lon", "lat", None),
        P("lon", "lat", None),
        P(None, "lon", "lat"),
        P(None, "lon", "lat"),
        P("lon", "lat"),
        P("lat"),
    )
    return jax.shard_map(
        local,
        mesh=mesh,
        in_specs=placed,
        out_specs=(P(None, "lon", "lat"), P(None, "lon", "lat"), P(None, "lon", "lat")),
        check_vma=False,
    )
```

profile of v0, /device:TPU:1, one launch (start us, length us, event | category | flops | bytes accessed | tf_op | source)
XLA Modules:
  0.0 370.6 jit_solution(10292727123586107859)
XLA Ops:
  4.9 5.7 %fusion.69 = (f32[1296,8,1]{2,0,1:T(8,128)}, f32[1296,8,1]{2,0,1:T(8,128)}) fusion(f32[1296,8,128]{2,0,1:T(8,128)S(1)} %copy_multiply_fusion), kind=kLoop, calls=%fused_computation.152 | loop fusion | bytes 165888 | tf_op jit(solution)/shard_map/slice | solution.py:41
  10.6 4.1 %copy.38 = f32[1296,8,1]{0,1,2:T(8,128)S(1)} copy(f32[1296,8,1]{2,0,1:T(8,128)} %get-tuple-element.25) | data formatting | bytes 82944 | tf_op jit(solution)/shard_map/slice | solution.py:41
  14.7 4.6 %collective-permute-start.2 = (f32[1296,8,1]{0,1,2:T(8,128)S(1)}, f32[1296,8,1]{0,1,2:T(8,128)S(1)}, u32[]{:S(2)}, u32[]{:S(2)}) collective-permute-start(f32[1296,8,1]{0,1,2:T(8,128)S(1)} %copy.38), channel_id=1, source_target_pairs={{0,1},{1,2},{2,3},{4,5},{5,6},{6,7},{8,9},{9,10},{10,11},{12,13},{... | collective-permute-start | bytes 124424 | tf_op jit(solution)/shard_map/ppermute | solution.py:12
  19.4 4.1 %copy.40 = f32[1296,8,1]{0,1,2:T(8,128)S(1)} copy(f32[1296,8,1]{2,0,1:T(8,128)} %get-tuple-element.26) | data formatting | bytes 82944 | tf_op jit(solution)/shard_map/slice | solution.py:42
  35.1 6.7 %reshape.167 = s32[36864,1]{0,1:T(1,128)S(1)} reshape(s32[24,384,4]{2,1,0:T(8,128)} %copy.53) | data formatting | bytes 294912 | tf_op jit(solution)/shard_map/reshape | solution.py:135
  42.0 9.5 %fusion.70 = (f32[1296,8,127]{2,0,1:T(8,128)}, f32[1296,8,127]{2,0,1:T(8,128)}) fusion(f32[1296,8,128]{2,0,1:T(8,128)} %copy-done.1), kind=kLoop, calls=%fused_computation.153 | loop fusion | bytes 21067776 | tf_op jit(solution)/shard_map/slice | solution.py:48
  59.2 13.4 %convert_bitcast_fusion.1 = (bf16[8,162,8,128]{3,2,1,0:T(8,128)(2,1)S(1)}, f32[1296,8,128]{2,0,1:T(8,128)S(1)}) fusion(f32[1296,8,1]{2,0,1:T(8,128)} %copy.41, f32[1296,8,127]{2,0,1:T(8,128)} %get-tuple-element.28, f32[1296]{0:T(1024)S(1)} %get-tuple-element.37, f32[1296,8,127]{2,0,1:T(8,128)} %get-tuple-element.27, f32[1296,8,1]{2,0,1:T(8,128)} %copy.39, ...), kind=kLoop, calls=%fused_computation.39 | loop fusion | flops 18579456 | bytes 25240896
  72.6 4.3 %multiply_bitcast_fusion.1 = f32[162,8,8,128]{3,2,1,0:T(8,128)S(1)} fusion(bf16[1296,1296]{1,0:T(8,128)(2,1)S(1)} %copy-done.10, bf16[8,162,8,128]{3,2,1,0:T(8,128)(2,1)S(1)} %get-tuple-element.15), kind=kOutput, calls=%fused_computation.31 | convolution fusion | flops 3441180672 | bytes 11321856 | tf_op jit(solution)/shard_map/dot_general | solution.py:62
  77.7 5.7 %fusion.66 = (f32[1296,8,1]{2,0,1:T(8,128)}, f32[1296,8,1]{2,0,1:T(8,128)}) fusion(f32[1296,8,128]{2,0,1:T(8,128)S(1)} %fusion.4), kind=kLoop, calls=%fused_computation.149 | loop fusion | bytes 165888 | tf_op jit(solution)/shard_map/slice | solution.py:41
  83.5 4.1 %copy.44 = f32[1296,8,1]{0,1,2:T(8,128)S(1)} copy(f32[1296,8,1]{2,0,1:T(8,128)} %get-tuple-element.19) | data formatting | bytes 82944 | tf_op jit(solution)/shard_map/slice | solution.py:41
  87.6 4.0 %collective-permute-start.6 = (f32[1296,8,1]{0,1,2:T(8,128)S(1)}, f32[1296,8,1]{0,1,2:T(8,128)S(1)}, u32[]{:S(2)}, u32[]{:S(2)}) collective-permute-start(f32[1296,8,1]{0,1,2:T(8,128)S(1)} %copy.44), channel_id=1, source_target_pairs={{0,1},{1,2},{2,3},{4,5},{5,6},{6,7},{8,9},{9,10},{10,11},{12,13},{... | collective-permute-start | bytes 124424 | tf_op jit(solution)/shard_map/ppermute | solution.py:12
  91.6 4.1 %copy.46 = f32[1296,8,1]{0,1,2:T(8,128)S(1)} copy(f32[1296,8,1]{2,0,1:T(8,128)} %get-tuple-element.20) | data formatting | bytes 82944 | tf_op jit(solution)/shard_map/slice | solution.py:42
  97.7 4.1 %collective-permute-start.5 = (f32[1296,1,128]{2,0,1:T(8,128)S(1)}, f32[1296,1,128]{2,0,1:T(8,128)S(1)}, u32[]{:S(2)}, u32[]{:S(2)}) collective-permute-start(f32[1296,1,128]{2,0,1:T(8,128)S(1)} %get-tuple-element.18), channel_id=1, source_target_pairs={{4,0},{8,4},{12,8},{16,12},{20,16},{24,20},{28,24},{0,28},{5,1},{9... | collective-permute-start | bytes 1990664 | tf_op jit(solution)/shard_map/ppermute | solution.py:23
  101.9 9.5 %fusion.67 = (f32[1296,8,127]{2,0,1:T(8,128)}, f32[1296,8,127]{2,0,1:T(8,128)}) fusion(f32[1296,8,128]{2,0,1:T(8,128)} %copy-done.2), kind=kLoop, calls=%fused_computation.150 | loop fusion | bytes 21067776 | tf_op jit(solution)/shard_map/slice | solution.py:48
  119.1 5.6 %collective-permute-done.4 = f32[1296,1,128]{2,0,1:T(8,128)S(1)} collective-permute-done((f32[1296,1,128]{2,0,1:T(8,128)S(1)}, f32[1296,1,128]{2,0,1:T(8,128)S(1)}, u32[]{:S(2)}, u32[]{:S(2)}) %collective-permute-start.4) | collective-permute-done | bytes 663584 | tf_op jit(solution)/shard_map/ppermute | solution.py:22
  126.9 13.2 %convert_bitcast_fusion = (bf16[8,162,8,128]{3,2,1,0:T(8,128)(2,1)S(1)}, f32[1296,8,128]{2,0,1:T(8,128)S(1)}) fusion(f32[1296,8,1]{2,0,1:T(8,128)} %copy.47, f32[1296,8,127]{2,0,1:T(8,128)} %get-tuple-element.22, f32[1296]{0:T(1024)S(1)} %get-tuple-element.37, f32[1296,8,127]{2,0,1:T(8,128)} %get-tuple-element.21, f32[1296,8,1]{2,0,1:T(8,128)} %copy.45, ...), kind=kLoop, calls=%fused_computation.38 | loop fusion | flops 18579456 | bytes 25240896
  140.1 4.3 %multiply_bitcast_fusion = f32[162,8,8,128]{3,2,1,0:T(8,128)S(1)} fusion(bf16[1296,1296]{1,0:T(8,128)(2,1)S(1)} %copy-done.11, bf16[8,162,8,128]{3,2,1,0:T(8,128)(2,1)S(1)} %get-tuple-element.13), kind=kOutput, calls=%fused_computation.30 | convolution fusion | flops 3441180672 | bytes 11321856 | tf_op jit(solution)/shard_map/dot_general | solution.py:62
  150.2 4.1 %collective-permute-start.9 = (f32[5,8,128]{2,1,0:T(8,128)S(1)}, f32[5,8,128]{2,1,0:T(8,128)S(1)}, u32[]{:S(2)}, u32[]{:S(2)}) collective-permute-start(f32[5,8,128]{2,1,0:T(8,128)S(1)} %bitcast.61), channel_id=1, source_target_pairs={{4,0},{8,4},{12,8},{16,12},{20,16},{24,20},{28,24},{0,28},{5,1},{9... | collective-permute-start | bytes 61448 | tf_op jit(solution)/shard_map/ppermute | solution.py:23
  159.8 122.5 %gather_fusion = f32[36864,5]{1,0:T(8,128)} fusion(f32[5,3072]{0,1:T(8,128)S(1)} %bitcast.54, s32[36864]{0:T(1024)S(1)} %broadcast_clamp_fusion), kind=kCustom, calls=%fused_computation | custom fusion | bytes 1622016 | tf_op jit(solution)/shard_map/jit(_take)/gather | solution.py:135
  282.3 55.7 %multiply_reduce_fusion = f32[5,24,384]{0,2,1:T(8,128)} fusion(f32[5,24,384,4]{0,3,2,1:T(4,128)} %bitcast.58, f32[24,384,4]{2,1,0:T(8,128)} %copy.54, pred[24,384,4]{2,1,0:T(8,128)(4,1)S(1)} %copy.50), kind=kLoop, calls=%fused_computation.1 | loop fusion | flops 506880 | bytes 1105920 | tf_op jit(solution)/shard_map/reduce_sum | solution.py:136
  341.8 4.1 %collective-permute-start.11 = (f32[19,1,384]{2,1,0:T(1,128)S(1)}, f32[19,1,384]{2,1,0:T(1,128)S(1)}, u32[]{:S(2)}, u32[]{:S(2)}) collective-permute-start(f32[19,1,384]{2,1,0:T(1,128)S(1)} %get-tuple-element.34), channel_id=1, source_target_pairs={{4,0},{8,4},{12,8},{16,12},{20,16},{24,20},{28,24},{0,28},{5,1},{9... | collective-permute-start | bytes 87560 | tf_op jit(solution)/shard_map/ppermute | solution.py:23
  346.0 7.8 %copy.56 = f32[1296,8,128]{2,1,0:T(8,128)} copy(f32[1296,8,128]{2,0,1:T(8,128)} %copy-done.3) | data formatting | bytes 10616832
  354.0 5.5 %collective-permute-start.12 = (f32[19,26,1]{2,1,0:T(8,128)S(1)}, f32[19,26,1]{2,1,0:T(8,128)S(1)}, u32[]{:S(2)}, u32[]{:S(2)}) collective-permute-start(f32[19,26,1]{2,1,0:T(8,128)S(1)} %get-tuple-element.32), channel_id=1, source_target_pairs={{0,1},{1,2},{2,3},{4,5},{5,6},{6,7},{8,9},{9,10},{10,11},{12,13},{... | collective-permute-start | bytes 5936 | tf_op jit(solution)/shard_map/ppermute | solution.py:22
  361.5 4.9 %slice_reduce_fusion = (f32[24,384]{1,0:T(8,128)S(1)}, f32[24,384]{1,0:T(8,128)S(1)}) fusion(f32[5,24,384]{0,2,1:T(8,128)S(1)} %bitcast.57), kind=kLoop, calls=%fused_computation.32 | loop fusion | bytes 147456 | tf_op jit(solution)/shard_map/slice | solution.py:144
  (85 shorter events, 57.5 us)
Async XLA Ops:
  0.6 146.6 %copy-start = (f32[5,1296]{1,0:T(8,128)S(1)}, f32[5,1296]{1,0:T(8,128)}, u32[]{:S(2)}) copy-start(f32[5,1296]{1,0:T(8,128)} %param.13) | copy-start | bytes 77764
  14.7 17.0 %copy-start.7 = (s32[24,384,4]{1,2,0:T(4,128)S(1)}, s32[24,384,4]{1,2,0:T(4,128)}, u32[]{:S(2)}) copy-start(s32[24,384,4]{1,2,0:T(4,128)} %param.14) | copy-start | bytes 442372
  14.7 37.0 %collective-permute-start.2 = (f32[1296,8,1]{0,1,2:T(8,128)S(1)}, f32[1296,8,1]{0,1,2:T(8,128)S(1)}, u32[]{:S(2)}, u32[]{:S(2)}) collective-permute-start(f32[1296,8,1]{0,1,2:T(8,128)S(1)} %copy.38), channel_id=1, source_target_pairs={{0,1},{1,2},{2,3},{4,5},{5,6},{6,7},{8,9},{9,10},{10,11},{12,13},{... | collective-permute-start | bytes 124424 | tf_op jit(solution)/shard_map/ppermute | solution.py:12
  23.5 32.0 %collective-permute-start.3 = (f32[1296,8,1]{0,1,2:T(8,128)S(1)}, f32[1296,8,1]{0,1,2:T(8,128)S(1)}, u32[]{:S(2)}, u32[]{:S(2)}) collective-permute-start(f32[1296,8,1]{0,1,2:T(8,128)S(1)} %copy.40), channel_id=1, source_target_pairs={{1,0},{2,1},{3,2},{5,4},{6,5},{7,6},{9,8},{10,9},{11,10},{13,12},{... | collective-permute-start | bytes 124424 | tf_op jit(solution)/shard_map/ppermute | solution.py:12
  26.8 32.4 %collective-permute-start = (f32[1296,1,128]{2,0,1:T(8,128)S(1)}, f32[1296,1,128]{2,0,1:T(8,128)S(1)}, u32[]{:S(2)}, u32[]{:S(2)}) collective-permute-start(f32[1296,1,128]{2,0,1:T(8,128)S(1)} %get-tuple-element.23), channel_id=1, source_target_pairs={{0,4},{4,8},{8,12},{12,16},{16,20},{20,24},{24,28},{28,0},{1,5},{5... | collective-permute-start | bytes 1990664 | tf_op jit(solution)/shard_map/ppermute | solution.py:22
  28.1 31.1 %collective-permute-start.1 = (f32[1296,1,128]{2,0,1:T(8,128)S(1)}, f32[1296,1,128]{2,0,1:T(8,128)S(1)}, u32[]{:S(2)}, u32[]{:S(2)}) collective-permute-start(f32[1296,1,128]{2,0,1:T(8,128)S(1)} %get-tuple-element.24), channel_id=1, source_target_pairs={{4,0},{8,4},{12,8},{16,12},{20,16},{24,20},{28,24},{0,28},{5,1},{9... | collective-permute-start | bytes 1990664 | tf_op jit(solution)/shard_map/ppermute | solution.py:23
  59.2 13.4 %copy-start.10 = (bf16[1296,1296]{1,0:T(8,128)(2,1)S(1)}, bf16[1296,1296]{1,0:T(8,128)(2,1)}, u32[]{:S(2)}) copy-start(bf16[1296,1296]{1,0:T(8,128)(2,1)} %param.12) | copy-start | bytes 10077700
  87.6 23.8 %collective-permute-start.6 = (f32[1296,8,1]{0,1,2:T(8,128)S(1)}, f32[1296,8,1]{0,1,2:T(8,128)S(1)}, u32[]{:S(2)}, u32[]{:S(2)}) collective-permute-start(f32[1296,8,1]{0,1,2:T(8,128)S(1)} %copy.44), channel_id=1, source_target_pairs={{0,1},{1,2},{2,3},{4,5},{5,6},{6,7},{8,9},{9,10},{10,11},{12,13},{... | collective-permute-start | bytes 124424 | tf_op jit(solution)/shard_map/ppermute | solution.py:12
  95.8 19.7 %collective-permute-start.7 = (f32[1296,8,1]{0,1,2:T(8,128)S(1)}, f32[1296,8,1]{0,1,2:T(8,128)S(1)}, u32[]{:S(2)}, u32[]{:S(2)}) collective-permute-start(f32[1296,8,1]{0,1,2:T(8,128)S(1)} %copy.46), channel_id=1, source_target_pairs={{1,0},{2,1},{3,2},{5,4},{6,5},{7,6},{9,8},{10,9},{11,10},{13,12},{... | collective-permute-start | bytes 124424 | tf_op jit(solution)/shard_map/ppermute | solution.py:12
  97.7 27.0 %collective-permute-start.4 = (f32[1296,1,128]{2,0,1:T(8,128)S(1)}, f32[1296,1,128]{2,0,1:T(8,128)S(1)}, u32[]{:S(2)}, u32[]{:S(2)}) collective-permute-start(f32[1296,1,128]{2,0,1:T(8,128)S(1)} %get-tuple-element.17), channel_id=1, source_target_pairs={{0,4},{4,8},{8,12},{12,16},{16,20},{20,24},{24,28},{28,0},{1,5},{5... | collective-permute-start | bytes 1990664 | tf_op jit(solution)/shard_map/ppermute | solution.py:22
  97.7 29.2 %collective-permute-start.5 = (f32[1296,1,128]{2,0,1:T(8,128)S(1)}, f32[1296,1,128]{2,0,1:T(8,128)S(1)}, u32[]{:S(2)}, u32[]{:S(2)}) collective-permute-start(f32[1296,1,128]{2,0,1:T(8,128)S(1)} %get-tuple-element.18), channel_id=1, source_target_pairs={{4,0},{8,4},{12,8},{16,12},{20,16},{24,20},{28,24},{0,28},{5,1},{9... | collective-permute-start | bytes 1990664 | tf_op jit(solution)/shard_map/ppermute | solution.py:23
  126.9 13.2 %copy-start.11 = (bf16[1296,1296]{1,0:T(8,128)(2,1)S(1)}, bf16[1296,1296]{1,0:T(8,128)(2,1)}, u32[]{:S(2)}) copy-start(bf16[1296,1296]{1,0:T(8,128)(2,1)} %param.12) | copy-start | bytes 10077700
  147.3 9.1 %copy-start.6 = (f32[24,384,4]{1,2,0:T(4,128)S(1)}, f32[24,384,4]{1,2,0:T(4,128)}, u32[]{:S(2)}) copy-start(f32[24,384,4]{1,2,0:T(4,128)} %param.15) | copy-start | bytes 442372
  150.2 9.1 %collective-permute-start.8 = (f32[5,8,128]{2,1,0:T(8,128)S(1)}, f32[5,8,128]{2,1,0:T(8,128)S(1)}, u32[]{:S(2)}, u32[]{:S(2)}) collective-permute-start(f32[5,8,128]{2,1,0:T(8,128)S(1)} %bitcast.60), channel_id=1, source_target_pairs={{0,4},{4,8},{8,12},{12,16},{16,20},{20,24},{24,28},{28,0},{1,5},{5... | collective-permute-start | bytes 61448 | tf_op jit(solution)/shard_map/ppermute | solution.py:22
  150.2 9.0 %collective-permute-start.9 = (f32[5,8,128]{2,1,0:T(8,128)S(1)}, f32[5,8,128]{2,1,0:T(8,128)S(1)}, u32[]{:S(2)}, u32[]{:S(2)}) collective-permute-start(f32[5,8,128]{2,1,0:T(8,128)S(1)} %bitcast.61), channel_id=1, source_target_pairs={{4,0},{8,4},{12,8},{16,12},{20,16},{24,20},{28,24},{0,28},{5,1},{9... | collective-permute-start | bytes 61448 | tf_op jit(solution)/shard_map/ppermute | solution.py:23
  282.3 59.4 %copy-start.4 = (f32[8,24,384]{2,1,0:T(8,128)S(1)}, f32[8,24,384]{2,1,0:T(8,128)}, u32[]{:S(2)}) copy-start(f32[8,24,384]{2,1,0:T(8,128)} %param.17) | copy-start | bytes 884740
  282.3 59.5 %copy-start.5 = (f32[8,24,384]{2,1,0:T(8,128)S(1)}, f32[8,24,384]{2,1,0:T(8,128)}, u32[]{:S(2)}) copy-start(f32[8,24,384]{2,1,0:T(8,128)} %param.16) | copy-start | bytes 884740
  337.9 8.1 %copy-start.8 = (s32[24,384]{1,0:T(8,128)S(1)}, s32[24,384]{1,0:T(8,128)}, u32[]{:S(2)}) copy-start(s32[24,384]{1,0:T(8,128)} %param.18) | copy-start | bytes 110596
  341.8 12.0 %collective-permute-start.10 = (f32[19,1,384]{2,1,0:T(1,128)S(1)}, f32[19,1,384]{2,1,0:T(1,128)S(1)}, u32[]{:S(2)}, u32[]{:S(2)}) collective-permute-start(f32[19,1,384]{2,1,0:T(1,128)S(1)} %get-tuple-element.33), channel_id=1, source_target_pairs={{0,4},{4,8},{8,12},{12,16},{16,20},{20,24},{24,28},{28,0},{1,5},{5... | collective-permute-start | bytes 87560 | tf_op jit(solution)/shard_map/ppermute | solution.py:22
  341.8 12.0 %collective-permute-start.11 = (f32[19,1,384]{2,1,0:T(1,128)S(1)}, f32[19,1,384]{2,1,0:T(1,128)S(1)}, u32[]{:S(2)}, u32[]{:S(2)}) collective-permute-start(f32[19,1,384]{2,1,0:T(1,128)S(1)} %get-tuple-element.34), channel_id=1, source_target_pairs={{4,0},{8,4},{12,8},{16,12},{20,16},{24,20},{28,24},{0,28},{5,1},{9... | collective-permute-start | bytes 87560 | tf_op jit(solution)/shard_map/ppermute | solution.py:23
  346.0 15.4 %slice-start = ((s8[4718592]{0:T(1024)(128)(4,1)}), s8[4194304]{0:T(1024)(128)(4,1)S(1)}, s32[]{:S(2)}) async-start(s8[4718592]{0:T(1024)(128)(4,1)} %bitcast.56), calls=%async_computation | async-start | bytes 8388608
  346.0 15.4 %slice-start.1 = ((s8[4718592]{0:T(1024)(128)(4,1)}), s8[524288]{0:T(1024)(128)(4,1)S(1)}, s32[]{:S(2)}) async-start(s8[4718592]{0:T(1024)(128)(4,1)} %bitcast.56), calls=%async_computation.1 | async-start | bytes 1048576
  354.0 12.4 %collective-permute-start.12 = (f32[19,26,1]{2,1,0:T(8,128)S(1)}, f32[19,26,1]{2,1,0:T(8,128)S(1)}, u32[]{:S(2)}, u32[]{:S(2)}) collective-permute-start(f32[19,26,1]{2,1,0:T(8,128)S(1)} %get-tuple-element.32), channel_id=1, source_target_pairs={{0,1},{1,2},{2,3},{4,5},{5,6},{6,7},{8,9},{9,10},{10,11},{12,13},{... | collective-permute-start | bytes 5936 | tf_op jit(solution)/shard_map/ppermute | solution.py:22
  359.5 8.2 %collective-permute-start.13 = (f32[19,26,1]{2,1,0:T(8,128)S(1)}, f32[19,26,1]{2,1,0:T(8,128)S(1)}, u32[]{:S(2)}, u32[]{:S(2)}) collective-permute-start(f32[19,26,1]{2,1,0:T(8,128)S(1)} %get-tuple-element.31), channel_id=1, source_target_pairs={{1,0},{2,1},{3,2},{5,4},{6,5},{7,6},{9,8},{10,9},{11,10},{13,12},{... | collective-permute-start | bytes 5936 | tf_op jit(solution)/shard_map/ppermute | solution.py:23
  (4 other events, 20.9 us)
where the time goes:
time: 374 us; the launch traced here: 371 us
  local copies, waits for them, and re-layouts  220 us (59%)
  other arithmetic  91.3 us (24%)
  starting transfers between devices  37.4 us (10%)
  matrix products  11.5 us (3%)
  waiting for transfers between devices  9.13 us (2%)
    gather x1, local copies, waits for them, and re-layouts, local(): jnp.take(near, position.reshape(-1), axis=1)  122 us
    reduce_sum x1, other arithmetic, local(): forcing = jnp.sum(taken * remap_weight[None], axis=-1)  55.7 us
    unnamed x3, other arithmetic  26.5 us
    slice x4, local copies, waits for them, and re-layouts, lat_sides(): below = passed_along(centre[:, :, -1:], 'lat', 1)  19.7 us
    slice x2, local copies, waits for them, and re-layouts, advect(): south_side = jnp.concatenate([below, centre[:, :, :-1]], axis=2)  19 us
    ppermute x5, starting transfers between devices, with_halo(): after = lax.ppermute(first, axis, down)  18 us
    ppermute x4, local copies, waits for them, and re-layouts, passed_along(): lax.ppermute(value, axis, [(source, source + steps) for source in range(f...  15.2 us
    unnamed x31, local copies, waits for them, and re-layouts  13.1 us
  transfers between devices with their start and end apart: 14, of which 3 were waited for; matrix products, arithmetic and copies ran while one was open for 19% of the time, Pallas kernels for 0%

commit v1 on v0

v1 whole, which is shorter than its diff:
```python
import functools

import jax
import jax.numpy as jnp
import numpy as np
from jax import lax
from jax.experimental import pallas as pl
from jax.experimental.pallas import tpu as pltpu
from jax.sharding import PartitionSpec as P

NFREQ = 36
STEP = 16
LANES = 128
BULK = 5
F32 = jnp.float32
VMEM = pl.BlockSpec(memory_space=pltpu.VMEM)
ANY = pl.BlockSpec(memory_space=pl.ANY)
PARAMS = pltpu.CompilerParams(vmem_limit_bytes=40 << 20)


class Plan:
    def __init__(self, comps):
        dirs = comps // NFREQ
        k = np.arange(comps)
        theta = 2.0 * np.pi * ((k // NFREQ) + 0.5) / dirs
        speed = 1.1 ** (-(k % NFREQ).astype(np.float64))
        cx = 0.45 * speed * np.cos(theta)
        cy = 0.45 * speed * np.sin(theta)
        self.comps = comps
        self.coef = np.stack([1.0 - np.abs(cx) - np.abs(cy), np.abs(cx), np.abs(cy)], 1).astype(np.float32)
        self.flag = {"x": cx > 0, "y": cy > 0}
        self.seg = {}
        for axis, step in (("x", 8), ("y", STEP)):
            for sign in (True, False):
                self.seg[axis, sign] = self.runs(self.flag[axis] == sign, step)

    def runs(self, flag, step):
        out = []
        for n in np.flatnonzero(flag.reshape(-1, step).any(1)):
            if out and out[-1][1] == n * step:
                out[-1][1] = int(n + 1) * step
            else:
                out.append([int(n) * step, int(n + 1) * step])
        return [(a, b) for a, b in out]

    def rows(self, axis, sign):
        return sum(b - a for a, b in self.seg[axis, sign])

    def shift(self, axis, sign, first):
        used = np.flatnonzero(self.flag[axis][first : first + STEP] == sign) + first
        if not len(used):
            return None
        base = 0
        for a, b in self.seg[axis, sign]:
            if a <= used[0] < b:
                at = base + first - a
                assert used[-1] < b and 0 <= at <= self.rows(axis, sign) - STEP
                return base - a
            base += b - a
        raise ValueError("no segment")

    def regions(self):
        out = []
        for r in range(0, self.comps, STEP):
            sign = {}
            for axis in "xy":
                part = self.flag[axis][r : r + STEP]
                sign[axis] = 1 if part.all() else (0 if part.any() else -1)
            shifts = {(axis, s): self.shift(axis, s, r) for axis in "xy" for s in (True, False)}
            if out and sign["x"] and sign["y"] and out[-1][2:] == [sign["x"], sign["y"], shifts]:
                out[-1][1] = r + STEP
            else:
                out.append([r, r + STEP, sign["x"], sign["y"], shifts])
        return out


def for_range(count, body, unroll=1):
    if count == 1:
        body(0)
        return

    def step(n, carry):
        body(n)
        return carry

    lax.fori_loop(0, count, step, 0, unroll=unroll)


def chunk_rows(first, n):
    return pl.ds(pl.multiple_of(first + n * STEP, STEP), STEP)


def shifted_rows(first, n, shift):
    return pl.ds(pl.multiple_of(first + shift + n * STEP, 8), STEP)


def lanes_of(rows=STEP):
    return lax.broadcasted_iota(jnp.int32, (rows, LANES), 1)


def picked(flag, first):
    row = lax.broadcasted_iota(jnp.int32, (STEP, LANES), 0)
    part = flag[first : first + STEP]
    out, n = (None, 0)
    while n < STEP:
        if not part[n]:
            n += 1
            continue
        m = n
        while m < STEP and part[m]:
            m += 1
        here = (row >= n) & (row < m)
        out = here if out is None else out | here
        n = m
    return out


def upwind(plan, axis, sign, first, from_plus, from_minus):
    if sign > 0:
        return from_plus()
    if sign < 0:
        return from_minus()
    plus, minus = (from_plus(), from_minus())
    where = picked(plan.flag[axis], first)
    zero = jnp.zeros((STEP, LANES), F32)
    if plus is None and minus is None:
        return None
    return jnp.where(where, zero if plus is None else plus, zero if minus is None else minus)


def pack_lon_kernel(plan, spec, mask, u, v, east, west, sem):
    last_col, last_row, levels = (spec.shape[1] - 1, u.shape[1] - 1, u.shape[0])
    copies = []
    for out, sign, col in ((east, True, last_col), (west, False, 0)):
        at = 0
        for a, b in plan.seg["x", sign]:
            c = pltpu.make_async_copy(
                spec.at[pl.ds(a, b - a), col, 0, :], out.at[pl.ds(at, b - a), :], sem.at[len(copies)]
            )
            c.start()
            copies.append(c)
            at += b - a
    for out, row, sign in ((east, last_row, True), (west, 0, False)):
        at = plan.rows("x", sign)
        for field in (u, v):
            for m in range(u.shape[2] // LANES):
                out[at : at + levels, :] = field[:, row, m * LANES : (m + 1) * LANES]
                at += levels
    for c in copies:
        c.wait()
    for out, sign, col in ((east, True, last_col), (west, False, 0)):
        rows = plan.rows("x", sign)
        out[:rows, :] = out[:rows, :] * mask[col : col + 1, :].astype(F32)


def pack_lon(plan, spec4, mask, u, v):
    extra = 2 * u.shape[0] * u.shape[2] // LANES
    segments = sum(len(plan.seg["x", s]) for s in (True, False))
    return pl.pallas_call(
        functools.partial(pack_lon_kernel, plan),
        out_shape=[jax.ShapeDtypeStruct((plan.rows("x", s) + extra, LANES), F32) for s in (True, False)],
        in_specs=[pl.BlockSpec(memory_space=pltpu.HBM), VMEM, VMEM, VMEM],
        out_specs=[VMEM, VMEM],
        scratch_shapes=[pltpu.SemaphoreType.DMA((segments,))],
        compiler_params=PARAMS,
        name="pack_lon",
    )(spec4, mask, u, v)


def to_lane(acc, column, source, lane, lanes):
    return jnp.where(lanes == lane, pltpu.roll(column, (lane - source) % LANES, 1), acc)


def pack_lat_kernel(plan, spec, mask, u, v, north, south, cols, sem):
    width_x = spec.shape[1]
    copies = [pltpu.make_async_copy(spec.at[:, i, 0, :], cols.at[i], sem.at[i]) for i in range(width_x)]
    for c in copies:
        c.start()
    levels, ocean_x = u.shape[:2]
    last = u.shape[2] - LANES
    for out, source, sign, m in ((north, LANES - 1, True, last), (south, 0, False, 0)):
        at = plan.rows("y", sign)
        acc = jnp.zeros((ocean_x, LANES), F32)
        for f in range(2 * levels):
            field = (u, v)[f // levels]
            acc = to_lane(acc, field[f % levels, :, m : m + LANES], source, f, lanes_of(ocean_x))
        out[at : at + ocean_x, :] = acc
    for c in copies:
        c.wait()
    maskf = mask[...].astype(F32)
    for out, source, sign in ((north, LANES - 1, True), (south, 0, False)):
        (a, b), = plan.seg["y", sign]

        def body(n, a=a, out=out, source=source):
            rows = chunk_rows(a, n)
            acc = jnp.zeros((STEP, LANES), F32)
            for i in range(width_x):
                acc = to_lane(acc, cols[i, rows, :] * maskf[i : i + 1, :], source, i, lanes_of())
            out[chunk_rows(0, n), :] = acc

        for_range((b - a) // STEP, body)


def pack_lat(plan, spec4, mask, u, v):
    extra = u.shape[1]
    return pl.pallas_call(
        functools.partial(pack_lat_kernel, plan),
        out_shape=[jax.ShapeDtypeStruct((plan.rows("y", s) + extra, LANES), F32) for s in (True, False)],
        in_specs=[ANY, VMEM, VMEM, VMEM],
        out_specs=[VMEM, VMEM],
        scratch_shapes=[
            pltpu.VMEM((spec4.shape[1], plan.comps, LANES), F32),
            pltpu.SemaphoreType.DMA((spec4.shape[1],)),
        ],
        compiler_params=PARAMS,
        name="pack_lat",
    )(spec4, mask, u, v)


def advect_columns(plan, column, coefs, south, north, put):
    def run(first, last, xs, ys, shifts):
        def body(n):
            rows = chunk_rows(first, n)
            x = [column(i, rows) for i in range(put.width)]
            c = coefs[rows, :]
            keep, east, up = (jnp.broadcast_to(c[:, q : q + 1], (STEP, LANES)) for q in range(3))
            lanes = lanes_of()
            from_south = from_north = None
            if shifts["y", True] is not None:
                from_south = south[shifted_rows(first, n, shifts["y", True]), :]
            if shifts["y", False] is not None:
                from_north = north[shifted_rows(first, n, shifts["y", False]), :]
            for i in range(put.width):
                lat = upwind(
                    plan, "y", ys, first,
                    lambda: to_lane(pltpu.roll(x[i], 1, 1), from_south, i, 0, lanes),
                    lambda: to_lane(pltpu.roll(x[i], LANES - 1, 1), from_north, i, LANES - 1, lanes),
                )
                lon = upwind(
                    plan, "x", xs, first,
                    lambda: x[i - 1] if i else None,
                    lambda: x[i + 1] if i + 1 < put.width else None,
                )
                a = keep * x[i] + up * lat
                if lon is not None:
                    a = a + east * lon
                put(i, rows, a)

        for_range((last - first) // STEP, body)

    for region in plan.regions():
        run(*region)


def block_rows(comps):
    return max(b for b in range(STEP, 449, STEP) if comps % b == 0)


def source_blocks(transfer, moved, comps, body):
    block = block_rows(comps)

    def step(n):
        rows = pl.ds(pl.multiple_of(n * block, STEP), block)
        body(n, rows, jnp.dot(transfer[rows, :], moved[...], preferred_element_type=F32))

    for_range(comps // block, step)


def add_bulk(coefs, rows, first, state, total, slot):
    count = state.shape[0]
    for q in range(BULK):
        w = coefs[rows, 3 + q : 4 + q]
        part = (w * state).reshape(count // 8, 8, LANES).sum(0)
        total[q, slot] = total[q, slot] + part


def interior_kernel(plan, step, *refs):
    refs = list(refs)
    if step == 0:
        spec, south, north, transfer, coefs, mask = refs[:6]
        inner, edge, up, down = refs[6:10]
        cols, full, moved, sem = refs[10:]
        width = spec.shape[1]
        copies = [pltpu.make_async_copy(spec.at[:, i, 0, :], cols.at[i], sem.at[i]) for i in range(width)]
        for c in copies:
            c.start()
        for c in copies:
            c.wait()
    else:
        sides, middle, south, north, transfer, coefs, mask = refs[:7]
        out, edge, bulk = refs[7:10]
        inner, full, moved, total, sem = refs[10:]
        width = middle.shape[0] + 2
    maskf = mask[...].astype(F32)

    def column(i, rows):
        if step == 0:
            return cols[i, rows, :] * maskf[i : i + 1, :]
        if i in (0, width - 1):
            return sides[min(i, 1), rows, :]
        return middle[i - 1, rows, :]

    def put(i, rows, a):
        if i in (0, width - 1):
            edge[min(i, 1), rows, :] = a
        else:
            full[i - 1, rows, :] = a
            moved[rows, (i - 1) * LANES : i * LANES] = a.astype(jnp.bfloat16)

    put_ = Put(width, put)
    advect_columns(plan, column, coefs, south, north, put_)
    if step:
        total[...] = jnp.zeros_like(total)

    def done(n, rows, added):
        for i in range(1, width - 1):
            s = maskf[i : i + 1, :] * (full[i - 1, rows, :] + 0.5 * added[:, (i - 1) * LANES : i * LANES])
            inner[i - 1, rows, :] = s
            if step:
                add_bulk(coefs, rows, n, s, total, i - 1)

    source_blocks(transfer, moved, plan.comps, done)
    if step:
        copies = [pltpu.make_async_copy(inner.at[i - 1], out.at[:, i, 0, :], sem.at[i]) for i in range(1, width - 1)]
        for c in copies:
            c.start()
        for q in range(BULK):
            for i in range(1, width - 1):
                bulk[q, i : i + 1, :] = total[q, i - 1].sum(0, keepdims=True)
            bulk[q, 0:1, :] = jnp.zeros((1, LANES), F32)
            bulk[q, width - 1 : width, :] = jnp.zeros((1, LANES), F32)
        for c in copies:
            c.wait()
    else:
        for out_ref, source, sign in ((up, LANES - 1, True), (down, 0, False)):
            (a, b), = plan.seg["y", sign]

            def body(n, a=a, out_ref=out_ref, source=source):
                rows = chunk_rows(a, n)
                acc = jnp.zeros((STEP, LANES), F32)
                for i in range(1, width - 1):
                    acc = to_lane(acc, inner[i - 1, rows, :], source, i, lanes_of())
                out_ref[chunk_rows(0, n), :] = acc

            for_range((b - a) // STEP, body)


class Put:
    def __init__(self, width, put):
        self.width, self.put = (width, put)

    def __call__(self, *args):
        self.put(*args)


def interior(plan, step, state, south, north, transfer, coefs, mask):
    comps, width = (plan.comps, mask.shape[0])
    middle = (width - 2, comps, LANES)
    edge = jax.ShapeDtypeStruct((2, comps, LANES), F32)
    full = [pltpu.VMEM(middle, F32), pltpu.VMEM((comps, (width - 2) * LANES), jnp.bfloat16)]
    sems = pltpu.SemaphoreType.DMA((width,))
    if step == 0:
        outs = [jax.ShapeDtypeStruct(middle, F32), edge]
        outs += [jax.ShapeDtypeStruct((plan.rows("y", s), LANES), F32) for s in (True, False)]
        in_specs = [ANY] + [VMEM] * 5
        out_specs = [VMEM] * 4
        scratch = [pltpu.VMEM((width, comps, LANES), F32)] + full + [sems]
    else:
        outs = [
            jax.ShapeDtypeStruct((comps, width, 1, LANES), F32),
            edge,
            jax.ShapeDtypeStruct((BULK, width, LANES), F32),
        ]
        in_specs = [VMEM] * 7
        out_specs = [ANY, VMEM, VMEM]
        scratch = [pltpu.VMEM(middle, F32)] + full + [pltpu.VMEM((BULK, width - 2, 8, LANES), F32), sems]
    return pl.pallas_call(
        functools.partial(interior_kernel, plan, step),
        out_shape=outs,
        in_specs=in_specs,
        out_specs=out_specs,
        scratch_shapes=scratch,
        compiler_params=PARAMS,
        cost_estimate=pl.CostEstimate(
            flops=2 * comps * comps * (width - 2) * LANES, bytes_accessed=20 << 20, transcendentals=0
        ),
        name="interior",
    )(*state, south, north, transfer, coefs, mask)


def edges_kernel(plan, step, *refs):
    refs = list(refs)
    part, from_west, from_east, transfer, coefs, mask = refs[:6]
    if step == 0:
        up_in, down_in = refs[6:8]
        state, east, west, up, down = refs[8:13]
        full, moved = refs[13:]
    else:
        bulk_in = refs[6]
        state, bulk = refs[7:9]
        full, moved, total = refs[9:]
    width = mask.shape[0]
    maskf = jnp.concatenate([mask[0:1, :], mask[width - 1 : width, :]], axis=0).astype(F32)

    def run(first, last, xs, ys, shifts):
        def body(n):
            rows = chunk_rows(first, n)
            speed = jnp.broadcast_to(coefs[rows, 1:2], (STEP, LANES))
            for side, sign, buffer in ((0, True, from_west), (1, False, from_east)):
                a = part[side, rows, :]
                shift = shifts["x", sign]
                if shift is not None:
                    halo = buffer[shifted_rows(first, n, shift), :]
                    if xs == 0:
                        halo = jnp.where(picked(plan.flag["x"] == sign, first), halo, 0.0)
                    a = a + speed * halo
                full[side, rows, :] = a
                moved[rows, side * LANES : (side + 1) * LANES] = a.astype(jnp.bfloat16)

        for_range((last - first) // STEP, body)

    for region in plan.regions():
        run(*region)
    if step:
        total[...] = jnp.zeros_like(total)

    def done(n, rows, added):
        for side in range(2):
            s = maskf[side : side + 1, :] * (full[side, rows, :] + 0.5 * added[:, side * LANES : (side + 1) * LANES])
            state[side, rows, :] = s
            if step:
                add_bulk(coefs, rows, n, s, total, side)

    source_blocks(transfer, moved, plan.comps, done)
    if step:
        for q in range(BULK):
            bulk[q] = bulk_in[q]
            bulk[q, 0:1, :] = total[q, 0].sum(0, keepdims=True)
            bulk[q, width - 1 : width, :] = total[q, 1].sum(0, keepdims=True)
        return
    for out, side, sign in ((east, 1, True), (west, 0, False)):
        at = 0
        for a, b in plan.seg["x", sign]:
            out[at : at + b - a, :] = state[side, a:b, :]
            at += b - a
    for out, given, source, sign in ((up, up_in, LANES - 1, True), (down, down_in, 0, False)):
        (a, b), = plan.seg["y", sign]

        def body(n, a=a, out=out, given=given, source=source):
            rows = chunk_rows(a, n)
            acc = given[chunk_rows(0, n), :]
            for side, lane in ((0, 0), (1, width - 1)):
                acc = to_lane(acc, state[side, rows, :], source, lane, lanes_of())
            out[chunk_rows(0, n), :] = acc

        for_range((b - a) // STEP, body)


def edges(plan, step, part, from_west, from_east, transfer, coefs, mask, *more):
    comps, width = (plan.comps, mask.shape[0])
    outs = [jax.ShapeDtypeStruct((2, comps, LANES), F32)]
    scratch = [pltpu.VMEM((2, comps, LANES), F32), pltpu.VMEM((comps, 2 * LANES), jnp.bfloat16)]
    if step == 0:
        for axis in "xy":
            outs += [jax.ShapeDtypeStruct((plan.rows(axis, s), LANES), F32) for s in (True, False)]
    else:
        outs += [jax.ShapeDtypeStruct((BULK, width, LANES), F32)]
        scratch += [pltpu.VMEM((BULK, 2, 8, LANES), F32)]
    return pl.pallas_call(
        functools.partial(edges_kernel, plan, step),
        out_shape=outs,
        in_specs=[VMEM] * (6 + len(more)),
        out_specs=[VMEM] * len(outs),
        scratch_shapes=scratch,
        compiler_params=PARAMS,
        cost_estimate=pl.CostEstimate(
            flops=2 * comps * comps * 2 * LANES, bytes_accessed=8 << 20, transcendentals=0
        ),
        name="edges",
    )(part, from_west, from_east, transfer, coefs, mask, *more)


def finish_kernel(state, given, out, sem):
    width = out.shape[1]
    copies = [
        pltpu.make_async_copy(state.at[side], out.at[:, col, 0, :], sem.at[side])
        for side, col in ((0, 0), (1, width - 1))
    ]
    for c in copies:
        c.start()
    for c in copies:
        c.wait()


def finish(state, out4):
    return pl.pallas_call(
        finish_kernel,
        out_shape=jax.ShapeDtypeStruct(out4.shape, F32),
        in_specs=[ANY, ANY],
        out_specs=ANY,
        scratch_shapes=[pltpu.SemaphoreType.DMA((2,))],
        input_output_aliases={1: 0},
        compiler_params=PARAMS,
        name="finish",
    )(state, out4)


def ocean_shifts(q, west, east, south, north):
    rows, lanes = q.shape
    row = lax.broadcasted_iota(jnp.int32, q.shape, 0)
    lane = lax.broadcasted_iota(jnp.int32, q.shape, 1)
    before = jnp.where(row == 0, west, pltpu.roll(q, 1, 0))
    after = jnp.where(row == rows - 1, east, pltpu.roll(q, rows - 1, 0))
    below = jnp.where(lane == 0, south, pltpu.roll(q, 1, 1))
    above = jnp.where(lane == lanes - 1, north, pltpu.roll(q, lanes - 1, 1))
    return before, after, below, above


def ocean_base_kernel(plan, u, v, from_west, from_east, from_south, from_north, mask, coriolis, base_u, base_v):
    levels, ocean_x, ocean_y = u.shape
    tiles = ocean_y // LANES
    maskf = mask[...].astype(F32)
    half = 0.5 * coriolis[...]
    west_at, east_at = (plan.rows("x", s) for s in (True, False))
    south_at, north_at = (plan.rows("y", s) for s in (True, False))
    for f, (field, other, out, sign) in enumerate(((u, v, base_u, 1.0), (v, u, base_v, -1.0))):
        for level in range(levels):
            q = field[level]

            def line(buffer, at):
                parts = [buffer[at + (f * tiles + m) * levels + level, :][None, :] for m in range(tiles)]
                return jnp.concatenate(parts, axis=1)

            lane = f * levels + level
            before, after, below, above = ocean_shifts(
                q,
                line(from_west, west_at),
                line(from_east, east_at),
                from_south[south_at : south_at + ocean_x, lane : lane + 1],
                from_north[north_at : north_at + ocean_x, lane : lane + 1],
            )
            lap = before + after + below + above - 4.0 * q
            out[level] = maskf * (q + sign * half * other[level] + 0.1 * lap)


def ocean_base(plan, u, v, from_west, from_east, from_south, from_north, mask, coriolis):
    return pl.pallas_call(
        functools.partial(ocean_base_kernel, plan),
        out_shape=[jax.ShapeDtypeStruct(u.shape, F32)] * 2,
        in_specs=[VMEM] * 8,
        out_specs=[VMEM] * 2,
        compiler_params=PARAMS,
        name="ocean_base",
    )(u, v, from_west, from_east, from_south, from_north, mask, coriolis)


def remap_kernel(own, left, right, cell, offset, weight, stress, drift, east, west, north, south, table):
    ocean_x, ocean_y = cell.shape[1:]
    width = own.shape[1]
    ratio = ocean_x // width
    taps = cell.shape[0]
    for q in range(BULK):
        for b, ref in enumerate((left, own, right)):
            for r in range(ratio):
                table[q, pl.ds(b * width * ratio + r, width, stride=ratio), :] = ref[q]
    for t in range(ocean_x // 8):
        for m in range(ocean_y // LANES):
            rows, lanes = (pl.ds(8 * t, 8), pl.ds(m * LANES, LANES))
            at = [cell[p, rows, lanes] for p in range(taps)]
            off = [offset[p, rows, lanes] for p in range(taps)]
            w = [weight[p, rows, lanes] for p in range(taps)]
            acc = [jnp.zeros((8, LANES), F32) for _ in range(BULK)]
            for o in range(2 * width + 1):
                slabs = [table[q, pl.ds(8 * t + ratio * o, 8), :] for q in range(BULK)]
                for p in range(taps):
                    wp = jnp.where(off[p] == o, w[p], 0.0)
                    for q in range(BULK):
                        got = jnp.take_along_axis(slabs[q], at[p], axis=1, mode="promise_in_bounds")
                        acc[q] = acc[q] + wp * got
            for q in range(3):
                stress[q, rows, lanes] = acc[q]
            for q in range(2):
                drift[q, rows, lanes] = acc[3 + q]
    last = ocean_x - 1
    for out, row in ((east, last), (west, 0)):
        out[...] = jnp.zeros_like(out)
        for q in range(2):
            for m in range(ocean_y // LANES):
                n = q * (ocean_y // LANES) + m
                out[n : n + 1, :] = stress[q, row : row + 1, m * LANES : (m + 1) * LANES]
    for out, m, source in ((north, ocean_y - LANES, LANES - 1), (south, 0, 0)):
        acc = jnp.zeros((ocean_x, LANES), F32)
        for q in range(2):
            acc = to_lane(acc, stress[1 + q, :, m : m + LANES], source, q, lanes_of(ocean_x))
        out[...] = acc


def remap(own, left, right, cell, offset, weight):
    taps, ocean_x, ocean_y = cell.shape
    width = own.shape[1]
    side = jax.ShapeDtypeStruct((8 * pl.cdiv(2 * ocean_y // LANES, 8), LANES), F32)
    end = jax.ShapeDtypeStruct((ocean_x, LANES), F32)
    return pl.pallas_call(
        remap_kernel,
        out_shape=[
            jax.ShapeDtypeStruct((3, ocean_x, ocean_y), F32),
            jax.ShapeDtypeStruct((2, ocean_x, ocean_y), F32),
            side,
            side,
            end,
            end,
        ],
        in_specs=[VMEM] * 6,
        out_specs=[VMEM] * 6,
        scratch_shapes=[pltpu.VMEM((BULK, 3 * ocean_x, LANES), F32)],
        compiler_params=PARAMS,
        name="remap",
    )(own, left, right, cell, offset, weight)


def ocean_final_kernel(stress, drift, from_west, from_east, from_south, from_north, base_u, base_v, mask, coriolis, new_u, new_v):
    levels, ocean_x, ocean_y = base_u.shape
    tiles = ocean_y // LANES

    def line(buffer, q):
        return jnp.concatenate([buffer[q * tiles + m : q * tiles + m + 1, :] for m in range(tiles)], axis=1)

    zero_line = jnp.zeros((1, ocean_y), F32)
    zero_end = jnp.zeros((ocean_x, 1), F32)
    grad = []
    for q in range(3):
        lon = q < 2
        lat = q > 0
        before, after, below, above = ocean_shifts(
            stress[q],
            line(from_west, q) if lon else zero_line,
            line(from_east, q) if lon else zero_line,
            from_south[:, q - 1 : q] if lat else zero_end,
            from_north[:, q - 1 : q] if lat else zero_end,
        )
        grad.append((0.5 * (after - before), 0.5 * (above - below)))
    force_x = -(grad[0][0] + grad[1][1])
    force_y = -(grad[1][0] + grad[2][1])
    maskf = mask[...].astype(F32)
    half = 0.5 * coriolis[...]
    add_u = maskf * (half * drift[1] + 0.5 * force_x)
    add_v = maskf * (0.5 * force_y - half * drift[0])
    for level in range(levels):
        decay = np.float32(np.exp(np.float32(-level / 3.0)))
        new_u[level] = base_u[level] + decay * add_u
        new_v[level] = base_v[level] + decay * add_v


def ocean_final(stress, drift, halos, base_u, base_v, mask, coriolis):
    return pl.pallas_call(
        ocean_final_kernel,
        out_shape=[jax.ShapeDtypeStruct(base_u.shape, F32)] * 2,
        in_specs=[VMEM] * 10,
        out_specs=[VMEM] * 2,
        compiler_params=PARAMS,
        name="ocean_final",
    )(stress, drift, *halos, base_u, base_v, mask, coriolis)


def send(value, axis, step, wrap):
    count = lax.axis_size(axis)
    pairs = [(i, (i + step) % count) for i in range(count) if wrap or 0 <= i + step < count]
    return lax.ppermute(value, axis, pairs)


def exchange(east, west, north, south):
    from_west = send(east, "lon", 1, True)
    from_east = send(west, "lon", -1, True)
    from_south = send(north, "lat", 1, False)
    from_north = send(south, "lat", -1, False)
    return from_west, from_east, from_south, from_north


def local(
    spectrum,
    sea_mask,
    transfer,
    bulk_weight,
    remap_cell,
    remap_weight,
    ocean_u,
    ocean_v,
    ocean_mask,
    coriolis,
):
    comps, width_x, width_y = spectrum.shape
    plan = Plan(comps)
    spec4 = spectrum.reshape(comps, width_x, 1, width_y)
    east, west = pack_lon(plan, spec4, sea_mask, ocean_u, ocean_v)
    north, south = pack_lat(plan, spec4, sea_mask, ocean_u, ocean_v)
    from_west, from_east, from_south, from_north = exchange(east, west, north, south)

    coefs = jnp.concatenate([jnp.asarray(plan.coef), bulk_weight.T], axis=1)
    total_y = width_y * lax.axis_size("lat")
    taps_first = remap_cell.transpose(2, 0, 1)
    offset = taps_first // total_y
    cell = taps_first - offset * total_y - lax.axis_index("lat") * width_y
    weight = remap_weight.transpose(2, 0, 1)
    line = coriolis[None, :]

    middle, part, up, down = interior(plan, 0, (spec4,), from_south, from_north, transfer, coefs, sea_mask)
    base_u, base_v = ocean_base(
        plan, ocean_u, ocean_v, from_west, from_east, from_south, from_north, ocean_mask, line
    )
    sides, east, west, north, south = edges(
        plan, 0, part, from_west, from_east, transfer, coefs, sea_mask, up, down
    )
    from_west, from_east, from_south, from_north = exchange(east, west, north, south)
    out4, part, bulk = interior(plan, 1, (sides, middle), from_south, from_north, transfer, coefs, sea_mask)
    sides, bulk = edges(plan, 1, part, from_west, from_east, transfer, coefs, sea_mask, bulk)
    left = send(bulk, "lon", 1, True)
    right = send(bulk, "lon", -1, True)
    state = finish(sides, out4).reshape(spectrum.shape)
    stress, drift, east, west, north, south = remap(bulk, left, right, cell, offset, weight)
    halos = exchange(east, west, north, south)
    new_u, new_v = ocean_final(stress, drift, halos, base_u, base_v, ocean_mask, line)
    return (state, new_u, new_v)


def solution(mesh):
    placed = (
        P(None, "lon", "lat"),
        P("lon", "lat"),
        P(),
        P(),
        P("lon", "lat", None),
        P("lon", "lat", None),
        P(None, "lon", "lat"),
        P(None, "lon", "lat"),
        P("lon", "lat"),
        P("lat"),
    )
    return jax.shard_map(
        local,
        mesh=mesh,
        in_specs=placed,
        out_specs=(P(None, "lon", "lat"), P(None, "lon", "lat"), P(None, "lon", "lat")),
        check_vma=False,
    )
```

time: 374 us -> 141 us (0.38)
  local copies, waits for them, and re-layouts: 220 us -> 13.5 us
  other arithmetic: 91.3 us -> 0.12 us
  Pallas kernels: 0 us -> 83.3 us
  matrix products: 11.5 us -> 0 us
  starting transfers between devices: 37.4 us -> 33.4 us
    gather x1 -> x0, local copies, waits for them, and re-layouts: 122 us -> none  [local(): jnp.take(near, position.reshape(-1), axis=1)]
    pallas_call x0 -> x10, Pallas kernels: none -> 83.3 us  [the longest x2 39.7 us: interior(): pl.pallas_call(functools.partial(interior_kernel, plan, step), out_shape=...]
    slice x12 -> x0, local copies, waits for them, and re-layouts: 57.1 us -> none  [the longest x4 19.7 us: lat_sides(): below = passed_along(centre[:, :, -1:], 'lat', 1)]
    reduce_sum x1 -> x0, other arithmetic: 55.7 us -> none  [local(): forcing = jnp.sum(taken * remap_weight[None], axis=-1)]
    unnamed x3 -> x0, other arithmetic: 26.5 us -> none
    ppermute x4 -> x0, local copies, waits for them, and re-layouts: 15.2 us -> none  [passed_along(): lax.ppermute(value, axis, [(source, source + steps) for source in range(f...]
    dot_general x3 -> x0, matrix products: 11.5 us -> none  [the longest x2 8.62 us: source(): jnp.dot(transfer, flat, preferred_element_type=jnp.float32)]
    mul x6 -> x0, other arithmetic: 7.08 us -> none  [the longest x1 3.53 us: local(): state = spectrum * maskf]
  transfers between devices with their start and end apart: 14 -> 14, of which waited for: 3 -> 4; matrix products, arithmetic and copies ran while one was open for 19% -> 0% of each run, Pallas kernels for 0% -> 30%
where the time goes in v1:
time: 141 us; the launch traced here: 140 us
  Pallas kernels  83.3 us (59%)
  starting transfers between devices  33.4 us (24%)
  local copies, waits for them, and re-layouts  13.5 us (10%)
  waiting for transfers between devices  8.88 us (6%)
    pallas_call x2, Pallas kernels, interior(): pl.pallas_call(functools.partial(interior_kernel, plan, step), out_shape=...  39.7 us
    ppermute x14, starting transfers between devices, send(): return lax.ppermute(value, axis, pairs)  33.4 us
    pallas_call x2, Pallas kernels, edges(): pl.pallas_call(functools.partial(edges_kernel, plan, step), out_shape=out...  23.7 us
    unnamed x37, local copies, waits for them, and re-layouts  13.3 us
    pallas_call x1, Pallas kernels, pack_lat(): pl.pallas_call(functools.partial(pack_lat_kernel, plan), out_shape=[jax.S...  11.4 us
    ppermute x14, waiting for transfers between devices, send(): return lax.ppermute(value, axis, pairs)  8.88 us
    pallas_call x1, Pallas kernels, remap(): pl.pallas_call(remap_kernel, out_shape=[jax.ShapeDtypeStruct((3, ocean_x,...  5.31 us
  transfers between devices with their start and end apart: 14, of which 4 were waited for; matrix products, arithmetic and copies ran while one was open for 0% of the time, Pallas kernels for 30%

profile of v1, /device:TPU:1, one launch (start us, length us, event | category | flops | bytes accessed | tf_op | source)
XLA Modules:
  0.0 140.1 jit_solution(3774525786673334521)
XLA Ops:
  0.6 2.5 %copy-done.3 = f32[1296,8,128]{2,1,0:T(8,128)S(1)} copy-done((f32[1296,8,128]{2,1,0:T(8,128)S(1)}, f32[1296,8,128]{2,1,0:T(8,128)}, u32[]{:S(2)}) %copy-start.3) | copy-done | bytes 5308440
  5.7 11.4 %pack_lat.1 = (f32[680,128]{1,0:T(8,128)}, f32[680,128]{1,0:T(8,128)S(1)}) custom-call(f32[1296,8,1,128]{3,2,1,0:T(1,128)S(1)} %bitcast.28, s32[8,128]{1,0:T(8,128)S(1)} %copy-done.10, f32[8,24,384]{2,1,0:T(8,128)S(1)} %copy-done.6, f32[8,24,384]{2,1,0:T(8,128)S(1)} %copy-done.8), custom_call_target="tpu_custom_call" | custom-call | tf_op jit(solution)/shard_map/pack_lat/pallas_call | solution.py:206
  17.2 4.6 %collective-permute-start = (f32[680,128]{1,0:T(8,128)}, f32[680,128]{1,0:T(8,128)S(1)}, u32[]{:S(2)}, u32[]{:S(2)}) collective-permute-start(f32[680,128]{1,0:T(8,128)} %get-tuple-element.31), channel_id=1, source_target_pairs={{0,1},{1,2},{2,3},{4,5},{5,6},{6,7},{8,9},{9,10},{10,11},{12,13},{... | collective-permute-start | bytes 1044488 | tf_op jit(solution)/shard_map/ppermute | solution.py:668
  21.9 1.9 %collective-permute-start.1 = (f32[680,128]{1,0:T(8,128)S(1)}, f32[680,128]{1,0:T(8,128)S(1)}, u32[]{:S(2)}, u32[]{:S(2)}) collective-permute-start(f32[680,128]{1,0:T(8,128)S(1)} %get-tuple-element.32), channel_id=1, source_target_pairs={{1,0},{2,1},{3,2},{5,4},{6,5},{7,6},{9,8},{10,9},{11,10},{13,12},{... | collective-permute-start | bytes 1044488 | tf_op jit(solution)/shard_map/ppermute | solution.py:668
  25.7 3.1 %collective-permute-start.3 = (f32[704,128]{1,0:T(8,128)S(1)}, f32[704,128]{1,0:T(8,128)S(1)}, u32[]{:S(2)}, u32[]{:S(2)}) collective-permute-start(f32[704,128]{1,0:T(8,128)S(1)} %get-tuple-element.35), channel_id=1, source_target_pairs={{0,28},{4,0},{8,4},{12,8},{16,12},{20,16},{24,20},{28,24},{1,29},{... | collective-permute-start | bytes 1081352 | tf_op jit(solution)/shard_map/ppermute | solution.py:668
  29.0 1.7 %collective-permute-done.1.refs_2_.from_north = f32[680,128]{1,0:T(8,128)S(1)} collective-permute-done((f32[680,128]{1,0:T(8,128)S(1)}, f32[680,128]{1,0:T(8,128)S(1)}, u32[]{:S(2)}, u32[]{:S(2)}) %collective-permute-start.1) | collective-permute-done | bytes 348192 | tf_op jit(solution)/shard_map/ppermute | solution.py:668
  30.8 2.0 %copy-done = bf16[1296,1296]{1,0:T(8,128)(2,1)S(1)} copy-done((bf16[1296,1296]{1,0:T(8,128)(2,1)S(1)}, bf16[1296,1296]{1,0:T(8,128)(2,1)}, u32[]{:S(2)}) %copy-start) | copy-done | bytes 3359256
  32.8 22.1 %interior.2 = (f32[6,1296,128]{2,1,0:T(8,128)S(1)}, f32[2,1296,128]{2,1,0:T(8,128)S(1)}, f32[656,128]{1,0:T(8,128)S(1)}, f32[656,128]{1,0:T(8,128)S(1)}) custom-call(f32[1296,8,1,128]{3,2,1,0:T(1,128)} %bitcast.27, f32[680,128]{1,0:T(8,128)S(1)} %collective-permute-done.refs_1_.from_south, f32[680,128]{1,0:T(8,128)S(1)} %collective-permute-done.1.refs_2_.from_north, ...), custom_call_target="tpu_custom_call" | custom-call | flops 2579890176 | bytes 20971520 | tf_op jit(solution)/shard_map/interior/pallas_call | solution.py:377
  55.0 1.9 %copy-done.4 = f32[6,1296,128]{2,1,0:T(8,128)} copy-done((f32[6,1296,128]{2,1,0:T(8,128)}, f32[6,1296,128]{2,1,0:T(8,128)S(1)}, u32[]{:S(2)}) %copy-start.4) | copy-done | bytes 3981336
  56.9 14.4 %edges.2 = (f32[2,1296,128]{2,1,0:T(8,128)S(1)}, f32[656,128]{1,0:T(8,128)}, f32[656,128]{1,0:T(8,128)}, f32[656,128]{1,0:T(8,128)}, f32[656,128]{1,0:T(8,128)}) custom-call(f32[2,1296,128]{2,1,0:T(8,128)S(1)} %get-tuple-element.33.refs_0_, f32[704,128]{1,0:T(8,128)S(1)} %collective-permute-done.2.refs_1_.from_west, ...), custom_call_target="tpu_custom_call" | custom-call | flops 859963392 | bytes 8388608 | tf_op jit(solution)/shard_map/edges/pallas_call | solution.py:469
  71.3 2.3 %collective-permute-start.4 = (f32[656,128]{1,0:T(8,128)}, f32[656,128]{1,0:T(8,128)}, u32[]{:S(2)}, u32[]{:S(2)}) collective-permute-start(f32[656,128]{1,0:T(8,128)} %get-tuple-element.40), channel_id=1, source_target_pairs={{0,1},{1,2},{2,3},{4,5},{5,6},{6,7},{8,9},{9,10},{10,11},{12,13},{... | collective-permute-start | bytes 1007624 | tf_op jit(solution)/shard_map/ppermute | solution.py:668
  73.6 2.8 %collective-permute-start.5 = (f32[656,128]{1,0:T(8,128)}, f32[656,128]{1,0:T(8,128)}, u32[]{:S(2)}, u32[]{:S(2)}) collective-permute-start(f32[656,128]{1,0:T(8,128)} %get-tuple-element.41), channel_id=1, source_target_pairs={{1,0},{2,1},{3,2},{5,4},{6,5},{7,6},{9,8},{10,9},{11,10},{13,12},{... | collective-permute-start | bytes 1007624 | tf_op jit(solution)/shard_map/ppermute | solution.py:668
  77.7 3.1 %collective-permute-start.7 = (f32[656,128]{1,0:T(8,128)}, f32[656,128]{1,0:T(8,128)}, u32[]{:S(2)}, u32[]{:S(2)}) collective-permute-start(f32[656,128]{1,0:T(8,128)} %get-tuple-element.44), channel_id=1, source_target_pairs={{0,28},{4,0},{8,4},{12,8},{16,12},{20,16},{24,20},{28,24},{1,29},{... | collective-permute-start | bytes 1007624 | tf_op jit(solution)/shard_map/ppermute | solution.py:668
  80.8 1.9 %collective-permute-done.5.refs_3_ = f32[656,128]{1,0:T(8,128)} collective-permute-done((f32[656,128]{1,0:T(8,128)}, f32[656,128]{1,0:T(8,128)}, u32[]{:S(2)}, u32[]{:S(2)}) %collective-permute-start.5) | collective-permute-done | bytes 335904 | tf_op jit(solution)/shard_map/ppermute | solution.py:668
  82.7 2.0 %copy-done.2 = bf16[1296,1296]{1,0:T(8,128)(2,1)S(1)} copy-done((bf16[1296,1296]{1,0:T(8,128)(2,1)S(1)}, bf16[1296,1296]{1,0:T(8,128)(2,1)}, u32[]{:S(2)}) %copy-start.2) | copy-done | bytes 3359256
  84.7 2.1 %copy-done.5 = f32[6,1296,128]{2,1,0:T(8,128)S(1)} copy-done((f32[6,1296,128]{2,1,0:T(8,128)S(1)}, f32[6,1296,128]{2,1,0:T(8,128)}, u32[]{:S(2)}) %copy-start.5) | copy-done | bytes 3981336
  86.9 17.6 %interior.3 = (f32[1296,8,1,128]{3,2,1,0:T(1,128)}, f32[2,1296,128]{2,1,0:T(8,128)S(1)}, f32[5,8,128]{2,1,0:T(8,128)S(1)}) custom-call(f32[2,1296,128]{2,1,0:T(8,128)S(1)} %get-tuple-element.38.refs_0_, f32[6,1296,128]{2,1,0:T(8,128)S(1)} %copy-done.5, f32[656,128]{1,0:T(8,128)} %collective-permute-done.4.refs_2_, ...), custom_call_target="tpu_custom_call" | custom-call | flops 2579890176 | bytes 20971520 | tf_op jit(solution)/shard_map/interior/pallas_call | solution.py:377
  104.5 9.3 %edges.3 = (f32[2,1296,128]{2,1,0:T(8,128)S(1)}, f32[5,8,128]{2,1,0:T(8,128)S(1)}) custom-call(f32[2,1296,128]{2,1,0:T(8,128)S(1)} %get-tuple-element.42.refs_0_, f32[656,128]{1,0:T(8,128)} %collective-permute-done.6.refs_1_, f32[656,128]{1,0:T(8,128)} %collective-permute-done.7.refs_2_, bf16[1296,1296]{1,0:T(8,128)(2,1)S(1)} %copy-done.2, ...), custom_call_target="tpu_custom_call" | custom-call | flops 859963392 | bytes 8388608 | tf_op jit(solution)/shard_map/edges/pallas_call | solution.py:469
  113.8 3.9 %collective-permute-start.9 = (f32[5,8,128]{2,1,0:T(8,128)S(1)}, f32[5,8,128]{2,1,0:T(8,128)S(1)}, u32[]{:S(2)}, u32[]{:S(2)}) collective-permute-start(f32[5,8,128]{2,1,0:T(8,128)S(1)} %get-tuple-element.48.own), channel_id=1, source_target_pairs={{0,28},{4,0},{8,4},{12,8},{16,12},{20,16},{24,20},{28,24},{1,29},{... | collective-permute-start | bytes 61448 | tf_op jit(solution)/shard_map/ppermute | solution.py:668
  118.7 4.4 %collective-permute-done.8.left = f32[5,8,128]{2,1,0:T(8,128)S(1)} collective-permute-done((f32[5,8,128]{2,1,0:T(8,128)S(1)}, f32[5,8,128]{2,1,0:T(8,128)S(1)}, u32[]{:S(2)}, u32[]{:S(2)}) %collective-permute-start.8) | collective-permute-done | bytes 20512 | tf_op jit(solution)/shard_map/ppermute | solution.py:668
  123.1 5.3 %remap.1 = (f32[3,24,384]{2,1,0:T(8,128)S(1)}, f32[2,24,384]{2,1,0:T(8,128)S(1)}, f32[8,128]{1,0:T(8,128)S(1)}, f32[8,128]{1,0:T(8,128)S(1)}, f32[24,128]{1,0:T(8,128)S(1)}, /*index=5*/f32[24,128]{1,0:T(8,128)S(1)}) custom-call(f32[5,8,128]{2,1,0:T(8,128)S(1)} %get-tuple-element.48.own, f32[5,8,128]{2,1,0:T(8,128)S(1)} %collective-permute-done.8.left, ...), custom_call_target="tpu_custom_call" | custom-call | tf_op jit(solution)/shard_map/remap/pallas_call | solution.py:603
  128.4 2.9 %collective-permute-start.12 = (f32[24,128]{1,0:T(8,128)S(1)}, f32[24,128]{1,0:T(8,128)S(1)}, u32[]{:S(2)}, u32[]{:S(2)}) collective-permute-start(f32[24,128]{1,0:T(8,128)S(1)} %get-tuple-element.53), channel_id=1, source_target_pairs={{0,1},{1,2},{2,3},{4,5},{5,6},{6,7},{8,9},{9,10},{10,11},{12,13},{... | collective-permute-start | bytes 36872 | tf_op jit(solution)/shard_map/ppermute | solution.py:668
  131.3 1.9 %collective-permute-start.13 = (f32[24,128]{1,0:T(8,128)S(1)}, f32[24,128]{1,0:T(8,128)S(1)}, u32[]{:S(2)}, u32[]{:S(2)}) collective-permute-start(f32[24,128]{1,0:T(8,128)S(1)} %get-tuple-element.54), channel_id=1, source_target_pairs={{1,0},{2,1},{3,2},{5,4},{6,5},{7,6},{9,8},{10,9},{11,10},{13,12},{... | collective-permute-start | bytes 36872 | tf_op jit(solution)/shard_map/ppermute | solution.py:668
  133.3 4.1 %collective-permute-start.11 = (f32[8,128]{1,0:T(8,128)S(1)}, f32[8,128]{1,0:T(8,128)S(1)}, u32[]{:S(2)}, u32[]{:S(2)}) collective-permute-start(f32[8,128]{1,0:T(8,128)S(1)} %get-tuple-element.52), channel_id=1, source_target_pairs={{0,28},{4,0},{8,4},{12,8},{16,12},{20,16},{24,20},{28,24},{1,29},{... | collective-permute-start | bytes 12296 | tf_op jit(solution)/shard_map/ppermute | solution.py:668
  (55 shorter events, 9.6 us)
Async XLA Ops:
  17.2 11.6 %copy-start.15 = (f32[5,1296]{1,0:T(8,128)S(1)}, f32[5,1296]{1,0:T(8,128)}, u32[]{:S(2)}) copy-start(f32[5,1296]{1,0:T(8,128)} %param.14) | copy-start | bytes 77764
  17.2 11.6 %copy-start.16 = (f32[1296,3]{0,1:T(4,128)S(1)}, f32[1296,3]{0,1:T(4,128)}, u32[]{:S(2)}) copy-start(f32[1296,3]{0,1:T(4,128)} %constant.26.clone) | copy-start | bytes 46660
  17.2 13.6 %copy-start.11 = (s32[8,128]{1,0:T(8,128)S(1)}, s32[8,128]{1,0:T(8,128)}, u32[]{:S(2)}) copy-start(s32[8,128]{1,0:T(8,128)} %refs_5_.5) | copy-start | bytes 12292
  17.2 11.8 %collective-permute-start = (f32[680,128]{1,0:T(8,128)}, f32[680,128]{1,0:T(8,128)S(1)}, u32[]{:S(2)}, u32[]{:S(2)}) collective-permute-start(f32[680,128]{1,0:T(8,128)} %get-tuple-element.31), channel_id=1, source_target_pairs={{0,1},{1,2},{2,3},{4,5},{5,6},{6,7},{8,9},{9,10},{10,11},{12,13},{... | collective-permute-start | bytes 1044488 | tf_op jit(solution)/shard_map/ppermute | solution.py:668
  21.9 8.9 %collective-permute-start.1 = (f32[680,128]{1,0:T(8,128)S(1)}, f32[680,128]{1,0:T(8,128)S(1)}, u32[]{:S(2)}, u32[]{:S(2)}) collective-permute-start(f32[680,128]{1,0:T(8,128)S(1)} %get-tuple-element.32), channel_id=1, source_target_pairs={{1,0},{2,1},{3,2},{5,4},{6,5},{7,6},{9,8},{10,9},{11,10},{13,12},{... | collective-permute-start | bytes 1044488 | tf_op jit(solution)/shard_map/ppermute | solution.py:668
  24.4 32.5 %collective-permute-start.2 = (f32[704,128]{1,0:T(8,128)S(1)}, f32[704,128]{1,0:T(8,128)S(1)}, u32[]{:S(2)}, u32[]{:S(2)}) collective-permute-start(f32[704,128]{1,0:T(8,128)S(1)} %get-tuple-element.34), channel_id=1, source_target_pairs={{0,4},{4,8},{8,12},{12,16},{16,20},{20,24},{24,28},{28,0},{1,5},{5... | collective-permute-start | bytes 1081352 | tf_op jit(solution)/shard_map/ppermute | solution.py:668
  25.7 31.2 %collective-permute-start.3 = (f32[704,128]{1,0:T(8,128)S(1)}, f32[704,128]{1,0:T(8,128)S(1)}, u32[]{:S(2)}, u32[]{:S(2)}) collective-permute-start(f32[704,128]{1,0:T(8,128)S(1)} %get-tuple-element.35), channel_id=1, source_target_pairs={{0,28},{4,0},{8,4},{12,8},{16,12},{20,16},{24,20},{28,24},{1,29},{... | collective-permute-start | bytes 1081352 | tf_op jit(solution)/shard_map/ppermute | solution.py:668
  32.8 24.1 %copy-start.1 = (bf16[1296,1296]{1,0:T(8,128)(2,1)S(1)}, bf16[1296,1296]{1,0:T(8,128)(2,1)}, u32[]{:S(2)}) copy-start(bf16[1296,1296]{1,0:T(8,128)(2,1)} %refs_3_.5) | copy-start | bytes 10077700
  71.3 9.5 %collective-permute-start.4 = (f32[656,128]{1,0:T(8,128)}, f32[656,128]{1,0:T(8,128)}, u32[]{:S(2)}, u32[]{:S(2)}) collective-permute-start(f32[656,128]{1,0:T(8,128)} %get-tuple-element.40), channel_id=1, source_target_pairs={{0,1},{1,2},{2,3},{4,5},{5,6},{6,7},{8,9},{9,10},{10,11},{12,13},{... | collective-permute-start | bytes 1007624 | tf_op jit(solution)/shard_map/ppermute | solution.py:668
  73.6 9.1 %collective-permute-start.5 = (f32[656,128]{1,0:T(8,128)}, f32[656,128]{1,0:T(8,128)}, u32[]{:S(2)}, u32[]{:S(2)}) collective-permute-start(f32[656,128]{1,0:T(8,128)} %get-tuple-element.41), channel_id=1, source_target_pairs={{1,0},{2,1},{3,2},{5,4},{6,5},{7,6},{9,8},{10,9},{11,10},{13,12},{... | collective-permute-start | bytes 1007624 | tf_op jit(solution)/shard_map/ppermute | solution.py:668
  76.4 28.1 %collective-permute-start.6 = (f32[656,128]{1,0:T(8,128)}, f32[656,128]{1,0:T(8,128)}, u32[]{:S(2)}, u32[]{:S(2)}) collective-permute-start(f32[656,128]{1,0:T(8,128)} %get-tuple-element.43), channel_id=1, source_target_pairs={{0,4},{4,8},{8,12},{12,16},{16,20},{20,24},{24,28},{28,0},{1,5},{5... | collective-permute-start | bytes 1007624 | tf_op jit(solution)/shard_map/ppermute | solution.py:668
  77.7 26.8 %collective-permute-start.7 = (f32[656,128]{1,0:T(8,128)}, f32[656,128]{1,0:T(8,128)}, u32[]{:S(2)}, u32[]{:S(2)}) collective-permute-start(f32[656,128]{1,0:T(8,128)} %get-tuple-element.44), channel_id=1, source_target_pairs={{0,28},{4,0},{8,4},{12,8},{16,12},{20,16},{24,20},{28,24},{1,29},{... | collective-permute-start | bytes 1007624 | tf_op jit(solution)/shard_map/ppermute | solution.py:668
  104.4 13.3 %copy-start.14 = (s32[24,384,4]{1,2,0:T(4,128)S(1)}, s32[24,384,4]{1,2,0:T(4,128)}, u32[]{:S(2)}) copy-start(s32[24,384,4]{1,2,0:T(4,128)} %param.15) | copy-start | bytes 442372
  104.5 13.4 %copy-start.13 = (f32[24,384,4]{1,2,0:T(4,128)S(1)}, f32[24,384,4]{1,2,0:T(4,128)}, u32[]{:S(2)}) copy-start(f32[24,384,4]{1,2,0:T(4,128)} %param.16) | copy-start | bytes 442372
  104.5 33.0 %copy-start.17 = (f32[384]{0:T(512)S(1)}, f32[384]{0:T(512)}, u32[]{:S(2)}) copy-start(f32[384]{0:T(512)} %param.20) | copy-start | bytes 4612
  104.5 33.0 %copy-start.7 = (f32[8,24,384]{2,1,0:T(8,128)S(1)}, f32[8,24,384]{2,1,0:T(8,128)}, u32[]{:S(2)}) copy-start(f32[8,24,384]{2,1,0:T(8,128)} %u.5) | copy-start | bytes 884740
  104.5 33.0 %copy-start.9 = (f32[8,24,384]{2,1,0:T(8,128)S(1)}, f32[8,24,384]{2,1,0:T(8,128)}, u32[]{:S(2)}) copy-start(f32[8,24,384]{2,1,0:T(8,128)} %v.5) | copy-start | bytes 884740
  104.5 32.9 %copy-start.12 = (s32[24,384]{1,0:T(8,128)S(1)}, s32[24,384]{1,0:T(8,128)}, u32[]{:S(2)}) copy-start(s32[24,384]{1,0:T(8,128)} %mask.7) | copy-start | bytes 110596
  113.8 4.9 %collective-permute-start.9 = (f32[5,8,128]{2,1,0:T(8,128)S(1)}, f32[5,8,128]{2,1,0:T(8,128)S(1)}, u32[]{:S(2)}, u32[]{:S(2)}) collective-permute-start(f32[5,8,128]{2,1,0:T(8,128)S(1)} %get-tuple-element.48.own), channel_id=1, source_target_pairs={{0,28},{4,0},{8,4},{12,8},{16,12},{20,16},{24,20},{28,24},{1,29},{... | collective-permute-start | bytes 61448 | tf_op jit(solution)/shard_map/ppermute | solution.py:668
  117.8 5.3 %collective-permute-start.8 = (f32[5,8,128]{2,1,0:T(8,128)S(1)}, f32[5,8,128]{2,1,0:T(8,128)S(1)}, u32[]{:S(2)}, u32[]{:S(2)}) collective-permute-start(f32[5,8,128]{2,1,0:T(8,128)S(1)} %get-tuple-element.48.own), channel_id=1, source_target_pairs={{0,4},{4,8},{8,12},{12,16},{16,20},{20,24},{24,28},{28,0},{1,5},{5... | collective-permute-start | bytes 61448 | tf_op jit(solution)/shard_map/ppermute | solution.py:668
  128.4 10.7 %collective-permute-start.12 = (f32[24,128]{1,0:T(8,128)S(1)}, f32[24,128]{1,0:T(8,128)S(1)}, u32[]{:S(2)}, u32[]{:S(2)}) collective-permute-start(f32[24,128]{1,0:T(8,128)S(1)} %get-tuple-element.53), channel_id=1, source_target_pairs={{0,1},{1,2},{2,3},{4,5},{5,6},{6,7},{8,9},{9,10},{10,11},{12,13},{... | collective-permute-start | bytes 36872 | tf_op jit(solution)/shard_map/ppermute | solution.py:668
  131.3 7.8 %collective-permute-start.13 = (f32[24,128]{1,0:T(8,128)S(1)}, f32[24,128]{1,0:T(8,128)S(1)}, u32[]{:S(2)}, u32[]{:S(2)}) collective-permute-start(f32[24,128]{1,0:T(8,128)S(1)} %get-tuple-element.54), channel_id=1, source_target_pairs={{1,0},{2,1},{3,2},{5,4},{6,5},{7,6},{9,8},{10,9},{11,10},{13,12},{... | collective-permute-start | bytes 36872 | tf_op jit(solution)/shard_map/ppermute | solution.py:668
  133.2 5.9 %collective-permute-start.10 = (f32[8,128]{1,0:T(8,128)S(1)}, f32[8,128]{1,0:T(8,128)S(1)}, u32[]{:S(2)}, u32[]{:S(2)}) collective-permute-start(f32[8,128]{1,0:T(8,128)S(1)} %get-tuple-element.51), channel_id=1, source_target_pairs={{0,4},{4,8},{8,12},{12,16},{16,20},{20,24},{24,28},{28,0},{1,5},{5... | collective-permute-start | bytes 12296 | tf_op jit(solution)/shard_map/ppermute | solution.py:668
  133.3 5.8 %collective-permute-start.11 = (f32[8,128]{1,0:T(8,128)S(1)}, f32[8,128]{1,0:T(8,128)S(1)}, u32[]{:S(2)}, u32[]{:S(2)}) collective-permute-start(f32[8,128]{1,0:T(8,128)S(1)} %get-tuple-element.52), channel_id=1, source_target_pairs={{0,28},{4,0},{8,4},{12,8},{16,12},{20,16},{24,20},{28,24},{1,29},{... | collective-permute-start | bytes 12296 | tf_op jit(solution)/shard_map/ppermute | solution.py:668
  (8 other events, 13.3 us)

commit v2 on v1

v2 whole, which is shorter than its diff:
```python
import functools

import jax
import jax.numpy as jnp
import numpy as np
from jax import lax
from jax.experimental import pallas as pl
from jax.experimental.pallas import tpu as pltpu
from jax.sharding import PartitionSpec as P

NFREQ = 36
STEP = 16
LANES = 128
BULK = 5
GROUPS = 4
OFFSETS = 17
BLOCK = 80
F32 = jnp.float32
VMEM = pl.BlockSpec(memory_space=pltpu.VMEM)
ANY = pl.BlockSpec(memory_space=pl.ANY)
HBM = pl.BlockSpec(memory_space=pltpu.HBM)
PARAMS = pltpu.CompilerParams(vmem_limit_bytes=24 << 20)
CHEAP = pl.CostEstimate(flops=1, bytes_accessed=1, transcendentals=0)


def pinned(*arrays):
    return [pltpu.with_memory_space_constraint(x, pltpu.HBM) for x in arrays]


class Plan:
    def __init__(self, comps):
        dirs = comps // NFREQ
        k = np.arange(comps)
        theta = 2.0 * np.pi * ((k // NFREQ) + 0.5) / dirs
        speed = 1.1 ** (-(k % NFREQ).astype(np.float64))
        cx = 0.45 * speed * np.cos(theta)
        cy = 0.45 * speed * np.sin(theta)
        self.comps = comps
        self.coef = np.stack([1.0 - np.abs(cx) - np.abs(cy), np.abs(cx), np.abs(cy)], 1).astype(np.float32)
        self.flag = {"x": cx > 0, "y": cy > 0}
        self.seg = {}
        for axis, step in (("x", 8), ("y", STEP)):
            for sign in (True, False):
                self.seg[axis, sign] = self.runs(self.flag[axis] == sign, step)

    def runs(self, flag, step):
        out = []
        for n in np.flatnonzero(flag.reshape(-1, step).any(1)):
            if out and out[-1][1] == n * step:
                out[-1][1] = int(n + 1) * step
            else:
                out.append([int(n) * step, int(n + 1) * step])
        return [(a, b) for a, b in out]

    def rows(self, axis, sign):
        return sum(b - a for a, b in self.seg[axis, sign])

    def lat_rows(self, sign):
        ((a, b),) = self.seg["y", sign]
        return -(-(b - a) // (GROUPS * STEP)) * STEP

    def lat_cuts(self):
        cuts = set()
        for sign in (True, False):
            ((a, b),) = self.seg["y", sign]
            cuts |= set(range(a, b, self.lat_rows(sign))) | {b}
        return cuts

    def lat_place(self, sign, first, last, width):
        ((a, _),) = self.seg["y", sign]
        group, row = divmod(first - a, self.lat_rows(sign))
        assert row + last - first <= self.lat_rows(sign) and (group + 1) * width <= LANES
        return slice(row, row + last - first), group * width

    def lat_blocks(self, sign, first=0, last=None):
        ((a, b),) = self.seg["y", sign]
        a, b = (max(a, first), b if last is None else min(b, last))
        return split(a, b, self.lat_cuts()) if a < b else []

    def shift(self, axis, sign, first):
        used = np.flatnonzero(self.flag[axis][first : first + STEP] == sign) + first
        if not len(used):
            return None
        base = 0
        for a, b in self.seg[axis, sign]:
            if a <= used[0] < b:
                at = base + first - a
                assert used[-1] < b and 0 <= at <= self.rows(axis, sign) - STEP
                return base - a
            base += b - a
        raise ValueError("no segment")

    def blocks(self):
        cuts = self.lat_cuts()
        return [(a, b, *rest) for first, last, *rest in self.regions() for a, b in split(first, last, cuts)]

    def regions(self):
        out = []
        for r in range(0, self.comps, STEP):
            sign = {}
            for axis in "xy":
                part = self.flag[axis][r : r + STEP]
                sign[axis] = 1 if part.all() else (0 if part.any() else -1)
            shifts = {(axis, s): self.shift(axis, s, r) for axis in "xy" for s in (True, False)}
            if out and sign["x"] and sign["y"] and out[-1][2:] == [sign["x"], sign["y"], shifts]:
                out[-1][1] = r + STEP
            else:
                out.append([r, r + STEP, sign["x"], sign["y"], shifts])
        return out


def split(first, last, cuts=(), most=BLOCK):
    out = []
    edges = [first] + sorted(c for c in cuts if first < c < last) + [last]
    for start, stop in zip(edges[:-1], edges[1:]):
        chunks = (stop - start) // STEP
        count = -(-chunks * STEP // most)
        at = [start + chunks * n // count * STEP for n in range(count + 1)]
        out += list(zip(at[:-1], at[1:]))
    return out


def lanes_of(rows):
    return lax.broadcasted_iota(jnp.int32, (rows, LANES), 1)


def picked(flag, first):
    row = lax.broadcasted_iota(jnp.int32, (STEP, LANES), 0)
    part = flag[first : first + STEP]
    out, n = (None, 0)
    while n < STEP:
        if not part[n]:
            n += 1
            continue
        m = n
        while m < STEP and part[m]:
            m += 1
        here = (row >= n) & (row < m)
        out = here if out is None else out | here
        n = m
    return out


def upwind(plan, axis, sign, first, from_plus, from_minus):
    if sign > 0:
        return from_plus()
    if sign < 0:
        return from_minus()
    plus, minus = (from_plus(), from_minus())
    where = picked(plan.flag[axis], first)
    zero = jnp.zeros((STEP, LANES), F32)
    if plus is None and minus is None:
        return None
    return jnp.where(where, zero if plus is None else plus, zero if minus is None else minus)


def pack_lon_kernel(plan, spec, mask, u, v, east, west, sides, maskv, sem):
    last_col, last_row, levels = (spec.shape[1] - 1, u.shape[1] - 8, u.shape[0])
    copies = [pltpu.make_async_copy(mask, maskv, sem.at[0])]
    for out, sign, col in ((east, True, last_col), (west, False, 0)):
        at = 0
        for a, b in plan.seg["x", sign]:
            copies.append(
                pltpu.make_async_copy(
                    spec.at[pl.ds(a, b - a), col, 0, :], out.at[pl.ds(at, b - a), :], sem.at[len(copies)]
                )
            )
            at += b - a
    for f, field in enumerate((u, v)):
        for side, row in enumerate((last_row, 0)):
            copies.append(
                pltpu.make_async_copy(field.at[:, pl.ds(row, 8), :], sides.at[f, side], sem.at[len(copies)])
            )
    for c in copies:
        c.start()
    for c in copies:
        c.wait()
    for side, (out, sign, col) in enumerate(((east, True, last_col), (west, False, 0))):
        at = plan.rows("x", sign)
        out[:at, :] = out[:at, :] * maskv[col : col + 1, :].astype(F32)
        for f in range(2):
            for m in range(u.shape[2] // LANES):
                out[at : at + levels, :] = sides[f, side, :, 7 - 7 * side, m * LANES : (m + 1) * LANES]
                at += levels


def pack_lon(plan, spec4, mask, u, v):
    extra = 2 * u.shape[0] * u.shape[2] // LANES
    segments = sum(len(plan.seg["x", s]) for s in (True, False))
    return pl.pallas_call(
        functools.partial(pack_lon_kernel, plan),
        out_shape=[jax.ShapeDtypeStruct((plan.rows("x", s) + extra, LANES), F32) for s in (True, False)],
        in_specs=[HBM] * 4,
        out_specs=[VMEM, VMEM],
        scratch_shapes=[
            pltpu.VMEM((2, 2, u.shape[0], 8, u.shape[2]), F32),
            pltpu.VMEM(mask.shape, mask.dtype),
            pltpu.SemaphoreType.DMA((segments + 5,)),
        ],
        compiler_params=PARAMS,
        name="pack_lon",
    )(*pinned(spec4, mask, u, v))


def to_lane(acc, column, source, lane, lanes):
    return jnp.where(lanes == lane, pltpu.roll(column, (lane - source) % LANES, 1), acc)


def pack_lat_kernel(plan, spec_hbm, mask, u_hbm, v_hbm, after, north, south, spec, u, v, maskv, sem):
    del after
    width_x = mask.shape[0]
    levels, ocean_x, ocean_y = u.shape
    last = ocean_y - LANES
    first = pltpu.make_async_copy(mask, maskv, sem.at[0])
    first.start()
    cuts = [a for a, _ in split(0, plan.comps)] + [plan.comps]
    parts = []
    for n in range(len(cuts) - 1):
        rows = pl.ds(cuts[n] * width_x, (cuts[n + 1] - cuts[n]) * width_x)
        parts.append(pltpu.make_async_copy(spec_hbm.at[rows, :], spec.at[rows, :], sem.at[3 + n]))
        parts[-1].start()
    fields = [pltpu.make_async_copy(x, y, sem.at[1 + n]) for n, (x, y) in enumerate(((u_hbm, u), (v_hbm, v)))]
    for c in fields:
        c.start()
    first.wait()
    maskf = maskv[...].astype(F32)
    here = 0
    for out, source, sign in ((north, LANES - 1, True), (south, 0, False)):
        for a, b in plan.lat_blocks(sign):
            while cuts[here] < b:
                parts[here].wait()
                here += 1
            rows, lane = plan.lat_place(sign, a, b, width_x)
            acc = out[rows, :] if lane else jnp.zeros((b - a, LANES), F32)
            for i in range(width_x):
                x = spec[pl.ds(a * width_x + i, b - a, stride=width_x), :] * maskf[i : i + 1, :]
                acc = to_lane(acc, x, source, lane + i, lanes_of(b - a))
            out[rows, :] = acc
    assert here == len(parts)
    for c in fields:
        c.wait()
    for out, source, sign, m in ((north, LANES - 1, True, last), (south, 0, False, 0)):
        at = plan.lat_rows(sign)
        acc = jnp.zeros((ocean_x, LANES), F32)
        for f in range(2 * levels):
            field = (u, v)[f // levels]
            acc = to_lane(acc, field[f % levels, :, m : m + LANES], source, f, lanes_of(ocean_x))
        out[at : at + ocean_x, :] = acc


def pack_lat(plan, spec2, mask, u, v, after):
    extra = u.shape[1]
    return pl.pallas_call(
        functools.partial(pack_lat_kernel, plan),
        out_shape=[jax.ShapeDtypeStruct((plan.lat_rows(s) + extra, LANES), F32) for s in (True, False)],
        in_specs=[HBM] * 4 + [ANY],
        out_specs=[VMEM] * 2,
        cost_estimate=CHEAP,
        scratch_shapes=[pltpu.VMEM(x.shape, F32) for x in (spec2, u, v)]
        + [
            pltpu.VMEM(mask.shape, mask.dtype),
            pltpu.SemaphoreType.DMA((3 + len(split(0, plan.comps)),)),
        ],
        compiler_params=PARAMS,
        name="pack_lat",
    )(*pinned(spec2, mask, u, v), after)


def advect_kernel(plan, step, *refs):
    if step == 0:
        state_hbm, transfer_hbm, coefs, mask, part, transfer, state, sem = refs
    else:
        state_hbm, transfer_hbm, coefs, sides, part, transfer, state, sem = refs
    width = part.shape[0]
    blocks = plan.blocks()
    parts = []
    for first, last, *_ in blocks:
        if step == 0:
            rows = pl.ds(first * width, (last - first) * width)
            copy = pltpu.make_async_copy(state_hbm.at[rows, :], state.at[rows, :], sem.at[1 + len(parts)])
        else:
            rows = pl.ds(first, last - first)
            copy = pltpu.make_async_copy(state_hbm.at[:, rows, :], state.at[:, rows, :], sem.at[1 + len(parts)])
        copy.start()
        parts.append(copy)
    fetch = pltpu.make_async_copy(transfer_hbm, transfer, sem.at[0])
    fetch.start()
    if step == 0:
        maskf = mask[...].astype(F32)

    def column(i, first, last):
        if step == 0:
            return state[pl.ds(first * width + i, last - first, stride=width), :] * maskf[i : i + 1, :]
        if i in (0, width - 1):
            return sides[min(i, 1), first:last, :]
        return state[i - 1, first:last, :]

    for copy, (first, last, xs, ys, _) in zip(parts, blocks):
        count = last - first
        keep, east, up = (jnp.broadcast_to(coefs[first:last, q : q + 1], (count, LANES)) for q in range(3))
        lanes = lanes_of(count)
        copy.wait()
        x = [column(i, first, last) for i in range(width)]
        for i in range(width):
            lat = upwind(
                plan, "y", ys, first,
                lambda: jnp.where(lanes == 0, 0.0, pltpu.roll(x[i], 1, 1)),
                lambda: jnp.where(lanes == LANES - 1, 0.0, pltpu.roll(x[i], LANES - 1, 1)),
            )
            lon = upwind(
                plan, "x", xs, first,
                lambda: x[i - 1] if i else None,
                lambda: x[i + 1] if i + 1 < width else None,
            )
            a = keep * x[i] + up * lat
            if lon is not None:
                a = a + east * lon
            part[i, first:last, :] = a
    fetch.wait()


def advect(plan, step, state, transfer, coefs, more):
    comps, width = (plan.comps, state.shape[0] // plan.comps if step == 0 else state.shape[0] + 2)
    hbm_state, hbm_transfer = pinned(state, transfer)
    return pl.pallas_call(
        functools.partial(advect_kernel, plan, step),
        out_shape=[
            jax.ShapeDtypeStruct((width, comps, LANES), F32),
            jax.ShapeDtypeStruct(transfer.shape, transfer.dtype),
        ],
        in_specs=[HBM, HBM, VMEM, VMEM],
        out_specs=[VMEM, VMEM],
        scratch_shapes=[pltpu.VMEM(state.shape, F32), pltpu.SemaphoreType.DMA((1 + len(plan.blocks()),))],
        compiler_params=PARAMS,
        cost_estimate=CHEAP,
        name="advect",
    )(hbm_state, hbm_transfer, coefs, more)


def block_rows(comps):
    return max(b for b in range(STEP, 449, STEP) if comps % b == 0)


def source_blocks(transfer, moved, comps, body):
    block = block_rows(comps)

    for n in range(comps // block):
        rows = slice(n * block, (n + 1) * block)
        body(n, rows, jnp.dot(transfer[rows, :], moved[...], preferred_element_type=F32))


def add_bulk(coefs, weights, rows, state, total):
    count = rows.stop - rows.start
    for q in range(BULK):
        if coefs is None:
            w = weights[q, rows, :]
        else:
            w = jnp.broadcast_to(coefs[rows, 3 + q : 4 + q], (count, LANES))
            weights[q, rows, :] = w
        for i in range(state.shape[0]):
            part = (w * state[i, rows, :]).reshape(count // 8, 8, LANES).sum(0)
            total[q, i] = total[q, i] + part


def interior_kernel(plan, step, *refs):
    part, south, north, transfer, coefs, mask = refs[:6]
    if step == 0:
        out, edge, up, down = refs[6:10]
        inner, full, moved, sem = refs[10:]
    else:
        out, edge, bulk, weights = refs[6:10]
        inner, full, moved, total, sem = refs[10:]
        total[...] = jnp.zeros_like(total)
    width = part.shape[0]
    maskf = mask[...].astype(F32)
    for first, last, _, ys, shifts in plan.blocks():
        rows, count = (slice(first, last), last - first)
        lanes = lanes_of(count)
        speed = jnp.broadcast_to(coefs[rows, 2:3], (count, LANES))
        halos = []
        for sign, buffer, lane in ((True, south, 0), (False, north, LANES - 1)):
            if shifts["y", sign] is not None:
                at, base = plan.lat_place(sign, first, last, width)
                here = lanes == lane
                if ys == 0:
                    here = here & picked(plan.flag["y"] == sign, first)
                halos.append((buffer[at, :] * speed, here, lane, base))
        for i in range(width):
            a = part[i, rows, :]
            for halo, here, lane, base in halos:
                a = a + jnp.where(here, pltpu.roll(halo, (lane - base - i) % LANES, 1), 0.0)
            if i in (0, width - 1):
                edge[min(i, 1), rows, :] = a
            else:
                full[i - 1, rows, :] = a
                moved[rows, (i - 1) * LANES : i * LANES] = a.astype(jnp.bfloat16)
    copies = []

    def done(n, rows, added):
        span = pl.ds(rows.start, rows.stop - rows.start)
        for i in range(1, width - 1):
            s = maskf[i : i + 1, :] * (full[i - 1, rows, :] + 0.5 * added[:, (i - 1) * LANES : i * LANES])
            inner[i - 1, rows, :] = s
            to = out.at[span, i, 0, :] if step else out.at[i - 1, span, :]
            copies.append(pltpu.make_async_copy(inner.at[i - 1, span, :], to, sem.at[len(copies)]))
            copies[-1].start()
        if step:
            add_bulk(coefs, weights, rows, inner, total)
            return
        for packed, source, sign in ((up, LANES - 1, True), (down, 0, False)):
            for a, b in plan.lat_blocks(sign, rows.start, rows.stop):
                at, base = plan.lat_place(sign, a, b, width)
                acc = packed[at, :] if base else jnp.zeros((b - a, LANES), F32)
                for i in range(1, width - 1):
                    acc = to_lane(acc, inner[i - 1, a:b, :], source, base + i, lanes_of(b - a))
                packed[at, :] = acc

    source_blocks(transfer, moved, plan.comps, done)
    if step:
        for q in range(BULK):
            for i in range(1, width - 1):
                bulk[q, i : i + 1, :] = total[q, i - 1].sum(0, keepdims=True)
            bulk[q, 0:1, :] = jnp.zeros((1, LANES), F32)
            bulk[q, width - 1 : width, :] = jnp.zeros((1, LANES), F32)
    for c in copies:
        c.wait()


def interior(plan, step, part, south, north, transfer, coefs, mask):
    comps, width = (plan.comps, mask.shape[0])
    middle = (width - 2, comps, LANES)
    edge = jax.ShapeDtypeStruct((2, comps, LANES), F32)
    scratch = [
        pltpu.VMEM(middle, F32),
        pltpu.VMEM(middle, F32),
        pltpu.VMEM((comps, (width - 2) * LANES), jnp.bfloat16),
    ]
    if step == 0:
        outs = [pltpu.HBM(middle, F32), edge]
        outs += [jax.ShapeDtypeStruct((plan.lat_rows(s), LANES), F32) for s in (True, False)]
    else:
        outs = [pltpu.HBM((comps, width, 1, LANES), F32), edge, jax.ShapeDtypeStruct((BULK, width, LANES), F32)]
        outs += [jax.ShapeDtypeStruct((BULK, comps, LANES), F32)]
        scratch += [pltpu.VMEM((BULK, width - 2, 8, LANES), F32)]
    scratch += [pltpu.SemaphoreType.DMA(((width - 2) * comps // block_rows(comps),))]
    return pl.pallas_call(
        functools.partial(interior_kernel, plan, step),
        out_shape=outs,
        in_specs=[VMEM] * 6,
        out_specs=[HBM] + [VMEM] * (len(outs) - 1),
        scratch_shapes=scratch,
        compiler_params=PARAMS,
        cost_estimate=CHEAP,
        name="interior",
    )(part, south, north, transfer, coefs, mask)


def edges_kernel(plan, step, *refs):
    refs = list(refs)
    part, from_west, from_east, transfer, coefs, mask = refs[:6]
    if step == 0:
        state, east, west = refs[6:9]
        full, moved = refs[9:]
    else:
        bulk_in, weights = refs[6:8]
        state, bulk = refs[8:10]
        full, moved, total = refs[10:]
    width = mask.shape[0]
    maskf = jnp.concatenate([mask[0:1, :], mask[width - 1 : width, :]], axis=0).astype(F32)

    for first, last, xs, ys, shifts in plan.blocks():
        rows, count = (slice(first, last), last - first)
        speed = jnp.broadcast_to(coefs[rows, 1:2], (count, LANES))
        for side, sign, buffer in ((0, True, from_west), (1, False, from_east)):
            a = part[side, rows, :]
            shift = shifts["x", sign]
            if shift is not None:
                halo = buffer[first + shift : last + shift, :]
                if xs == 0:
                    halo = jnp.where(picked(plan.flag["x"] == sign, first), halo, 0.0)
                a = a + speed * halo
            full[side, rows, :] = a
            moved[rows, side * LANES : (side + 1) * LANES] = a.astype(jnp.bfloat16)
    if step:
        total[...] = jnp.zeros_like(total)

    def done(n, rows, added):
        for side in range(2):
            s = maskf[side : side + 1, :] * (full[side, rows, :] + 0.5 * added[:, side * LANES : (side + 1) * LANES])
            state[side, rows, :] = s
        if step:
            add_bulk(None, weights, rows, state, total)

    source_blocks(transfer, moved, plan.comps, done)
    if step:
        for q in range(BULK):
            bulk[q] = bulk_in[q]
            bulk[q, 0:1, :] = total[q, 0].sum(0, keepdims=True)
            bulk[q, width - 1 : width, :] = total[q, 1].sum(0, keepdims=True)
        return
    for out, side, sign in ((east, 1, True), (west, 0, False)):
        at = 0
        for a, b in plan.seg["x", sign]:
            out[at : at + b - a, :] = state[side, a:b, :]
            at += b - a


def merge_lat_kernel(plan, width, state, up_in, down_in, up, down):
    for out, given, source, sign in ((up, up_in, LANES - 1, True), (down, down_in, 0, False)):
        for a, b in plan.lat_blocks(sign):
            at, base = plan.lat_place(sign, a, b, width)
            acc = out[at, :] if base else given[at, :]
            for side, lane in ((0, base), (1, base + width - 1)):
                acc = to_lane(acc, state[side, a:b, :], source, lane, lanes_of(b - a))
            out[at, :] = acc


def merge_lat(plan, width, state, up, down):
    return pl.pallas_call(
        functools.partial(merge_lat_kernel, plan, width),
        out_shape=[jax.ShapeDtypeStruct(x.shape, F32) for x in (up, down)],
        in_specs=[VMEM] * 3,
        out_specs=[VMEM] * 2,
        compiler_params=PARAMS,
        cost_estimate=CHEAP,
        name="merge_lat",
    )(state, up, down)


def edges(plan, step, part, from_west, from_east, transfer, coefs, mask, *more):
    comps, width = (plan.comps, mask.shape[0])
    outs = [jax.ShapeDtypeStruct((2, comps, LANES), F32)]
    scratch = [pltpu.VMEM((2, comps, LANES), F32), pltpu.VMEM((comps, 2 * LANES), jnp.bfloat16)]
    if step == 0:
        outs += [jax.ShapeDtypeStruct((plan.rows("x", s), LANES), F32) for s in (True, False)]
    else:
        outs += [jax.ShapeDtypeStruct((BULK, width, LANES), F32)]
        scratch += [pltpu.VMEM((BULK, 2, 8, LANES), F32)]
    return pl.pallas_call(
        functools.partial(edges_kernel, plan, step),
        out_shape=outs,
        in_specs=[VMEM] * (6 + len(more)),
        out_specs=[VMEM] * len(outs),
        scratch_shapes=scratch,
        compiler_params=PARAMS,
        cost_estimate=CHEAP,
        name="edges",
    )(part, from_west, from_east, transfer, coefs, mask, *more)


def finish_kernel(state, given, out, sem):
    width = out.shape[1]
    copies = [
        pltpu.make_async_copy(state.at[side], out.at[:, col, 0, :], sem.at[side])
        for side, col in ((0, 0), (1, width - 1))
    ]
    for c in copies:
        c.start()
    for c in copies:
        c.wait()


def finish(state, out4):
    return pl.pallas_call(
        finish_kernel,
        out_shape=jax.ShapeDtypeStruct(out4.shape, F32),
        in_specs=[ANY, ANY],
        out_specs=ANY,
        scratch_shapes=[pltpu.SemaphoreType.DMA((2,))],
        input_output_aliases={1: 0},
        compiler_params=PARAMS,
        name="finish",
    )(state, out4)


def ocean_shifts(q, west, east, south, north):
    rows, lanes = q.shape
    row = lax.broadcasted_iota(jnp.int32, q.shape, 0)
    lane = lax.broadcasted_iota(jnp.int32, q.shape, 1)
    before = jnp.where(row == 0, west, pltpu.roll(q, 1, 0))
    after = jnp.where(row == rows - 1, east, pltpu.roll(q, rows - 1, 0))
    below = jnp.where(lane == 0, south, pltpu.roll(q, 1, 1))
    above = jnp.where(lane == lanes - 1, north, pltpu.roll(q, lanes - 1, 1))
    return before, after, below, above


def ocean_base_kernel(plan, u, v, from_west, from_east, from_south, from_north, mask, coriolis, base_u, base_v):
    levels, ocean_x, ocean_y = u.shape
    tiles = ocean_y // LANES
    maskf = mask[...].astype(F32)
    half = 0.5 * coriolis[...]
    west_at, east_at = (plan.rows("x", s) for s in (True, False))
    south_at, north_at = (plan.lat_rows(s) for s in (True, False))
    for f, (field, other, out, sign) in enumerate(((u, v, base_u, 1.0), (v, u, base_v, -1.0))):
        for level in range(levels):
            q = field[level]

            def line(buffer, at):
                parts = [buffer[at + (f * tiles + m) * levels + level, :][None, :] for m in range(tiles)]
                return jnp.concatenate(parts, axis=1)

            lane = f * levels + level
            before, after, below, above = ocean_shifts(
                q,
                line(from_west, west_at),
                line(from_east, east_at),
                from_south[south_at : south_at + ocean_x, lane : lane + 1],
                from_north[north_at : north_at + ocean_x, lane : lane + 1],
            )
            lap = before + after + below + above - 4.0 * q
            out[level] = maskf * (q + sign * half * other[level] + 0.1 * lap)


def ocean_base(plan, u, v, from_west, from_east, from_south, from_north, mask, coriolis):
    return pl.pallas_call(
        functools.partial(ocean_base_kernel, plan),
        out_shape=[jax.ShapeDtypeStruct(u.shape, F32)] * 2,
        in_specs=[VMEM] * 8,
        out_specs=[VMEM] * 2,
        compiler_params=PARAMS,
        name="ocean_base",
    )(u, v, from_west, from_east, from_south, from_north, mask, coriolis)


def gathered(slabs, at, off, weight, count):
    acc = [0.0] * count
    for o in range(OFFSETS):
        rows = [slabs(o, q) for q in range(count)]
        for p in range(len(at)):
            w = jnp.where(off[p] == o, weight[p], 0.0)
            for q in range(count):
                acc[q] = acc[q] + w * jnp.take_along_axis(rows[q], at[p], axis=1, mode="promise_in_bounds")
    return acc


def fill_table(table, left, own, right, ratio, fields):
    width = own.shape[1]
    for q in fields:
        for b, ref in enumerate((left, own, right)):
            for r in range(ratio):
                table[q, pl.ds(b * width * ratio + r, width, stride=ratio), :] = ref[q]


def remap_lon_kernel(own, left, right, cell, offset, weight, east, west, rows):
    taps, ocean_x, ocean_y = cell.shape
    width = own.shape[1]
    tiles = ocean_y // LANES
    last_row = ocean_x - 8
    for b, ref in enumerate((left, own, right)):
        rows[:, b * width : (b + 1) * width, :] = ref[0:2]
    first_half = lax.broadcasted_iota(jnp.int32, (8, LANES), 0) < 4
    for m in range(tiles):
        lanes = slice(m * LANES, (m + 1) * LANES)
        at, off, w = (
            [jnp.where(first_half, x[p, 0:8, lanes], x[p, last_row : last_row + 8, lanes]) for p in range(taps)]
            for x in (cell, offset, weight)
        )
        acc = gathered(lambda o, q: rows[q, o : o + 8, :], at, off, w, 2)
        for q in range(2):
            n = q * tiles + m
            east[n : n + 1, :] = acc[q][7:8, :]
            west[n : n + 1, :] = acc[q][0:1, :]
    if 2 * tiles < east.shape[0]:
        for out in (east, west):
            out[2 * tiles :, :] = jnp.zeros((out.shape[0] - 2 * tiles, LANES), F32)


def remap_lat_kernel(own, left, right, cell, offset, weight, after, north, south, table):
    del after
    taps, ocean_x, ocean_y = cell.shape
    ratio = ocean_x // own.shape[1]
    last_lane = ocean_y - LANES
    fill_table(table, left, own, right, ratio, range(1, 3))
    lanes = lanes_of(8)
    for t in range(ocean_x // 8):
        here = slice(8 * t, 8 * t + 8)
        at, off, w = (
            [jnp.where(lanes < LANES // 2, x[p, here, 0:LANES], x[p, here, last_lane:]) for p in range(taps)]
            for x in (cell, offset, weight)
        )
        acc = gathered(lambda o, q: table[1 + q, 8 * t + ratio * o : 8 * t + ratio * o + 8, :], at, off, w, 2)
        for out, source in ((north, LANES - 1), (south, 0)):
            packed = jnp.zeros((8, LANES), F32)
            for q in range(2):
                packed = to_lane(packed, acc[q], source, q, lanes)
            out[here, :] = packed


def remap_lon(own, left, right, cell, offset, weight):
    _, ocean_x, ocean_y = cell.shape
    width = own.shape[1]
    assert width == 8 and ocean_x % width == 0
    side = jax.ShapeDtypeStruct((8 * pl.cdiv(2 * ocean_y // LANES, 8), LANES), F32)
    return pl.pallas_call(
        remap_lon_kernel,
        out_shape=[side, side],
        in_specs=[VMEM] * 6,
        out_specs=[VMEM] * 2,
        scratch_shapes=[pltpu.VMEM((2, 3 * width, LANES), F32)],
        compiler_params=PARAMS,
        cost_estimate=CHEAP,
        name="remap_lon",
    )(own, left, right, cell, offset, weight)


def remap_lat(own, left, right, cell, offset, weight, after):
    ocean_x = cell.shape[1]
    end = jax.ShapeDtypeStruct((ocean_x, LANES), F32)
    return pl.pallas_call(
        remap_lat_kernel,
        out_shape=[end, end],
        in_specs=[VMEM] * 6 + [ANY],
        out_specs=[VMEM] * 2,
        scratch_shapes=[pltpu.VMEM((BULK, 3 * ocean_x, LANES), F32)],
        compiler_params=PARAMS,
        cost_estimate=CHEAP,
        name="remap_lat",
    )(own, left, right, cell, offset, weight, after)


def remap_kernel(own, left, right, cell, offset, weight, stress, drift, table):
    taps, ocean_x, ocean_y = cell.shape
    ratio = ocean_x // own.shape[1]
    fill_table(table, left, own, right, ratio, range(BULK))
    for t in range(ocean_x // 8):
        for m in range(ocean_y // LANES):
            rows, lanes = (slice(8 * t, 8 * t + 8), slice(m * LANES, (m + 1) * LANES))
            at, off, w = ([x[p, rows, lanes] for p in range(taps)] for x in (cell, offset, weight))
            acc = gathered(
                lambda o, q: table[q, 8 * t + ratio * o : 8 * t + ratio * o + 8, :], at, off, w, BULK
            )
            for q in range(3):
                stress[q, rows, lanes] = acc[q]
            for q in range(2):
                drift[q, rows, lanes] = acc[3 + q]


def remap(own, left, right, cell, offset, weight):
    _, ocean_x, ocean_y = cell.shape
    return pl.pallas_call(
        remap_kernel,
        out_shape=[jax.ShapeDtypeStruct((n, ocean_x, ocean_y), F32) for n in (3, 2)],
        in_specs=[VMEM] * 6,
        out_specs=[VMEM] * 2,
        scratch_shapes=[pltpu.VMEM((BULK, 3 * ocean_x, LANES), F32)],
        compiler_params=PARAMS,
        cost_estimate=CHEAP,
        name="remap",
    )(own, left, right, cell, offset, weight)


def ocean_final_kernel(stress, drift, from_west, from_east, from_south, from_north, base_u, base_v, mask, coriolis, new_u, new_v):
    levels, ocean_x, ocean_y = base_u.shape
    tiles = ocean_y // LANES

    def line(buffer, q):
        return jnp.concatenate([buffer[q * tiles + m : q * tiles + m + 1, :] for m in range(tiles)], axis=1)

    zero_line = jnp.zeros((1, ocean_y), F32)
    zero_end = jnp.zeros((ocean_x, 1), F32)
    grad = []
    for q in range(3):
        lon = q < 2
        lat = q > 0
        before, after, below, above = ocean_shifts(
            stress[q],
            line(from_west, q) if lon else zero_line,
            line(from_east, q) if lon else zero_line,
            from_south[:, q - 1 : q] if lat else zero_end,
            from_north[:, q - 1 : q] if lat else zero_end,
        )
        grad.append((0.5 * (after - before), 0.5 * (above - below)))
    force_x = -(grad[0][0] + grad[1][1])
    force_y = -(grad[1][0] + grad[2][1])
    maskf = mask[...].astype(F32)
    half = 0.5 * coriolis[...]
    add_u = maskf * (half * drift[1] + 0.5 * force_x)
    add_v = maskf * (0.5 * force_y - half * drift[0])
    for level in range(levels):
        decay = np.float32(np.exp(np.float32(-level / 3.0)))
        new_u[level] = base_u[level] + decay * add_u
        new_v[level] = base_v[level] + decay * add_v


def ocean_final(stress, drift, halos, base_u, base_v, mask, coriolis):
    return pl.pallas_call(
        ocean_final_kernel,
        out_shape=[jax.ShapeDtypeStruct(base_u.shape, F32)] * 2,
        in_specs=[VMEM] * 10,
        out_specs=[VMEM] * 2,
        compiler_params=PARAMS,
        name="ocean_final",
    )(stress, drift, *halos, base_u, base_v, mask, coriolis)


def send(value, axis, step, wrap):
    count = lax.axis_size(axis)
    pairs = [(i, (i + step) % count) for i in range(count) if wrap or 0 <= i + step < count]
    return lax.ppermute(value, axis, pairs)


def exchange(east, west, north, south):
    from_south = send(north, "lat", 1, False)
    from_north = send(south, "lat", -1, False)
    from_west = send(east, "lon", 1, True)
    from_east = send(west, "lon", -1, True)
    return from_west, from_east, from_south, from_north


def local(
    spectrum,
    sea_mask,
    transfer,
    bulk_weight,
    remap_cell,
    remap_weight,
    ocean_u,
    ocean_v,
    ocean_mask,
    coriolis,
):
    comps, width_x, width_y = spectrum.shape
    plan = Plan(comps)
    spec2 = spectrum.reshape(comps * width_x, width_y)
    east, west = pack_lon(plan, spectrum.reshape(comps, width_x, 1, width_y), sea_mask, ocean_u, ocean_v)
    north, south = pack_lat(plan, spec2, sea_mask, ocean_u, ocean_v, east)
    from_west, from_east, from_south, from_north = exchange(east, west, north, south)

    coefs = jnp.concatenate([jnp.asarray(plan.coef), bulk_weight.T], axis=1)
    total_y = width_y * lax.axis_size("lat")
    taps_first = remap_cell.transpose(2, 0, 1)
    offset = taps_first // total_y
    cell = taps_first - offset * total_y - lax.axis_index("lat") * width_y
    weight = remap_weight.transpose(2, 0, 1)
    line = coriolis[None, :]

    part, held = advect(plan, 0, spec2, transfer, coefs, sea_mask)
    middle, edge, up, down = interior(plan, 0, part, from_south, from_north, held, coefs, sea_mask)
    base_u, base_v = ocean_base(
        plan, ocean_u, ocean_v, from_west, from_east, from_south, from_north, ocean_mask, line
    )
    sides, east, west = edges(plan, 0, edge, from_west, from_east, held, coefs, sea_mask)
    north, south = merge_lat(plan, width_x, sides, up, down)
    from_west, from_east, from_south, from_north = exchange(east, west, north, south)

    part, held = advect(plan, 1, middle, transfer, coefs, sides)
    out4, edge, bulk, weights = interior(plan, 1, part, from_south, from_north, held, coefs, sea_mask)
    sides, bulk = edges(plan, 1, edge, from_west, from_east, held, coefs, sea_mask, bulk, weights)
    left = send(bulk, "lon", 1, True)
    right = send(bulk, "lon", -1, True)
    state = finish(sides, out4).reshape(spectrum.shape)

    remapped = (bulk, left, right, cell, offset, weight)
    east, west = remap_lon(*remapped)
    north, south = remap_lat(*remapped, east)
    halos = exchange(east, west, north, south)
    stress, drift = remap(*remapped)
    new_u, new_v = ocean_final(stress, drift, halos, base_u, base_v, ocean_mask, line)
    return (state, new_u, new_v)


def solution(mesh):
    placed = (
        P(None, "lon", "lat"),
        P("lon", "lat"),
        P(),
        P(),
        P("lon", "lat", None),
        P("lon", "lat", None),
        P(None, "lon", "lat"),
        P(None, "lon", "lat"),
        P("lon", "lat"),
        P("lat"),
    )
    return jax.shard_map(
        local,
        mesh=mesh,
        in_specs=placed,
        out_specs=(P(None, "lon", "lat"), P(None, "lon", "lat"), P(None, "lon", "lat")),
        check_vma=False,
    )
```

time: 141 us -> 83.3 us (0.59)
  Pallas kernels: 83.3 us -> 43.2 us
  local copies, waits for them, and re-layouts: 13.5 us -> 0.3 us
  waiting for transfers between devices: 8.88 us -> 1.06 us
  starting transfers between devices: 33.4 us -> 37.3 us
    pallas_call x2, Pallas kernels: 39.7 us -> 12.3 us  [interior(): pl.pallas_call(functools.partial(interior_kernel, plan, step), out_shape=...]
    pallas_call x2, Pallas kernels: 23.7 us -> 5.09 us  [edges(): pl.pallas_call(functools.partial(edges_kernel, plan, step), out_shape=out...]
    unnamed x37 -> x19, local copies, waits for them, and re-layouts: 13.3 us -> 0.07 us
    pallas_call x1 -> x6, Pallas kernels: 5.31 us -> 17.9 us  [the longest x2 9.48 us: advect(): pl.pallas_call(functools.partial(advect_kernel, plan, step), out_shape=[j...]
    ppermute x14, waiting for transfers between devices: 8.88 us -> 1.06 us  [send(): return lax.ppermute(value, axis, pairs)]
    pallas_call x1, Pallas kernels: 11.4 us -> 3.89 us  [pack_lat(): pl.pallas_call(functools.partial(pack_lat_kernel, plan), out_shape=[jax.S...]
    ppermute x14, starting transfers between devices: 33.4 us -> 37.3 us  [send(): return lax.ppermute(value, axis, pairs)]
  transfers between devices with their start and end apart: 14 -> 14, of which waited for: 4 -> 1; matrix products, arithmetic and copies ran while one was open for 0% -> 0% of each run, Pallas kernels for 30% -> 40%
where the time goes in v2:
time: 83.3 us; the launch traced here: 83.1 us
  Pallas kernels  43.2 us (52%)
  starting transfers between devices  37.3 us (45%)
  waiting for transfers between devices  1.06 us (1%)
  between operations  1.01 us (1%)
    ppermute x14, starting transfers between devices, send(): return lax.ppermute(value, axis, pairs)  37.3 us
    pallas_call x2, Pallas kernels, interior(): pl.pallas_call(functools.partial(interior_kernel, plan, step), out_shape=...  12.3 us
    pallas_call x2, Pallas kernels, advect(): pl.pallas_call(functools.partial(advect_kernel, plan, step), out_shape=[j...  9.48 us
    pallas_call x1, Pallas kernels, remap(): pl.pallas_call(remap_kernel, out_shape=[jax.ShapeDtypeStruct((n, ocean_x,...  5.23 us
    pallas_call x2, Pallas kernels, edges(): pl.pallas_call(functools.partial(edges_kernel, plan, step), out_shape=out...  5.09 us
    pallas_call x1, Pallas kernels, pack_lat(): pl.pallas_call(functools.partial(pack_lat_kernel, plan), out_shape=[jax.S...  3.89 us
  transfers between devices with their start and end apart: 14, of which 1 were waited for; matrix products, arithmetic and copies ran while one was open for 0% of the time, Pallas kernels for 40%

profile of v2, /device:TPU:1, one launch (start us, length us, event | category | flops | bytes accessed | tf_op | source)
XLA Modules:
  0.0 83.1 jit_solution(1482189895286114560)
XLA Ops:
  0.6 1.4 %pack_lon.1 = (f32[704,128]{1,0:T(8,128)S(1)}, f32[704,128]{1,0:T(8,128)S(1)}) custom-call(f32[1296,8,1,128]{3,2,1,0:T(1,128)} %bitcast.31, s32[8,128]{1,0:T(8,128)} %refs_5_.7, f32[8,24,384]{2,1,0:T(8,128)} %u.3, f32[8,24,384]{2,1,0:T(8,128)} %v.3), custom_call_target="tpu_custom_call" | custom-call | tf_op jit(solution)/shard_map/pack_lon/pallas_call | solution.py:190
  2.1 2.1 %collective-permute-start.2 = (f32[704,128]{1,0:T(8,128)S(1)}, f32[704,128]{1,0:T(8,128)S(1)}, u32[]{:S(2)}, u32[]{:S(2)}) collective-permute-start(f32[704,128]{1,0:T(8,128)S(1)} %get-tuple-element.37.after), channel_id=1, source_target_pairs={{0,4},{4,8},{8,12},{12,16},{16,20},{20,24},{24,28},{28,0},{1,5},{5... | collective-permute-start | bytes 1081352 | tf_op jit(solution)/shard_map/ppermute | solution.py:799
  4.2 3.1 %collective-permute-start.3 = (f32[704,128]{1,0:T(8,128)S(1)}, f32[704,128]{1,0:T(8,128)S(1)}, u32[]{:S(2)}, u32[]{:S(2)}) collective-permute-start(f32[704,128]{1,0:T(8,128)S(1)} %get-tuple-element.43), channel_id=1, source_target_pairs={{0,28},{4,0},{8,4},{12,8},{16,12},{20,16},{24,20},{28,24},{1,29},{... | collective-permute-start | bytes 1081352 | tf_op jit(solution)/shard_map/ppermute | solution.py:799
  7.3 3.9 %pack_lat.1 = (f32[200,128]{1,0:T(8,128)S(1)}, f32[200,128]{1,0:T(8,128)S(1)}) custom-call(f32[10368,128]{1,0:T(8,128)} %bitcast.32, s32[8,128]{1,0:T(8,128)} %refs_5_.7, f32[8,24,384]{2,1,0:T(8,128)} %u.3, f32[8,24,384]{2,1,0:T(8,128)} %v.3, f32[704,128]{1,0:T(8,128)S(1)} %get-tuple-element.37.after), custom_call_target="tpu_custom_call" | custom-call | flops 1 | bytes 1 | tf_op jit(solution)/shard_map/pack_lat/pallas_call | solution.py:253
  11.2 4.1 %collective-permute-start = (f32[200,128]{1,0:T(8,128)S(1)}, f32[200,128]{1,0:T(8,128)S(1)}, u32[]{:S(2)}, u32[]{:S(2)}) collective-permute-start(f32[200,128]{1,0:T(8,128)S(1)} %get-tuple-element.38), channel_id=1, source_target_pairs={{0,1},{1,2},{2,3},{4,5},{5,6},{6,7},{8,9},{9,10},{10,11},{12,13},{... | collective-permute-start | bytes 307208 | tf_op jit(solution)/shard_map/ppermute | solution.py:799
  15.3 1.9 %collective-permute-start.1 = (f32[200,128]{1,0:T(8,128)S(1)}, f32[200,128]{1,0:T(8,128)S(1)}, u32[]{:S(2)}, u32[]{:S(2)}) collective-permute-start(f32[200,128]{1,0:T(8,128)S(1)} %get-tuple-element.39), channel_id=1, source_target_pairs={{1,0},{2,1},{3,2},{5,4},{6,5},{7,6},{9,8},{10,9},{11,10},{13,12},{... | collective-permute-start | bytes 307208 | tf_op jit(solution)/shard_map/ppermute | solution.py:799
  17.5 4.8 %advect.2 = (f32[8,1296,128]{2,1,0:T(8,128)S(1)}, bf16[1296,1296]{1,0:T(8,128)(2,1)S(1)}) custom-call(f32[10368,128]{1,0:T(8,128)} %bitcast.33, bf16[1296,1296]{1,0:T(8,128)(2,1)} %refs_1_.3, f32[1296,8]{1,0:T(8,128)S(1)} %copy.18.refs_2_.refs_4_, s32[8,128]{1,0:T(8,128)S(1)} %copy-done.2), custom_call_target="tpu_custom_call" | custom-call | flops 1 | bytes 1 | tf_op jit(solution)/shard_map/advect/pallas_call | solution.py:325
  22.3 5.5 %interior.2 = (f32[6,1296,128]{2,1,0:T(8,128)}, f32[2,1296,128]{2,1,0:T(8,128)S(1)}, f32[176,128]{1,0:T(8,128)S(1)}, f32[176,128]{1,0:T(8,128)S(1)}) custom-call(f32[8,1296,128]{2,1,0:T(8,128)S(1)} %get-tuple-element.36.refs_0_, f32[200,128]{1,0:T(8,128)S(1)} %collective-permute-done.refs_1_.from_south, ...), custom_call_target="tpu_custom_call" | custom-call | flops 1 | bytes 1 | tf_op jit(solution)/shard_map/interior/pallas_call | solution.py:446
  27.8 2.2 %edges.2 = (f32[2,1296,128]{2,1,0:T(8,128)S(1)}, f32[656,128]{1,0:T(8,128)}, f32[656,128]{1,0:T(8,128)}) custom-call(f32[2,1296,128]{2,1,0:T(8,128)S(1)} %get-tuple-element.42.refs_0_, f32[704,128]{1,0:T(8,128)S(1)} %collective-permute-done.2.refs_1_.from_west, f32[704,128]{1,0:T(8,128)S(1)} %collective-permute-done.3.refs_2_.from_east, ...), custom_call_target="tpu_custom_call" | custom-call | flops 1 | bytes 1 | tf_op jit(solution)/shard_map/edges/pallas_call | solution.py:539
  30.0 4.2 %collective-permute-start.7 = (f32[656,128]{1,0:T(8,128)}, f32[656,128]{1,0:T(8,128)}, u32[]{:S(2)}, u32[]{:S(2)}) collective-permute-start(f32[656,128]{1,0:T(8,128)} %get-tuple-element.53), channel_id=1, source_target_pairs={{0,28},{4,0},{8,4},{12,8},{16,12},{20,16},{24,20},{28,24},{1,29},{... | collective-permute-start | bytes 1007624 | tf_op jit(solution)/shard_map/ppermute | solution.py:799
  35.1 4.2 %collective-permute-start.4 = (f32[176,128]{1,0:T(8,128)}, f32[176,128]{1,0:T(8,128)S(1)}, u32[]{:S(2)}, u32[]{:S(2)}) collective-permute-start(f32[176,128]{1,0:T(8,128)} %get-tuple-element.48), channel_id=1, source_target_pairs={{0,1},{1,2},{2,3},{4,5},{5,6},{6,7},{8,9},{9,10},{10,11},{12,13},{... | collective-permute-start | bytes 270344 | tf_op jit(solution)/shard_map/ppermute | solution.py:799
  39.3 2.1 %collective-permute-start.5 = (f32[176,128]{1,0:T(8,128)S(1)}, f32[176,128]{1,0:T(8,128)S(1)}, u32[]{:S(2)}, u32[]{:S(2)}) collective-permute-start(f32[176,128]{1,0:T(8,128)S(1)} %get-tuple-element.49), channel_id=1, source_target_pairs={{1,0},{2,1},{3,2},{5,4},{6,5},{7,6},{9,8},{10,9},{11,10},{13,12},{... | collective-permute-start | bytes 270344 | tf_op jit(solution)/shard_map/ppermute | solution.py:799
  41.4 4.7 %advect.3 = (f32[8,1296,128]{2,1,0:T(8,128)S(1)}, bf16[1296,1296]{1,0:T(8,128)(2,1)S(1)}) custom-call(f32[6,1296,128]{2,1,0:T(8,128)} %get-tuple-element.41.refs_0_, bf16[1296,1296]{1,0:T(8,128)(2,1)} %refs_1_.3, f32[1296,8]{1,0:T(8,128)S(1)} %copy.18.refs_2_.refs_4_, f32[2,1296,128]{2,1,0:T(8,128)S(1)} %get-tuple-element.44.refs_3_.state), custom_call_target="tpu_custom_call" | custom-call | flops 1 | bytes 1 | tf_op jit(solution)/shard_map/advect/pallas_call | solution.py:325
  46.1 6.8 %interior.3 = (f32[1296,8,1,128]{3,2,1,0:T(1,128)}, f32[2,1296,128]{2,1,0:T(8,128)S(1)}, f32[5,8,128]{2,1,0:T(8,128)S(1)}, f32[5,1296,128]{2,1,0:T(8,128)S(1)}) custom-call(f32[8,1296,128]{2,1,0:T(8,128)S(1)} %get-tuple-element.45.refs_0_, f32[176,128]{1,0:T(8,128)S(1)} %collective-permute-done.4.refs_1_, f32[176,128]{1,0:T(8,128)S(1)} %collective-permute-done.5.refs_2_, ...), custom_call_target="tpu_custom_call" | custom-call | flops 1 | bytes 1 | tf_op jit(solution)/shard_map/interior/pallas_call | solution.py:446
  53.0 2.9 %edges.3 = (f32[2,1296,128]{2,1,0:T(8,128)S(1)}, f32[5,8,128]{2,1,0:T(8,128)S(1)}) custom-call(f32[2,1296,128]{2,1,0:T(8,128)S(1)} %get-tuple-element.51.refs_0_, f32[656,128]{1,0:T(8,128)S(1)} %collective-permute-done.6.refs_1_, f32[656,128]{1,0:T(8,128)} %collective-permute-done.7.refs_2_, bf16[1296,1296]{1,0:T(8,128)(2,1)S(1)} %get-tuple-element.50.refs_3_, ...), custom_call_target="tpu_custom_call" | custom-call | flops 1 | bytes 1 | tf_op jit(solution)/shard_map/edges/pallas_call | solution.py:539
  56.0 4.1 %collective-permute-start.9 = (f32[5,8,128]{2,1,0:T(8,128)S(1)}, f32[5,8,128]{2,1,0:T(8,128)S(1)}, u32[]{:S(2)}, u32[]{:S(2)}) collective-permute-start(f32[5,8,128]{2,1,0:T(8,128)S(1)} %get-tuple-element.58.own), channel_id=1, source_target_pairs={{0,28},{4,0},{8,4},{12,8},{16,12},{20,16},{24,20},{28,24},{1,29},{... | collective-permute-start | bytes 61448 | tf_op jit(solution)/shard_map/ppermute | solution.py:799
  60.3 1.0 %collective-permute-done.8.left = f32[5,8,128]{2,1,0:T(8,128)S(1)} collective-permute-done((f32[5,8,128]{2,1,0:T(8,128)S(1)}, f32[5,8,128]{2,1,0:T(8,128)S(1)}, u32[]{:S(2)}, u32[]{:S(2)}) %collective-permute-start.8) | collective-permute-done | bytes 20512 | tf_op jit(solution)/shard_map/ppermute | solution.py:799
  61.3 1.1 %remap_lon.1 = (f32[8,128]{1,0:T(8,128)S(1)}, f32[8,128]{1,0:T(8,128)S(1)}) custom-call(f32[5,8,128]{2,1,0:T(8,128)S(1)} %get-tuple-element.58.own, f32[5,8,128]{2,1,0:T(8,128)S(1)} %collective-permute-done.8.left, f32[5,8,128]{2,1,0:T(8,128)S(1)} %collective-permute-done.9.right, s32[4,24,384]{2,1,0:T(8,128)S(1)} %get-tuple-element.70.cell, ...), custom_call_target="tpu_custom_call" | custom-call | flops 1 | bytes 1 | tf_op jit(solution)/shard_map/remap_lon/pallas_call | solution.py:694
  62.4 1.3 %remap_lat.1 = (f32[24,128]{1,0:T(8,128)S(1)}, f32[24,128]{1,0:T(8,128)S(1)}) custom-call(f32[5,8,128]{2,1,0:T(8,128)S(1)} %get-tuple-element.58.own, f32[5,8,128]{2,1,0:T(8,128)S(1)} %collective-permute-done.8.left, f32[5,8,128]{2,1,0:T(8,128)S(1)} %collective-permute-done.9.right, s32[4,24,384]{2,1,0:T(8,128)S(1)} %get-tuple-element.70.cell, ...), custom_call_target="tpu_custom_call" | custom-call | flops 1 | bytes 1 | tf_op jit(solution)/shard_map/remap_lat/pallas_call | solution.py:709
  63.6 4.8 %collective-permute-start.12 = (f32[24,128]{1,0:T(8,128)S(1)}, f32[24,128]{1,0:T(8,128)S(1)}, u32[]{:S(2)}, u32[]{:S(2)}) collective-permute-start(f32[24,128]{1,0:T(8,128)S(1)} %get-tuple-element.63), channel_id=1, source_target_pairs={{0,1},{1,2},{2,3},{4,5},{5,6},{6,7},{8,9},{9,10},{10,11},{12,13},{... | collective-permute-start | bytes 36872 | tf_op jit(solution)/shard_map/ppermute | solution.py:799
  68.4 1.9 %collective-permute-start.13 = (f32[24,128]{1,0:T(8,128)S(1)}, f32[24,128]{1,0:T(8,128)S(1)}, u32[]{:S(2)}, u32[]{:S(2)}) collective-permute-start(f32[24,128]{1,0:T(8,128)S(1)} %get-tuple-element.64), channel_id=1, source_target_pairs={{1,0},{2,1},{3,2},{5,4},{6,5},{7,6},{9,8},{10,9},{11,10},{13,12},{... | collective-permute-start | bytes 36872 | tf_op jit(solution)/shard_map/ppermute | solution.py:799
  70.4 4.7 %collective-permute-start.11 = (f32[8,128]{1,0:T(8,128)S(1)}, f32[8,128]{1,0:T(8,128)S(1)}, u32[]{:S(2)}, u32[]{:S(2)}) collective-permute-start(f32[8,128]{1,0:T(8,128)S(1)} %get-tuple-element.62), channel_id=1, source_target_pairs={{0,28},{4,0},{8,4},{12,8},{16,12},{20,16},{24,20},{28,24},{1,29},{... | collective-permute-start | bytes 12296 | tf_op jit(solution)/shard_map/ppermute | solution.py:799
  75.7 1.1 %finish.1 = f32[1296,8,1,128]{3,2,1,0:T(1,128)} custom-call(f32[2,1296,128]{2,1,0:T(8,128)S(1)} %get-tuple-element.56.state, f32[1296,8,1,128]{3,2,1,0:T(1,128)} %get-tuple-element.57.given), custom_call_target="tpu_custom_call", output_to_operand_aliasing={{}: (1, {})} | custom-call | tf_op jit(solution)/shard_map/finish/pallas_call | solution.py:564
  76.8 5.2 %remap.1 = (f32[3,24,384]{2,1,0:T(8,128)S(1)}, f32[2,24,384]{2,1,0:T(8,128)S(1)}) custom-call(f32[5,8,128]{2,1,0:T(8,128)S(1)} %get-tuple-element.58.own, f32[5,8,128]{2,1,0:T(8,128)S(1)} %collective-permute-done.8.left, f32[5,8,128]{2,1,0:T(8,128)S(1)} %collective-permute-done.9.right, s32[4,24,384]{2,1,0:T(8,128)S(1)} %get-tuple-element.70.cell, ...), custom_call_target="tpu_custom_call" | custom-call | flops 1 | bytes 1 | tf_op jit(solution)/shard_map/remap/pallas_call | solution.py:740
  (42 shorter events, 3.0 us)
Async XLA Ops:
  2.0 15.2 %copy-start.6 = (f32[5,1296]{1,0:T(8,128)S(1)}, f32[5,1296]{1,0:T(8,128)}, u32[]{:S(2)}) copy-start(f32[5,1296]{1,0:T(8,128)} %param.14) | copy-start | bytes 77764
  2.1 15.2 %copy-start.7 = (f32[1296,3]{0,1:T(4,128)S(1)}, f32[1296,3]{0,1:T(4,128)}, u32[]{:S(2)}) copy-start(f32[1296,3]{0,1:T(4,128)} %constant.26.clone) | copy-start | bytes 46660
  2.1 15.4 %copy-start.2 = (s32[8,128]{1,0:T(8,128)S(1)}, s32[8,128]{1,0:T(8,128)}, u32[]{:S(2)}) copy-start(s32[8,128]{1,0:T(8,128)} %refs_5_.7) | copy-start | bytes 12292
  2.1 25.7 %collective-permute-start.2 = (f32[704,128]{1,0:T(8,128)S(1)}, f32[704,128]{1,0:T(8,128)S(1)}, u32[]{:S(2)}, u32[]{:S(2)}) collective-permute-start(f32[704,128]{1,0:T(8,128)S(1)} %get-tuple-element.37.after), channel_id=1, source_target_pairs={{0,4},{4,8},{8,12},{12,16},{16,20},{20,24},{24,28},{28,0},{1,5},{5... | collective-permute-start | bytes 1081352 | tf_op jit(solution)/shard_map/ppermute | solution.py:799
  4.2 23.6 %collective-permute-start.3 = (f32[704,128]{1,0:T(8,128)S(1)}, f32[704,128]{1,0:T(8,128)S(1)}, u32[]{:S(2)}, u32[]{:S(2)}) collective-permute-start(f32[704,128]{1,0:T(8,128)S(1)} %get-tuple-element.43), channel_id=1, source_target_pairs={{0,28},{4,0},{8,4},{12,8},{16,12},{20,16},{24,20},{28,24},{1,29},{... | collective-permute-start | bytes 1081352 | tf_op jit(solution)/shard_map/ppermute | solution.py:799
  11.2 11.1 %collective-permute-start = (f32[200,128]{1,0:T(8,128)S(1)}, f32[200,128]{1,0:T(8,128)S(1)}, u32[]{:S(2)}, u32[]{:S(2)}) collective-permute-start(f32[200,128]{1,0:T(8,128)S(1)} %get-tuple-element.38), channel_id=1, source_target_pairs={{0,1},{1,2},{2,3},{4,5},{5,6},{6,7},{8,9},{9,10},{10,11},{12,13},{... | collective-permute-start | bytes 307208 | tf_op jit(solution)/shard_map/ppermute | solution.py:799
  15.3 7.0 %collective-permute-start.1 = (f32[200,128]{1,0:T(8,128)S(1)}, f32[200,128]{1,0:T(8,128)S(1)}, u32[]{:S(2)}, u32[]{:S(2)}) collective-permute-start(f32[200,128]{1,0:T(8,128)S(1)} %get-tuple-element.39), channel_id=1, source_target_pairs={{1,0},{2,1},{3,2},{5,4},{6,5},{7,6},{9,8},{10,9},{11,10},{13,12},{... | collective-permute-start | bytes 307208 | tf_op jit(solution)/shard_map/ppermute | solution.py:799
  30.0 22.9 %collective-permute-start.6 = (f32[656,128]{1,0:T(8,128)}, f32[656,128]{1,0:T(8,128)S(1)}, u32[]{:S(2)}, u32[]{:S(2)}) collective-permute-start(f32[656,128]{1,0:T(8,128)} %get-tuple-element.52), channel_id=1, source_target_pairs={{0,4},{4,8},{8,12},{12,16},{16,20},{20,24},{24,28},{28,0},{1,5},{5... | collective-permute-start | bytes 1007624 | tf_op jit(solution)/shard_map/ppermute | solution.py:799
  30.0 22.9 %collective-permute-start.7 = (f32[656,128]{1,0:T(8,128)}, f32[656,128]{1,0:T(8,128)}, u32[]{:S(2)}, u32[]{:S(2)}) collective-permute-start(f32[656,128]{1,0:T(8,128)} %get-tuple-element.53), channel_id=1, source_target_pairs={{0,28},{4,0},{8,4},{12,8},{16,12},{20,16},{24,20},{28,24},{1,29},{... | collective-permute-start | bytes 1007624 | tf_op jit(solution)/shard_map/ppermute | solution.py:799
  35.1 11.0 %collective-permute-start.4 = (f32[176,128]{1,0:T(8,128)}, f32[176,128]{1,0:T(8,128)S(1)}, u32[]{:S(2)}, u32[]{:S(2)}) collective-permute-start(f32[176,128]{1,0:T(8,128)} %get-tuple-element.48), channel_id=1, source_target_pairs={{0,1},{1,2},{2,3},{4,5},{5,6},{6,7},{8,9},{9,10},{10,11},{12,13},{... | collective-permute-start | bytes 270344 | tf_op jit(solution)/shard_map/ppermute | solution.py:799
  39.3 6.8 %collective-permute-start.5 = (f32[176,128]{1,0:T(8,128)S(1)}, f32[176,128]{1,0:T(8,128)S(1)}, u32[]{:S(2)}, u32[]{:S(2)}) collective-permute-start(f32[176,128]{1,0:T(8,128)S(1)} %get-tuple-element.49), channel_id=1, source_target_pairs={{1,0},{2,1},{3,2},{5,4},{6,5},{7,6},{9,8},{10,9},{11,10},{13,12},{... | collective-permute-start | bytes 270344 | tf_op jit(solution)/shard_map/ppermute | solution.py:799
  53.0 7.2 %copy-start.5 = (s32[24,384,4]{1,2,0:T(4,128)S(1)}, s32[24,384,4]{1,2,0:T(4,128)}, u32[]{:S(2)}) copy-start(s32[24,384,4]{1,2,0:T(4,128)} %param.15) | copy-start | bytes 442372
  53.0 7.3 %copy-start.4 = (f32[24,384,4]{1,2,0:T(4,128)S(1)}, f32[24,384,4]{1,2,0:T(4,128)}, u32[]{:S(2)}) copy-start(f32[24,384,4]{1,2,0:T(4,128)} %param.16) | copy-start | bytes 442372
  53.0 22.2 %copy-start.8 = (f32[384]{0:T(512)S(1)}, f32[384]{0:T(512)}, u32[]{:S(2)}) copy-start(f32[384]{0:T(512)} %param.20) | copy-start | bytes 4612
  53.0 22.2 %copy-start = (f32[8,24,384]{2,1,0:T(8,128)S(1)}, f32[8,24,384]{2,1,0:T(8,128)}, u32[]{:S(2)}) copy-start(f32[8,24,384]{2,1,0:T(8,128)} %u.3) | copy-start | bytes 884740
  53.0 22.1 %copy-start.1 = (f32[8,24,384]{2,1,0:T(8,128)S(1)}, f32[8,24,384]{2,1,0:T(8,128)}, u32[]{:S(2)}) copy-start(f32[8,24,384]{2,1,0:T(8,128)} %v.3) | copy-start | bytes 884740
  53.0 22.1 %copy-start.3 = (s32[24,384]{1,0:T(8,128)S(1)}, s32[24,384]{1,0:T(8,128)}, u32[]{:S(2)}) copy-start(s32[24,384]{1,0:T(8,128)} %mask.7) | copy-start | bytes 110596
  55.9 5.4 %collective-permute-start.8 = (f32[5,8,128]{2,1,0:T(8,128)S(1)}, f32[5,8,128]{2,1,0:T(8,128)S(1)}, u32[]{:S(2)}, u32[]{:S(2)}) collective-permute-start(f32[5,8,128]{2,1,0:T(8,128)S(1)} %get-tuple-element.58.own), channel_id=1, source_target_pairs={{0,4},{4,8},{8,12},{12,16},{16,20},{20,24},{24,28},{28,0},{1,5},{5... | collective-permute-start | bytes 61448 | tf_op jit(solution)/shard_map/ppermute | solution.py:799
  56.0 5.3 %collective-permute-start.9 = (f32[5,8,128]{2,1,0:T(8,128)S(1)}, f32[5,8,128]{2,1,0:T(8,128)S(1)}, u32[]{:S(2)}, u32[]{:S(2)}) collective-permute-start(f32[5,8,128]{2,1,0:T(8,128)S(1)} %get-tuple-element.58.own), channel_id=1, source_target_pairs={{0,28},{4,0},{8,4},{12,8},{16,12},{20,16},{24,20},{28,24},{1,29},{... | collective-permute-start | bytes 61448 | tf_op jit(solution)/shard_map/ppermute | solution.py:799
  63.6 18.4 %collective-permute-start.12 = (f32[24,128]{1,0:T(8,128)S(1)}, f32[24,128]{1,0:T(8,128)S(1)}, u32[]{:S(2)}, u32[]{:S(2)}) collective-permute-start(f32[24,128]{1,0:T(8,128)S(1)} %get-tuple-element.63), channel_id=1, source_target_pairs={{0,1},{1,2},{2,3},{4,5},{5,6},{6,7},{8,9},{9,10},{10,11},{12,13},{... | collective-permute-start | bytes 36872 | tf_op jit(solution)/shard_map/ppermute | solution.py:799
  68.4 13.6 %collective-permute-start.13 = (f32[24,128]{1,0:T(8,128)S(1)}, f32[24,128]{1,0:T(8,128)S(1)}, u32[]{:S(2)}, u32[]{:S(2)}) collective-permute-start(f32[24,128]{1,0:T(8,128)S(1)} %get-tuple-element.64), channel_id=1, source_target_pairs={{1,0},{2,1},{3,2},{5,4},{6,5},{7,6},{9,8},{10,9},{11,10},{13,12},{... | collective-permute-start | bytes 36872 | tf_op jit(solution)/shard_map/ppermute | solution.py:799
  70.4 11.7 %collective-permute-start.10 = (f32[8,128]{1,0:T(8,128)S(1)}, f32[8,128]{1,0:T(8,128)S(1)}, u32[]{:S(2)}, u32[]{:S(2)}) collective-permute-start(f32[8,128]{1,0:T(8,128)S(1)} %get-tuple-element.61.after), channel_id=1, source_target_pairs={{0,4},{4,8},{8,12},{12,16},{16,20},{20,24},{24,28},{28,0},{1,5},{5... | collective-permute-start | bytes 12296 | tf_op jit(solution)/shard_map/ppermute | solution.py:799
  70.4 11.6 %collective-permute-start.11 = (f32[8,128]{1,0:T(8,128)S(1)}, f32[8,128]{1,0:T(8,128)S(1)}, u32[]{:S(2)}, u32[]{:S(2)}) collective-permute-start(f32[8,128]{1,0:T(8,128)S(1)} %get-tuple-element.62), channel_id=1, source_target_pairs={{0,28},{4,0},{8,4},{12,8},{16,12},{20,16},{24,20},{28,24},{1,29},{... | collective-permute-start | bytes 12296 | tf_op jit(solution)/shard_map/ppermute | solution.py:799

commit v3 on v2

--- a/solution.py
+++ b/solution.py
@@ -25,6 +25,14 @@
 
 def pinned(*arrays):
     return [pltpu.with_memory_space_constraint(x, pltpu.HBM) for x in arrays]
+
+
+def kept(array):
+    return pltpu.with_memory_space_constraint(array, pltpu.VMEM)
+
+
+def parity():
+    return lax.rem(lax.axis_index("lat"), 2)
 
 
 class Plan:
@@ -152,6 +160,31 @@
     if plus is None and minus is None:
         return None
     return jnp.where(where, zero if plus is None else plus, zero if minus is None else minus)
+
+
+def columns_kernel(coef, bulk_weight, columns, rows):
+    rows[...] = jnp.zeros_like(rows)
+    rows[3 : 3 + BULK, : bulk_weight.shape[1]] = bulk_weight[...]
+    for at in range(0, rows.shape[1], LANES):
+        count = min(LANES, columns.shape[0] - at)
+        turned = rows[:, at : at + LANES].T
+        columns[at : at + count, :] = coef[at : at + count, :] + turned[:count, :]
+
+
+def columns_of(plan, bulk_weight):
+    comps = plan.comps
+    coef = np.zeros((comps, 3 + BULK), np.float32)
+    coef[:, :3] = plan.coef
+    return pl.pallas_call(
+        columns_kernel,
+        out_shape=jax.ShapeDtypeStruct(coef.shape, F32),
+        in_specs=[VMEM] * 2,
+        out_specs=VMEM,
+        scratch_shapes=[pltpu.VMEM((3 + BULK, -(-comps // LANES) * LANES), F32)],
+        compiler_params=PARAMS,
+        cost_estimate=CHEAP,
+        name="columns",
+    )(jnp.asarray(coef), bulk_weight)
 
 
 def pack_lon_kernel(plan, spec, mask, u, v, east, west, sides, maskv, sem):
@@ -206,8 +239,9 @@
     return jnp.where(lanes == lane, pltpu.roll(column, (lane - source) % LANES, 1), acc)
 
 
-def pack_lat_kernel(plan, spec_hbm, mask, u_hbm, v_hbm, after, north, south, spec, u, v, maskv, sem):
+def pack_lat_kernel(plan, spec_hbm, mask, u_hbm, v_hbm, after, odd, even, spec, u, v, maskv, both, sem):
     del after
+    north, south = (both.at[parity()], both.at[1 - parity()])
     width_x = mask.shape[0]
     levels, ocean_x, ocean_y = u.shape
     last = ocean_y - LANES
@@ -246,19 +280,23 @@
             field = (u, v)[f // levels]
             acc = to_lane(acc, field[f % levels, :, m : m + LANES], source, f, lanes_of(ocean_x))
         out[at : at + ocean_x, :] = acc
+    odd[...] = both[0]
+    even[...] = both[1]
 
 
 def pack_lat(plan, spec2, mask, u, v, after):
-    extra = u.shape[1]
+    assert plan.lat_rows(True) == plan.lat_rows(False)
+    shape = (plan.lat_rows(True) + u.shape[1], LANES)
     return pl.pallas_call(
         functools.partial(pack_lat_kernel, plan),
-        out_shape=[jax.ShapeDtypeStruct((plan.lat_rows(s) + extra, LANES), F32) for s in (True, False)],
+        out_shape=[jax.ShapeDtypeStruct(shape, F32)] * 2 + [pltpu.VMEM(spec2.shape, F32)],
         in_specs=[HBM] * 4 + [ANY],
-        out_specs=[VMEM] * 2,
-        cost_estimate=CHEAP,
-        scratch_shapes=[pltpu.VMEM(x.shape, F32) for x in (spec2, u, v)]
+        out_specs=[VMEM] * 3,
+        cost_estimate=CHEAP,
+        scratch_shapes=[pltpu.VMEM(x.shape, F32) for x in (u, v)]
         + [
             pltpu.VMEM(mask.shape, mask.dtype),
+            pltpu.VMEM((2, *shape), F32),
             pltpu.SemaphoreType.DMA((3 + len(split(0, plan.comps)),)),
         ],
         compiler_params=PARAMS,
@@ -266,40 +304,22 @@
     )(*pinned(spec2, mask, u, v), after)
 
 
-def advect_kernel(plan, step, *refs):
+def advect_kernel(plan, step, state, coefs, more, part):
+    width = part.shape[0]
     if step == 0:
-        state_hbm, transfer_hbm, coefs, mask, part, transfer, state, sem = refs
-    else:
-        state_hbm, transfer_hbm, coefs, sides, part, transfer, state, sem = refs
-    width = part.shape[0]
-    blocks = plan.blocks()
-    parts = []
-    for first, last, *_ in blocks:
-        if step == 0:
-            rows = pl.ds(first * width, (last - first) * width)
-            copy = pltpu.make_async_copy(state_hbm.at[rows, :], state.at[rows, :], sem.at[1 + len(parts)])
-        else:
-            rows = pl.ds(first, last - first)
-            copy = pltpu.make_async_copy(state_hbm.at[:, rows, :], state.at[:, rows, :], sem.at[1 + len(parts)])
-        copy.start()
-        parts.append(copy)
-    fetch = pltpu.make_async_copy(transfer_hbm, transfer, sem.at[0])
-    fetch.start()
-    if step == 0:
-        maskf = mask[...].astype(F32)
+        maskf = more[...].astype(F32)
 
     def column(i, first, last):
         if step == 0:
             return state[pl.ds(first * width + i, last - first, stride=width), :] * maskf[i : i + 1, :]
         if i in (0, width - 1):
-            return sides[min(i, 1), first:last, :]
+            return more[min(i, 1), first:last, :]
         return state[i - 1, first:last, :]
 
-    for copy, (first, last, xs, ys, _) in zip(parts, blocks):
+    for first, last, xs, ys, _ in plan.blocks():
         count = last - first
         keep, east, up = (jnp.broadcast_to(coefs[first:last, q : q + 1], (count, LANES)) for q in range(3))
         lanes = lanes_of(count)
-        copy.wait()
         x = [column(i, first, last) for i in range(width)]
         for i in range(width):
             lat = upwind(
@@ -316,25 +336,19 @@
             if lon is not None:
                 a = a + east * lon
             part[i, first:last, :] = a
-    fetch.wait()
-
-
-def advect(plan, step, state, transfer, coefs, more):
+
+
+def advect(plan, step, state, coefs, more):
     comps, width = (plan.comps, state.shape[0] // plan.comps if step == 0 else state.shape[0] + 2)
-    hbm_state, hbm_transfer = pinned(state, transfer)
     return pl.pallas_call(
         functools.partial(advect_kernel, plan, step),
-        out_shape=[
-            jax.ShapeDtypeStruct((width, comps, LANES), F32),
-            jax.ShapeDtypeStruct(transfer.shape, transfer.dtype),
-        ],
-        in_specs=[HBM, HBM, VMEM, VMEM],
-        out_specs=[VMEM, VMEM],
-        scratch_shapes=[pltpu.VMEM(state.shape, F32), pltpu.SemaphoreType.DMA((1 + len(plan.blocks()),))],
+        out_shape=jax.ShapeDtypeStruct((width, comps, LANES), F32),
+        in_specs=[VMEM] * 3,
+        out_specs=VMEM,
         compiler_params=PARAMS,
         cost_estimate=CHEAP,
         name="advect",
-    )(hbm_state, hbm_transfer, coefs, more)
+    )(kept(state), coefs, more)
 
 
 def block_rows(comps):
@@ -363,16 +377,19 @@
 
 
 def interior_kernel(plan, step, *refs):
-    part, south, north, transfer, coefs, mask = refs[:6]
+    part, from_odd, from_even, transfer, coefs, mask = refs[:6]
     if step == 0:
-        out, edge, up, down = refs[6:10]
-        inner, full, moved, sem = refs[10:]
+        inner, edge, up, down = refs[6:10]
+        full, moved, both = refs[10:]
     else:
         out, edge, bulk, weights = refs[6:10]
-        inner, full, moved, total, sem = refs[10:]
+        inner, full, moved, both, total, sem = refs[10:]
         total[...] = jnp.zeros_like(total)
     width = part.shape[0]
     maskf = mask[...].astype(F32)
+    both[0] = from_odd[: both.shape[1], :]
+    both[1] = from_even[: both.shape[1], :]
+    north, south = (both.at[parity()], both.at[1 - parity()])
     for first, last, _, ys, shifts in plan.blocks():
         rows, count = (slice(first, last), last - first)
         lanes = lanes_of(count)
@@ -401,9 +418,10 @@
         for i in range(1, width - 1):
             s = maskf[i : i + 1, :] * (full[i - 1, rows, :] + 0.5 * added[:, (i - 1) * LANES : i * LANES])
             inner[i - 1, rows, :] = s
-            to = out.at[span, i, 0, :] if step else out.at[i - 1, span, :]
-            copies.append(pltpu.make_async_copy(inner.at[i - 1, span, :], to, sem.at[len(copies)]))
-            copies[-1].start()
+            if step:
+                to = out.at[span, i, 0, :]
+                copies.append(pltpu.make_async_copy(inner.at[i - 1, span, :], to, sem.at[len(copies)]))
+                copies[-1].start()
         if step:
             add_bulk(coefs, weights, rows, inner, total)
             return
@@ -426,33 +444,33 @@
         c.wait()
 
 
-def interior(plan, step, part, south, north, transfer, coefs, mask):
+def interior(plan, step, part, from_odd, from_even, transfer, coefs, mask):
     comps, width = (plan.comps, mask.shape[0])
     middle = (width - 2, comps, LANES)
     edge = jax.ShapeDtypeStruct((2, comps, LANES), F32)
     scratch = [
         pltpu.VMEM(middle, F32),
-        pltpu.VMEM(middle, F32),
         pltpu.VMEM((comps, (width - 2) * LANES), jnp.bfloat16),
+        pltpu.VMEM((2, plan.lat_rows(True), LANES), F32),
     ]
     if step == 0:
-        outs = [pltpu.HBM(middle, F32), edge]
+        outs = [pltpu.VMEM(middle, F32), edge]
         outs += [jax.ShapeDtypeStruct((plan.lat_rows(s), LANES), F32) for s in (True, False)]
     else:
         outs = [pltpu.HBM((comps, width, 1, LANES), F32), edge, jax.ShapeDtypeStruct((BULK, width, LANES), F32)]
         outs += [jax.ShapeDtypeStruct((BULK, comps, LANES), F32)]
-        scratch += [pltpu.VMEM((BULK, width - 2, 8, LANES), F32)]
-    scratch += [pltpu.SemaphoreType.DMA(((width - 2) * comps // block_rows(comps),))]
+        scratch = [pltpu.VMEM(middle, F32)] + scratch + [pltpu.VMEM((BULK, width - 2, 8, LANES), F32)]
+        scratch += [pltpu.SemaphoreType.DMA(((width - 2) * comps // block_rows(comps),))]
     return pl.pallas_call(
         functools.partial(interior_kernel, plan, step),
         out_shape=outs,
         in_specs=[VMEM] * 6,
-        out_specs=[HBM] + [VMEM] * (len(outs) - 1),
+        out_specs=[HBM if step else VMEM] + [VMEM] * (len(outs) - 1),
         scratch_shapes=scratch,
         compiler_params=PARAMS,
         cost_estimate=CHEAP,
         name="interior",
-    )(part, south, north, transfer, coefs, mask)
+    )(part, from_odd, from_even, transfer, coefs, mask)
 
 
 def edges_kernel(plan, step, *refs):
@@ -505,7 +523,8 @@
             at += b - a
 
 
-def merge_lat_kernel(plan, width, state, up_in, down_in, up, down):
+def merge_lat_kernel(plan, width, state, up_in, down_in, odd, even, both):
+    up, down = (both.at[parity()], both.at[1 - parity()])
     for out, given, source, sign in ((up, up_in, LANES - 1, True), (down, down_in, 0, False)):
         for a, b in plan.lat_blocks(sign):
             at, base = plan.lat_place(sign, a, b, width)
@@ -513,6 +532,8 @@
             for side, lane in ((0, base), (1, base + width - 1)):
                 acc = to_lane(acc, state[side, a:b, :], source, lane, lanes_of(b - a))
             out[at, :] = acc
+    odd[...] = both[0]
+    even[...] = both[1]
 
 
 def merge_lat(plan, width, state, up, down):
@@ -521,6 +542,7 @@
         out_shape=[jax.ShapeDtypeStruct(x.shape, F32) for x in (up, down)],
         in_specs=[VMEM] * 3,
         out_specs=[VMEM] * 2,
+        scratch_shapes=[pltpu.VMEM((2, *up.shape), F32)],
         compiler_params=PARAMS,
         cost_estimate=CHEAP,
         name="merge_lat",
@@ -569,6 +591,7 @@
         scratch_shapes=[pltpu.SemaphoreType.DMA((2,))],
         input_output_aliases={1: 0},
         compiler_params=PARAMS,
+        cost_estimate=CHEAP,
         name="finish",
     )(state, out4)
 
@@ -584,13 +607,16 @@
     return before, after, below, above
 
 
-def ocean_base_kernel(plan, u, v, from_west, from_east, from_south, from_north, mask, coriolis, base_u, base_v):
+def ocean_base_kernel(plan, u, v, from_west, from_east, from_odd, from_even, mask, coriolis, base_u, base_v, both):
     levels, ocean_x, ocean_y = u.shape
+    start = plan.lat_rows(True)
+    both[0] = from_odd[start : start + ocean_x, :]
+    both[1] = from_even[start : start + ocean_x, :]
+    from_north, from_south = (both.at[parity()], both.at[1 - parity()])
     tiles = ocean_y // LANES
     maskf = mask[...].astype(F32)
     half = 0.5 * coriolis[...]
     west_at, east_at = (plan.rows("x", s) for s in (True, False))
-    south_at, north_at = (plan.lat_rows(s) for s in (True, False))
     for f, (field, other, out, sign) in enumerate(((u, v, base_u, 1.0), (v, u, base_v, -1.0))):
         for level in range(levels):
             q = field[level]
@@ -604,27 +630,29 @@
                 q,
                 line(from_west, west_at),
                 line(from_east, east_at),
-                from_south[south_at : south_at + ocean_x, lane : lane + 1],
-                from_north[north_at : north_at + ocean_x, lane : lane + 1],
+                from_south[:, lane : lane + 1],
+                from_north[:, lane : lane + 1],
             )
             lap = before + after + below + above - 4.0 * q
             out[level] = maskf * (q + sign * half * other[level] + 0.1 * lap)
 
 
-def ocean_base(plan, u, v, from_west, from_east, from_south, from_north, mask, coriolis):
+def ocean_base(plan, u, v, from_west, from_east, from_odd, from_even, mask, coriolis):
     return pl.pallas_call(
         functools.partial(ocean_base_kernel, plan),
         out_shape=[jax.ShapeDtypeStruct(u.shape, F32)] * 2,
         in_specs=[VMEM] * 8,
         out_specs=[VMEM] * 2,
+        scratch_shapes=[pltpu.VMEM((2, u.shape[1], LANES), F32)],
+        cost_estimate=CHEAP,
         compiler_params=PARAMS,
         name="ocean_base",
-    )(u, v, from_west, from_east, from_south, from_north, mask, coriolis)
-
-
-def gathered(slabs, at, off, weight, count):
-    acc = [0.0] * count
-    for o in range(OFFSETS):
+    )(u, v, from_west, from_east, from_odd, from_even, mask, coriolis)
+
+
+def gathered(slabs, at, off, weight, count, acc=None, offsets=range(OFFSETS)):
+    acc = [0.0] * count if acc is None else acc
+    for o in offsets:
         rows = [slabs(o, q) for q in range(count)]
         for p in range(len(at)):
             w = jnp.where(off[p] == o, weight[p], 0.0)
@@ -634,14 +662,16 @@
 
 
 def fill_table(table, left, own, right, ratio, fields):
-    width = own.shape[1]
+    width = table.shape[1] // (3 * ratio)
     for q in fields:
         for b, ref in enumerate((left, own, right)):
             for r in range(ratio):
-                table[q, pl.ds(b * width * ratio + r, width, stride=ratio), :] = ref[q]
-
-
-def remap_lon_kernel(own, left, right, cell, offset, weight, east, west, rows):
+                rows = pl.ds(b * width * ratio + r, width, stride=ratio)
+                table[q, rows, :] = jnp.zeros((width, LANES), F32) if ref is None else ref[q]
+
+
+def remap_lon_kernel(own, left, right, cell, offset, weight, *refs):
+    east, west, rows = refs[-3:]
     taps, ocean_x, ocean_y = cell.shape
     width = own.shape[1]
     tiles = ocean_y // LANES
@@ -665,8 +695,9 @@
             out[2 * tiles :, :] = jnp.zeros((out.shape[0] - 2 * tiles, LANES), F32)
 
 
-def remap_lat_kernel(own, left, right, cell, offset, weight, after, north, south, table):
+def remap_lat_kernel(own, left, right, cell, offset, weight, after, odd, even, table, both):
     del after
+    north, south = (both.at[parity()], both.at[1 - parity()])
     taps, ocean_x, ocean_y = cell.shape
     ratio = ocean_x // own.shape[1]
     last_lane = ocean_y - LANES
@@ -684,23 +715,25 @@
             for q in range(2):
                 packed = to_lane(packed, acc[q], source, q, lanes)
             out[here, :] = packed
-
-
-def remap_lon(own, left, right, cell, offset, weight):
+    odd[...] = both[0]
+    even[...] = both[1]
+
+
+def remap_lon(own, left, right, cell, offset, weight, *after):
     _, ocean_x, ocean_y = cell.shape
     width = own.shape[1]
     assert width == 8 and ocean_x % width == 0
-    side = jax.ShapeDtypeStruct((8 * pl.cdiv(2 * ocean_y // LANES, 8), LANES), F32)
+    side = jax.ShapeDtypeStruct((max(ocean_x + 8, 8 * pl.cdiv(2 * ocean_y // LANES, 8)), LANES), F32)
     return pl.pallas_call(
         remap_lon_kernel,
         out_shape=[side, side],
-        in_specs=[VMEM] * 6,
+        in_specs=[VMEM] * 6 + [ANY] * len(after),
         out_specs=[VMEM] * 2,
         scratch_shapes=[pltpu.VMEM((2, 3 * width, LANES), F32)],
         compiler_params=PARAMS,
         cost_estimate=CHEAP,
         name="remap_lon",
-    )(own, left, right, cell, offset, weight)
+    )(own, left, right, cell, offset, weight, *after)
 
 
 def remap_lat(own, left, right, cell, offset, weight, after):
@@ -711,46 +744,65 @@
         out_shape=[end, end],
         in_specs=[VMEM] * 6 + [ANY],
         out_specs=[VMEM] * 2,
-        scratch_shapes=[pltpu.VMEM((BULK, 3 * ocean_x, LANES), F32)],
+        scratch_shapes=[pltpu.VMEM((BULK, 3 * ocean_x, LANES), F32), pltpu.VMEM((2, ocean_x, LANES), F32)],
         compiler_params=PARAMS,
         cost_estimate=CHEAP,
         name="remap_lat",
     )(own, left, right, cell, offset, weight, after)
 
 
-def remap_kernel(own, left, right, cell, offset, weight, stress, drift, table):
+def remap_kernel(mine, *refs):
+    if mine:
+        own, cell, offset, weight, forcing, table = refs
+        left = right = None
+    else:
+        left, right, cell, offset, weight, begun, forcing, table = refs
+        own = None
     taps, ocean_x, ocean_y = cell.shape
-    ratio = ocean_x // own.shape[1]
+    ratio = table.shape[1] // ocean_x
+    width = ocean_x // ratio
     fill_table(table, left, own, right, ratio, range(BULK))
     for t in range(ocean_x // 8):
+        used = []
+        for o in range(OFFSETS):
+            inside = [0 <= i // ratio + o - width < width for i in range(8 * t, 8 * t + 8)]
+            if any(inside) if mine else not all(inside):
+                used.append(o)
         for m in range(ocean_y // LANES):
             rows, lanes = (slice(8 * t, 8 * t + 8), slice(m * LANES, (m + 1) * LANES))
             at, off, w = ([x[p, rows, lanes] for p in range(taps)] for x in (cell, offset, weight))
             acc = gathered(
-                lambda o, q: table[q, 8 * t + ratio * o : 8 * t + ratio * o + 8, :], at, off, w, BULK
+                lambda o, q: table[q, 8 * t + ratio * o : 8 * t + ratio * o + 8, :],
+                at, off, w, BULK,
+                None if mine else [begun[q, rows, lanes] for q in range(BULK)],
+                used,
             )
-            for q in range(3):
-                stress[q, rows, lanes] = acc[q]
-            for q in range(2):
-                drift[q, rows, lanes] = acc[3 + q]
-
-
-def remap(own, left, right, cell, offset, weight):
+            for q in range(BULK):
+                forcing[q, rows, lanes] = acc[q]
+
+
+def remap(mine, *args):
+    cell = args[1] if mine else args[2]
     _, ocean_x, ocean_y = cell.shape
     return pl.pallas_call(
-        remap_kernel,
-        out_shape=[jax.ShapeDtypeStruct((n, ocean_x, ocean_y), F32) for n in (3, 2)],
-        in_specs=[VMEM] * 6,
-        out_specs=[VMEM] * 2,
+        functools.partial(remap_kernel, mine),
+        out_shape=jax.ShapeDtypeStruct((BULK, ocean_x, ocean_y), F32),
+        in_specs=[VMEM] * len(args),
+        out_specs=VMEM,
         scratch_shapes=[pltpu.VMEM((BULK, 3 * ocean_x, LANES), F32)],
         compiler_params=PARAMS,
         cost_estimate=CHEAP,
-        name="remap",
-    )(own, left, right, cell, offset, weight)
-
-
-def ocean_final_kernel(stress, drift, from_west, from_east, from_south, from_north, base_u, base_v, mask, coriolis, new_u, new_v):
+        name="remap_own" if mine else "remap_rest",
+    )(*args)
+
+
+def ocean_final_kernel(
+    forcing, from_west, from_east, from_odd, from_even, base_u, base_v, mask, coriolis, new_u, new_v, both
+):
     levels, ocean_x, ocean_y = base_u.shape
+    both[0] = from_odd[...]
+    both[1] = from_even[...]
+    from_north, from_south = (both.at[parity()], both.at[1 - parity()])
     tiles = ocean_y // LANES
 
     def line(buffer, q):
@@ -763,7 +815,7 @@
         lon = q < 2
         lat = q > 0
         before, after, below, above = ocean_shifts(
-            stress[q],
+            forcing[q],
             line(from_west, q) if lon else zero_line,
             line(from_east, q) if lon else zero_line,
             from_south[:, q - 1 : q] if lat else zero_end,
@@ -774,37 +826,44 @@
     force_y = -(grad[1][0] + grad[2][1])
     maskf = mask[...].astype(F32)
     half = 0.5 * coriolis[...]
-    add_u = maskf * (half * drift[1] + 0.5 * force_x)
-    add_v = maskf * (0.5 * force_y - half * drift[0])
+    add_u = maskf * (half * forcing[4] + 0.5 * force_x)
+    add_v = maskf * (0.5 * force_y - half * forcing[3])
     for level in range(levels):
         decay = np.float32(np.exp(np.float32(-level / 3.0)))
         new_u[level] = base_u[level] + decay * add_u
         new_v[level] = base_v[level] + decay * add_v
 
 
-def ocean_final(stress, drift, halos, base_u, base_v, mask, coriolis):
+def ocean_final(forcing, halos, base_u, base_v, mask, coriolis):
     return pl.pallas_call(
         ocean_final_kernel,
         out_shape=[jax.ShapeDtypeStruct(base_u.shape, F32)] * 2,
-        in_specs=[VMEM] * 10,
+        in_specs=[VMEM] * 9,
         out_specs=[VMEM] * 2,
-        compiler_params=PARAMS,
+        scratch_shapes=[pltpu.VMEM((2, base_u.shape[1], LANES), F32)],
+        compiler_params=PARAMS,
+        cost_estimate=CHEAP,
         name="ocean_final",
-    )(stress, drift, *halos, base_u, base_v, mask, coriolis)
-
-
-def send(value, axis, step, wrap):
+    )(forcing, *halos, base_u, base_v, mask, coriolis)
+
+
+def shifted(value, axis, step):
     count = lax.axis_size(axis)
-    pairs = [(i, (i + step) % count) for i in range(count) if wrap or 0 <= i + step < count]
-    return lax.ppermute(value, axis, pairs)
-
-
-def exchange(east, west, north, south):
-    from_south = send(north, "lat", 1, False)
-    from_north = send(south, "lat", -1, False)
-    from_west = send(east, "lon", 1, True)
-    from_east = send(west, "lon", -1, True)
-    return from_west, from_east, from_south, from_north
+    return lax.ppermute(value, axis, [(i, (i + step) % count) for i in range(count)])
+
+
+def swapped(value, axis, first):
+    count = lax.axis_size(axis)
+    pairs = [(i, i + 1) for i in range(first, count - 1, 2)]
+    return lax.ppermute(value, axis, pairs + [(j, i) for i, j in pairs])
+
+
+def exchange(east, west, odd, even):
+    from_odd = swapped(odd, "lat", 0)
+    from_even = swapped(even, "lat", 1)
+    from_west = shifted(east, "lon", 1)
+    from_east = shifted(west, "lon", -1)
+    return from_west, from_east, from_odd, from_even
 
 
 def local(
@@ -823,39 +882,38 @@
     plan = Plan(comps)
     spec2 = spectrum.reshape(comps * width_x, width_y)
     east, west = pack_lon(plan, spectrum.reshape(comps, width_x, 1, width_y), sea_mask, ocean_u, ocean_v)
-    north, south = pack_lat(plan, spec2, sea_mask, ocean_u, ocean_v, east)
-    from_west, from_east, from_south, from_north = exchange(east, west, north, south)
-
-    coefs = jnp.concatenate([jnp.asarray(plan.coef), bulk_weight.T], axis=1)
+    odd, even, spec2 = pack_lat(plan, spec2, sea_mask, ocean_u, ocean_v, east)
+    begun = exchange(east, west, odd, even)
+
+    coefs = columns_of(plan, bulk_weight)
     total_y = width_y * lax.axis_size("lat")
     taps_first = remap_cell.transpose(2, 0, 1)
     offset = taps_first // total_y
-    cell = taps_first - offset * total_y - lax.axis_index("lat") * width_y
+    cell = taps_first % width_y
     weight = remap_weight.transpose(2, 0, 1)
     line = coriolis[None, :]
 
-    part, held = advect(plan, 0, spec2, transfer, coefs, sea_mask)
-    middle, edge, up, down = interior(plan, 0, part, from_south, from_north, held, coefs, sea_mask)
-    base_u, base_v = ocean_base(
-        plan, ocean_u, ocean_v, from_west, from_east, from_south, from_north, ocean_mask, line
-    )
-    sides, east, west = edges(plan, 0, edge, from_west, from_east, held, coefs, sea_mask)
-    north, south = merge_lat(plan, width_x, sides, up, down)
-    from_west, from_east, from_south, from_north = exchange(east, west, north, south)
-
-    part, held = advect(plan, 1, middle, transfer, coefs, sides)
-    out4, edge, bulk, weights = interior(plan, 1, part, from_south, from_north, held, coefs, sea_mask)
-    sides, bulk = edges(plan, 1, edge, from_west, from_east, held, coefs, sea_mask, bulk, weights)
-    left = send(bulk, "lon", 1, True)
-    right = send(bulk, "lon", -1, True)
-    state = finish(sides, out4).reshape(spectrum.shape)
+    part = advect(plan, 0, spec2, coefs, sea_mask)
+    middle, edge, up, down = interior(plan, 0, part, *begun[2:], transfer, coefs, sea_mask)
+    sides, east, west = edges(plan, 0, edge, *begun[:2], transfer, coefs, sea_mask)
+    halos = exchange(east, west, *merge_lat(plan, width_x, sides, up, down))
+
+    part = advect(plan, 1, middle, coefs, sides)
+    out4, edge, bulk, weights = interior(plan, 1, part, *halos[2:], transfer, coefs, sea_mask)
+    sides, bulk = edges(plan, 1, edge, *halos[:2], transfer, coefs, sea_mask, bulk, weights)
+    left = shifted(bulk, "lon", 1)
+    right = shifted(bulk, "lon", -1)
+    state4 = finish(sides, out4)
+    state = state4.reshape(spectrum.shape)
+    base_u, base_v = ocean_base(plan, ocean_u, ocean_v, *begun, ocean_mask, line)
+    forcing = remap(True, bulk, cell, offset, weight)
 
     remapped = (bulk, left, right, cell, offset, weight)
-    east, west = remap_lon(*remapped)
-    north, south = remap_lat(*remapped, east)
-    halos = exchange(east, west, north, south)
-    stress, drift = remap(*remapped)
-    new_u, new_v = ocean_final(stress, drift, halos, base_u, base_v, ocean_mask, line)
+    east, west = remap_lon(*remapped, forcing, base_u, *pinned(state4))
+    odd, even = remap_lat(*remapped, east)
+    halos = exchange(east, west, odd, even)
+    forcing = remap(False, left, right, cell, offset, weight, forcing)
+    new_u, new_v = ocean_final(forcing, halos, base_u, base_v, ocean_mask, line)
     return (state, new_u, new_v)
 
 

time: 83.3 us -> 68.7 us (0.82)
  starting transfers between devices: 37.3 us -> 29.4 us
  Pallas kernels: 43.2 us -> 37.8 us
  waiting for transfers between devices: 1.06 us -> 0.04 us
    ppermute x14, starting transfers between devices: 37.3 us -> 29.4 us  [the longest x8 17.8 us: shifted(): lax.ppermute(value, axis, [(i, (i + step) % count) for i in range(count)])]
    pallas_call x3 -> x5, Pallas kernels: 14.7 us -> 12.7 us  [the longest x2 6.71 us: remap(): pl.pallas_call(functools.partial(remap_kernel, mine), out_shape=jax.Shape...]
    pallas_call x2, Pallas kernels: 5.09 us -> 3.16 us  [edges(): pl.pallas_call(functools.partial(edges_kernel, plan, step), out_shape=out...]
    pallas_call x2, Pallas kernels: 12.3 us -> 11.2 us  [interior(): pl.pallas_call(functools.partial(interior_kernel, plan, step), out_shape=...]
    ppermute x14, waiting for transfers between devices: 1.06 us -> 0.04 us  [the longest x8 0.02 us: shifted(): lax.ppermute(value, axis, [(i, (i + step) % count) for i in range(count)])]
  transfers between devices with their start and end apart: 14 -> 14, of which waited for: 1 -> 0; matrix products, arithmetic and copies ran while one was open for 0% -> 0% of each run, Pallas kernels for 40% -> 46%
where the time goes in v3:
time: 68.7 us; the launch traced here: 68.5 us
  Pallas kernels  37.8 us (55%)
  starting transfers between devices  29.4 us (43%)
  between operations  1.05 us (2%)
    ppermute x8, starting transfers between devices, shifted(): lax.ppermute(value, axis, [(i, (i + step) % count) for i in range(count)])  17.8 us
    ppermute x6, starting transfers between devices, swapped(): return lax.ppermute(value, axis, pairs + [(j, i) for i, j in pairs])  11.5 us
    pallas_call x2, Pallas kernels, interior(): pl.pallas_call(functools.partial(interior_kernel, plan, step), out_shape=...  11.2 us
    pallas_call x2, Pallas kernels, remap(): pl.pallas_call(functools.partial(remap_kernel, mine), out_shape=jax.Shape...  6.71 us
    pallas_call x2, Pallas kernels, advect(): pl.pallas_call(functools.partial(advect_kernel, plan, step), out_shape=ja...  5.78 us
    pallas_call x1, Pallas kernels, pack_lat(): pl.pallas_call(functools.partial(pack_lat_kernel, plan), out_shape=[jax.S...  3.9 us
    pallas_call x2, Pallas kernels, edges(): pl.pallas_call(functools.partial(edges_kernel, plan, step), out_shape=out...  3.16 us
    pallas_call x1, Pallas kernels, pack_lon(): pl.pallas_call(functools.partial(pack_lon_kernel, plan), out_shape=[jax.S...  1.41 us
  transfers between devices with their start and end apart: 14, of which 0 were waited for; matrix products, arithmetic and copies ran while one was open for 0% of the time, Pallas kernels for 46%

profile of v3, /device:TPU:1, one launch (start us, length us, event | category | flops | bytes accessed | tf_op | source)
XLA Modules:
  0.0 68.5 jit_solution(11064936071687028674)
XLA Ops:
  0.6 1.4 %pack_lon.1 = (f32[704,128]{1,0:T(8,128)S(1)}, f32[704,128]{1,0:T(8,128)S(1)}) custom-call(f32[1296,8,1,128]{3,2,1,0:T(1,128)} %bitcast.32, s32[8,128]{1,0:T(8,128)} %refs_5_.7, f32[8,24,384]{2,1,0:T(8,128)} %u.3, f32[8,24,384]{2,1,0:T(8,128)} %v.3), custom_call_target="tpu_custom_call" | custom-call | tf_op jit(solution)/shard_map/pack_lon/pallas_call | solution.py:223
  2.1 2.1 %collective-permute-start.2 = (f32[704,128]{1,0:T(8,128)S(1)}, f32[704,128]{1,0:T(8,128)S(1)}, u32[]{:S(2)}, u32[]{:S(2)}) collective-permute-start(f32[704,128]{1,0:T(8,128)S(1)} %get-tuple-element.31.after), channel_id=1, source_target_pairs={{0,4},{4,8},{8,12},{12,16},{16,20},{20,24},{24,28},{28,0},{1,5},{5... | collective-permute-start | bytes 1081352 | tf_op jit(solution)/shard_map/ppermute | solution.py:852
  4.2 3.1 %collective-permute-start.3 = (f32[704,128]{1,0:T(8,128)S(1)}, f32[704,128]{1,0:T(8,128)S(1)}, u32[]{:S(2)}, u32[]{:S(2)}) collective-permute-start(f32[704,128]{1,0:T(8,128)S(1)} %get-tuple-element.37), channel_id=1, source_target_pairs={{0,28},{4,0},{8,4},{12,8},{16,12},{20,16},{24,20},{28,24},{1,29},{... | collective-permute-start | bytes 1081352 | tf_op jit(solution)/shard_map/ppermute | solution.py:852
  7.3 3.9 %pack_lat.1 = (f32[200,128]{1,0:T(8,128)S(1)}, f32[200,128]{1,0:T(8,128)S(1)}, f32[10368,128]{1,0:T(8,128)S(1)}) custom-call(f32[10368,128]{1,0:T(8,128)} %bitcast.33, s32[8,128]{1,0:T(8,128)} %refs_5_.7, f32[8,24,384]{2,1,0:T(8,128)} %u.3, f32[8,24,384]{2,1,0:T(8,128)} %v.3, f32[704,128]{1,0:T(8,128)S(1)} %get-tuple-element.31.after), custom_call_target="tpu_custom_call" | custom-call | flops 1 | bytes 1 | tf_op jit(solution)/shard_map/pack_lat/pallas_call | solution.py:290
  11.2 1.0 %collective-permute-start = (f32[200,128]{1,0:T(8,128)S(1)}, f32[200,128]{1,0:T(8,128)S(1)}, u32[]{:S(2)}, u32[]{:S(2)}) collective-permute-start(f32[200,128]{1,0:T(8,128)S(1)} %get-tuple-element.33), channel_id=1, source_target_pairs={{0,1},{2,3},{1,0},{3,2},{4,5},{6,7},{5,4},{7,6},{8,9},{10,11},{9,8... | collective-permute-start | bytes 307208 | tf_op jit(solution)/shard_map/ppermute | solution.py:858
  12.2 3.1 %collective-permute-start.1 = (f32[200,128]{1,0:T(8,128)S(1)}, f32[200,128]{1,0:T(8,128)S(1)}, u32[]{:S(2)}, u32[]{:S(2)}) collective-permute-start(f32[200,128]{1,0:T(8,128)S(1)} %get-tuple-element.34), channel_id=1, source_target_pairs={{1,2},{2,1},{5,6},{6,5},{9,10},{10,9},{13,14},{14,13},{17,18},{18,... | collective-permute-start | bytes 307208 | tf_op jit(solution)/shard_map/ppermute | solution.py:858
  15.7 2.9 %advect.2.refs_0_ = f32[8,1296,128]{2,1,0:T(8,128)S(1)} custom-call(f32[10368,128]{1,0:T(8,128)S(1)} %get-tuple-element.32.state, f32[1296,8]{1,0:T(8,128)S(1)} %columns.1.coefs.refs_4_, s32[8,128]{1,0:T(8,128)S(1)} %copy-done.4), custom_call_target="tpu_custom_call" | custom-call | flops 1 | bytes 1 | tf_op jit(solution)/shard_map/advect/pallas_call | solution.py:343
  18.6 4.6 %interior.2 = (f32[6,1296,128]{2,1,0:T(8,128)S(1)}, f32[2,1296,128]{2,1,0:T(8,128)S(1)}, f32[176,128]{1,0:T(8,128)S(1)}, f32[176,128]{1,0:T(8,128)S(1)}) custom-call(f32[8,1296,128]{2,1,0:T(8,128)S(1)} %advect.2.refs_0_, f32[200,128]{1,0:T(8,128)S(1)} %collective-permute-done.refs_1_.from_odd, f32[200,128]{1,0:T(8,128)S(1)} %collective-permute-done.1.refs_2_.from_even, ...), custom_call_target="tpu_custom_call" | custom-call | flops 1 | bytes 1 | tf_op jit(solution)/shard_map/interior/pallas_call | solution.py:464
  23.2 1.4 %edges.2 = (f32[2,1296,128]{2,1,0:T(8,128)S(1)}, f32[656,128]{1,0:T(8,128)S(1)}, f32[656,128]{1,0:T(8,128)S(1)}) custom-call(f32[2,1296,128]{2,1,0:T(8,128)S(1)} %get-tuple-element.36.refs_0_, f32[704,128]{1,0:T(8,128)S(1)} %collective-permute-done.2.refs_1_.from_west, f32[704,128]{1,0:T(8,128)S(1)} %collective-permute-done.3.refs_2_.from_east, ...), custom_call_target="tpu_custom_call" | custom-call | flops 1 | bytes 1 | tf_op jit(solution)/shard_map/edges/pallas_call | solution.py:561
  24.6 4.1 %collective-permute-start.7 = (f32[656,128]{1,0:T(8,128)S(1)}, f32[656,128]{1,0:T(8,128)S(1)}, u32[]{:S(2)}, u32[]{:S(2)}) collective-permute-start(f32[656,128]{1,0:T(8,128)S(1)} %get-tuple-element.45), channel_id=1, source_target_pairs={{0,28},{4,0},{8,4},{12,8},{16,12},{20,16},{24,20},{28,24},{1,29},{... | collective-permute-start | bytes 1007624 | tf_op jit(solution)/shard_map/ppermute | solution.py:852
  29.4 3.3 %collective-permute-start.5 = (f32[176,128]{1,0:T(8,128)S(1)}, f32[176,128]{1,0:T(8,128)S(1)}, u32[]{:S(2)}, u32[]{:S(2)}) collective-permute-start(f32[176,128]{1,0:T(8,128)S(1)} %get-tuple-element.42), channel_id=1, source_target_pairs={{1,2},{2,1},{5,6},{6,5},{9,10},{10,9},{13,14},{14,13},{17,18},{18,... | collective-permute-start | bytes 270344 | tf_op jit(solution)/shard_map/ppermute | solution.py:858
  32.8 2.9 %advect.3.refs_0_ = f32[8,1296,128]{2,1,0:T(8,128)S(1)} custom-call(f32[6,1296,128]{2,1,0:T(8,128)S(1)} %get-tuple-element.35.state, f32[1296,8]{1,0:T(8,128)S(1)} %columns.1.coefs.refs_4_, f32[2,1296,128]{2,1,0:T(8,128)S(1)} %get-tuple-element.38.more.state), custom_call_target="tpu_custom_call" | custom-call | flops 1 | bytes 1 | tf_op jit(solution)/shard_map/advect/pallas_call | solution.py:343
  35.6 6.6 %interior.3 = (f32[1296,8,1,128]{3,2,1,0:T(1,128)}, f32[2,1296,128]{2,1,0:T(8,128)S(1)}, f32[5,8,128]{2,1,0:T(8,128)S(1)}, f32[5,1296,128]{2,1,0:T(8,128)S(1)}) custom-call(f32[8,1296,128]{2,1,0:T(8,128)S(1)} %advect.3.refs_0_, f32[176,128]{1,0:T(8,128)S(1)} %collective-permute-done.4.refs_1_, f32[176,128]{1,0:T(8,128)S(1)} %collective-permute-done.5.refs_2_, ...), custom_call_target="tpu_custom_call" | custom-call | flops 1 | bytes 1 | tf_op jit(solution)/shard_map/interior/pallas_call | solution.py:464
  42.4 1.8 %edges.3 = (f32[2,1296,128]{2,1,0:T(8,128)S(1)}, f32[5,8,128]{2,1,0:T(8,128)S(1)}) custom-call(f32[2,1296,128]{2,1,0:T(8,128)S(1)} %get-tuple-element.43.refs_0_, f32[656,128]{1,0:T(8,128)S(1)} %collective-permute-done.6.refs_1_, f32[656,128]{1,0:T(8,128)S(1)} %collective-permute-done.7.refs_2_, bf16[1296,1296]{1,0:T(8,128)(2,1)S(1)} %copy-done, ...), custom_call_target="tpu_custom_call" | custom-call | flops 1 | bytes 1 | tf_op jit(solution)/shard_map/edges/pallas_call | solution.py:561
  44.2 4.2 %collective-permute-start.9 = (f32[5,8,128]{2,1,0:T(8,128)S(1)}, f32[5,8,128]{2,1,0:T(8,128)S(1)}, u32[]{:S(2)}, u32[]{:S(2)}) collective-permute-start(f32[5,8,128]{2,1,0:T(8,128)S(1)} %get-tuple-element.50.refs_0_.own), channel_id=1, source_target_pairs={{0,28},{4,0},{8,4},{12,8},{16,12},{20,16},{24,20},{28,24},{1,29},{... | collective-permute-start | bytes 61448 | tf_op jit(solution)/shard_map/ppermute | solution.py:852
  49.2 1.1 %finish.1.refs_2_ = f32[1296,8,1,128]{3,2,1,0:T(1,128)} custom-call(f32[2,1296,128]{2,1,0:T(8,128)S(1)} %get-tuple-element.48.state, f32[1296,8,1,128]{3,2,1,0:T(1,128)} %get-tuple-element.49.given), custom_call_target="tpu_custom_call", output_to_operand_aliasing={{}: (1, {})} | custom-call | flops 1 | bytes 1 | tf_op jit(solution)/shard_map/finish/pallas_call | solution.py:586
  50.3 3.2 %remap_own.1.refs_5_.refs_0_ = f32[5,24,384]{2,1,0:T(8,128)S(1)} custom-call(f32[5,8,128]{2,1,0:T(8,128)S(1)} %get-tuple-element.50.refs_0_.own, s32[4,24,384]{2,1,0:T(8,128)S(1)} %get-tuple-element.60.refs_1_.refs_2_.cell, s32[4,24,384]{2,1,0:T(8,128)S(1)} %get-tuple-element.59.refs_2_.refs_3_.offset, f32[4,24,384]{2,1,0:T(8,128)S(1)} %bitcast.28), custom_call_target="tpu_custom_call" | custom-call | flops 1 | bytes 1 | tf_op jit(solution)/shard_map/remap_own/pallas_call | solution.py:787
  53.5 1.1 %remap_lon.1 = (f32[32,128]{1,0:T(8,128)S(1)}, f32[32,128]{1,0:T(8,128)S(1)}) custom-call(f32[5,8,128]{2,1,0:T(8,128)S(1)} %get-tuple-element.50.refs_0_.own, f32[5,8,128]{2,1,0:T(8,128)S(1)} %collective-permute-done.8.refs_0_.left, f32[5,8,128]{2,1,0:T(8,128)S(1)} %collective-permute-done.9.refs_1_.right, ...), custom_call_target="tpu_custom_call" | custom-call | flops 1 | bytes 1 | tf_op jit(solution)/shard_map/remap_lon/pallas_call | solution.py:727
  54.6 4.1 %collective-permute-start.11 = (f32[32,128]{1,0:T(8,128)S(1)}, f32[32,128]{1,0:T(8,128)S(1)}, u32[]{:S(2)}, u32[]{:S(2)}) collective-permute-start(f32[32,128]{1,0:T(8,128)S(1)} %get-tuple-element.53), channel_id=1, source_target_pairs={{0,28},{4,0},{8,4},{12,8},{16,12},{20,16},{24,20},{28,24},{1,29},{... | collective-permute-start | bytes 49160 | tf_op jit(solution)/shard_map/ppermute | solution.py:852
  58.8 1.3 %remap_lat.1 = (f32[24,128]{1,0:T(8,128)S(1)}, f32[24,128]{1,0:T(8,128)S(1)}) custom-call(f32[5,8,128]{2,1,0:T(8,128)S(1)} %get-tuple-element.50.refs_0_.own, f32[5,8,128]{2,1,0:T(8,128)S(1)} %collective-permute-done.8.refs_0_.left, f32[5,8,128]{2,1,0:T(8,128)S(1)} %collective-permute-done.9.refs_1_.right, ...), custom_call_target="tpu_custom_call" | custom-call | flops 1 | bytes 1 | tf_op jit(solution)/shard_map/remap_lat/pallas_call | solution.py:742
  60.1 1.0 %collective-permute-start.12 = (f32[24,128]{1,0:T(8,128)S(1)}, f32[24,128]{1,0:T(8,128)S(1)}, u32[]{:S(2)}, u32[]{:S(2)}) collective-permute-start(f32[24,128]{1,0:T(8,128)S(1)} %get-tuple-element.54), channel_id=1, source_target_pairs={{0,1},{2,3},{1,0},{3,2},{4,5},{6,7},{5,4},{7,6},{8,9},{10,11},{9,8... | collective-permute-start | bytes 36872 | tf_op jit(solution)/shard_map/ppermute | solution.py:858
  61.1 2.9 %collective-permute-start.13 = (f32[24,128]{1,0:T(8,128)S(1)}, f32[24,128]{1,0:T(8,128)S(1)}, u32[]{:S(2)}, u32[]{:S(2)}) collective-permute-start(f32[24,128]{1,0:T(8,128)S(1)} %get-tuple-element.55), channel_id=1, source_target_pairs={{1,2},{2,1},{5,6},{6,5},{9,10},{10,9},{13,14},{14,13},{17,18},{18,... | collective-permute-start | bytes 36872 | tf_op jit(solution)/shard_map/ppermute | solution.py:858
  64.0 3.5 %remap_rest.1.forcing = f32[5,24,384]{2,1,0:T(8,128)S(1)} custom-call(f32[5,8,128]{2,1,0:T(8,128)S(1)} %collective-permute-done.8.refs_0_.left, f32[5,8,128]{2,1,0:T(8,128)S(1)} %collective-permute-done.9.refs_1_.right, s32[4,24,384]{2,1,0:T(8,128)S(1)} %get-tuple-element.60.refs_1_.refs_2_.cell, s32[4,24,384]{2,1,0:T(8,128)S(1)} %get-tuple-element.59.refs_2_.refs_3_.offset, ...), custom_call_target="tpu_custom_call" | custom-call | flops 1 | bytes 1 | tf_op jit(solution)/shard_map/remap_rest/pallas_call | solution.py:787
  67.5 1.0 %ocean_final.1 = (f32[8,24,384]{2,1,0:T(8,128)}, f32[8,24,384]{2,1,0:T(8,128)}) custom-call(f32[5,24,384]{2,1,0:T(8,128)S(1)} %remap_rest.1.forcing, f32[32,128]{1,0:T(8,128)S(1)} %collective-permute-done.10.from_west, f32[32,128]{1,0:T(8,128)S(1)} %collective-permute-done.11.from_east, f32[24,128]{1,0:T(8,128)S(1)} %collective-permute-done.12.from_odd, ...), custom_call_target="tpu_custom_call" | custom-call | flops 1 | bytes 1 | tf_op jit(solution)/shard_map/ocean_final/pallas_call | solution.py:838
  (44 shorter events, 1.8 us)
Async XLA Ops:
  2.0 13.3 %copy-start.3 = (f32[1296,8]{1,0:T(8,128)S(1)}, f32[1296,8]{1,0:T(8,128)}, u32[]{:S(2)}) copy-start(f32[1296,8]{1,0:T(8,128)} %constant.32.clone.coef) | copy-start | bytes 124420
  2.1 13.3 %copy-start.6 = (f32[5,1296]{1,0:T(8,128)S(1)}, f32[5,1296]{1,0:T(8,128)}, u32[]{:S(2)}) copy-start(f32[5,1296]{1,0:T(8,128)} %bulk_weight.1) | copy-start | bytes 77764
  2.1 13.6 %copy-start.4 = (s32[8,128]{1,0:T(8,128)S(1)}, s32[8,128]{1,0:T(8,128)}, u32[]{:S(2)}) copy-start(s32[8,128]{1,0:T(8,128)} %refs_5_.7) | copy-start | bytes 12292
  2.1 21.1 %collective-permute-start.2 = (f32[704,128]{1,0:T(8,128)S(1)}, f32[704,128]{1,0:T(8,128)S(1)}, u32[]{:S(2)}, u32[]{:S(2)}) collective-permute-start(f32[704,128]{1,0:T(8,128)S(1)} %get-tuple-element.31.after), channel_id=1, source_target_pairs={{0,4},{4,8},{8,12},{12,16},{16,20},{20,24},{24,28},{28,0},{1,5},{5... | collective-permute-start | bytes 1081352 | tf_op jit(solution)/shard_map/ppermute | solution.py:852
  4.2 19.0 %collective-permute-start.3 = (f32[704,128]{1,0:T(8,128)S(1)}, f32[704,128]{1,0:T(8,128)S(1)}, u32[]{:S(2)}, u32[]{:S(2)}) collective-permute-start(f32[704,128]{1,0:T(8,128)S(1)} %get-tuple-element.37), channel_id=1, source_target_pairs={{0,28},{4,0},{8,4},{12,8},{16,12},{20,16},{24,20},{28,24},{1,29},{... | collective-permute-start | bytes 1081352 | tf_op jit(solution)/shard_map/ppermute | solution.py:852
  11.2 7.4 %collective-permute-start = (f32[200,128]{1,0:T(8,128)S(1)}, f32[200,128]{1,0:T(8,128)S(1)}, u32[]{:S(2)}, u32[]{:S(2)}) collective-permute-start(f32[200,128]{1,0:T(8,128)S(1)} %get-tuple-element.33), channel_id=1, source_target_pairs={{0,1},{2,3},{1,0},{3,2},{4,5},{6,7},{5,4},{7,6},{8,9},{10,11},{9,8... | collective-permute-start | bytes 307208 | tf_op jit(solution)/shard_map/ppermute | solution.py:858
  12.2 6.4 %collective-permute-start.1 = (f32[200,128]{1,0:T(8,128)S(1)}, f32[200,128]{1,0:T(8,128)S(1)}, u32[]{:S(2)}, u32[]{:S(2)}) collective-permute-start(f32[200,128]{1,0:T(8,128)S(1)} %get-tuple-element.34), channel_id=1, source_target_pairs={{1,2},{2,1},{5,6},{6,5},{9,10},{10,9},{13,14},{14,13},{17,18},{18,... | collective-permute-start | bytes 307208 | tf_op jit(solution)/shard_map/ppermute | solution.py:858
  15.7 3.0 %copy-start = (bf16[1296,1296]{1,0:T(8,128)(2,1)S(1)}, bf16[1296,1296]{1,0:T(8,128)(2,1)}, u32[]{:S(2)}) copy-start(bf16[1296,1296]{1,0:T(8,128)(2,1)} %refs_3_.7) | copy-start | bytes 10077700
  24.6 17.7 %collective-permute-start.6 = (f32[656,128]{1,0:T(8,128)S(1)}, f32[656,128]{1,0:T(8,128)S(1)}, u32[]{:S(2)}, u32[]{:S(2)}) collective-permute-start(f32[656,128]{1,0:T(8,128)S(1)} %get-tuple-element.44), channel_id=1, source_target_pairs={{0,4},{4,8},{8,12},{12,16},{16,20},{20,24},{24,28},{28,0},{1,5},{5... | collective-permute-start | bytes 1007624 | tf_op jit(solution)/shard_map/ppermute | solution.py:852
  24.6 17.7 %collective-permute-start.7 = (f32[656,128]{1,0:T(8,128)S(1)}, f32[656,128]{1,0:T(8,128)S(1)}, u32[]{:S(2)}, u32[]{:S(2)}) collective-permute-start(f32[656,128]{1,0:T(8,128)S(1)} %get-tuple-element.45), channel_id=1, source_target_pairs={{0,28},{4,0},{8,4},{12,8},{16,12},{20,16},{24,20},{28,24},{1,29},{... | collective-permute-start | bytes 1007624 | tf_op jit(solution)/shard_map/ppermute | solution.py:852
  29.2 6.4 %collective-permute-start.4 = (f32[176,128]{1,0:T(8,128)S(1)}, f32[176,128]{1,0:T(8,128)S(1)}, u32[]{:S(2)}, u32[]{:S(2)}) collective-permute-start(f32[176,128]{1,0:T(8,128)S(1)} %get-tuple-element.41), channel_id=1, source_target_pairs={{0,1},{2,3},{1,0},{3,2},{4,5},{6,7},{5,4},{7,6},{8,9},{10,11},{9,8... | collective-permute-start | bytes 270344 | tf_op jit(solution)/shard_map/ppermute | solution.py:858
  29.4 6.2 %collective-permute-start.5 = (f32[176,128]{1,0:T(8,128)S(1)}, f32[176,128]{1,0:T(8,128)S(1)}, u32[]{:S(2)}, u32[]{:S(2)}) collective-permute-start(f32[176,128]{1,0:T(8,128)S(1)} %get-tuple-element.42), channel_id=1, source_target_pairs={{1,2},{2,1},{5,6},{6,5},{9,10},{10,9},{13,14},{14,13},{17,18},{18,... | collective-permute-start | bytes 270344 | tf_op jit(solution)/shard_map/ppermute | solution.py:858
  42.3 6.1 %copy-start.7 = (s32[24,384,4]{1,2,0:T(4,128)S(1)}, s32[24,384,4]{1,2,0:T(4,128)}, u32[]{:S(2)}) copy-start(s32[24,384,4]{1,2,0:T(4,128)} %param.15) | copy-start | bytes 442372
  42.3 6.2 %copy-start.8 = (f32[24,384,4]{1,2,0:T(4,128)S(1)}, f32[24,384,4]{1,2,0:T(4,128)}, u32[]{:S(2)}) copy-start(f32[24,384,4]{1,2,0:T(4,128)} %param.16) | copy-start | bytes 442372
  42.3 6.2 %copy-start.9 = (f32[384]{0:T(512)S(1)}, f32[384]{0:T(512)}, u32[]{:S(2)}) copy-start(f32[384]{0:T(512)} %param.20) | copy-start | bytes 4612
  42.4 6.2 %copy-start.1 = (f32[8,24,384]{2,1,0:T(8,128)S(1)}, f32[8,24,384]{2,1,0:T(8,128)}, u32[]{:S(2)}) copy-start(f32[8,24,384]{2,1,0:T(8,128)} %u.3) | copy-start | bytes 884740
  42.4 6.2 %copy-start.2 = (f32[8,24,384]{2,1,0:T(8,128)S(1)}, f32[8,24,384]{2,1,0:T(8,128)}, u32[]{:S(2)}) copy-start(f32[8,24,384]{2,1,0:T(8,128)} %v.3) | copy-start | bytes 884740
  42.4 6.2 %copy-start.5 = (s32[24,384]{1,0:T(8,128)S(1)}, s32[24,384]{1,0:T(8,128)}, u32[]{:S(2)}) copy-start(s32[24,384]{1,0:T(8,128)} %mask.7) | copy-start | bytes 110596
  44.2 9.3 %collective-permute-start.8 = (f32[5,8,128]{2,1,0:T(8,128)S(1)}, f32[5,8,128]{2,1,0:T(8,128)S(1)}, u32[]{:S(2)}, u32[]{:S(2)}) collective-permute-start(f32[5,8,128]{2,1,0:T(8,128)S(1)} %get-tuple-element.50.refs_0_.own), channel_id=1, source_target_pairs={{0,4},{4,8},{8,12},{12,16},{16,20},{20,24},{24,28},{28,0},{1,5},{5... | collective-permute-start | bytes 61448 | tf_op jit(solution)/shard_map/ppermute | solution.py:852
  44.2 9.2 %collective-permute-start.9 = (f32[5,8,128]{2,1,0:T(8,128)S(1)}, f32[5,8,128]{2,1,0:T(8,128)S(1)}, u32[]{:S(2)}, u32[]{:S(2)}) collective-permute-start(f32[5,8,128]{2,1,0:T(8,128)S(1)} %get-tuple-element.50.refs_0_.own), channel_id=1, source_target_pairs={{0,28},{4,0},{8,4},{12,8},{16,12},{20,16},{24,20},{28,24},{1,29},{... | collective-permute-start | bytes 61448 | tf_op jit(solution)/shard_map/ppermute | solution.py:852
  54.6 12.9 %collective-permute-start.10 = (f32[32,128]{1,0:T(8,128)S(1)}, f32[32,128]{1,0:T(8,128)S(1)}, u32[]{:S(2)}, u32[]{:S(2)}) collective-permute-start(f32[32,128]{1,0:T(8,128)S(1)} %get-tuple-element.52.after), channel_id=1, source_target_pairs={{0,4},{4,8},{8,12},{12,16},{16,20},{20,24},{24,28},{28,0},{1,5},{5... | collective-permute-start | bytes 49160 | tf_op jit(solution)/shard_map/ppermute | solution.py:852
  54.6 12.9 %collective-permute-start.11 = (f32[32,128]{1,0:T(8,128)S(1)}, f32[32,128]{1,0:T(8,128)S(1)}, u32[]{:S(2)}, u32[]{:S(2)}) collective-permute-start(f32[32,128]{1,0:T(8,128)S(1)} %get-tuple-element.53), channel_id=1, source_target_pairs={{0,28},{4,0},{8,4},{12,8},{16,12},{20,16},{24,20},{28,24},{1,29},{... | collective-permute-start | bytes 49160 | tf_op jit(solution)/shard_map/ppermute | solution.py:852
  60.1 7.4 %collective-permute-start.12 = (f32[24,128]{1,0:T(8,128)S(1)}, f32[24,128]{1,0:T(8,128)S(1)}, u32[]{:S(2)}, u32[]{:S(2)}) collective-permute-start(f32[24,128]{1,0:T(8,128)S(1)} %get-tuple-element.54), channel_id=1, source_target_pairs={{0,1},{2,3},{1,0},{3,2},{4,5},{6,7},{5,4},{7,6},{8,9},{10,11},{9,8... | collective-permute-start | bytes 36872 | tf_op jit(solution)/shard_map/ppermute | solution.py:858
  61.1 6.4 %collective-permute-start.13 = (f32[24,128]{1,0:T(8,128)S(1)}, f32[24,128]{1,0:T(8,128)S(1)}, u32[]{:S(2)}, u32[]{:S(2)}) collective-permute-start(f32[24,128]{1,0:T(8,128)S(1)} %get-tuple-element.55), channel_id=1, source_target_pairs={{1,2},{2,1},{5,6},{6,5},{9,10},{10,9},{13,14},{14,13},{17,18},{18,... | collective-permute-start | bytes 36872 | tf_op jit(solution)/shard_map/ppermute | solution.py:858

commit v4 on v3

--- a/solution.py
+++ b/solution.py
@@ -31,8 +31,12 @@
     return pltpu.with_memory_space_constraint(array, pltpu.VMEM)
 
 
-def parity():
-    return lax.rem(lax.axis_index("lat"), 2)
+def parity(axis):
+    return lax.rem(lax.axis_index(axis), 2)
+
+
+def sides_of(both, axis):
+    return both.at[1 - parity(axis)], both.at[parity(axis)]
 
 
 class Plan:
@@ -187,8 +191,9 @@
     )(jnp.asarray(coef), bulk_weight)
 
 
-def pack_lon_kernel(plan, spec, mask, u, v, east, west, sides, maskv, sem):
-    last_col, last_row, levels = (spec.shape[1] - 1, u.shape[1] - 8, u.shape[0])
+def pack_lon_kernel(plan, spec, mask, odd, even, maskv, both, sem):
+    last_col = spec.shape[1] - 1
+    west, east = sides_of(both, "lon")
     copies = [pltpu.make_async_copy(mask, maskv, sem.at[0])]
     for out, sign, col in ((east, True, last_col), (west, False, 0)):
         at = 0
@@ -199,40 +204,34 @@
                 )
             )
             at += b - a
-    for f, field in enumerate((u, v)):
-        for side, row in enumerate((last_row, 0)):
-            copies.append(
-                pltpu.make_async_copy(field.at[:, pl.ds(row, 8), :], sides.at[f, side], sem.at[len(copies)])
-            )
     for c in copies:
         c.start()
     for c in copies:
         c.wait()
-    for side, (out, sign, col) in enumerate(((east, True, last_col), (west, False, 0))):
-        at = plan.rows("x", sign)
-        out[:at, :] = out[:at, :] * maskv[col : col + 1, :].astype(F32)
-        for f in range(2):
-            for m in range(u.shape[2] // LANES):
-                out[at : at + levels, :] = sides[f, side, :, 7 - 7 * side, m * LANES : (m + 1) * LANES]
-                at += levels
-
-
-def pack_lon(plan, spec4, mask, u, v):
-    extra = 2 * u.shape[0] * u.shape[2] // LANES
+    masks = [maskv[col : col + 1, :].astype(F32) for col in (last_col, 0)]
+    lower = jnp.full((1, LANES), parity("lon"), jnp.int32) == 0
+    odd[...] = both[0] * jnp.where(lower, masks[0], masks[1])
+    even[...] = both[1] * jnp.where(lower, masks[1], masks[0])
+
+
+def pack_lon(plan, spec4, mask):
     segments = sum(len(plan.seg["x", s]) for s in (True, False))
+    shape = (plan.rows("x", True), LANES)
+    assert plan.rows("x", True) == plan.rows("x", False)
     return pl.pallas_call(
         functools.partial(pack_lon_kernel, plan),
-        out_shape=[jax.ShapeDtypeStruct((plan.rows("x", s) + extra, LANES), F32) for s in (True, False)],
-        in_specs=[HBM] * 4,
+        out_shape=[jax.ShapeDtypeStruct(shape, F32)] * 2,
+        in_specs=[HBM] * 2,
         out_specs=[VMEM, VMEM],
         scratch_shapes=[
-            pltpu.VMEM((2, 2, u.shape[0], 8, u.shape[2]), F32),
             pltpu.VMEM(mask.shape, mask.dtype),
-            pltpu.SemaphoreType.DMA((segments + 5,)),
+            pltpu.VMEM((2, *shape), F32),
+            pltpu.SemaphoreType.DMA((segments + 1,)),
         ],
         compiler_params=PARAMS,
+        cost_estimate=CHEAP,
         name="pack_lon",
-    )(*pinned(spec4, mask, u, v))
+    )(*pinned(spec4, mask))
 
 
 def to_lane(acc, column, source, lane, lanes):
@@ -241,7 +240,7 @@
 
 def pack_lat_kernel(plan, spec_hbm, mask, u_hbm, v_hbm, after, odd, even, spec, u, v, maskv, both, sem):
     del after
-    north, south = (both.at[parity()], both.at[1 - parity()])
+    south, north = sides_of(both, "lat")
     width_x = mask.shape[0]
     levels, ocean_x, ocean_y = u.shape
     last = ocean_y - LANES
@@ -389,7 +388,7 @@
     maskf = mask[...].astype(F32)
     both[0] = from_odd[: both.shape[1], :]
     both[1] = from_even[: both.shape[1], :]
-    north, south = (both.at[parity()], both.at[1 - parity()])
+    south, north = sides_of(both, "lat")
     for first, last, _, ys, shifts in plan.blocks():
         rows, count = (slice(first, last), last - first)
         lanes = lanes_of(count)
@@ -474,18 +473,18 @@
 
 
 def edges_kernel(plan, step, *refs):
-    refs = list(refs)
-    part, from_west, from_east, transfer, coefs, mask = refs[:6]
+    part, from_odd, from_even, transfer, coefs, mask = refs[:6]
     if step == 0:
-        state, east, west = refs[6:9]
-        full, moved = refs[9:]
+        state, odd, even = refs[6:9]
+        full, moved, both = refs[9:]
     else:
         bulk_in, weights = refs[6:8]
-        state, bulk = refs[8:10]
-        full, moved, total = refs[10:]
+        state, bulk, full, moved, both, total = refs[-6:]
     width = mask.shape[0]
     maskf = jnp.concatenate([mask[0:1, :], mask[width - 1 : width, :]], axis=0).astype(F32)
-
+    both[0] = from_odd[...]
+    both[1] = from_even[...]
+    from_west, from_east = sides_of(both, "lon")
     for first, last, xs, ys, shifts in plan.blocks():
         rows, count = (slice(first, last), last - first)
         speed = jnp.broadcast_to(coefs[rows, 1:2], (count, LANES))
@@ -516,15 +515,17 @@
             bulk[q, 0:1, :] = total[q, 0].sum(0, keepdims=True)
             bulk[q, width - 1 : width, :] = total[q, 1].sum(0, keepdims=True)
         return
-    for out, side, sign in ((east, 1, True), (west, 0, False)):
+    for out, side, sign in ((from_east, 1, True), (from_west, 0, False)):
         at = 0
         for a, b in plan.seg["x", sign]:
             out[at : at + b - a, :] = state[side, a:b, :]
             at += b - a
+    odd[...] = both[0]
+    even[...] = both[1]
 
 
 def merge_lat_kernel(plan, width, state, up_in, down_in, odd, even, both):
-    up, down = (both.at[parity()], both.at[1 - parity()])
+    down, up = sides_of(both, "lat")
     for out, given, source, sign in ((up, up_in, LANES - 1, True), (down, down_in, 0, False)):
         for a, b in plan.lat_blocks(sign):
             at, base = plan.lat_place(sign, a, b, width)
@@ -549,10 +550,11 @@
     )(state, up, down)
 
 
-def edges(plan, step, part, from_west, from_east, transfer, coefs, mask, *more):
+def edges(plan, step, part, from_odd, from_even, transfer, coefs, mask, *more):
     comps, width = (plan.comps, mask.shape[0])
     outs = [jax.ShapeDtypeStruct((2, comps, LANES), F32)]
     scratch = [pltpu.VMEM((2, comps, LANES), F32), pltpu.VMEM((comps, 2 * LANES), jnp.bfloat16)]
+    scratch += [pltpu.VMEM((2, plan.rows("x", True), LANES), F32)]
     if step == 0:
         outs += [jax.ShapeDtypeStruct((plan.rows("x", s), LANES), F32) for s in (True, False)]
     else:
@@ -561,39 +563,13 @@
     return pl.pallas_call(
         functools.partial(edges_kernel, plan, step),
         out_shape=outs,
-        in_specs=[VMEM] * (6 + len(more)),
+        in_specs=[VMEM] * min(8, 6 + len(more)) + [ANY] * max(0, len(more) - 2),
         out_specs=[VMEM] * len(outs),
         scratch_shapes=scratch,
         compiler_params=PARAMS,
         cost_estimate=CHEAP,
         name="edges",
-    )(part, from_west, from_east, transfer, coefs, mask, *more)
-
-
-def finish_kernel(state, given, out, sem):
-    width = out.shape[1]
-    copies = [
-        pltpu.make_async_copy(state.at[side], out.at[:, col, 0, :], sem.at[side])
-        for side, col in ((0, 0), (1, width - 1))
-    ]
-    for c in copies:
-        c.start()
-    for c in copies:
-        c.wait()
-
-
-def finish(state, out4):
-    return pl.pallas_call(
-        finish_kernel,
-        out_shape=jax.ShapeDtypeStruct(out4.shape, F32),
-        in_specs=[ANY, ANY],
-        out_specs=ANY,
-        scratch_shapes=[pltpu.SemaphoreType.DMA((2,))],
-        input_output_aliases={1: 0},
-        compiler_params=PARAMS,
-        cost_estimate=CHEAP,
-        name="finish",
-    )(state, out4)
+    )(part, from_odd, from_even, transfer, coefs, mask, *more)
 
 
 def ocean_shifts(q, west, east, south, north):
@@ -607,29 +583,23 @@
     return before, after, below, above
 
 
-def ocean_base_kernel(plan, u, v, from_west, from_east, from_odd, from_even, mask, coriolis, base_u, base_v, both):
+def ocean_base_kernel(plan, u, v, from_odd, from_even, mask, coriolis, base_u, base_v, both):
     levels, ocean_x, ocean_y = u.shape
     start = plan.lat_rows(True)
     both[0] = from_odd[start : start + ocean_x, :]
     both[1] = from_even[start : start + ocean_x, :]
-    from_north, from_south = (both.at[parity()], both.at[1 - parity()])
-    tiles = ocean_y // LANES
+    from_south, from_north = sides_of(both, "lat")
     maskf = mask[...].astype(F32)
     half = 0.5 * coriolis[...]
-    west_at, east_at = (plan.rows("x", s) for s in (True, False))
     for f, (field, other, out, sign) in enumerate(((u, v, base_u, 1.0), (v, u, base_v, -1.0))):
         for level in range(levels):
             q = field[level]
 
-            def line(buffer, at):
-                parts = [buffer[at + (f * tiles + m) * levels + level, :][None, :] for m in range(tiles)]
-                return jnp.concatenate(parts, axis=1)
-
             lane = f * levels + level
             before, after, below, above = ocean_shifts(
                 q,
-                line(from_west, west_at),
-                line(from_east, east_at),
+                0.0,
+                0.0,
                 from_south[:, lane : lane + 1],
                 from_north[:, lane : lane + 1],
             )
@@ -637,17 +607,17 @@
             out[level] = maskf * (q + sign * half * other[level] + 0.1 * lap)
 
 
-def ocean_base(plan, u, v, from_west, from_east, from_odd, from_even, mask, coriolis):
+def ocean_base(plan, u, v, from_odd, from_even, mask, coriolis):
     return pl.pallas_call(
         functools.partial(ocean_base_kernel, plan),
         out_shape=[jax.ShapeDtypeStruct(u.shape, F32)] * 2,
-        in_specs=[VMEM] * 8,
+        in_specs=[VMEM] * 6,
         out_specs=[VMEM] * 2,
         scratch_shapes=[pltpu.VMEM((2, u.shape[1], LANES), F32)],
         cost_estimate=CHEAP,
         compiler_params=PARAMS,
         name="ocean_base",
-    )(u, v, from_west, from_east, from_odd, from_even, mask, coriolis)
+    )(u, v, from_odd, from_even, mask, coriolis)
 
 
 def gathered(slabs, at, off, weight, count, acc=None, offsets=range(OFFSETS)):
@@ -670,12 +640,24 @@
                 table[q, rows, :] = jnp.zeros((width, LANES), F32) if ref is None else ref[q]
 
 
-def remap_lon_kernel(own, left, right, cell, offset, weight, *refs):
-    east, west, rows = refs[-3:]
+def bands(from_odd, from_even, near):
+    near[0] = from_odd[...]
+    near[1] = from_even[...]
+    return sides_of(near, "lon")
+
+
+def line_rows(tiles):
+    return 8 * pl.cdiv(2 * tiles, 8)
+
+
+def remap_lon_kernel(own, from_odd, from_even, cell, offset, weight, u, v, *refs):
+    odd, even, rows, near, both = refs[-5:]
     taps, ocean_x, ocean_y = cell.shape
-    width = own.shape[1]
+    width, levels = (own.shape[1], u.shape[0])
     tiles = ocean_y // LANES
     last_row = ocean_x - 8
+    left, right = bands(from_odd, from_even, near)
+    west, east = sides_of(both, "lon")
     for b, ref in enumerate((left, own, right)):
         rows[:, b * width : (b + 1) * width, :] = ref[0:2]
     first_half = lax.broadcasted_iota(jnp.int32, (8, LANES), 0) < 4
@@ -690,14 +672,20 @@
             n = q * tiles + m
             east[n : n + 1, :] = acc[q][7:8, :]
             west[n : n + 1, :] = acc[q][0:1, :]
-    if 2 * tiles < east.shape[0]:
-        for out in (east, west):
-            out[2 * tiles :, :] = jnp.zeros((out.shape[0] - 2 * tiles, LANES), F32)
-
-
-def remap_lat_kernel(own, left, right, cell, offset, weight, after, odd, even, table, both):
+    for out, row in ((east, ocean_x - 1), (west, 0)):
+        at = line_rows(tiles)
+        for field in (u, v):
+            for m in range(tiles):
+                out[at : at + levels, :] = field[:, row, m * LANES : (m + 1) * LANES]
+                at += levels
+    odd[...] = both[0]
+    even[...] = both[1]
+
+
+def remap_lat_kernel(own, from_odd, from_even, cell, offset, weight, after, odd, even, table, near, both):
     del after
-    north, south = (both.at[parity()], both.at[1 - parity()])
+    left, right = bands(from_odd, from_even, near)
+    south, north = sides_of(both, "lat")
     taps, ocean_x, ocean_y = cell.shape
     ratio = ocean_x // own.shape[1]
     last_lane = ocean_y - LANES
@@ -719,24 +707,28 @@
     even[...] = both[1]
 
 
-def remap_lon(own, left, right, cell, offset, weight, *after):
+def remap_lon(own, from_odd, from_even, cell, offset, weight, u, v, *after):
     _, ocean_x, ocean_y = cell.shape
-    width = own.shape[1]
+    width, tiles = (own.shape[1], ocean_y // LANES)
     assert width == 8 and ocean_x % width == 0
-    side = jax.ShapeDtypeStruct((max(ocean_x + 8, 8 * pl.cdiv(2 * ocean_y // LANES, 8)), LANES), F32)
+    shape = (line_rows(tiles) + 2 * u.shape[0] * tiles, LANES)
     return pl.pallas_call(
         remap_lon_kernel,
-        out_shape=[side, side],
-        in_specs=[VMEM] * 6 + [ANY] * len(after),
+        out_shape=[jax.ShapeDtypeStruct(shape, F32)] * 2,
+        in_specs=[VMEM] * 8 + [ANY] * len(after),
         out_specs=[VMEM] * 2,
-        scratch_shapes=[pltpu.VMEM((2, 3 * width, LANES), F32)],
+        scratch_shapes=[
+            pltpu.VMEM((2, 3 * width, LANES), F32),
+            pltpu.VMEM((2, *own.shape), F32),
+            pltpu.VMEM((2, *shape), F32),
+        ],
         compiler_params=PARAMS,
         cost_estimate=CHEAP,
         name="remap_lon",
-    )(own, left, right, cell, offset, weight, *after)
-
-
-def remap_lat(own, left, right, cell, offset, weight, after):
+    )(own, from_odd, from_even, cell, offset, weight, u, v, *after)
+
+
+def remap_lat(own, from_odd, from_even, cell, offset, weight, after):
     ocean_x = cell.shape[1]
     end = jax.ShapeDtypeStruct((ocean_x, LANES), F32)
     return pl.pallas_call(
@@ -744,19 +736,31 @@
         out_shape=[end, end],
         in_specs=[VMEM] * 6 + [ANY],
         out_specs=[VMEM] * 2,
-        scratch_shapes=[pltpu.VMEM((BULK, 3 * ocean_x, LANES), F32), pltpu.VMEM((2, ocean_x, LANES), F32)],
+        scratch_shapes=[
+            pltpu.VMEM((BULK, 3 * ocean_x, LANES), F32),
+            pltpu.VMEM((2, *own.shape), F32),
+            pltpu.VMEM((2, ocean_x, LANES), F32),
+        ],
         compiler_params=PARAMS,
         cost_estimate=CHEAP,
         name="remap_lat",
-    )(own, left, right, cell, offset, weight, after)
+    )(own, from_odd, from_even, cell, offset, weight, after)
 
 
 def remap_kernel(mine, *refs):
     if mine:
-        own, cell, offset, weight, forcing, table = refs
+        own, cell, offset, weight, state, given, forcing, out, table, sem = refs
         left = right = None
+        last_col = out.shape[1] - 1
+        copies = [
+            pltpu.make_async_copy(state.at[side], out.at[:, col, 0, :], sem.at[side])
+            for side, col in ((0, 0), (1, last_col))
+        ]
+        for c in copies:
+            c.start()
     else:
-        left, right, cell, offset, weight, begun, forcing, table = refs
+        from_odd, from_even, cell, offset, weight, begun, forcing, table, near = refs
+        left, right = bands(from_odd, from_even, near)
         own = None
     taps, ocean_x, ocean_y = cell.shape
     ratio = table.shape[1] // ocean_x
@@ -779,30 +783,50 @@
             )
             for q in range(BULK):
                 forcing[q, rows, lanes] = acc[q]
-
-
-def remap(mine, *args):
-    cell = args[1] if mine else args[2]
+    if mine:
+        for c in copies:
+            c.wait()
+
+
+def remap_own(own, cell, offset, weight, state, out4):
     _, ocean_x, ocean_y = cell.shape
     return pl.pallas_call(
-        functools.partial(remap_kernel, mine),
-        out_shape=jax.ShapeDtypeStruct((BULK, ocean_x, ocean_y), F32),
-        in_specs=[VMEM] * len(args),
+        functools.partial(remap_kernel, True),
+        out_shape=[jax.ShapeDtypeStruct((BULK, ocean_x, ocean_y), F32), jax.ShapeDtypeStruct(out4.shape, F32)],
+        in_specs=[VMEM] * 4 + [ANY] + [HBM],
+        out_specs=[VMEM, HBM],
+        scratch_shapes=[pltpu.VMEM((BULK, 3 * ocean_x, LANES), F32), pltpu.SemaphoreType.DMA((2,))],
+        input_output_aliases={5: 1},
+        compiler_params=PARAMS,
+        cost_estimate=CHEAP,
+        name="remap_own",
+    )(own, cell, offset, weight, state, *pinned(out4))
+
+
+def remap_rest(from_odd, from_even, cell, offset, weight, begun):
+    ocean_x = cell.shape[1]
+    return pl.pallas_call(
+        functools.partial(remap_kernel, False),
+        out_shape=jax.ShapeDtypeStruct(begun.shape, F32),
+        in_specs=[VMEM] * 6,
         out_specs=VMEM,
-        scratch_shapes=[pltpu.VMEM((BULK, 3 * ocean_x, LANES), F32)],
-        compiler_params=PARAMS,
-        cost_estimate=CHEAP,
-        name="remap_own" if mine else "remap_rest",
-    )(*args)
+        scratch_shapes=[pltpu.VMEM((BULK, 3 * ocean_x, LANES), F32), pltpu.VMEM((2, *from_odd.shape), F32)],
+        compiler_params=PARAMS,
+        cost_estimate=CHEAP,
+        name="remap_rest",
+    )(from_odd, from_even, cell, offset, weight, begun)
 
 
 def ocean_final_kernel(
-    forcing, from_west, from_east, from_odd, from_even, base_u, base_v, mask, coriolis, new_u, new_v, both
+    forcing, lon_odd, lon_even, lat_odd, lat_even, base_u, base_v, mask, coriolis, new_u, new_v, lines, both
 ):
     levels, ocean_x, ocean_y = base_u.shape
-    both[0] = from_odd[...]
-    both[1] = from_even[...]
-    from_north, from_south = (both.at[parity()], both.at[1 - parity()])
+    lines[0] = lon_odd[...]
+    lines[1] = lon_even[...]
+    from_west, from_east = sides_of(lines, "lon")
+    both[0] = lat_odd[...]
+    both[1] = lat_even[...]
+    from_south, from_north = sides_of(both, "lat")
     tiles = ocean_y // LANES
 
     def line(buffer, q):
@@ -832,6 +856,17 @@
         decay = np.float32(np.exp(np.float32(-level / 3.0)))
         new_u[level] = base_u[level] + decay * add_u
         new_v[level] = base_v[level] + decay * add_v
+    row = lax.broadcasted_iota(jnp.int32, (8, LANES), 0)
+    for buffer, first, at in ((from_west, 0, 0), (from_east, ocean_x - 8, 7)):
+        rows = slice(first, first + 8)
+        for m in range(tiles):
+            lanes = slice(m * LANES, (m + 1) * LANES)
+            share = jnp.where(row == at, 0.1 * maskf[rows, lanes], 0.0)
+            for f, out in enumerate((new_u, new_v)):
+                start = line_rows(tiles) + (f * tiles + m) * levels
+                for level in range(levels):
+                    line_part = buffer[start + level : start + level + 1, :]
+                    out[level, rows, lanes] = out[level, rows, lanes] + share * line_part
 
 
 def ocean_final(forcing, halos, base_u, base_v, mask, coriolis):
@@ -840,30 +875,25 @@
         out_shape=[jax.ShapeDtypeStruct(base_u.shape, F32)] * 2,
         in_specs=[VMEM] * 9,
         out_specs=[VMEM] * 2,
-        scratch_shapes=[pltpu.VMEM((2, base_u.shape[1], LANES), F32)],
+        scratch_shapes=[pltpu.VMEM((2, *halos[0].shape), F32), pltpu.VMEM((2, base_u.shape[1], LANES), F32)],
         compiler_params=PARAMS,
         cost_estimate=CHEAP,
         name="ocean_final",
     )(forcing, *halos, base_u, base_v, mask, coriolis)
 
 
-def shifted(value, axis, step):
+def swap(odd, even, axis, wrap):
     count = lax.axis_size(axis)
-    return lax.ppermute(value, axis, [(i, (i + step) % count) for i in range(count)])
-
-
-def swapped(value, axis, first):
-    count = lax.axis_size(axis)
-    pairs = [(i, i + 1) for i in range(first, count - 1, 2)]
-    return lax.ppermute(value, axis, pairs + [(j, i) for i, j in pairs])
-
-
-def exchange(east, west, odd, even):
-    from_odd = swapped(odd, "lat", 0)
-    from_even = swapped(even, "lat", 1)
-    from_west = shifted(east, "lon", 1)
-    from_east = shifted(west, "lon", -1)
-    return from_west, from_east, from_odd, from_even
+    got = []
+    for first, value in ((0, odd), (1, even)):
+        pairs = [(i, (i + 1) % count) for i in range(first, count, 2) if wrap or i + 1 < count]
+        got.append(lax.ppermute(value, axis, pairs + [(j, i) for i, j in pairs]))
+    return got
+
+
+def exchange(lon, lat):
+    from_lat = swap(*lat, "lat", False)
+    return swap(*lon, "lon", True) + from_lat
 
 
 def local(
@@ -881,9 +911,9 @@
     comps, width_x, width_y = spectrum.shape
     plan = Plan(comps)
     spec2 = spectrum.reshape(comps * width_x, width_y)
-    east, west = pack_lon(plan, spectrum.reshape(comps, width_x, 1, width_y), sea_mask, ocean_u, ocean_v)
-    odd, even, spec2 = pack_lat(plan, spec2, sea_mask, ocean_u, ocean_v, east)
-    begun = exchange(east, west, odd, even)
+    lon = pack_lon(plan, spectrum.reshape(comps, width_x, 1, width_y), sea_mask)
+    *lat, spec2 = pack_lat(plan, spec2, sea_mask, ocean_u, ocean_v, lon[0])
+    begun = exchange(lon, lat)
 
     coefs = columns_of(plan, bulk_weight)
     total_y = width_y * lax.axis_size("lat")
@@ -895,25 +925,22 @@
 
     part = advect(plan, 0, spec2, coefs, sea_mask)
     middle, edge, up, down = interior(plan, 0, part, *begun[2:], transfer, coefs, sea_mask)
-    sides, east, west = edges(plan, 0, edge, *begun[:2], transfer, coefs, sea_mask)
-    halos = exchange(east, west, *merge_lat(plan, width_x, sides, up, down))
-
+    sides, *lon = edges(plan, 0, edge, *begun[:2], transfer, coefs, sea_mask)
+    halos = exchange(lon, merge_lat(plan, width_x, sides, up, down))
+
+    base_u, base_v = ocean_base(plan, ocean_u, ocean_v, *begun[2:], ocean_mask, line)
     part = advect(plan, 1, middle, coefs, sides)
     out4, edge, bulk, weights = interior(plan, 1, part, *halos[2:], transfer, coefs, sea_mask)
-    sides, bulk = edges(plan, 1, edge, *halos[:2], transfer, coefs, sea_mask, bulk, weights)
-    left = shifted(bulk, "lon", 1)
-    right = shifted(bulk, "lon", -1)
-    state4 = finish(sides, out4)
-    state = state4.reshape(spectrum.shape)
-    base_u, base_v = ocean_base(plan, ocean_u, ocean_v, *begun, ocean_mask, line)
-    forcing = remap(True, bulk, cell, offset, weight)
-
-    remapped = (bulk, left, right, cell, offset, weight)
-    east, west = remap_lon(*remapped, forcing, base_u, *pinned(state4))
-    odd, even = remap_lat(*remapped, east)
-    halos = exchange(east, west, odd, even)
-    forcing = remap(False, left, right, cell, offset, weight, forcing)
+    sides, bulk = edges(plan, 1, edge, *halos[:2], transfer, coefs, sea_mask, bulk, weights, base_u)
+    near = swap(bulk, bulk, "lon", True)
+    forcing, out4 = remap_own(bulk, cell, offset, weight, sides, out4)
+
+    remapped = (bulk, *near, cell, offset, weight)
+    lon = remap_lon(*remapped, ocean_u, ocean_v, forcing)
+    halos = exchange(lon, remap_lat(*remapped, lon[0]))
+    forcing = remap_rest(*near, cell, offset, weight, forcing)
     new_u, new_v = ocean_final(forcing, halos, base_u, base_v, ocean_mask, line)
+    state = out4.reshape(spectrum.shape)
     return (state, new_u, new_v)
 
 

time: 68.7 us -> 62.4 us (0.908)
  starting transfers between devices: 29.4 us -> 23.1 us
    ppermute x14, starting transfers between devices: 29.4 us -> 23.1 us  [swap(): got.append(lax.ppermute(value, axis, pairs + [(j, i) for i, j in pairs]))]
    pallas_call x4 -> x3, Pallas kernels: 8.86 us -> 8.72 us  [the longest x1 3.9 us: remap_own(): pl.pallas_call(functools.partial(remap_kernel, True), out_shape=[jax.Shap...]
  transfers between devices with their start and end apart: 14 -> 14, of which waited for: 0 -> 0; matrix products, arithmetic and copies ran while one was open for 0% -> 0% of each run, Pallas kernels for 46% -> 50%
where the time goes in v4:
time: 62.4 us; the launch traced here: 62.2 us
  Pallas kernels  37.8 us (61%)
  starting transfers between devices  23.1 us (37%)
  between operations  1.02 us (2%)
    ppermute x14, starting transfers between devices, swap(): got.append(lax.ppermute(value, axis, pairs + [(j, i) for i, j in pairs]))  23.1 us
    pallas_call x2, Pallas kernels, interior(): pl.pallas_call(functools.partial(interior_kernel, plan, step), out_shape=...  11.2 us
    pallas_call x2, Pallas kernels, advect(): pl.pallas_call(functools.partial(advect_kernel, plan, step), out_shape=ja...  5.78 us
    pallas_call x1, Pallas kernels, remap_own(): pl.pallas_call(functools.partial(remap_kernel, True), out_shape=[jax.Shap...  3.9 us
    pallas_call x1, Pallas kernels, pack_lat(): pl.pallas_call(functools.partial(pack_lat_kernel, plan), out_shape=[jax.S...  3.9 us
    pallas_call x1, Pallas kernels, remap_rest(): pl.pallas_call(functools.partial(remap_kernel, False), out_shape=jax.Shap...  3.53 us
    pallas_call x2, Pallas kernels, edges(): pl.pallas_call(functools.partial(edges_kernel, plan, step), out_shape=out...  3.46 us
    pallas_call x1, Pallas kernels, remap_lat(): pl.pallas_call(remap_lat_kernel, out_shape=[end, end], in_specs=[VMEM] *...  1.29 us
  transfers between devices with their start and end apart: 14, of which 0 were waited for; matrix products, arithmetic and copies ran while one was open for 0% of the time, Pallas kernels for 50%

profile of v4, /device:TPU:1, one launch (start us, length us, event | category | flops | bytes accessed | tf_op | source)
XLA Modules:
  0.0 62.2 jit_solution(3216241865177018365)
XLA Ops:
  0.6 1.2 %pack_lon.1 = (f32[656,128]{1,0:T(8,128)S(1)}, f32[656,128]{1,0:T(8,128)S(1)}) custom-call(f32[1296,8,1,128]{3,2,1,0:T(1,128)} %bitcast.32, s32[8,128]{1,0:T(8,128)} %refs_5_.7), custom_call_target="tpu_custom_call" | custom-call | flops 1 | bytes 1 | tf_op jit(solution)/shard_map/pack_lon/pallas_call | solution.py:221
  1.9 2.1 %collective-permute-start.2 = (f32[656,128]{1,0:T(8,128)S(1)}, f32[656,128]{1,0:T(8,128)S(1)}, u32[]{:S(2)}, u32[]{:S(2)}) collective-permute-start(f32[656,128]{1,0:T(8,128)S(1)} %get-tuple-element.33.after), channel_id=1, source_target_pairs={{0,4},{8,12},{16,20},{24,28},{4,0},{12,8},{20,16},{28,24},{1,5},{9... | collective-permute-start | bytes 1007624 | tf_op jit(solution)/shard_map/ppermute | solution.py:890
  4.1 3.3 %collective-permute-start.3 = (f32[656,128]{1,0:T(8,128)S(1)}, f32[656,128]{1,0:T(8,128)S(1)}, u32[]{:S(2)}, u32[]{:S(2)}) collective-permute-start(f32[656,128]{1,0:T(8,128)S(1)} %get-tuple-element.39), channel_id=1, source_target_pairs={{4,8},{12,16},{20,24},{28,0},{8,4},{16,12},{24,20},{0,28},{5,9},{1... | collective-permute-start | bytes 1007624 | tf_op jit(solution)/shard_map/ppermute | solution.py:890
  7.3 3.9 %pack_lat.1 = (f32[200,128]{1,0:T(8,128)S(1)}, f32[200,128]{1,0:T(8,128)S(1)}, f32[10368,128]{1,0:T(8,128)S(1)}) custom-call(f32[10368,128]{1,0:T(8,128)} %bitcast.33, s32[8,128]{1,0:T(8,128)} %refs_5_.7, f32[8,24,384]{2,1,0:T(8,128)} %u.3, f32[8,24,384]{2,1,0:T(8,128)} %v.3, f32[656,128]{1,0:T(8,128)S(1)} %get-tuple-element.33.after), custom_call_target="tpu_custom_call" | custom-call | flops 1 | bytes 1 | tf_op jit(solution)/shard_map/pack_lat/pallas_call | solution.py:289
  11.2 1.3 %collective-permute-start = (f32[200,128]{1,0:T(8,128)S(1)}, f32[200,128]{1,0:T(8,128)S(1)}, u32[]{:S(2)}, u32[]{:S(2)}) collective-permute-start(f32[200,128]{1,0:T(8,128)S(1)} %get-tuple-element.35), channel_id=1, source_target_pairs={{0,1},{2,3},{1,0},{3,2},{4,5},{6,7},{5,4},{7,6},{8,9},{10,11},{9,8... | collective-permute-start | bytes 307208 | tf_op jit(solution)/shard_map/ppermute | solution.py:890
  12.5 3.0 %collective-permute-start.1 = (f32[200,128]{1,0:T(8,128)S(1)}, f32[200,128]{1,0:T(8,128)S(1)}, u32[]{:S(2)}, u32[]{:S(2)}) collective-permute-start(f32[200,128]{1,0:T(8,128)S(1)} %get-tuple-element.36), channel_id=1, source_target_pairs={{1,2},{2,1},{5,6},{6,5},{9,10},{10,9},{13,14},{14,13},{17,18},{18,... | collective-permute-start | bytes 307208 | tf_op jit(solution)/shard_map/ppermute | solution.py:890
  15.9 2.9 %advect.2.refs_0_ = f32[8,1296,128]{2,1,0:T(8,128)S(1)} custom-call(f32[10368,128]{1,0:T(8,128)S(1)} %get-tuple-element.34.state, f32[1296,8]{1,0:T(8,128)S(1)} %columns.1.coefs.refs_4_, s32[8,128]{1,0:T(8,128)S(1)} %copy-done.4), custom_call_target="tpu_custom_call" | custom-call | flops 1 | bytes 1 | tf_op jit(solution)/shard_map/advect/pallas_call | solution.py:342
  18.8 4.5 %interior.2 = (f32[6,1296,128]{2,1,0:T(8,128)S(1)}, f32[2,1296,128]{2,1,0:T(8,128)S(1)}, f32[176,128]{1,0:T(8,128)S(1)}, f32[176,128]{1,0:T(8,128)S(1)}) custom-call(f32[8,1296,128]{2,1,0:T(8,128)S(1)} %advect.2.refs_0_, f32[200,128]{1,0:T(8,128)S(1)} %collective-permute-done.refs_1_.from_odd, f32[200,128]{1,0:T(8,128)S(1)} %collective-permute-done.1.refs_2_.from_even, ...), custom_call_target="tpu_custom_call" | custom-call | flops 1 | bytes 1 | tf_op jit(solution)/shard_map/interior/pallas_call | solution.py:463
  23.4 1.6 %edges.2 = (f32[2,1296,128]{2,1,0:T(8,128)S(1)}, f32[656,128]{1,0:T(8,128)S(1)}, f32[656,128]{1,0:T(8,128)S(1)}) custom-call(f32[2,1296,128]{2,1,0:T(8,128)S(1)} %get-tuple-element.38.refs_0_, f32[656,128]{1,0:T(8,128)S(1)} %collective-permute-done.2.refs_1_, f32[656,128]{1,0:T(8,128)S(1)} %collective-permute-done.3.refs_2_, bf16[1296,1296]{1,0:T(8,128)(2,1)S(1)} %copy-done, ...), custom_call_target="tpu_custom_call" | custom-call | flops 1 | bytes 1 | tf_op jit(solution)/shard_map/edges/pallas_call | solution.py:563
  25.1 1.3 %collective-permute-start.7 = (f32[656,128]{1,0:T(8,128)S(1)}, f32[656,128]{1,0:T(8,128)S(1)}, u32[]{:S(2)}, u32[]{:S(2)}) collective-permute-start(f32[656,128]{1,0:T(8,128)S(1)} %get-tuple-element.47), channel_id=1, source_target_pairs={{4,8},{12,16},{20,24},{28,0},{8,4},{16,12},{24,20},{0,28},{5,9},{1... | collective-permute-start | bytes 1007624 | tf_op jit(solution)/shard_map/ppermute | solution.py:890
  26.9 0.7 %collective-permute-start.4 = (f32[176,128]{1,0:T(8,128)S(1)}, f32[176,128]{1,0:T(8,128)S(1)}, u32[]{:S(2)}, u32[]{:S(2)}) collective-permute-start(f32[176,128]{1,0:T(8,128)S(1)} %get-tuple-element.43), channel_id=1, source_target_pairs={{0,1},{2,3},{1,0},{3,2},{4,5},{6,7},{5,4},{7,6},{8,9},{10,11},{9,8... | collective-permute-start | bytes 270344 | tf_op jit(solution)/shard_map/ppermute | solution.py:890
  27.5 3.2 %collective-permute-start.5 = (f32[176,128]{1,0:T(8,128)S(1)}, f32[176,128]{1,0:T(8,128)S(1)}, u32[]{:S(2)}, u32[]{:S(2)}) collective-permute-start(f32[176,128]{1,0:T(8,128)S(1)} %get-tuple-element.44), channel_id=1, source_target_pairs={{1,2},{2,1},{5,6},{6,5},{9,10},{10,9},{13,14},{14,13},{17,18},{18,... | collective-permute-start | bytes 270344 | tf_op jit(solution)/shard_map/ppermute | solution.py:890
  31.4 2.9 %advect.3.refs_0_ = f32[8,1296,128]{2,1,0:T(8,128)S(1)} custom-call(f32[6,1296,128]{2,1,0:T(8,128)S(1)} %get-tuple-element.37.state, f32[1296,8]{1,0:T(8,128)S(1)} %columns.1.coefs.refs_4_, f32[2,1296,128]{2,1,0:T(8,128)S(1)} %get-tuple-element.40.more.state), custom_call_target="tpu_custom_call" | custom-call | flops 1 | bytes 1 | tf_op jit(solution)/shard_map/advect/pallas_call | solution.py:342
  34.3 6.6 %interior.3 = (f32[1296,8,1,128]{3,2,1,0:T(1,128)}, f32[2,1296,128]{2,1,0:T(8,128)S(1)}, f32[5,8,128]{2,1,0:T(8,128)S(1)}, f32[5,1296,128]{2,1,0:T(8,128)S(1)}) custom-call(f32[8,1296,128]{2,1,0:T(8,128)S(1)} %advect.3.refs_0_, f32[176,128]{1,0:T(8,128)S(1)} %collective-permute-done.4.refs_1_, f32[176,128]{1,0:T(8,128)S(1)} %collective-permute-done.5.refs_2_, ...), custom_call_target="tpu_custom_call" | custom-call | flops 1 | bytes 1 | tf_op jit(solution)/shard_map/interior/pallas_call | solution.py:463
  41.0 1.8 %edges.3 = (f32[2,1296,128]{2,1,0:T(8,128)S(1)}, f32[5,8,128]{2,1,0:T(8,128)S(1)}) custom-call(f32[2,1296,128]{2,1,0:T(8,128)S(1)} %get-tuple-element.45.refs_0_, f32[656,128]{1,0:T(8,128)S(1)} %collective-permute-done.6.refs_1_, f32[656,128]{1,0:T(8,128)S(1)} %collective-permute-done.7.refs_2_, bf16[1296,1296]{1,0:T(8,128)(2,1)S(1)} %copy-done, ...), custom_call_target="tpu_custom_call" | custom-call | flops 1 | bytes 1 | tf_op jit(solution)/shard_map/edges/pallas_call | solution.py:563
  42.9 2.3 %collective-permute-start.9 = (f32[5,8,128]{2,1,0:T(8,128)S(1)}, f32[5,8,128]{2,1,0:T(8,128)S(1)}, u32[]{:S(2)}, u32[]{:S(2)}) collective-permute-start(f32[5,8,128]{2,1,0:T(8,128)S(1)} %get-tuple-element.51.refs_0_.own), channel_id=1, source_target_pairs={{4,8},{12,16},{20,24},{28,0},{8,4},{16,12},{24,20},{0,28},{5,9},{1... | collective-permute-start | bytes 61448 | tf_op jit(solution)/shard_map/ppermute | solution.py:890
  45.4 3.9 %remap_own.1 = (f32[5,24,384]{2,1,0:T(8,128)S(1)}, f32[1296,8,1,128]{3,2,1,0:T(1,128)}) custom-call(f32[5,8,128]{2,1,0:T(8,128)S(1)} %get-tuple-element.51.refs_0_.own, s32[4,24,384]{2,1,0:T(8,128)S(1)} %get-tuple-element.64.refs_1_.refs_2_.cell, s32[4,24,384]{2,1,0:T(8,128)S(1)} %get-tuple-element.63.refs_2_.refs_3_.offset, ...), custom_call_target="tpu_custom_call", output_to_operand_aliasing={{1}: (5, {})} | custom-call | flops 1 | bytes 1 | tf_op jit(solution)/shard_map/remap_own/pallas_call | solution.py:793
  49.4 1.3 %remap_lon.1 = (f32[56,128]{1,0:T(8,128)S(1)}, f32[56,128]{1,0:T(8,128)S(1)}) custom-call(f32[5,8,128]{2,1,0:T(8,128)S(1)} %get-tuple-element.51.refs_0_.own, f32[5,8,128]{2,1,0:T(8,128)S(1)} %collective-permute-done.8.refs_0_.from_odd, f32[5,8,128]{2,1,0:T(8,128)S(1)} %collective-permute-done.9.refs_1_.from_even, ...), custom_call_target="tpu_custom_call" | custom-call | flops 1 | bytes 1 | tf_op jit(solution)/shard_map/remap_lon/pallas_call | solution.py:715
  50.8 1.8 %collective-permute-start.11 = (f32[56,128]{1,0:T(8,128)S(1)}, f32[56,128]{1,0:T(8,128)S(1)}, u32[]{:S(2)}, u32[]{:S(2)}) collective-permute-start(f32[56,128]{1,0:T(8,128)S(1)} %get-tuple-element.57), channel_id=1, source_target_pairs={{4,8},{12,16},{20,24},{28,0},{8,4},{16,12},{24,20},{0,28},{5,9},{1... | collective-permute-start | bytes 86024 | tf_op jit(solution)/shard_map/ppermute | solution.py:890
  52.6 1.3 %remap_lat.1 = (f32[24,128]{1,0:T(8,128)S(1)}, f32[24,128]{1,0:T(8,128)S(1)}) custom-call(f32[5,8,128]{2,1,0:T(8,128)S(1)} %get-tuple-element.51.refs_0_.own, f32[5,8,128]{2,1,0:T(8,128)S(1)} %collective-permute-done.8.refs_0_.from_odd, f32[5,8,128]{2,1,0:T(8,128)S(1)} %collective-permute-done.9.refs_1_.from_even, ...), custom_call_target="tpu_custom_call" | custom-call | flops 1 | bytes 1 | tf_op jit(solution)/shard_map/remap_lat/pallas_call | solution.py:734
  53.9 1.7 %collective-permute-start.12 = (f32[24,128]{1,0:T(8,128)S(1)}, f32[24,128]{1,0:T(8,128)S(1)}, u32[]{:S(2)}, u32[]{:S(2)}) collective-permute-start(f32[24,128]{1,0:T(8,128)S(1)} %get-tuple-element.58), channel_id=1, source_target_pairs={{0,1},{2,3},{1,0},{3,2},{4,5},{6,7},{5,4},{7,6},{8,9},{10,11},{9,8... | collective-permute-start | bytes 36872 | tf_op jit(solution)/shard_map/ppermute | solution.py:890
  55.7 1.9 %collective-permute-start.13 = (f32[24,128]{1,0:T(8,128)S(1)}, f32[24,128]{1,0:T(8,128)S(1)}, u32[]{:S(2)}, u32[]{:S(2)}) collective-permute-start(f32[24,128]{1,0:T(8,128)S(1)} %get-tuple-element.59), channel_id=1, source_target_pairs={{1,2},{2,1},{5,6},{6,5},{9,10},{10,9},{13,14},{14,13},{17,18},{18,... | collective-permute-start | bytes 36872 | tf_op jit(solution)/shard_map/ppermute | solution.py:890
  57.6 3.5 %remap_rest.1.forcing = f32[5,24,384]{2,1,0:T(8,128)S(1)} custom-call(f32[5,8,128]{2,1,0:T(8,128)S(1)} %collective-permute-done.8.refs_0_.from_odd, f32[5,8,128]{2,1,0:T(8,128)S(1)} %collective-permute-done.9.refs_1_.from_even, s32[4,24,384]{2,1,0:T(8,128)S(1)} %get-tuple-element.64.refs_1_.refs_2_.cell, ...), custom_call_target="tpu_custom_call" | custom-call | flops 1 | bytes 1 | tf_op jit(solution)/shard_map/remap_rest/pallas_call | solution.py:808
  61.1 1.0 %ocean_final.1 = (f32[8,24,384]{2,1,0:T(8,128)}, f32[8,24,384]{2,1,0:T(8,128)}) custom-call(f32[5,24,384]{2,1,0:T(8,128)S(1)} %remap_rest.1.forcing, f32[56,128]{1,0:T(8,128)S(1)} %collective-permute-done.10.lon_odd, f32[56,128]{1,0:T(8,128)S(1)} %collective-permute-done.11.lon_even, f32[24,128]{1,0:T(8,128)S(1)} %collective-permute-done.12.lat_odd, ...), custom_call_target="tpu_custom_call" | custom-call | flops 1 | bytes 1 | tf_op jit(solution)/shard_map/ocean_final/pallas_call | solution.py:873
  (43 shorter events, 1.9 us)
Async XLA Ops:
  1.9 13.7 %copy-start.3 = (f32[1296,8]{1,0:T(8,128)S(1)}, f32[1296,8]{1,0:T(8,128)}, u32[]{:S(2)}) copy-start(f32[1296,8]{1,0:T(8,128)} %constant.32.clone.coef) | copy-start | bytes 124420
  1.9 13.7 %copy-start.6 = (f32[5,1296]{1,0:T(8,128)S(1)}, f32[5,1296]{1,0:T(8,128)}, u32[]{:S(2)}) copy-start(f32[5,1296]{1,0:T(8,128)} %bulk_weight.1) | copy-start | bytes 77764
  1.9 13.9 %copy-start.4 = (s32[8,128]{1,0:T(8,128)S(1)}, s32[8,128]{1,0:T(8,128)}, u32[]{:S(2)}) copy-start(s32[8,128]{1,0:T(8,128)} %refs_5_.7) | copy-start | bytes 12292
  1.9 21.5 %collective-permute-start.2 = (f32[656,128]{1,0:T(8,128)S(1)}, f32[656,128]{1,0:T(8,128)S(1)}, u32[]{:S(2)}, u32[]{:S(2)}) collective-permute-start(f32[656,128]{1,0:T(8,128)S(1)} %get-tuple-element.33.after), channel_id=1, source_target_pairs={{0,4},{8,12},{16,20},{24,28},{4,0},{12,8},{20,16},{28,24},{1,5},{9... | collective-permute-start | bytes 1007624 | tf_op jit(solution)/shard_map/ppermute | solution.py:890
  4.1 19.4 %collective-permute-start.3 = (f32[656,128]{1,0:T(8,128)S(1)}, f32[656,128]{1,0:T(8,128)S(1)}, u32[]{:S(2)}, u32[]{:S(2)}) collective-permute-start(f32[656,128]{1,0:T(8,128)S(1)} %get-tuple-element.39), channel_id=1, source_target_pairs={{4,8},{12,16},{20,24},{28,0},{8,4},{16,12},{24,20},{0,28},{5,9},{1... | collective-permute-start | bytes 1007624 | tf_op jit(solution)/shard_map/ppermute | solution.py:890
  11.2 7.5 %collective-permute-start = (f32[200,128]{1,0:T(8,128)S(1)}, f32[200,128]{1,0:T(8,128)S(1)}, u32[]{:S(2)}, u32[]{:S(2)}) collective-permute-start(f32[200,128]{1,0:T(8,128)S(1)} %get-tuple-element.35), channel_id=1, source_target_pairs={{0,1},{2,3},{1,0},{3,2},{4,5},{6,7},{5,4},{7,6},{8,9},{10,11},{9,8... | collective-permute-start | bytes 307208 | tf_op jit(solution)/shard_map/ppermute | solution.py:890
  12.5 6.3 %collective-permute-start.1 = (f32[200,128]{1,0:T(8,128)S(1)}, f32[200,128]{1,0:T(8,128)S(1)}, u32[]{:S(2)}, u32[]{:S(2)}) collective-permute-start(f32[200,128]{1,0:T(8,128)S(1)} %get-tuple-element.36), channel_id=1, source_target_pairs={{1,2},{2,1},{5,6},{6,5},{9,10},{10,9},{13,14},{14,13},{17,18},{18,... | collective-permute-start | bytes 307208 | tf_op jit(solution)/shard_map/ppermute | solution.py:890
  15.8 3.0 %copy-start = (bf16[1296,1296]{1,0:T(8,128)(2,1)S(1)}, bf16[1296,1296]{1,0:T(8,128)(2,1)}, u32[]{:S(2)}) copy-start(bf16[1296,1296]{1,0:T(8,128)(2,1)} %refs_3_.7) | copy-start | bytes 10077700
  23.4 7.4 %copy-start.9 = (f32[384]{0:T(512)S(1)}, f32[384]{0:T(512)}, u32[]{:S(2)}) copy-start(f32[384]{0:T(512)} %param.20) | copy-start | bytes 4612
  23.4 7.4 %copy-start.1 = (f32[8,24,384]{2,1,0:T(8,128)S(1)}, f32[8,24,384]{2,1,0:T(8,128)}, u32[]{:S(2)}) copy-start(f32[8,24,384]{2,1,0:T(8,128)} %u.3) | copy-start | bytes 884740
  23.4 7.4 %copy-start.2 = (f32[8,24,384]{2,1,0:T(8,128)S(1)}, f32[8,24,384]{2,1,0:T(8,128)}, u32[]{:S(2)}) copy-start(f32[8,24,384]{2,1,0:T(8,128)} %v.3) | copy-start | bytes 884740
  23.4 7.4 %copy-start.5 = (s32[24,384]{1,0:T(8,128)S(1)}, s32[24,384]{1,0:T(8,128)}, u32[]{:S(2)}) copy-start(s32[24,384]{1,0:T(8,128)} %mask.7) | copy-start | bytes 110596
  25.0 15.9 %collective-permute-start.6 = (f32[656,128]{1,0:T(8,128)S(1)}, f32[656,128]{1,0:T(8,128)S(1)}, u32[]{:S(2)}, u32[]{:S(2)}) collective-permute-start(f32[656,128]{1,0:T(8,128)S(1)} %get-tuple-element.46), channel_id=1, source_target_pairs={{0,4},{8,12},{16,20},{24,28},{4,0},{12,8},{20,16},{28,24},{1,5},{9... | collective-permute-start | bytes 1007624 | tf_op jit(solution)/shard_map/ppermute | solution.py:890
  25.1 15.8 %collective-permute-start.7 = (f32[656,128]{1,0:T(8,128)S(1)}, f32[656,128]{1,0:T(8,128)S(1)}, u32[]{:S(2)}, u32[]{:S(2)}) collective-permute-start(f32[656,128]{1,0:T(8,128)S(1)} %get-tuple-element.47), channel_id=1, source_target_pairs={{4,8},{12,16},{20,24},{28,0},{8,4},{16,12},{24,20},{0,28},{5,9},{1... | collective-permute-start | bytes 1007624 | tf_op jit(solution)/shard_map/ppermute | solution.py:890
  26.9 7.4 %collective-permute-start.4 = (f32[176,128]{1,0:T(8,128)S(1)}, f32[176,128]{1,0:T(8,128)S(1)}, u32[]{:S(2)}, u32[]{:S(2)}) collective-permute-start(f32[176,128]{1,0:T(8,128)S(1)} %get-tuple-element.43), channel_id=1, source_target_pairs={{0,1},{2,3},{1,0},{3,2},{4,5},{6,7},{5,4},{7,6},{8,9},{10,11},{9,8... | collective-permute-start | bytes 270344 | tf_op jit(solution)/shard_map/ppermute | solution.py:890
  27.5 6.7 %collective-permute-start.5 = (f32[176,128]{1,0:T(8,128)S(1)}, f32[176,128]{1,0:T(8,128)S(1)}, u32[]{:S(2)}, u32[]{:S(2)}) collective-permute-start(f32[176,128]{1,0:T(8,128)S(1)} %get-tuple-element.44), channel_id=1, source_target_pairs={{1,2},{2,1},{5,6},{6,5},{9,10},{10,9},{13,14},{14,13},{17,18},{18,... | collective-permute-start | bytes 270344 | tf_op jit(solution)/shard_map/ppermute | solution.py:890
  40.9 4.3 %copy-start.7 = (s32[24,384,4]{1,2,0:T(4,128)S(1)}, s32[24,384,4]{1,2,0:T(4,128)}, u32[]{:S(2)}) copy-start(s32[24,384,4]{1,2,0:T(4,128)} %param.15) | copy-start | bytes 442372
  41.0 4.4 %copy-start.8 = (f32[24,384,4]{1,2,0:T(4,128)S(1)}, f32[24,384,4]{1,2,0:T(4,128)}, u32[]{:S(2)}) copy-start(f32[24,384,4]{1,2,0:T(4,128)} %param.16) | copy-start | bytes 442372
  42.8 6.5 %collective-permute-start.8 = (f32[5,8,128]{2,1,0:T(8,128)S(1)}, f32[5,8,128]{2,1,0:T(8,128)S(1)}, u32[]{:S(2)}, u32[]{:S(2)}) collective-permute-start(f32[5,8,128]{2,1,0:T(8,128)S(1)} %get-tuple-element.51.refs_0_.own), channel_id=1, source_target_pairs={{0,4},{8,12},{16,20},{24,28},{4,0},{12,8},{20,16},{28,24},{1,5},{9... | collective-permute-start | bytes 61448 | tf_op jit(solution)/shard_map/ppermute | solution.py:890
  42.9 6.4 %collective-permute-start.9 = (f32[5,8,128]{2,1,0:T(8,128)S(1)}, f32[5,8,128]{2,1,0:T(8,128)S(1)}, u32[]{:S(2)}, u32[]{:S(2)}) collective-permute-start(f32[5,8,128]{2,1,0:T(8,128)S(1)} %get-tuple-element.51.refs_0_.own), channel_id=1, source_target_pairs={{4,8},{12,16},{20,24},{28,0},{8,4},{16,12},{24,20},{0,28},{5,9},{1... | collective-permute-start | bytes 61448 | tf_op jit(solution)/shard_map/ppermute | solution.py:890
  50.6 10.5 %collective-permute-start.10 = (f32[56,128]{1,0:T(8,128)S(1)}, f32[56,128]{1,0:T(8,128)S(1)}, u32[]{:S(2)}, u32[]{:S(2)}) collective-permute-start(f32[56,128]{1,0:T(8,128)S(1)} %get-tuple-element.56.after), channel_id=1, source_target_pairs={{0,4},{8,12},{16,20},{24,28},{4,0},{12,8},{20,16},{28,24},{1,5},{9... | collective-permute-start | bytes 86024 | tf_op jit(solution)/shard_map/ppermute | solution.py:890
  50.8 10.3 %collective-permute-start.11 = (f32[56,128]{1,0:T(8,128)S(1)}, f32[56,128]{1,0:T(8,128)S(1)}, u32[]{:S(2)}, u32[]{:S(2)}) collective-permute-start(f32[56,128]{1,0:T(8,128)S(1)} %get-tuple-element.57), channel_id=1, source_target_pairs={{4,8},{12,16},{20,24},{28,0},{8,4},{16,12},{24,20},{0,28},{5,9},{1... | collective-permute-start | bytes 86024 | tf_op jit(solution)/shard_map/ppermute | solution.py:890
  53.9 7.2 %collective-permute-start.12 = (f32[24,128]{1,0:T(8,128)S(1)}, f32[24,128]{1,0:T(8,128)S(1)}, u32[]{:S(2)}, u32[]{:S(2)}) collective-permute-start(f32[24,128]{1,0:T(8,128)S(1)} %get-tuple-element.58), channel_id=1, source_target_pairs={{0,1},{2,3},{1,0},{3,2},{4,5},{6,7},{5,4},{7,6},{8,9},{10,11},{9,8... | collective-permute-start | bytes 36872 | tf_op jit(solution)/shard_map/ppermute | solution.py:890
  55.7 5.5 %collective-permute-start.13 = (f32[24,128]{1,0:T(8,128)S(1)}, f32[24,128]{1,0:T(8,128)S(1)}, u32[]{:S(2)}, u32[]{:S(2)}) collective-permute-start(f32[24,128]{1,0:T(8,128)S(1)} %get-tuple-element.59), channel_id=1, source_target_pairs={{1,2},{2,1},{5,6},{6,5},{9,10},{10,9},{13,14},{14,13},{17,18},{18,... | collective-permute-start | bytes 36872 | tf_op jit(solution)/shard_map/ppermute | solution.py:890

commit v5 on v4

--- a/solution.py
+++ b/solution.py
@@ -14,7 +14,7 @@
 BULK = 5
 GROUPS = 4
 OFFSETS = 17
-BLOCK = 80
+BLOCK = 176
 F32 = jnp.float32
 VMEM = pl.BlockSpec(memory_space=pltpu.VMEM)
 ANY = pl.BlockSpec(memory_space=pl.ANY)
@@ -238,38 +238,24 @@
     return jnp.where(lanes == lane, pltpu.roll(column, (lane - source) % LANES, 1), acc)
 
 
-def pack_lat_kernel(plan, spec_hbm, mask, u_hbm, v_hbm, after, odd, even, spec, u, v, maskv, both, sem):
+def pack_lat_kernel(plan, spec, mask, u_hbm, v_hbm, after, odd, even, both, u, v, sem):
     del after
+    fields = [pltpu.make_async_copy(x, y, sem.at[n]) for n, (x, y) in enumerate(((u_hbm, u), (v_hbm, v)))]
+    for c in fields:
+        c.start()
     south, north = sides_of(both, "lat")
     width_x = mask.shape[0]
     levels, ocean_x, ocean_y = u.shape
     last = ocean_y - LANES
-    first = pltpu.make_async_copy(mask, maskv, sem.at[0])
-    first.start()
-    cuts = [a for a, _ in split(0, plan.comps)] + [plan.comps]
-    parts = []
-    for n in range(len(cuts) - 1):
-        rows = pl.ds(cuts[n] * width_x, (cuts[n + 1] - cuts[n]) * width_x)
-        parts.append(pltpu.make_async_copy(spec_hbm.at[rows, :], spec.at[rows, :], sem.at[3 + n]))
-        parts[-1].start()
-    fields = [pltpu.make_async_copy(x, y, sem.at[1 + n]) for n, (x, y) in enumerate(((u_hbm, u), (v_hbm, v)))]
-    for c in fields:
-        c.start()
-    first.wait()
-    maskf = maskv[...].astype(F32)
-    here = 0
+    maskf = mask[...].astype(F32)
     for out, source, sign in ((north, LANES - 1, True), (south, 0, False)):
         for a, b in plan.lat_blocks(sign):
-            while cuts[here] < b:
-                parts[here].wait()
-                here += 1
             rows, lane = plan.lat_place(sign, a, b, width_x)
             acc = out[rows, :] if lane else jnp.zeros((b - a, LANES), F32)
             for i in range(width_x):
                 x = spec[pl.ds(a * width_x + i, b - a, stride=width_x), :] * maskf[i : i + 1, :]
                 acc = to_lane(acc, x, source, lane + i, lanes_of(b - a))
             out[rows, :] = acc
-    assert here == len(parts)
     for c in fields:
         c.wait()
     for out, source, sign, m in ((north, LANES - 1, True, last), (south, 0, False, 0)):
@@ -288,19 +274,16 @@
     shape = (plan.lat_rows(True) + u.shape[1], LANES)
     return pl.pallas_call(
         functools.partial(pack_lat_kernel, plan),
-        out_shape=[jax.ShapeDtypeStruct(shape, F32)] * 2 + [pltpu.VMEM(spec2.shape, F32)],
-        in_specs=[HBM] * 4 + [ANY],
-        out_specs=[VMEM] * 3,
-        cost_estimate=CHEAP,
-        scratch_shapes=[pltpu.VMEM(x.shape, F32) for x in (u, v)]
-        + [
-            pltpu.VMEM(mask.shape, mask.dtype),
-            pltpu.VMEM((2, *shape), F32),
-            pltpu.SemaphoreType.DMA((3 + len(split(0, plan.comps)),)),
-        ],
+        out_shape=[jax.ShapeDtypeStruct(shape, F32)] * 2,
+        in_specs=[VMEM] * 2 + [HBM] * 2 + [ANY],
+        out_specs=[VMEM] * 2,
+        cost_estimate=CHEAP,
+        scratch_shapes=[pltpu.VMEM((2, *shape), F32)]
+        + [pltpu.VMEM(x.shape, F32) for x in (u, v)]
+        + [pltpu.SemaphoreType.DMA((2,))],
         compiler_params=PARAMS,
         name="pack_lat",
-    )(*pinned(spec2, mask, u, v), after)
+    )(kept(spec2), mask, *pinned(u, v), after)
 
 
 def advect_kernel(plan, step, state, coefs, more, part):
@@ -363,16 +346,21 @@
 
 
 def add_bulk(coefs, weights, rows, state, total):
-    count = rows.stop - rows.start
+    count, columns = (rows.stop - rows.start, state.shape[0])
+    if coefs is not None:
+        for q in range(BULK):
+            weights[q, rows, :] = jnp.broadcast_to(coefs[rows, 3 + q : 4 + q], (count, LANES))
+    acc = [[total[q, i] for i in range(columns)] for q in range(BULK)]
+    for first in range(rows.start, rows.stop, 8):
+        here = slice(first, first + 8)
+        s = [state[i, here, :] for i in range(columns)]
+        for q in range(BULK):
+            w = weights[q, here, :]
+            for i in range(columns):
+                acc[q][i] = acc[q][i] + w * s[i]
     for q in range(BULK):
-        if coefs is None:
-            w = weights[q, rows, :]
-        else:
-            w = jnp.broadcast_to(coefs[rows, 3 + q : 4 + q], (count, LANES))
-            weights[q, rows, :] = w
-        for i in range(state.shape[0]):
-            part = (w * state[i, rows, :]).reshape(count // 8, 8, LANES).sum(0)
-            total[q, i] = total[q, i] + part
+        for i in range(columns):
+            total[q, i] = acc[q][i]
 
 
 def interior_kernel(plan, step, *refs):
@@ -622,12 +610,13 @@
 
 def gathered(slabs, at, off, weight, count, acc=None, offsets=range(OFFSETS)):
     acc = [0.0] * count if acc is None else acc
-    for o in offsets:
-        rows = [slabs(o, q) for q in range(count)]
-        for p in range(len(at)):
-            w = jnp.where(off[p] == o, weight[p], 0.0)
-            for q in range(count):
-                acc[q] = acc[q] + w * jnp.take_along_axis(rows[q], at[p], axis=1, mode="promise_in_bounds")
+    for p in range(len(at)):
+        for q in range(count):
+            got = 0.0
+            for o in offsets:
+                new = jnp.take_along_axis(slabs(o, q), at[p], axis=1, mode="promise_in_bounds")
+                got = jnp.where(off[p] == o, new, got)
+            acc[q] = acc[q] + weight[p] * got
     return acc
 
 
@@ -912,7 +901,7 @@
     plan = Plan(comps)
     spec2 = spectrum.reshape(comps * width_x, width_y)
     lon = pack_lon(plan, spectrum.reshape(comps, width_x, 1, width_y), sea_mask)
-    *lat, spec2 = pack_lat(plan, spec2, sea_mask, ocean_u, ocean_v, lon[0])
+    lat = pack_lat(plan, spec2, sea_mask, ocean_u, ocean_v, lon[0])
     begun = exchange(lon, lat)
 
     coefs = columns_of(plan, bulk_weight)

time: 62.4 us -> 59.9 us (0.960)
  Pallas kernels: 37.8 us -> 32.8 us
  waiting for transfers between devices: 0.04 us -> 1.78 us
  starting transfers between devices: 23.1 us -> 23.9 us
    ppermute x14, waiting for transfers between devices: 0.04 us -> 1.78 us  [swap(): got.append(lax.ppermute(value, axis, pairs + [(j, i) for i, j in pairs]))]
    pallas_call x1, Pallas kernels: 3.9 us -> 2.19 us  [remap_own(): pl.pallas_call(functools.partial(remap_kernel, True), out_shape=[jax.Shap...]
    pallas_call x1, Pallas kernels: 3.53 us -> 2.37 us  [remap_rest(): pl.pallas_call(functools.partial(remap_kernel, False), out_shape=jax.Shap...]
    pallas_call x1, Pallas kernels: 3.9 us -> 2.8 us  [pack_lat(): pl.pallas_call(functools.partial(pack_lat_kernel, plan), out_shape=[jax.S...]
    ppermute x14, starting transfers between devices: 23.1 us -> 23.9 us  [swap(): got.append(lax.ppermute(value, axis, pairs + [(j, i) for i, j in pairs]))]
    pallas_call x1, Pallas kernels: 1.29 us -> 0.56 us  [remap_lon(): pl.pallas_call(remap_lon_kernel, out_shape=[jax.ShapeDtypeStruct(shape, F...]
  transfers between devices with their start and end apart: 14 -> 14, of which waited for: 0 -> 2; matrix products, arithmetic and copies ran while one was open for 0% -> 0% of each run, Pallas kernels for 50% -> 44%
where the time goes in v5:
time: 59.9 us; the launch traced here: 59.8 us
  Pallas kernels  32.8 us (55%)
  starting transfers between devices  23.9 us (40%)
  waiting for transfers between devices  1.78 us (3%)
  between operations  1.02 us (2%)
    ppermute x14, starting transfers between devices, swap(): got.append(lax.ppermute(value, axis, pairs + [(j, i) for i, j in pairs]))  23.9 us
    pallas_call x2, Pallas kernels, interior(): pl.pallas_call(functools.partial(interior_kernel, plan, step), out_shape=...  10.9 us
    pallas_call x2, Pallas kernels, advect(): pl.pallas_call(functools.partial(advect_kernel, plan, step), out_shape=ja...  5.93 us
    pallas_call x2, Pallas kernels, edges(): pl.pallas_call(functools.partial(edges_kernel, plan, step), out_shape=out...  3.45 us
    pallas_call x1, Pallas kernels, pack_lat(): pl.pallas_call(functools.partial(pack_lat_kernel, plan), out_shape=[jax.S...  2.8 us
    pallas_call x1, Pallas kernels, remap_rest(): pl.pallas_call(functools.partial(remap_kernel, False), out_shape=jax.Shap...  2.37 us
    pallas_call x1, Pallas kernels, remap_own(): pl.pallas_call(functools.partial(remap_kernel, True), out_shape=[jax.Shap...  2.19 us
    ppermute x14, waiting for transfers between devices, swap(): got.append(lax.ppermute(value, axis, pairs + [(j, i) for i, j in pairs]))  1.78 us
  transfers between devices with their start and end apart: 14, of which 2 were waited for; matrix products, arithmetic and copies ran while one was open for 0% of the time, Pallas kernels for 44%

profile of v5, /device:TPU:1, one launch (start us, length us, event | category | flops | bytes accessed | tf_op | source)
XLA Modules:
  0.0 59.8 jit_solution(5294880745488909903)
XLA Ops:
  0.6 1.4 %pack_lon.1 = (f32[656,128]{1,0:T(8,128)S(1)}, f32[656,128]{1,0:T(8,128)S(1)}) custom-call(f32[1296,8,1,128]{3,2,1,0:T(1,128)} %bitcast.28, s32[8,128]{1,0:T(8,128)} %refs_5_.7), custom_call_target="tpu_custom_call" | custom-call | flops 1 | bytes 1 | tf_op jit(solution)/shard_map/pack_lon/pallas_call | solution.py:221
  2.1 2.1 %collective-permute-start.2 = (f32[656,128]{1,0:T(8,128)S(1)}, f32[656,128]{1,0:T(8,128)S(1)}, u32[]{:S(2)}, u32[]{:S(2)}) collective-permute-start(f32[656,128]{1,0:T(8,128)S(1)} %get-tuple-element.32.after), channel_id=1, source_target_pairs={{0,4},{8,12},{16,20},{24,28},{4,0},{12,8},{20,16},{28,24},{1,5},{9... | collective-permute-start | bytes 1007624 | tf_op jit(solution)/shard_map/ppermute | solution.py:879
  4.2 3.3 %collective-permute-start.3 = (f32[656,128]{1,0:T(8,128)S(1)}, f32[656,128]{1,0:T(8,128)S(1)}, u32[]{:S(2)}, u32[]{:S(2)}) collective-permute-start(f32[656,128]{1,0:T(8,128)S(1)} %get-tuple-element.37), channel_id=1, source_target_pairs={{4,8},{12,16},{20,24},{28,0},{8,4},{16,12},{24,20},{0,28},{5,9},{1... | collective-permute-start | bytes 1007624 | tf_op jit(solution)/shard_map/ppermute | solution.py:879
  7.5 2.8 %pack_lat.1 = (f32[200,128]{1,0:T(8,128)S(1)}, f32[200,128]{1,0:T(8,128)S(1)}) custom-call(f32[10368,128]{1,0:T(8,128)S(1)} %bitcast.29, s32[8,128]{1,0:T(8,128)S(1)} %copy-done.5, f32[8,24,384]{2,1,0:T(8,128)} %u.3, f32[8,24,384]{2,1,0:T(8,128)} %v.3, f32[656,128]{1,0:T(8,128)S(1)} %get-tuple-element.32.after), custom_call_target="tpu_custom_call" | custom-call | flops 1 | bytes 1 | tf_op jit(solution)/shard_map/pack_lat/pallas_call | solution.py:275
  10.3 1.3 %collective-permute-start = (f32[200,128]{1,0:T(8,128)S(1)}, f32[200,128]{1,0:T(8,128)S(1)}, u32[]{:S(2)}, u32[]{:S(2)}) collective-permute-start(f32[200,128]{1,0:T(8,128)S(1)} %get-tuple-element.33), channel_id=1, source_target_pairs={{0,1},{2,3},{1,0},{3,2},{4,5},{6,7},{5,4},{7,6},{8,9},{10,11},{9,8... | collective-permute-start | bytes 307208 | tf_op jit(solution)/shard_map/ppermute | solution.py:879
  11.6 3.0 %collective-permute-start.1 = (f32[200,128]{1,0:T(8,128)S(1)}, f32[200,128]{1,0:T(8,128)S(1)}, u32[]{:S(2)}, u32[]{:S(2)}) collective-permute-start(f32[200,128]{1,0:T(8,128)S(1)} %get-tuple-element.34), channel_id=1, source_target_pairs={{1,2},{2,1},{5,6},{6,5},{9,10},{10,9},{13,14},{14,13},{17,18},{18,... | collective-permute-start | bytes 307208 | tf_op jit(solution)/shard_map/ppermute | solution.py:879
  14.9 3.0 %advect.2.refs_0_ = f32[8,1296,128]{2,1,0:T(8,128)S(1)} custom-call(f32[10368,128]{1,0:T(8,128)S(1)} %bitcast.30, f32[1296,8]{1,0:T(8,128)S(1)} %columns.1.coefs.refs_4_, s32[8,128]{1,0:T(8,128)S(1)} %copy-done.5), custom_call_target="tpu_custom_call" | custom-call | flops 1 | bytes 1 | tf_op jit(solution)/shard_map/advect/pallas_call | solution.py:325
  17.9 4.6 %interior.2 = (f32[6,1296,128]{2,1,0:T(8,128)S(1)}, f32[2,1296,128]{2,1,0:T(8,128)S(1)}, f32[176,128]{1,0:T(8,128)S(1)}, f32[176,128]{1,0:T(8,128)S(1)}) custom-call(f32[8,1296,128]{2,1,0:T(8,128)S(1)} %advect.2.refs_0_, f32[200,128]{1,0:T(8,128)S(1)} %collective-permute-done.refs_1_.from_odd, f32[200,128]{1,0:T(8,128)S(1)} %collective-permute-done.1.refs_2_.from_even, ...), custom_call_target="tpu_custom_call" | custom-call | flops 1 | bytes 1 | tf_op jit(solution)/shard_map/interior/pallas_call | solution.py:451
  22.5 1.6 %edges.2 = (f32[2,1296,128]{2,1,0:T(8,128)S(1)}, f32[656,128]{1,0:T(8,128)S(1)}, f32[656,128]{1,0:T(8,128)S(1)}) custom-call(f32[2,1296,128]{2,1,0:T(8,128)S(1)} %get-tuple-element.36.refs_0_, f32[656,128]{1,0:T(8,128)S(1)} %collective-permute-done.2.refs_1_, f32[656,128]{1,0:T(8,128)S(1)} %collective-permute-done.3.refs_2_, bf16[1296,1296]{1,0:T(8,128)(2,1)S(1)} %copy-done, ...), custom_call_target="tpu_custom_call" | custom-call | flops 1 | bytes 1 | tf_op jit(solution)/shard_map/edges/pallas_call | solution.py:551
  24.2 1.3 %collective-permute-start.7 = (f32[656,128]{1,0:T(8,128)S(1)}, f32[656,128]{1,0:T(8,128)S(1)}, u32[]{:S(2)}, u32[]{:S(2)}) collective-permute-start(f32[656,128]{1,0:T(8,128)S(1)} %get-tuple-element.45), channel_id=1, source_target_pairs={{4,8},{12,16},{20,24},{28,0},{8,4},{16,12},{24,20},{0,28},{5,9},{1... | collective-permute-start | bytes 1007624 | tf_op jit(solution)/shard_map/ppermute | solution.py:879
  26.0 1.7 %collective-permute-start.4 = (f32[176,128]{1,0:T(8,128)S(1)}, f32[176,128]{1,0:T(8,128)S(1)}, u32[]{:S(2)}, u32[]{:S(2)}) collective-permute-start(f32[176,128]{1,0:T(8,128)S(1)} %get-tuple-element.41), channel_id=1, source_target_pairs={{0,1},{2,3},{1,0},{3,2},{4,5},{6,7},{5,4},{7,6},{8,9},{10,11},{9,8... | collective-permute-start | bytes 270344 | tf_op jit(solution)/shard_map/ppermute | solution.py:879
  27.7 3.2 %collective-permute-start.5 = (f32[176,128]{1,0:T(8,128)S(1)}, f32[176,128]{1,0:T(8,128)S(1)}, u32[]{:S(2)}, u32[]{:S(2)}) collective-permute-start(f32[176,128]{1,0:T(8,128)S(1)} %get-tuple-element.42), channel_id=1, source_target_pairs={{1,2},{2,1},{5,6},{6,5},{9,10},{10,9},{13,14},{14,13},{17,18},{18,... | collective-permute-start | bytes 270344 | tf_op jit(solution)/shard_map/ppermute | solution.py:879
  31.5 2.9 %advect.3.refs_0_ = f32[8,1296,128]{2,1,0:T(8,128)S(1)} custom-call(f32[6,1296,128]{2,1,0:T(8,128)S(1)} %get-tuple-element.35.state, f32[1296,8]{1,0:T(8,128)S(1)} %columns.1.coefs.refs_4_, f32[2,1296,128]{2,1,0:T(8,128)S(1)} %get-tuple-element.38.more.state), custom_call_target="tpu_custom_call" | custom-call | flops 1 | bytes 1 | tf_op jit(solution)/shard_map/advect/pallas_call | solution.py:325
  34.5 6.3 %interior.3 = (f32[1296,8,1,128]{3,2,1,0:T(1,128)}, f32[2,1296,128]{2,1,0:T(8,128)S(1)}, f32[5,8,128]{2,1,0:T(8,128)S(1)}, f32[5,1296,128]{2,1,0:T(8,128)S(1)}) custom-call(f32[8,1296,128]{2,1,0:T(8,128)S(1)} %advect.3.refs_0_, f32[176,128]{1,0:T(8,128)S(1)} %collective-permute-done.4.refs_1_, f32[176,128]{1,0:T(8,128)S(1)} %collective-permute-done.5.refs_2_, ...), custom_call_target="tpu_custom_call" | custom-call | flops 1 | bytes 1 | tf_op jit(solution)/shard_map/interior/pallas_call | solution.py:451
  40.9 1.9 %edges.3 = (f32[2,1296,128]{2,1,0:T(8,128)S(1)}, f32[5,8,128]{2,1,0:T(8,128)S(1)}) custom-call(f32[2,1296,128]{2,1,0:T(8,128)S(1)} %get-tuple-element.43.refs_0_, f32[656,128]{1,0:T(8,128)S(1)} %collective-permute-done.6.refs_1_, f32[656,128]{1,0:T(8,128)S(1)} %collective-permute-done.7.refs_2_, bf16[1296,1296]{1,0:T(8,128)(2,1)S(1)} %copy-done, ...), custom_call_target="tpu_custom_call" | custom-call | flops 1 | bytes 1 | tf_op jit(solution)/shard_map/edges/pallas_call | solution.py:551
  42.8 1.3 %collective-permute-start.9 = (f32[5,8,128]{2,1,0:T(8,128)S(1)}, f32[5,8,128]{2,1,0:T(8,128)S(1)}, u32[]{:S(2)}, u32[]{:S(2)}) collective-permute-start(f32[5,8,128]{2,1,0:T(8,128)S(1)} %get-tuple-element.49.refs_0_.own), channel_id=1, source_target_pairs={{4,8},{12,16},{20,24},{28,0},{8,4},{16,12},{24,20},{0,28},{5,9},{1... | collective-permute-start | bytes 61448 | tf_op jit(solution)/shard_map/ppermute | solution.py:879
  44.3 2.2 %remap_own.1 = (f32[5,24,384]{2,1,0:T(8,128)S(1)}, f32[1296,8,1,128]{3,2,1,0:T(1,128)}) custom-call(f32[5,8,128]{2,1,0:T(8,128)S(1)} %get-tuple-element.49.refs_0_.own, s32[4,24,384]{2,1,0:T(8,128)S(1)} %get-tuple-element.62.refs_1_.refs_2_.cell, s32[4,24,384]{2,1,0:T(8,128)S(1)} %get-tuple-element.61.refs_2_.refs_3_.offset, ...), custom_call_target="tpu_custom_call", output_to_operand_aliasing={{1}: (5, {})} | custom-call | flops 1 | bytes 1 | tf_op jit(solution)/shard_map/remap_own/pallas_call | solution.py:782
  46.5 1.7 %collective-permute-done.9.refs_1_.from_even = f32[5,8,128]{2,1,0:T(8,128)S(1)} collective-permute-done((f32[5,8,128]{2,1,0:T(8,128)S(1)}, f32[5,8,128]{2,1,0:T(8,128)S(1)}, u32[]{:S(2)}, u32[]{:S(2)}) %collective-permute-start.9) | collective-permute-done | bytes 20512 | tf_op jit(solution)/shard_map/ppermute | solution.py:879
  48.9 1.3 %collective-permute-start.11 = (f32[56,128]{1,0:T(8,128)S(1)}, f32[56,128]{1,0:T(8,128)S(1)}, u32[]{:S(2)}, u32[]{:S(2)}) collective-permute-start(f32[56,128]{1,0:T(8,128)S(1)} %get-tuple-element.55), channel_id=1, source_target_pairs={{4,8},{12,16},{20,24},{28,0},{8,4},{16,12},{24,20},{0,28},{5,9},{1... | collective-permute-start | bytes 86024 | tf_op jit(solution)/shard_map/ppermute | solution.py:879
  50.2 1.0 %remap_lat.1 = (f32[24,128]{1,0:T(8,128)S(1)}, f32[24,128]{1,0:T(8,128)S(1)}) custom-call(f32[5,8,128]{2,1,0:T(8,128)S(1)} %get-tuple-element.49.refs_0_.own, f32[5,8,128]{2,1,0:T(8,128)S(1)} %collective-permute-done.8.refs_0_.from_odd, f32[5,8,128]{2,1,0:T(8,128)S(1)} %collective-permute-done.9.refs_1_.from_even, ...), custom_call_target="tpu_custom_call" | custom-call | flops 1 | bytes 1 | tf_op jit(solution)/shard_map/remap_lat/pallas_call | solution.py:723
  51.2 2.5 %collective-permute-start.12 = (f32[24,128]{1,0:T(8,128)S(1)}, f32[24,128]{1,0:T(8,128)S(1)}, u32[]{:S(2)}, u32[]{:S(2)}) collective-permute-start(f32[24,128]{1,0:T(8,128)S(1)} %get-tuple-element.56), channel_id=1, source_target_pairs={{0,1},{2,3},{1,0},{3,2},{4,5},{6,7},{5,4},{7,6},{8,9},{10,11},{9,8... | collective-permute-start | bytes 36872 | tf_op jit(solution)/shard_map/ppermute | solution.py:879
  53.7 2.6 %collective-permute-start.13 = (f32[24,128]{1,0:T(8,128)S(1)}, f32[24,128]{1,0:T(8,128)S(1)}, u32[]{:S(2)}, u32[]{:S(2)}) collective-permute-start(f32[24,128]{1,0:T(8,128)S(1)} %get-tuple-element.57), channel_id=1, source_target_pairs={{1,2},{2,1},{5,6},{6,5},{9,10},{10,9},{13,14},{14,13},{17,18},{18,... | collective-permute-start | bytes 36872 | tf_op jit(solution)/shard_map/ppermute | solution.py:879
  56.3 2.4 %remap_rest.1.forcing = f32[5,24,384]{2,1,0:T(8,128)S(1)} custom-call(f32[5,8,128]{2,1,0:T(8,128)S(1)} %collective-permute-done.8.refs_0_.from_odd, f32[5,8,128]{2,1,0:T(8,128)S(1)} %collective-permute-done.9.refs_1_.from_even, s32[4,24,384]{2,1,0:T(8,128)S(1)} %get-tuple-element.62.refs_1_.refs_2_.cell, ...), custom_call_target="tpu_custom_call" | custom-call | flops 1 | bytes 1 | tf_op jit(solution)/shard_map/remap_rest/pallas_call | solution.py:797
  58.7 1.0 %ocean_final.1 = (f32[8,24,384]{2,1,0:T(8,128)}, f32[8,24,384]{2,1,0:T(8,128)}) custom-call(f32[5,24,384]{2,1,0:T(8,128)S(1)} %remap_rest.1.forcing, f32[56,128]{1,0:T(8,128)S(1)} %collective-permute-done.10.lon_odd, f32[56,128]{1,0:T(8,128)S(1)} %collective-permute-done.11.lon_even, f32[24,128]{1,0:T(8,128)S(1)} %collective-permute-done.12.lat_odd, ...), custom_call_target="tpu_custom_call" | custom-call | flops 1 | bytes 1 | tf_op jit(solution)/shard_map/ocean_final/pallas_call | solution.py:862
  (45 shorter events, 2.3 us)
Async XLA Ops:
  0.6 6.8 %copy-start.5 = (s32[8,128]{1,0:T(8,128)S(1)}, s32[8,128]{1,0:T(8,128)}, u32[]{:S(2)}) copy-start(s32[8,128]{1,0:T(8,128)} %refs_5_.7) | copy-start | bytes 12292
  0.6 6.8 %copy-start.1 = (f32[1296,8,128]{2,1,0:T(8,128)S(1)}, f32[1296,8,128]{2,1,0:T(8,128)}, u32[]{:S(2)}) copy-start(f32[1296,8,128]{2,1,0:T(8,128)} %param.11) | copy-start | bytes 15925252
  2.0 12.6 %copy-start.4 = (f32[1296,8]{1,0:T(8,128)S(1)}, f32[1296,8]{1,0:T(8,128)}, u32[]{:S(2)}) copy-start(f32[1296,8]{1,0:T(8,128)} %constant.32.clone.coef) | copy-start | bytes 124420
  2.1 12.6 %copy-start.7 = (f32[5,1296]{1,0:T(8,128)S(1)}, f32[5,1296]{1,0:T(8,128)}, u32[]{:S(2)}) copy-start(f32[5,1296]{1,0:T(8,128)} %bulk_weight.1) | copy-start | bytes 77764
  2.1 20.5 %collective-permute-start.2 = (f32[656,128]{1,0:T(8,128)S(1)}, f32[656,128]{1,0:T(8,128)S(1)}, u32[]{:S(2)}, u32[]{:S(2)}) collective-permute-start(f32[656,128]{1,0:T(8,128)S(1)} %get-tuple-element.32.after), channel_id=1, source_target_pairs={{0,4},{8,12},{16,20},{24,28},{4,0},{12,8},{20,16},{28,24},{1,5},{9... | collective-permute-start | bytes 1007624 | tf_op jit(solution)/shard_map/ppermute | solution.py:879
  4.2 18.3 %collective-permute-start.3 = (f32[656,128]{1,0:T(8,128)S(1)}, f32[656,128]{1,0:T(8,128)S(1)}, u32[]{:S(2)}, u32[]{:S(2)}) collective-permute-start(f32[656,128]{1,0:T(8,128)S(1)} %get-tuple-element.37), channel_id=1, source_target_pairs={{4,8},{12,16},{20,24},{28,0},{8,4},{16,12},{24,20},{0,28},{5,9},{1... | collective-permute-start | bytes 1007624 | tf_op jit(solution)/shard_map/ppermute | solution.py:879
  10.3 7.6 %collective-permute-start = (f32[200,128]{1,0:T(8,128)S(1)}, f32[200,128]{1,0:T(8,128)S(1)}, u32[]{:S(2)}, u32[]{:S(2)}) collective-permute-start(f32[200,128]{1,0:T(8,128)S(1)} %get-tuple-element.33), channel_id=1, source_target_pairs={{0,1},{2,3},{1,0},{3,2},{4,5},{6,7},{5,4},{7,6},{8,9},{10,11},{9,8... | collective-permute-start | bytes 307208 | tf_op jit(solution)/shard_map/ppermute | solution.py:879
  11.6 6.3 %collective-permute-start.1 = (f32[200,128]{1,0:T(8,128)S(1)}, f32[200,128]{1,0:T(8,128)S(1)}, u32[]{:S(2)}, u32[]{:S(2)}) collective-permute-start(f32[200,128]{1,0:T(8,128)S(1)} %get-tuple-element.34), channel_id=1, source_target_pairs={{1,2},{2,1},{5,6},{6,5},{9,10},{10,9},{13,14},{14,13},{17,18},{18,... | collective-permute-start | bytes 307208 | tf_op jit(solution)/shard_map/ppermute | solution.py:879
  22.5 8.4 %copy-start.10 = (f32[384]{0:T(512)S(1)}, f32[384]{0:T(512)}, u32[]{:S(2)}) copy-start(f32[384]{0:T(512)} %param.20) | copy-start | bytes 4612
  22.5 8.4 %copy-start.2 = (f32[8,24,384]{2,1,0:T(8,128)S(1)}, f32[8,24,384]{2,1,0:T(8,128)}, u32[]{:S(2)}) copy-start(f32[8,24,384]{2,1,0:T(8,128)} %u.3) | copy-start | bytes 884740
  22.5 8.4 %copy-start.3 = (f32[8,24,384]{2,1,0:T(8,128)S(1)}, f32[8,24,384]{2,1,0:T(8,128)}, u32[]{:S(2)}) copy-start(f32[8,24,384]{2,1,0:T(8,128)} %v.3) | copy-start | bytes 884740
  22.5 8.4 %copy-start.6 = (s32[24,384]{1,0:T(8,128)S(1)}, s32[24,384]{1,0:T(8,128)}, u32[]{:S(2)}) copy-start(s32[24,384]{1,0:T(8,128)} %mask.7) | copy-start | bytes 110596
  24.1 16.7 %collective-permute-start.6 = (f32[656,128]{1,0:T(8,128)S(1)}, f32[656,128]{1,0:T(8,128)S(1)}, u32[]{:S(2)}, u32[]{:S(2)}) collective-permute-start(f32[656,128]{1,0:T(8,128)S(1)} %get-tuple-element.44), channel_id=1, source_target_pairs={{0,4},{8,12},{16,20},{24,28},{4,0},{12,8},{20,16},{28,24},{1,5},{9... | collective-permute-start | bytes 1007624 | tf_op jit(solution)/shard_map/ppermute | solution.py:879
  24.2 16.6 %collective-permute-start.7 = (f32[656,128]{1,0:T(8,128)S(1)}, f32[656,128]{1,0:T(8,128)S(1)}, u32[]{:S(2)}, u32[]{:S(2)}) collective-permute-start(f32[656,128]{1,0:T(8,128)S(1)} %get-tuple-element.45), channel_id=1, source_target_pairs={{4,8},{12,16},{20,24},{28,0},{8,4},{16,12},{24,20},{0,28},{5,9},{1... | collective-permute-start | bytes 1007624 | tf_op jit(solution)/shard_map/ppermute | solution.py:879
  26.0 8.5 %collective-permute-start.4 = (f32[176,128]{1,0:T(8,128)S(1)}, f32[176,128]{1,0:T(8,128)S(1)}, u32[]{:S(2)}, u32[]{:S(2)}) collective-permute-start(f32[176,128]{1,0:T(8,128)S(1)} %get-tuple-element.41), channel_id=1, source_target_pairs={{0,1},{2,3},{1,0},{3,2},{4,5},{6,7},{5,4},{7,6},{8,9},{10,11},{9,8... | collective-permute-start | bytes 270344 | tf_op jit(solution)/shard_map/ppermute | solution.py:879
  27.7 6.8 %collective-permute-start.5 = (f32[176,128]{1,0:T(8,128)S(1)}, f32[176,128]{1,0:T(8,128)S(1)}, u32[]{:S(2)}, u32[]{:S(2)}) collective-permute-start(f32[176,128]{1,0:T(8,128)S(1)} %get-tuple-element.42), channel_id=1, source_target_pairs={{1,2},{2,1},{5,6},{6,5},{9,10},{10,9},{13,14},{14,13},{17,18},{18,... | collective-permute-start | bytes 270344 | tf_op jit(solution)/shard_map/ppermute | solution.py:879
  40.9 3.3 %copy-start.8 = (s32[24,384,4]{1,2,0:T(4,128)S(1)}, s32[24,384,4]{1,2,0:T(4,128)}, u32[]{:S(2)}) copy-start(s32[24,384,4]{1,2,0:T(4,128)} %param.15) | copy-start | bytes 442372
  40.9 3.4 %copy-start.9 = (f32[24,384,4]{1,2,0:T(4,128)S(1)}, f32[24,384,4]{1,2,0:T(4,128)}, u32[]{:S(2)}) copy-start(f32[24,384,4]{1,2,0:T(4,128)} %param.16) | copy-start | bytes 442372
  42.7 3.8 %collective-permute-start.8 = (f32[5,8,128]{2,1,0:T(8,128)S(1)}, f32[5,8,128]{2,1,0:T(8,128)S(1)}, u32[]{:S(2)}, u32[]{:S(2)}) collective-permute-start(f32[5,8,128]{2,1,0:T(8,128)S(1)} %get-tuple-element.49.refs_0_.own), channel_id=1, source_target_pairs={{0,4},{8,12},{16,20},{24,28},{4,0},{12,8},{20,16},{28,24},{1,5},{9... | collective-permute-start | bytes 61448 | tf_op jit(solution)/shard_map/ppermute | solution.py:879
  42.8 5.4 %collective-permute-start.9 = (f32[5,8,128]{2,1,0:T(8,128)S(1)}, f32[5,8,128]{2,1,0:T(8,128)S(1)}, u32[]{:S(2)}, u32[]{:S(2)}) collective-permute-start(f32[5,8,128]{2,1,0:T(8,128)S(1)} %get-tuple-element.49.refs_0_.own), channel_id=1, source_target_pairs={{4,8},{12,16},{20,24},{28,0},{8,4},{16,12},{24,20},{0,28},{5,9},{1... | collective-permute-start | bytes 61448 | tf_op jit(solution)/shard_map/ppermute | solution.py:879
  48.8 10.0 %collective-permute-start.10 = (f32[56,128]{1,0:T(8,128)S(1)}, f32[56,128]{1,0:T(8,128)S(1)}, u32[]{:S(2)}, u32[]{:S(2)}) collective-permute-start(f32[56,128]{1,0:T(8,128)S(1)} %get-tuple-element.54.after), channel_id=1, source_target_pairs={{0,4},{8,12},{16,20},{24,28},{4,0},{12,8},{20,16},{28,24},{1,5},{9... | collective-permute-start | bytes 86024 | tf_op jit(solution)/shard_map/ppermute | solution.py:879
  48.9 9.9 %collective-permute-start.11 = (f32[56,128]{1,0:T(8,128)S(1)}, f32[56,128]{1,0:T(8,128)S(1)}, u32[]{:S(2)}, u32[]{:S(2)}) collective-permute-start(f32[56,128]{1,0:T(8,128)S(1)} %get-tuple-element.55), channel_id=1, source_target_pairs={{4,8},{12,16},{20,24},{28,0},{8,4},{16,12},{24,20},{0,28},{5,9},{1... | collective-permute-start | bytes 86024 | tf_op jit(solution)/shard_map/ppermute | solution.py:879
  51.2 7.5 %collective-permute-start.12 = (f32[24,128]{1,0:T(8,128)S(1)}, f32[24,128]{1,0:T(8,128)S(1)}, u32[]{:S(2)}, u32[]{:S(2)}) collective-permute-start(f32[24,128]{1,0:T(8,128)S(1)} %get-tuple-element.56), channel_id=1, source_target_pairs={{0,1},{2,3},{1,0},{3,2},{4,5},{6,7},{5,4},{7,6},{8,9},{10,11},{9,8... | collective-permute-start | bytes 36872 | tf_op jit(solution)/shard_map/ppermute | solution.py:879
  53.7 5.0 %collective-permute-start.13 = (f32[24,128]{1,0:T(8,128)S(1)}, f32[24,128]{1,0:T(8,128)S(1)}, u32[]{:S(2)}, u32[]{:S(2)}) collective-permute-start(f32[24,128]{1,0:T(8,128)S(1)} %get-tuple-element.57), channel_id=1, source_target_pairs={{1,2},{2,1},{5,6},{6,5},{9,10},{10,9},{13,14},{14,13},{17,18},{18,... | collective-permute-start | bytes 36872 | tf_op jit(solution)/shard_map/ppermute | solution.py:879
  (1 other events, 3.0 us)

commit v6 on v5

--- a/solution.py
+++ b/solution.py
@@ -467,7 +467,7 @@
         full, moved, both = refs[9:]
     else:
         bulk_in, weights = refs[6:8]
-        state, bulk, full, moved, both, total = refs[-6:]
+        state, bulk, longer, full, moved, both, total = refs[-7:]
     width = mask.shape[0]
     maskf = jnp.concatenate([mask[0:1, :], mask[width - 1 : width, :]], axis=0).astype(F32)
     both[0] = from_odd[...]
@@ -502,6 +502,8 @@
             bulk[q] = bulk_in[q]
             bulk[q, 0:1, :] = total[q, 0].sum(0, keepdims=True)
             bulk[q, width - 1 : width, :] = total[q, 1].sum(0, keepdims=True)
+        longer[:BULK] = bulk[...]
+        longer[BULK:] = jnp.zeros((longer.shape[0] - BULK, width, LANES), F32)
         return
     for out, side, sign in ((from_east, 1, True), (from_west, 0, False)):
         at = 0
@@ -546,7 +548,7 @@
     if step == 0:
         outs += [jax.ShapeDtypeStruct((plan.rows("x", s), LANES), F32) for s in (True, False)]
     else:
-        outs += [jax.ShapeDtypeStruct((BULK, width, LANES), F32)]
+        outs += [jax.ShapeDtypeStruct((BULK + extra, width, LANES), F32) for extra in (0, 1)]
         scratch += [pltpu.VMEM((BULK, 2, 8, LANES), F32)]
     return pl.pallas_call(
         functools.partial(edges_kernel, plan, step),
@@ -571,7 +573,8 @@
     return before, after, below, above
 
 
-def ocean_base_kernel(plan, u, v, from_odd, from_even, mask, coriolis, base_u, base_v, both):
+def ocean_base_kernel(plan, u, v, from_odd, from_even, mask, coriolis, after, base_u, base_v, both):
+    del after
     levels, ocean_x, ocean_y = u.shape
     start = plan.lat_rows(True)
     both[0] = from_odd[start : start + ocean_x, :]
@@ -595,17 +598,17 @@
             out[level] = maskf * (q + sign * half * other[level] + 0.1 * lap)
 
 
-def ocean_base(plan, u, v, from_odd, from_even, mask, coriolis):
+def ocean_base(plan, u, v, from_odd, from_even, mask, coriolis, after):
     return pl.pallas_call(
         functools.partial(ocean_base_kernel, plan),
         out_shape=[jax.ShapeDtypeStruct(u.shape, F32)] * 2,
-        in_specs=[VMEM] * 6,
+        in_specs=[VMEM] * 6 + [ANY],
         out_specs=[VMEM] * 2,
         scratch_shapes=[pltpu.VMEM((2, u.shape[1], LANES), F32)],
         cost_estimate=CHEAP,
         compiler_params=PARAMS,
         name="ocean_base",
-    )(u, v, from_odd, from_even, mask, coriolis)
+    )(u, v, from_odd, from_even, mask, coriolis, after)
 
 
 def gathered(slabs, at, off, weight, count, acc=None, offsets=range(OFFSETS)):
@@ -631,7 +634,7 @@
 
 def bands(from_odd, from_even, near):
     near[0] = from_odd[...]
-    near[1] = from_even[...]
+    near[1] = from_even[: near.shape[1]]
     return sides_of(near, "lon")
 
 
@@ -668,7 +671,8 @@
                 out[at : at + levels, :] = field[:, row, m * LANES : (m + 1) * LANES]
                 at += levels
     odd[...] = both[0]
-    even[...] = both[1]
+    even[: both.shape[1], :] = both[1]
+    even[both.shape[1] :, :] = jnp.zeros((even.shape[0] - both.shape[1], LANES), F32)
 
 
 def remap_lat_kernel(own, from_odd, from_even, cell, offset, weight, after, odd, even, table, near, both):
@@ -703,7 +707,7 @@
     shape = (line_rows(tiles) + 2 * u.shape[0] * tiles, LANES)
     return pl.pallas_call(
         remap_lon_kernel,
-        out_shape=[jax.ShapeDtypeStruct(shape, F32)] * 2,
+        out_shape=[jax.ShapeDtypeStruct((shape[0] + extra, LANES), F32) for extra in (0, 8)],
         in_specs=[VMEM] * 8 + [ANY] * len(after),
         out_specs=[VMEM] * 2,
         scratch_shapes=[
@@ -811,7 +815,7 @@
 ):
     levels, ocean_x, ocean_y = base_u.shape
     lines[0] = lon_odd[...]
-    lines[1] = lon_even[...]
+    lines[1] = lon_even[: lines.shape[1], :]
     from_west, from_east = sides_of(lines, "lon")
     both[0] = lat_odd[...]
     both[1] = lat_even[...]
@@ -917,15 +921,15 @@
     sides, *lon = edges(plan, 0, edge, *begun[:2], transfer, coefs, sea_mask)
     halos = exchange(lon, merge_lat(plan, width_x, sides, up, down))
 
-    base_u, base_v = ocean_base(plan, ocean_u, ocean_v, *begun[2:], ocean_mask, line)
     part = advect(plan, 1, middle, coefs, sides)
     out4, edge, bulk, weights = interior(plan, 1, part, *halos[2:], transfer, coefs, sea_mask)
-    sides, bulk = edges(plan, 1, edge, *halos[:2], transfer, coefs, sea_mask, bulk, weights, base_u)
-    near = swap(bulk, bulk, "lon", True)
+    sides, bulk, longer = edges(plan, 1, edge, *halos[:2], transfer, coefs, sea_mask, bulk, weights)
+    near = swap(bulk, longer, "lon", True)
     forcing, out4 = remap_own(bulk, cell, offset, weight, sides, out4)
+    base_u, base_v = ocean_base(plan, ocean_u, ocean_v, *begun[2:], ocean_mask, line, bulk)
 
     remapped = (bulk, *near, cell, offset, weight)
-    lon = remap_lon(*remapped, ocean_u, ocean_v, forcing)
+    lon = remap_lon(*remapped, ocean_u, ocean_v, forcing, base_u)
     halos = exchange(lon, remap_lat(*remapped, lon[0]))
     forcing = remap_rest(*near, cell, offset, weight, forcing)
     new_u, new_v = ocean_final(forcing, halos, base_u, base_v, ocean_mask, line)

time: 59.9 us -> 59.3 us (0.990)
  transfers between devices with their start and end apart: 14 -> 14, of which waited for: 2 -> 1; matrix products, arithmetic and copies ran while one was open for 0% -> 0% of each run, Pallas kernels for 44% -> 45%
where the time goes in v6:
time: 59.3 us; the launch traced here: 59.2 us
  Pallas kernels  32.8 us (55%)
  starting transfers between devices  23.9 us (40%)
  waiting for transfers between devices  1.23 us (2%)
  between operations  1.02 us (2%)
    ppermute x14, starting transfers between devices, swap(): got.append(lax.ppermute(value, axis, pairs + [(j, i) for i, j in pairs]))  23.9 us
    pallas_call x2, Pallas kernels, interior(): pl.pallas_call(functools.partial(interior_kernel, plan, step), out_shape=...  10.9 us
    pallas_call x2, Pallas kernels, advect(): pl.pallas_call(functools.partial(advect_kernel, plan, step), out_shape=ja...  5.93 us
    pallas_call x2, Pallas kernels, edges(): pl.pallas_call(functools.partial(edges_kernel, plan, step), out_shape=out...  3.42 us
    pallas_call x1, Pallas kernels, pack_lat(): pl.pallas_call(functools.partial(pack_lat_kernel, plan), out_shape=[jax.S...  2.8 us
    pallas_call x1, Pallas kernels, remap_rest(): pl.pallas_call(functools.partial(remap_kernel, False), out_shape=jax.Shap...  2.35 us
    pallas_call x1, Pallas kernels, remap_own(): pl.pallas_call(functools.partial(remap_kernel, True), out_shape=[jax.Shap...  2.19 us
    pallas_call x1, Pallas kernels, pack_lon(): pl.pallas_call(functools.partial(pack_lon_kernel, plan), out_shape=[jax.S...  1.38 us
  transfers between devices with their start and end apart: 14, of which 1 were waited for; matrix products, arithmetic and copies ran while one was open for 0% of the time, Pallas kernels for 45%

profile of v6, /device:TPU:1, one launch (start us, length us, event | category | flops | bytes accessed | tf_op | source)
XLA Modules:
  0.0 59.2 jit_solution(12931001071404733937)
XLA Ops:
  0.6 1.4 %pack_lon.1 = (f32[656,128]{1,0:T(8,128)S(1)}, f32[656,128]{1,0:T(8,128)S(1)}) custom-call(f32[1296,8,1,128]{3,2,1,0:T(1,128)} %bitcast.28, s32[8,128]{1,0:T(8,128)} %refs_5_.7), custom_call_target="tpu_custom_call" | custom-call | flops 1 | bytes 1 | tf_op jit(solution)/shard_map/pack_lon/pallas_call | solution.py:221
  2.1 2.1 %collective-permute-start.2 = (f32[656,128]{1,0:T(8,128)S(1)}, f32[656,128]{1,0:T(8,128)S(1)}, u32[]{:S(2)}, u32[]{:S(2)}) collective-permute-start(f32[656,128]{1,0:T(8,128)S(1)} %get-tuple-element.33.after), channel_id=1, source_target_pairs={{0,4},{8,12},{16,20},{24,28},{4,0},{12,8},{20,16},{28,24},{1,5},{9... | collective-permute-start | bytes 1007624 | tf_op jit(solution)/shard_map/ppermute | solution.py:883
  4.2 3.3 %collective-permute-start.3 = (f32[656,128]{1,0:T(8,128)S(1)}, f32[656,128]{1,0:T(8,128)S(1)}, u32[]{:S(2)}, u32[]{:S(2)}) collective-permute-start(f32[656,128]{1,0:T(8,128)S(1)} %get-tuple-element.38), channel_id=1, source_target_pairs={{4,8},{12,16},{20,24},{28,0},{8,4},{16,12},{24,20},{0,28},{5,9},{1... | collective-permute-start | bytes 1007624 | tf_op jit(solution)/shard_map/ppermute | solution.py:883
  7.5 2.8 %pack_lat.1 = (f32[200,128]{1,0:T(8,128)S(1)}, f32[200,128]{1,0:T(8,128)S(1)}) custom-call(f32[10368,128]{1,0:T(8,128)S(1)} %bitcast.29, s32[8,128]{1,0:T(8,128)S(1)} %copy-done.5, f32[8,24,384]{2,1,0:T(8,128)} %u.3, f32[8,24,384]{2,1,0:T(8,128)} %v.3, f32[656,128]{1,0:T(8,128)S(1)} %get-tuple-element.33.after), custom_call_target="tpu_custom_call" | custom-call | flops 1 | bytes 1 | tf_op jit(solution)/shard_map/pack_lat/pallas_call | solution.py:275
  10.3 1.3 %collective-permute-start = (f32[200,128]{1,0:T(8,128)S(1)}, f32[200,128]{1,0:T(8,128)S(1)}, u32[]{:S(2)}, u32[]{:S(2)}) collective-permute-start(f32[200,128]{1,0:T(8,128)S(1)} %get-tuple-element.34), channel_id=1, source_target_pairs={{0,1},{2,3},{1,0},{3,2},{4,5},{6,7},{5,4},{7,6},{8,9},{10,11},{9,8... | collective-permute-start | bytes 307208 | tf_op jit(solution)/shard_map/ppermute | solution.py:883
  11.6 3.0 %collective-permute-start.1 = (f32[200,128]{1,0:T(8,128)S(1)}, f32[200,128]{1,0:T(8,128)S(1)}, u32[]{:S(2)}, u32[]{:S(2)}) collective-permute-start(f32[200,128]{1,0:T(8,128)S(1)} %get-tuple-element.35), channel_id=1, source_target_pairs={{1,2},{2,1},{5,6},{6,5},{9,10},{10,9},{13,14},{14,13},{17,18},{18,... | collective-permute-start | bytes 307208 | tf_op jit(solution)/shard_map/ppermute | solution.py:883
  14.9 3.0 %advect.2.refs_0_ = f32[8,1296,128]{2,1,0:T(8,128)S(1)} custom-call(f32[10368,128]{1,0:T(8,128)S(1)} %bitcast.30, f32[1296,8]{1,0:T(8,128)S(1)} %columns.1.coefs.refs_4_, s32[8,128]{1,0:T(8,128)S(1)} %copy-done.5), custom_call_target="tpu_custom_call" | custom-call | flops 1 | bytes 1 | tf_op jit(solution)/shard_map/advect/pallas_call | solution.py:325
  17.9 4.6 %interior.2 = (f32[6,1296,128]{2,1,0:T(8,128)S(1)}, f32[2,1296,128]{2,1,0:T(8,128)S(1)}, f32[176,128]{1,0:T(8,128)S(1)}, f32[176,128]{1,0:T(8,128)S(1)}) custom-call(f32[8,1296,128]{2,1,0:T(8,128)S(1)} %advect.2.refs_0_, f32[200,128]{1,0:T(8,128)S(1)} %collective-permute-done.refs_1_.from_odd, f32[200,128]{1,0:T(8,128)S(1)} %collective-permute-done.1.refs_2_.from_even, ...), custom_call_target="tpu_custom_call" | custom-call | flops 1 | bytes 1 | tf_op jit(solution)/shard_map/interior/pallas_call | solution.py:451
  22.5 1.6 %edges.2 = (f32[2,1296,128]{2,1,0:T(8,128)S(1)}, f32[656,128]{1,0:T(8,128)S(1)}, f32[656,128]{1,0:T(8,128)S(1)}) custom-call(f32[2,1296,128]{2,1,0:T(8,128)S(1)} %get-tuple-element.37.refs_0_, f32[656,128]{1,0:T(8,128)S(1)} %collective-permute-done.2.refs_1_, f32[656,128]{1,0:T(8,128)S(1)} %collective-permute-done.3.refs_2_, bf16[1296,1296]{1,0:T(8,128)(2,1)S(1)} %copy-done, ...), custom_call_target="tpu_custom_call" | custom-call | flops 1 | bytes 1 | tf_op jit(solution)/shard_map/edges/pallas_call | solution.py:553
  24.2 1.3 %collective-permute-start.7 = (f32[656,128]{1,0:T(8,128)S(1)}, f32[656,128]{1,0:T(8,128)S(1)}, u32[]{:S(2)}, u32[]{:S(2)}) collective-permute-start(f32[656,128]{1,0:T(8,128)S(1)} %get-tuple-element.46), channel_id=1, source_target_pairs={{4,8},{12,16},{20,24},{28,0},{8,4},{16,12},{24,20},{0,28},{5,9},{1... | collective-permute-start | bytes 1007624 | tf_op jit(solution)/shard_map/ppermute | solution.py:883
  25.9 1.7 %collective-permute-start.4 = (f32[176,128]{1,0:T(8,128)S(1)}, f32[176,128]{1,0:T(8,128)S(1)}, u32[]{:S(2)}, u32[]{:S(2)}) collective-permute-start(f32[176,128]{1,0:T(8,128)S(1)} %get-tuple-element.42), channel_id=1, source_target_pairs={{0,1},{2,3},{1,0},{3,2},{4,5},{6,7},{5,4},{7,6},{8,9},{10,11},{9,8... | collective-permute-start | bytes 270344 | tf_op jit(solution)/shard_map/ppermute | solution.py:883
  27.7 3.2 %collective-permute-start.5 = (f32[176,128]{1,0:T(8,128)S(1)}, f32[176,128]{1,0:T(8,128)S(1)}, u32[]{:S(2)}, u32[]{:S(2)}) collective-permute-start(f32[176,128]{1,0:T(8,128)S(1)} %get-tuple-element.43), channel_id=1, source_target_pairs={{1,2},{2,1},{5,6},{6,5},{9,10},{10,9},{13,14},{14,13},{17,18},{18,... | collective-permute-start | bytes 270344 | tf_op jit(solution)/shard_map/ppermute | solution.py:883
  30.9 2.9 %advect.3.refs_0_ = f32[8,1296,128]{2,1,0:T(8,128)S(1)} custom-call(f32[6,1296,128]{2,1,0:T(8,128)S(1)} %get-tuple-element.36.state, f32[1296,8]{1,0:T(8,128)S(1)} %columns.1.coefs.refs_4_, f32[2,1296,128]{2,1,0:T(8,128)S(1)} %get-tuple-element.39.more.state), custom_call_target="tpu_custom_call" | custom-call | flops 1 | bytes 1 | tf_op jit(solution)/shard_map/advect/pallas_call | solution.py:325
  33.9 6.4 %interior.3 = (f32[1296,8,1,128]{3,2,1,0:T(1,128)}, f32[2,1296,128]{2,1,0:T(8,128)S(1)}, f32[5,8,128]{2,1,0:T(8,128)S(1)}, f32[5,1296,128]{2,1,0:T(8,128)S(1)}) custom-call(f32[8,1296,128]{2,1,0:T(8,128)S(1)} %advect.3.refs_0_, f32[176,128]{1,0:T(8,128)S(1)} %collective-permute-done.4.refs_1_, f32[176,128]{1,0:T(8,128)S(1)} %collective-permute-done.5.refs_2_, ...), custom_call_target="tpu_custom_call" | custom-call | flops 1 | bytes 1 | tf_op jit(solution)/shard_map/interior/pallas_call | solution.py:451
  40.3 1.8 %edges.3 = (f32[2,1296,128]{2,1,0:T(8,128)S(1)}, f32[5,8,128]{2,1,0:T(8,128)S(1)}, f32[6,8,128]{2,1,0:T(8,128)S(1)}) custom-call(f32[2,1296,128]{2,1,0:T(8,128)S(1)} %get-tuple-element.44.refs_0_, f32[656,128]{1,0:T(8,128)S(1)} %collective-permute-done.6.refs_1_, f32[656,128]{1,0:T(8,128)S(1)} %collective-permute-done.7.refs_2_, ...), custom_call_target="tpu_custom_call" | custom-call | flops 1 | bytes 1 | tf_op jit(solution)/shard_map/edges/pallas_call | solution.py:553
  42.1 1.2 %collective-permute-start.9 = (f32[6,8,128]{2,1,0:T(8,128)S(1)}, f32[6,8,128]{2,1,0:T(8,128)S(1)}, u32[]{:S(2)}, u32[]{:S(2)}) collective-permute-start(f32[6,8,128]{2,1,0:T(8,128)S(1)} %get-tuple-element.53), channel_id=1, source_target_pairs={{4,8},{12,16},{20,24},{28,0},{8,4},{16,12},{24,20},{0,28},{5,9},{1... | collective-permute-start | bytes 73736 | tf_op jit(solution)/shard_map/ppermute | solution.py:883
  43.6 2.2 %remap_own.1 = (f32[5,24,384]{2,1,0:T(8,128)S(1)}, f32[1296,8,1,128]{3,2,1,0:T(1,128)}) custom-call(f32[5,8,128]{2,1,0:T(8,128)S(1)} %get-tuple-element.49.refs_0_.after.own, s32[4,24,384]{2,1,0:T(8,128)S(1)} %get-tuple-element.64.refs_1_.refs_2_.cell, s32[4,24,384]{2,1,0:T(8,128)S(1)} %get-tuple-element.63.refs_2_.refs_3_.offset, ...), custom_call_target="tpu_custom_call", output_to_operand_aliasing={{1}: (5, {})} | custom-call | flops 1 | bytes 1 | tf_op jit(solution)/shard_map/remap_own/pallas_call | solution.py:786
  46.4 1.2 %collective-permute-done.9.refs_1_.from_even = f32[6,8,128]{2,1,0:T(8,128)S(1)} collective-permute-done((f32[6,8,128]{2,1,0:T(8,128)S(1)}, f32[6,8,128]{2,1,0:T(8,128)S(1)}, u32[]{:S(2)}, u32[]{:S(2)}) %collective-permute-start.9) | collective-permute-done | bytes 24608 | tf_op jit(solution)/shard_map/ppermute | solution.py:883
  48.1 2.0 %collective-permute-start.11 = (f32[64,128]{1,0:T(8,128)S(1)}, f32[64,128]{1,0:T(8,128)S(1)}, u32[]{:S(2)}, u32[]{:S(2)}) collective-permute-start(f32[64,128]{1,0:T(8,128)S(1)} %get-tuple-element.57), channel_id=1, source_target_pairs={{4,8},{12,16},{20,24},{28,0},{8,4},{16,12},{24,20},{0,28},{5,9},{1... | collective-permute-start | bytes 98312 | tf_op jit(solution)/shard_map/ppermute | solution.py:883
  50.1 1.0 %remap_lat.1 = (f32[24,128]{1,0:T(8,128)S(1)}, f32[24,128]{1,0:T(8,128)S(1)}) custom-call(f32[5,8,128]{2,1,0:T(8,128)S(1)} %get-tuple-element.49.refs_0_.after.own, f32[5,8,128]{2,1,0:T(8,128)S(1)} %collective-permute-done.8.refs_0_.from_odd, f32[6,8,128]{2,1,0:T(8,128)S(1)} %collective-permute-done.9.refs_1_.from_even, ...), custom_call_target="tpu_custom_call" | custom-call | flops 1 | bytes 1 | tf_op jit(solution)/shard_map/remap_lat/pallas_call | solution.py:727
  51.1 1.8 %collective-permute-start.12 = (f32[24,128]{1,0:T(8,128)S(1)}, f32[24,128]{1,0:T(8,128)S(1)}, u32[]{:S(2)}, u32[]{:S(2)}) collective-permute-start(f32[24,128]{1,0:T(8,128)S(1)} %get-tuple-element.58), channel_id=1, source_target_pairs={{0,1},{2,3},{1,0},{3,2},{4,5},{6,7},{5,4},{7,6},{8,9},{10,11},{9,8... | collective-permute-start | bytes 36872 | tf_op jit(solution)/shard_map/ppermute | solution.py:883
  52.9 2.8 %collective-permute-start.13 = (f32[24,128]{1,0:T(8,128)S(1)}, f32[24,128]{1,0:T(8,128)S(1)}, u32[]{:S(2)}, u32[]{:S(2)}) collective-permute-start(f32[24,128]{1,0:T(8,128)S(1)} %get-tuple-element.59), channel_id=1, source_target_pairs={{1,2},{2,1},{5,6},{6,5},{9,10},{10,9},{13,14},{14,13},{17,18},{18,... | collective-permute-start | bytes 36872 | tf_op jit(solution)/shard_map/ppermute | solution.py:883
  55.7 2.4 %remap_rest.1.forcing = f32[5,24,384]{2,1,0:T(8,128)S(1)} custom-call(f32[5,8,128]{2,1,0:T(8,128)S(1)} %collective-permute-done.8.refs_0_.from_odd, f32[6,8,128]{2,1,0:T(8,128)S(1)} %collective-permute-done.9.refs_1_.from_even, s32[4,24,384]{2,1,0:T(8,128)S(1)} %get-tuple-element.64.refs_1_.refs_2_.cell, ...), custom_call_target="tpu_custom_call" | custom-call | flops 1 | bytes 1 | tf_op jit(solution)/shard_map/remap_rest/pallas_call | solution.py:801
  58.1 1.0 %ocean_final.1 = (f32[8,24,384]{2,1,0:T(8,128)}, f32[8,24,384]{2,1,0:T(8,128)}) custom-call(f32[5,24,384]{2,1,0:T(8,128)S(1)} %remap_rest.1.forcing, f32[56,128]{1,0:T(8,128)S(1)} %collective-permute-done.10.lon_odd, f32[64,128]{1,0:T(8,128)S(1)} %collective-permute-done.11.lon_even, f32[24,128]{1,0:T(8,128)S(1)} %collective-permute-done.12.lat_odd, ...), custom_call_target="tpu_custom_call" | custom-call | flops 1 | bytes 1 | tf_op jit(solution)/shard_map/ocean_final/pallas_call | solution.py:866
  (45 shorter events, 2.1 us)
Async XLA Ops:
  0.6 6.8 %copy-start.5 = (s32[8,128]{1,0:T(8,128)S(1)}, s32[8,128]{1,0:T(8,128)}, u32[]{:S(2)}) copy-start(s32[8,128]{1,0:T(8,128)} %refs_5_.7) | copy-start | bytes 12292
  0.6 6.8 %copy-start.1 = (f32[1296,8,128]{2,1,0:T(8,128)S(1)}, f32[1296,8,128]{2,1,0:T(8,128)}, u32[]{:S(2)}) copy-start(f32[1296,8,128]{2,1,0:T(8,128)} %param.11) | copy-start | bytes 15925252
  2.0 12.6 %copy-start.4 = (f32[1296,8]{1,0:T(8,128)S(1)}, f32[1296,8]{1,0:T(8,128)}, u32[]{:S(2)}) copy-start(f32[1296,8]{1,0:T(8,128)} %constant.32.clone.coef) | copy-start | bytes 124420
  2.1 12.6 %copy-start.7 = (f32[5,1296]{1,0:T(8,128)S(1)}, f32[5,1296]{1,0:T(8,128)}, u32[]{:S(2)}) copy-start(f32[5,1296]{1,0:T(8,128)} %bulk_weight.1) | copy-start | bytes 77764
  2.1 20.4 %collective-permute-start.2 = (f32[656,128]{1,0:T(8,128)S(1)}, f32[656,128]{1,0:T(8,128)S(1)}, u32[]{:S(2)}, u32[]{:S(2)}) collective-permute-start(f32[656,128]{1,0:T(8,128)S(1)} %get-tuple-element.33.after), channel_id=1, source_target_pairs={{0,4},{8,12},{16,20},{24,28},{4,0},{12,8},{20,16},{28,24},{1,5},{9... | collective-permute-start | bytes 1007624 | tf_op jit(solution)/shard_map/ppermute | solution.py:883
  4.2 18.3 %collective-permute-start.3 = (f32[656,128]{1,0:T(8,128)S(1)}, f32[656,128]{1,0:T(8,128)S(1)}, u32[]{:S(2)}, u32[]{:S(2)}) collective-permute-start(f32[656,128]{1,0:T(8,128)S(1)} %get-tuple-element.38), channel_id=1, source_target_pairs={{4,8},{12,16},{20,24},{28,0},{8,4},{16,12},{24,20},{0,28},{5,9},{1... | collective-permute-start | bytes 1007624 | tf_op jit(solution)/shard_map/ppermute | solution.py:883
  10.3 7.6 %collective-permute-start = (f32[200,128]{1,0:T(8,128)S(1)}, f32[200,128]{1,0:T(8,128)S(1)}, u32[]{:S(2)}, u32[]{:S(2)}) collective-permute-start(f32[200,128]{1,0:T(8,128)S(1)} %get-tuple-element.34), channel_id=1, source_target_pairs={{0,1},{2,3},{1,0},{3,2},{4,5},{6,7},{5,4},{7,6},{8,9},{10,11},{9,8... | collective-permute-start | bytes 307208 | tf_op jit(solution)/shard_map/ppermute | solution.py:883
  11.6 6.3 %collective-permute-start.1 = (f32[200,128]{1,0:T(8,128)S(1)}, f32[200,128]{1,0:T(8,128)S(1)}, u32[]{:S(2)}, u32[]{:S(2)}) collective-permute-start(f32[200,128]{1,0:T(8,128)S(1)} %get-tuple-element.35), channel_id=1, source_target_pairs={{1,2},{2,1},{5,6},{6,5},{9,10},{10,9},{13,14},{14,13},{17,18},{18,... | collective-permute-start | bytes 307208 | tf_op jit(solution)/shard_map/ppermute | solution.py:883
  24.1 16.1 %collective-permute-start.6 = (f32[656,128]{1,0:T(8,128)S(1)}, f32[656,128]{1,0:T(8,128)S(1)}, u32[]{:S(2)}, u32[]{:S(2)}) collective-permute-start(f32[656,128]{1,0:T(8,128)S(1)} %get-tuple-element.45), channel_id=1, source_target_pairs={{0,4},{8,12},{16,20},{24,28},{4,0},{12,8},{20,16},{28,24},{1,5},{9... | collective-permute-start | bytes 1007624 | tf_op jit(solution)/shard_map/ppermute | solution.py:883
  24.2 16.1 %collective-permute-start.7 = (f32[656,128]{1,0:T(8,128)S(1)}, f32[656,128]{1,0:T(8,128)S(1)}, u32[]{:S(2)}, u32[]{:S(2)}) collective-permute-start(f32[656,128]{1,0:T(8,128)S(1)} %get-tuple-element.46), channel_id=1, source_target_pairs={{4,8},{12,16},{20,24},{28,0},{8,4},{16,12},{24,20},{0,28},{5,9},{1... | collective-permute-start | bytes 1007624 | tf_op jit(solution)/shard_map/ppermute | solution.py:883
  25.9 7.9 %collective-permute-start.4 = (f32[176,128]{1,0:T(8,128)S(1)}, f32[176,128]{1,0:T(8,128)S(1)}, u32[]{:S(2)}, u32[]{:S(2)}) collective-permute-start(f32[176,128]{1,0:T(8,128)S(1)} %get-tuple-element.42), channel_id=1, source_target_pairs={{0,1},{2,3},{1,0},{3,2},{4,5},{6,7},{5,4},{7,6},{8,9},{10,11},{9,8... | collective-permute-start | bytes 270344 | tf_op jit(solution)/shard_map/ppermute | solution.py:883
  27.7 6.2 %collective-permute-start.5 = (f32[176,128]{1,0:T(8,128)S(1)}, f32[176,128]{1,0:T(8,128)S(1)}, u32[]{:S(2)}, u32[]{:S(2)}) collective-permute-start(f32[176,128]{1,0:T(8,128)S(1)} %get-tuple-element.43), channel_id=1, source_target_pairs={{1,2},{2,1},{5,6},{6,5},{9,10},{10,9},{13,14},{14,13},{17,18},{18,... | collective-permute-start | bytes 270344 | tf_op jit(solution)/shard_map/ppermute | solution.py:883
  40.2 3.1 %copy-start.8 = (s32[24,384,4]{1,2,0:T(4,128)S(1)}, s32[24,384,4]{1,2,0:T(4,128)}, u32[]{:S(2)}) copy-start(s32[24,384,4]{1,2,0:T(4,128)} %param.15) | copy-start | bytes 442372
  40.2 3.3 %copy-start.9 = (f32[24,384,4]{1,2,0:T(4,128)S(1)}, f32[24,384,4]{1,2,0:T(4,128)}, u32[]{:S(2)}) copy-start(f32[24,384,4]{1,2,0:T(4,128)} %param.16) | copy-start | bytes 442372
  40.3 3.3 %copy-start.10 = (f32[384]{0:T(512)S(1)}, f32[384]{0:T(512)}, u32[]{:S(2)}) copy-start(f32[384]{0:T(512)} %param.20) | copy-start | bytes 4612
  42.1 3.7 %copy-start.2 = (f32[8,24,384]{2,1,0:T(8,128)S(1)}, f32[8,24,384]{2,1,0:T(8,128)}, u32[]{:S(2)}) copy-start(f32[8,24,384]{2,1,0:T(8,128)} %u.3) | copy-start | bytes 884740
  42.1 3.7 %copy-start.3 = (f32[8,24,384]{2,1,0:T(8,128)S(1)}, f32[8,24,384]{2,1,0:T(8,128)}, u32[]{:S(2)}) copy-start(f32[8,24,384]{2,1,0:T(8,128)} %v.3) | copy-start | bytes 884740
  42.1 3.7 %copy-start.6 = (s32[24,384]{1,0:T(8,128)S(1)}, s32[24,384]{1,0:T(8,128)}, u32[]{:S(2)}) copy-start(s32[24,384]{1,0:T(8,128)} %mask.7) | copy-start | bytes 110596
  42.1 5.4 %collective-permute-start.9 = (f32[6,8,128]{2,1,0:T(8,128)S(1)}, f32[6,8,128]{2,1,0:T(8,128)S(1)}, u32[]{:S(2)}, u32[]{:S(2)}) collective-permute-start(f32[6,8,128]{2,1,0:T(8,128)S(1)} %get-tuple-element.53), channel_id=1, source_target_pairs={{4,8},{12,16},{20,24},{28,0},{8,4},{16,12},{24,20},{0,28},{5,9},{1... | collective-permute-start | bytes 73736 | tf_op jit(solution)/shard_map/ppermute | solution.py:883
  43.4 3.0 %collective-permute-start.8 = (f32[5,8,128]{2,1,0:T(8,128)S(1)}, f32[5,8,128]{2,1,0:T(8,128)S(1)}, u32[]{:S(2)}, u32[]{:S(2)}) collective-permute-start(f32[5,8,128]{2,1,0:T(8,128)S(1)} %get-tuple-element.49.refs_0_.after.own), channel_id=1, source_target_pairs={{0,4},{8,12},{16,20},{24,28},{4,0},{12,8},{20,16},{28,24},{1,5},{9... | collective-permute-start | bytes 61448 | tf_op jit(solution)/shard_map/ppermute | solution.py:883
  48.1 10.0 %collective-permute-start.11 = (f32[64,128]{1,0:T(8,128)S(1)}, f32[64,128]{1,0:T(8,128)S(1)}, u32[]{:S(2)}, u32[]{:S(2)}) collective-permute-start(f32[64,128]{1,0:T(8,128)S(1)} %get-tuple-element.57), channel_id=1, source_target_pairs={{4,8},{12,16},{20,24},{28,0},{8,4},{16,12},{24,20},{0,28},{5,9},{1... | collective-permute-start | bytes 98312 | tf_op jit(solution)/shard_map/ppermute | solution.py:883
  50.1 8.0 %collective-permute-start.10 = (f32[56,128]{1,0:T(8,128)S(1)}, f32[56,128]{1,0:T(8,128)S(1)}, u32[]{:S(2)}, u32[]{:S(2)}) collective-permute-start(f32[56,128]{1,0:T(8,128)S(1)} %get-tuple-element.56.after), channel_id=1, source_target_pairs={{0,4},{8,12},{16,20},{24,28},{4,0},{12,8},{20,16},{28,24},{1,5},{9... | collective-permute-start | bytes 86024 | tf_op jit(solution)/shard_map/ppermute | solution.py:883
  51.1 7.0 %collective-permute-start.12 = (f32[24,128]{1,0:T(8,128)S(1)}, f32[24,128]{1,0:T(8,128)S(1)}, u32[]{:S(2)}, u32[]{:S(2)}) collective-permute-start(f32[24,128]{1,0:T(8,128)S(1)} %get-tuple-element.58), channel_id=1, source_target_pairs={{0,1},{2,3},{1,0},{3,2},{4,5},{6,7},{5,4},{7,6},{8,9},{10,11},{9,8... | collective-permute-start | bytes 36872 | tf_op jit(solution)/shard_map/ppermute | solution.py:883
  52.9 5.2 %collective-permute-start.13 = (f32[24,128]{1,0:T(8,128)S(1)}, f32[24,128]{1,0:T(8,128)S(1)}, u32[]{:S(2)}, u32[]{:S(2)}) collective-permute-start(f32[24,128]{1,0:T(8,128)S(1)} %get-tuple-element.59), channel_id=1, source_target_pairs={{1,2},{2,1},{5,6},{6,5},{9,10},{10,9},{13,14},{14,13},{17,18},{18,... | collective-permute-start | bytes 36872 | tf_op jit(solution)/shard_map/ppermute | solution.py:883
  (1 other events, 3.0 us)

commit v7 on v6

--- a/solution.py
+++ b/solution.py
@@ -191,27 +191,37 @@
     )(jnp.asarray(coef), bulk_weight)
 
 
-def pack_lon_kernel(plan, spec, mask, odd, even, maskv, both, sem):
+def by_parity(axis, body):
+    for lower in (True, False):
+        pl.when(parity(axis) == (0 if lower else 1))(functools.partial(body, lower))
+
+
+def pack_lon_kernel(plan, spec, mask, odd, even, maskv, sem):
     last_col = spec.shape[1] - 1
-    west, east = sides_of(both, "lon")
-    copies = [pltpu.make_async_copy(mask, maskv, sem.at[0])]
-    for out, sign, col in ((east, True, last_col), (west, False, 0)):
-        at = 0
-        for a, b in plan.seg["x", sign]:
-            copies.append(
-                pltpu.make_async_copy(
-                    spec.at[pl.ds(a, b - a), col, 0, :], out.at[pl.ds(at, b - a), :], sem.at[len(copies)]
+    first = pltpu.make_async_copy(mask, maskv, sem.at[0])
+    first.start()
+
+    def fetch(lower):
+        copies = []
+        for out, sign in ((odd, lower), (even, not lower)):
+            at = 0
+            for a, b in plan.seg["x", sign]:
+                from_ref = spec.at[pl.ds(a, b - a), last_col if sign else 0, 0, :]
+                copies.append(
+                    pltpu.make_async_copy(from_ref, out.at[pl.ds(at, b - a), :], sem.at[1 + len(copies)])
                 )
-            )
-            at += b - a
-    for c in copies:
-        c.start()
-    for c in copies:
-        c.wait()
+                at += b - a
+        for c in copies:
+            c.start()
+        for c in copies:
+            c.wait()
+
+    by_parity("lon", fetch)
+    first.wait()
     masks = [maskv[col : col + 1, :].astype(F32) for col in (last_col, 0)]
     lower = jnp.full((1, LANES), parity("lon"), jnp.int32) == 0
-    odd[...] = both[0] * jnp.where(lower, masks[0], masks[1])
-    even[...] = both[1] * jnp.where(lower, masks[1], masks[0])
+    odd[...] = odd[...] * jnp.where(lower, masks[0], masks[1])
+    even[...] = even[...] * jnp.where(lower, masks[1], masks[0])
 
 
 def pack_lon(plan, spec4, mask):
@@ -225,7 +235,6 @@
         out_specs=[VMEM, VMEM],
         scratch_shapes=[
             pltpu.VMEM(mask.shape, mask.dtype),
-            pltpu.VMEM((2, *shape), F32),
             pltpu.SemaphoreType.DMA((segments + 1,)),
         ],
         compiler_params=PARAMS,
@@ -505,13 +514,15 @@
         longer[:BULK] = bulk[...]
         longer[BULK:] = jnp.zeros((longer.shape[0] - BULK, width, LANES), F32)
         return
-    for out, side, sign in ((from_east, 1, True), (from_west, 0, False)):
-        at = 0
-        for a, b in plan.seg["x", sign]:
-            out[at : at + b - a, :] = state[side, a:b, :]
-            at += b - a
-    odd[...] = both[0]
-    even[...] = both[1]
+
+    def hand_over(lower):
+        for out, sign in ((odd, lower), (even, not lower)):
+            at = 0
+            for a, b in plan.seg["x", sign]:
+                out[at : at + b - a, :] = state[1 if sign else 0, a:b, :]
+                at += b - a
+
+    by_parity("lon", hand_over)
 
 
 def merge_lat_kernel(plan, width, state, up_in, down_in, odd, even, both):

time: 59.3 us -> 59.2 us (level)
  no operation moved by 1% of the time
where the time goes in v7:
time: 59.2 us; the launch traced here: 59 us
  Pallas kernels  32.6 us (55%)
  starting transfers between devices  23.9 us (40%)
  waiting for transfers between devices  1.22 us (2%)
  between operations  1.02 us (2%)
    ppermute x14, starting transfers between devices, swap(): got.append(lax.ppermute(value, axis, pairs + [(j, i) for i, j in pairs]))  23.9 us
    pallas_call x2, Pallas kernels, interior(): pl.pallas_call(functools.partial(interior_kernel, plan, step), out_shape=...  10.9 us
    pallas_call x2, Pallas kernels, advect(): pl.pallas_call(functools.partial(advect_kernel, plan, step), out_shape=ja...  5.93 us
    pallas_call x2, Pallas kernels, edges(): pl.pallas_call(functools.partial(edges_kernel, plan, step), out_shape=out...  3.3 us
    pallas_call x1, Pallas kernels, pack_lat(): pl.pallas_call(functools.partial(pack_lat_kernel, plan), out_shape=[jax.S...  2.8 us
    pallas_call x1, Pallas kernels, remap_rest(): pl.pallas_call(functools.partial(remap_kernel, False), out_shape=jax.Shap...  2.35 us
    pallas_call x1, Pallas kernels, remap_own(): pl.pallas_call(functools.partial(remap_kernel, True), out_shape=[jax.Shap...  2.19 us
    pallas_call x1, Pallas kernels, pack_lon(): pl.pallas_call(functools.partial(pack_lon_kernel, plan), out_shape=[jax.S...  1.39 us
  transfers between devices with their start and end apart: 14, of which 1 were waited for; matrix products, arithmetic and copies ran while one was open for 0% of the time, Pallas kernels for 45%

profile of v7, /device:TPU:1, one launch (start us, length us, event | category | flops | bytes accessed | tf_op | source)
XLA Modules:
  0.0 59.0 jit_solution(10949491565660741126)
XLA Ops:
  0.6 1.4 %pack_lon.1 = (f32[656,128]{1,0:T(8,128)S(1)}, f32[656,128]{1,0:T(8,128)S(1)}) custom-call(f32[1296,8,1,128]{3,2,1,0:T(1,128)} %bitcast.28, s32[8,128]{1,0:T(8,128)} %refs_5_.7), custom_call_target="tpu_custom_call" | custom-call | flops 1 | bytes 1 | tf_op jit(solution)/shard_map/pack_lon/pallas_call | solution.py:231
  2.1 2.1 %collective-permute-start.2 = (f32[656,128]{1,0:T(8,128)S(1)}, f32[656,128]{1,0:T(8,128)S(1)}, u32[]{:S(2)}, u32[]{:S(2)}) collective-permute-start(f32[656,128]{1,0:T(8,128)S(1)} %get-tuple-element.33.after), channel_id=1, source_target_pairs={{0,4},{8,12},{16,20},{24,28},{4,0},{12,8},{20,16},{28,24},{1,5},{9... | collective-permute-start | bytes 1007624 | tf_op jit(solution)/shard_map/ppermute | solution.py:894
  4.2 3.3 %collective-permute-start.3 = (f32[656,128]{1,0:T(8,128)S(1)}, f32[656,128]{1,0:T(8,128)S(1)}, u32[]{:S(2)}, u32[]{:S(2)}) collective-permute-start(f32[656,128]{1,0:T(8,128)S(1)} %get-tuple-element.38), channel_id=1, source_target_pairs={{4,8},{12,16},{20,24},{28,0},{8,4},{16,12},{24,20},{0,28},{5,9},{1... | collective-permute-start | bytes 1007624 | tf_op jit(solution)/shard_map/ppermute | solution.py:894
  7.5 2.8 %pack_lat.1 = (f32[200,128]{1,0:T(8,128)S(1)}, f32[200,128]{1,0:T(8,128)S(1)}) custom-call(f32[10368,128]{1,0:T(8,128)S(1)} %bitcast.29, s32[8,128]{1,0:T(8,128)S(1)} %copy-done.5, f32[8,24,384]{2,1,0:T(8,128)} %u.3, f32[8,24,384]{2,1,0:T(8,128)} %v.3, f32[656,128]{1,0:T(8,128)S(1)} %get-tuple-element.33.after), custom_call_target="tpu_custom_call" | custom-call | flops 1 | bytes 1 | tf_op jit(solution)/shard_map/pack_lat/pallas_call | solution.py:284
  10.3 1.3 %collective-permute-start = (f32[200,128]{1,0:T(8,128)S(1)}, f32[200,128]{1,0:T(8,128)S(1)}, u32[]{:S(2)}, u32[]{:S(2)}) collective-permute-start(f32[200,128]{1,0:T(8,128)S(1)} %get-tuple-element.34), channel_id=1, source_target_pairs={{0,1},{2,3},{1,0},{3,2},{4,5},{6,7},{5,4},{7,6},{8,9},{10,11},{9,8... | collective-permute-start | bytes 307208 | tf_op jit(solution)/shard_map/ppermute | solution.py:894
  11.6 3.0 %collective-permute-start.1 = (f32[200,128]{1,0:T(8,128)S(1)}, f32[200,128]{1,0:T(8,128)S(1)}, u32[]{:S(2)}, u32[]{:S(2)}) collective-permute-start(f32[200,128]{1,0:T(8,128)S(1)} %get-tuple-element.35), channel_id=1, source_target_pairs={{1,2},{2,1},{5,6},{6,5},{9,10},{10,9},{13,14},{14,13},{17,18},{18,... | collective-permute-start | bytes 307208 | tf_op jit(solution)/shard_map/ppermute | solution.py:894
  14.9 3.0 %advect.2.refs_0_ = f32[8,1296,128]{2,1,0:T(8,128)S(1)} custom-call(f32[10368,128]{1,0:T(8,128)S(1)} %bitcast.30, f32[1296,8]{1,0:T(8,128)S(1)} %columns.1.coefs.refs_4_, s32[8,128]{1,0:T(8,128)S(1)} %copy-done.5), custom_call_target="tpu_custom_call" | custom-call | flops 1 | bytes 1 | tf_op jit(solution)/shard_map/advect/pallas_call | solution.py:334
  17.9 4.5 %interior.2 = (f32[6,1296,128]{2,1,0:T(8,128)S(1)}, f32[2,1296,128]{2,1,0:T(8,128)S(1)}, f32[176,128]{1,0:T(8,128)S(1)}, f32[176,128]{1,0:T(8,128)S(1)}) custom-call(f32[8,1296,128]{2,1,0:T(8,128)S(1)} %advect.2.refs_0_, f32[200,128]{1,0:T(8,128)S(1)} %collective-permute-done.refs_1_.from_odd, f32[200,128]{1,0:T(8,128)S(1)} %collective-permute-done.1.refs_2_.from_even, ...), custom_call_target="tpu_custom_call" | custom-call | flops 1 | bytes 1 | tf_op jit(solution)/shard_map/interior/pallas_call | solution.py:460
  22.5 1.5 %edges.2 = (f32[2,1296,128]{2,1,0:T(8,128)S(1)}, f32[656,128]{1,0:T(8,128)S(1)}, f32[656,128]{1,0:T(8,128)S(1)}) custom-call(f32[2,1296,128]{2,1,0:T(8,128)S(1)} %get-tuple-element.37.refs_0_, f32[656,128]{1,0:T(8,128)S(1)} %collective-permute-done.2.refs_1_, f32[656,128]{1,0:T(8,128)S(1)} %collective-permute-done.3.refs_2_, bf16[1296,1296]{1,0:T(8,128)(2,1)S(1)} %copy-done, ...), custom_call_target="tpu_custom_call" | custom-call | flops 1 | bytes 1 | tf_op jit(solution)/shard_map/edges/pallas_call | solution.py:564
  24.1 1.3 %collective-permute-start.7 = (f32[656,128]{1,0:T(8,128)S(1)}, f32[656,128]{1,0:T(8,128)S(1)}, u32[]{:S(2)}, u32[]{:S(2)}) collective-permute-start(f32[656,128]{1,0:T(8,128)S(1)} %get-tuple-element.46), channel_id=1, source_target_pairs={{4,8},{12,16},{20,24},{28,0},{8,4},{16,12},{24,20},{0,28},{5,9},{1... | collective-permute-start | bytes 1007624 | tf_op jit(solution)/shard_map/ppermute | solution.py:894
  25.8 1.7 %collective-permute-start.4 = (f32[176,128]{1,0:T(8,128)S(1)}, f32[176,128]{1,0:T(8,128)S(1)}, u32[]{:S(2)}, u32[]{:S(2)}) collective-permute-start(f32[176,128]{1,0:T(8,128)S(1)} %get-tuple-element.42), channel_id=1, source_target_pairs={{0,1},{2,3},{1,0},{3,2},{4,5},{6,7},{5,4},{7,6},{8,9},{10,11},{9,8... | collective-permute-start | bytes 270344 | tf_op jit(solution)/shard_map/ppermute | solution.py:894
  27.6 3.2 %collective-permute-start.5 = (f32[176,128]{1,0:T(8,128)S(1)}, f32[176,128]{1,0:T(8,128)S(1)}, u32[]{:S(2)}, u32[]{:S(2)}) collective-permute-start(f32[176,128]{1,0:T(8,128)S(1)} %get-tuple-element.43), channel_id=1, source_target_pairs={{1,2},{2,1},{5,6},{6,5},{9,10},{10,9},{13,14},{14,13},{17,18},{18,... | collective-permute-start | bytes 270344 | tf_op jit(solution)/shard_map/ppermute | solution.py:894
  30.8 2.9 %advect.3.refs_0_ = f32[8,1296,128]{2,1,0:T(8,128)S(1)} custom-call(f32[6,1296,128]{2,1,0:T(8,128)S(1)} %get-tuple-element.36.state, f32[1296,8]{1,0:T(8,128)S(1)} %columns.1.coefs.refs_4_, f32[2,1296,128]{2,1,0:T(8,128)S(1)} %get-tuple-element.39.more.state), custom_call_target="tpu_custom_call" | custom-call | flops 1 | bytes 1 | tf_op jit(solution)/shard_map/advect/pallas_call | solution.py:334
  33.7 6.3 %interior.3 = (f32[1296,8,1,128]{3,2,1,0:T(1,128)}, f32[2,1296,128]{2,1,0:T(8,128)S(1)}, f32[5,8,128]{2,1,0:T(8,128)S(1)}, f32[5,1296,128]{2,1,0:T(8,128)S(1)}) custom-call(f32[8,1296,128]{2,1,0:T(8,128)S(1)} %advect.3.refs_0_, f32[176,128]{1,0:T(8,128)S(1)} %collective-permute-done.4.refs_1_, f32[176,128]{1,0:T(8,128)S(1)} %collective-permute-done.5.refs_2_, ...), custom_call_target="tpu_custom_call" | custom-call | flops 1 | bytes 1 | tf_op jit(solution)/shard_map/interior/pallas_call | solution.py:460
  40.2 1.8 %edges.3 = (f32[2,1296,128]{2,1,0:T(8,128)S(1)}, f32[5,8,128]{2,1,0:T(8,128)S(1)}, f32[6,8,128]{2,1,0:T(8,128)S(1)}) custom-call(f32[2,1296,128]{2,1,0:T(8,128)S(1)} %get-tuple-element.44.refs_0_, f32[656,128]{1,0:T(8,128)S(1)} %collective-permute-done.6.refs_1_, f32[656,128]{1,0:T(8,128)S(1)} %collective-permute-done.7.refs_2_, ...), custom_call_target="tpu_custom_call" | custom-call | flops 1 | bytes 1 | tf_op jit(solution)/shard_map/edges/pallas_call | solution.py:564
  42.0 1.3 %collective-permute-start.9 = (f32[6,8,128]{2,1,0:T(8,128)S(1)}, f32[6,8,128]{2,1,0:T(8,128)S(1)}, u32[]{:S(2)}, u32[]{:S(2)}) collective-permute-start(f32[6,8,128]{2,1,0:T(8,128)S(1)} %get-tuple-element.53), channel_id=1, source_target_pairs={{4,8},{12,16},{20,24},{28,0},{8,4},{16,12},{24,20},{0,28},{5,9},{1... | collective-permute-start | bytes 73736 | tf_op jit(solution)/shard_map/ppermute | solution.py:894
  43.4 2.2 %remap_own.1 = (f32[5,24,384]{2,1,0:T(8,128)S(1)}, f32[1296,8,1,128]{3,2,1,0:T(1,128)}) custom-call(f32[5,8,128]{2,1,0:T(8,128)S(1)} %get-tuple-element.49.refs_0_.after.own, s32[4,24,384]{2,1,0:T(8,128)S(1)} %get-tuple-element.64.refs_1_.refs_2_.cell, s32[4,24,384]{2,1,0:T(8,128)S(1)} %get-tuple-element.63.refs_2_.refs_3_.offset, ...), custom_call_target="tpu_custom_call", output_to_operand_aliasing={{1}: (5, {})} | custom-call | flops 1 | bytes 1 | tf_op jit(solution)/shard_map/remap_own/pallas_call | solution.py:797
  46.3 1.2 %collective-permute-done.9.refs_1_.from_even = f32[6,8,128]{2,1,0:T(8,128)S(1)} collective-permute-done((f32[6,8,128]{2,1,0:T(8,128)S(1)}, f32[6,8,128]{2,1,0:T(8,128)S(1)}, u32[]{:S(2)}, u32[]{:S(2)}) %collective-permute-start.9) | collective-permute-done | bytes 24608 | tf_op jit(solution)/shard_map/ppermute | solution.py:894
  48.0 2.0 %collective-permute-start.11 = (f32[64,128]{1,0:T(8,128)S(1)}, f32[64,128]{1,0:T(8,128)S(1)}, u32[]{:S(2)}, u32[]{:S(2)}) collective-permute-start(f32[64,128]{1,0:T(8,128)S(1)} %get-tuple-element.57), channel_id=1, source_target_pairs={{4,8},{12,16},{20,24},{28,0},{8,4},{16,12},{24,20},{0,28},{5,9},{1... | collective-permute-start | bytes 98312 | tf_op jit(solution)/shard_map/ppermute | solution.py:894
  50.0 1.0 %remap_lat.1 = (f32[24,128]{1,0:T(8,128)S(1)}, f32[24,128]{1,0:T(8,128)S(1)}) custom-call(f32[5,8,128]{2,1,0:T(8,128)S(1)} %get-tuple-element.49.refs_0_.after.own, f32[5,8,128]{2,1,0:T(8,128)S(1)} %collective-permute-done.8.refs_0_.from_odd, f32[6,8,128]{2,1,0:T(8,128)S(1)} %collective-permute-done.9.refs_1_.from_even, ...), custom_call_target="tpu_custom_call" | custom-call | flops 1 | bytes 1 | tf_op jit(solution)/shard_map/remap_lat/pallas_call | solution.py:738
  51.0 1.8 %collective-permute-start.12 = (f32[24,128]{1,0:T(8,128)S(1)}, f32[24,128]{1,0:T(8,128)S(1)}, u32[]{:S(2)}, u32[]{:S(2)}) collective-permute-start(f32[24,128]{1,0:T(8,128)S(1)} %get-tuple-element.58), channel_id=1, source_target_pairs={{0,1},{2,3},{1,0},{3,2},{4,5},{6,7},{5,4},{7,6},{8,9},{10,11},{9,8... | collective-permute-start | bytes 36872 | tf_op jit(solution)/shard_map/ppermute | solution.py:894
  52.8 2.8 %collective-permute-start.13 = (f32[24,128]{1,0:T(8,128)S(1)}, f32[24,128]{1,0:T(8,128)S(1)}, u32[]{:S(2)}, u32[]{:S(2)}) collective-permute-start(f32[24,128]{1,0:T(8,128)S(1)} %get-tuple-element.59), channel_id=1, source_target_pairs={{1,2},{2,1},{5,6},{6,5},{9,10},{10,9},{13,14},{14,13},{17,18},{18,... | collective-permute-start | bytes 36872 | tf_op jit(solution)/shard_map/ppermute | solution.py:894
  55.6 2.4 %remap_rest.1.forcing = f32[5,24,384]{2,1,0:T(8,128)S(1)} custom-call(f32[5,8,128]{2,1,0:T(8,128)S(1)} %collective-permute-done.8.refs_0_.from_odd, f32[6,8,128]{2,1,0:T(8,128)S(1)} %collective-permute-done.9.refs_1_.from_even, s32[4,24,384]{2,1,0:T(8,128)S(1)} %get-tuple-element.64.refs_1_.refs_2_.cell, ...), custom_call_target="tpu_custom_call" | custom-call | flops 1 | bytes 1 | tf_op jit(solution)/shard_map/remap_rest/pallas_call | solution.py:812
  58.0 1.0 %ocean_final.1 = (f32[8,24,384]{2,1,0:T(8,128)}, f32[8,24,384]{2,1,0:T(8,128)}) custom-call(f32[5,24,384]{2,1,0:T(8,128)S(1)} %remap_rest.1.forcing, f32[56,128]{1,0:T(8,128)S(1)} %collective-permute-done.10.lon_odd, f32[64,128]{1,0:T(8,128)S(1)} %collective-permute-done.11.lon_even, f32[24,128]{1,0:T(8,128)S(1)} %collective-permute-done.12.lat_odd, ...), custom_call_target="tpu_custom_call" | custom-call | flops 1 | bytes 1 | tf_op jit(solution)/shard_map/ocean_final/pallas_call | solution.py:877
  (45 shorter events, 2.1 us)
Async XLA Ops:
  0.6 6.8 %copy-start.5 = (s32[8,128]{1,0:T(8,128)S(1)}, s32[8,128]{1,0:T(8,128)}, u32[]{:S(2)}) copy-start(s32[8,128]{1,0:T(8,128)} %refs_5_.7) | copy-start | bytes 12292
  0.6 6.8 %copy-start.1 = (f32[1296,8,128]{2,1,0:T(8,128)S(1)}, f32[1296,8,128]{2,1,0:T(8,128)}, u32[]{:S(2)}) copy-start(f32[1296,8,128]{2,1,0:T(8,128)} %param.11) | copy-start | bytes 15925252
  2.0 12.6 %copy-start.4 = (f32[1296,8]{1,0:T(8,128)S(1)}, f32[1296,8]{1,0:T(8,128)}, u32[]{:S(2)}) copy-start(f32[1296,8]{1,0:T(8,128)} %constant.32.clone.coef) | copy-start | bytes 124420
  2.1 12.6 %copy-start.7 = (f32[5,1296]{1,0:T(8,128)S(1)}, f32[5,1296]{1,0:T(8,128)}, u32[]{:S(2)}) copy-start(f32[5,1296]{1,0:T(8,128)} %bulk_weight.1) | copy-start | bytes 77764
  2.1 20.4 %collective-permute-start.2 = (f32[656,128]{1,0:T(8,128)S(1)}, f32[656,128]{1,0:T(8,128)S(1)}, u32[]{:S(2)}, u32[]{:S(2)}) collective-permute-start(f32[656,128]{1,0:T(8,128)S(1)} %get-tuple-element.33.after), channel_id=1, source_target_pairs={{0,4},{8,12},{16,20},{24,28},{4,0},{12,8},{20,16},{28,24},{1,5},{9... | collective-permute-start | bytes 1007624 | tf_op jit(solution)/shard_map/ppermute | solution.py:894
  4.2 18.3 %collective-permute-start.3 = (f32[656,128]{1,0:T(8,128)S(1)}, f32[656,128]{1,0:T(8,128)S(1)}, u32[]{:S(2)}, u32[]{:S(2)}) collective-permute-start(f32[656,128]{1,0:T(8,128)S(1)} %get-tuple-element.38), channel_id=1, source_target_pairs={{4,8},{12,16},{20,24},{28,0},{8,4},{16,12},{24,20},{0,28},{5,9},{1... | collective-permute-start | bytes 1007624 | tf_op jit(solution)/shard_map/ppermute | solution.py:894
  10.3 7.6 %collective-permute-start = (f32[200,128]{1,0:T(8,128)S(1)}, f32[200,128]{1,0:T(8,128)S(1)}, u32[]{:S(2)}, u32[]{:S(2)}) collective-permute-start(f32[200,128]{1,0:T(8,128)S(1)} %get-tuple-element.34), channel_id=1, source_target_pairs={{0,1},{2,3},{1,0},{3,2},{4,5},{6,7},{5,4},{7,6},{8,9},{10,11},{9,8... | collective-permute-start | bytes 307208 | tf_op jit(solution)/shard_map/ppermute | solution.py:894
  11.6 6.3 %collective-permute-start.1 = (f32[200,128]{1,0:T(8,128)S(1)}, f32[200,128]{1,0:T(8,128)S(1)}, u32[]{:S(2)}, u32[]{:S(2)}) collective-permute-start(f32[200,128]{1,0:T(8,128)S(1)} %get-tuple-element.35), channel_id=1, source_target_pairs={{1,2},{2,1},{5,6},{6,5},{9,10},{10,9},{13,14},{14,13},{17,18},{18,... | collective-permute-start | bytes 307208 | tf_op jit(solution)/shard_map/ppermute | solution.py:894
  24.0 16.1 %collective-permute-start.6 = (f32[656,128]{1,0:T(8,128)S(1)}, f32[656,128]{1,0:T(8,128)S(1)}, u32[]{:S(2)}, u32[]{:S(2)}) collective-permute-start(f32[656,128]{1,0:T(8,128)S(1)} %get-tuple-element.45), channel_id=1, source_target_pairs={{0,4},{8,12},{16,20},{24,28},{4,0},{12,8},{20,16},{28,24},{1,5},{9... | collective-permute-start | bytes 1007624 | tf_op jit(solution)/shard_map/ppermute | solution.py:894
  24.1 16.0 %collective-permute-start.7 = (f32[656,128]{1,0:T(8,128)S(1)}, f32[656,128]{1,0:T(8,128)S(1)}, u32[]{:S(2)}, u32[]{:S(2)}) collective-permute-start(f32[656,128]{1,0:T(8,128)S(1)} %get-tuple-element.46), channel_id=1, source_target_pairs={{4,8},{12,16},{20,24},{28,0},{8,4},{16,12},{24,20},{0,28},{5,9},{1... | collective-permute-start | bytes 1007624 | tf_op jit(solution)/shard_map/ppermute | solution.py:894
  25.8 7.9 %collective-permute-start.4 = (f32[176,128]{1,0:T(8,128)S(1)}, f32[176,128]{1,0:T(8,128)S(1)}, u32[]{:S(2)}, u32[]{:S(2)}) collective-permute-start(f32[176,128]{1,0:T(8,128)S(1)} %get-tuple-element.42), channel_id=1, source_target_pairs={{0,1},{2,3},{1,0},{3,2},{4,5},{6,7},{5,4},{7,6},{8,9},{10,11},{9,8... | collective-permute-start | bytes 270344 | tf_op jit(solution)/shard_map/ppermute | solution.py:894
  27.6 6.2 %collective-permute-start.5 = (f32[176,128]{1,0:T(8,128)S(1)}, f32[176,128]{1,0:T(8,128)S(1)}, u32[]{:S(2)}, u32[]{:S(2)}) collective-permute-start(f32[176,128]{1,0:T(8,128)S(1)} %get-tuple-element.43), channel_id=1, source_target_pairs={{1,2},{2,1},{5,6},{6,5},{9,10},{10,9},{13,14},{14,13},{17,18},{18,... | collective-permute-start | bytes 270344 | tf_op jit(solution)/shard_map/ppermute | solution.py:894
  40.1 3.2 %copy-start.8 = (s32[24,384,4]{1,2,0:T(4,128)S(1)}, s32[24,384,4]{1,2,0:T(4,128)}, u32[]{:S(2)}) copy-start(s32[24,384,4]{1,2,0:T(4,128)} %param.15) | copy-start | bytes 442372
  40.1 3.3 %copy-start.9 = (f32[24,384,4]{1,2,0:T(4,128)S(1)}, f32[24,384,4]{1,2,0:T(4,128)}, u32[]{:S(2)}) copy-start(f32[24,384,4]{1,2,0:T(4,128)} %param.16) | copy-start | bytes 442372
  40.1 3.3 %copy-start.10 = (f32[384]{0:T(512)S(1)}, f32[384]{0:T(512)}, u32[]{:S(2)}) copy-start(f32[384]{0:T(512)} %param.20) | copy-start | bytes 4612
  42.0 3.7 %copy-start.2 = (f32[8,24,384]{2,1,0:T(8,128)S(1)}, f32[8,24,384]{2,1,0:T(8,128)}, u32[]{:S(2)}) copy-start(f32[8,24,384]{2,1,0:T(8,128)} %u.3) | copy-start | bytes 884740
  42.0 3.7 %copy-start.3 = (f32[8,24,384]{2,1,0:T(8,128)S(1)}, f32[8,24,384]{2,1,0:T(8,128)}, u32[]{:S(2)}) copy-start(f32[8,24,384]{2,1,0:T(8,128)} %v.3) | copy-start | bytes 884740
  42.0 3.7 %copy-start.6 = (s32[24,384]{1,0:T(8,128)S(1)}, s32[24,384]{1,0:T(8,128)}, u32[]{:S(2)}) copy-start(s32[24,384]{1,0:T(8,128)} %mask.7) | copy-start | bytes 110596
  42.0 5.4 %collective-permute-start.9 = (f32[6,8,128]{2,1,0:T(8,128)S(1)}, f32[6,8,128]{2,1,0:T(8,128)S(1)}, u32[]{:S(2)}, u32[]{:S(2)}) collective-permute-start(f32[6,8,128]{2,1,0:T(8,128)S(1)} %get-tuple-element.53), channel_id=1, source_target_pairs={{4,8},{12,16},{20,24},{28,0},{8,4},{16,12},{24,20},{0,28},{5,9},{1... | collective-permute-start | bytes 73736 | tf_op jit(solution)/shard_map/ppermute | solution.py:894
  43.3 3.0 %collective-permute-start.8 = (f32[5,8,128]{2,1,0:T(8,128)S(1)}, f32[5,8,128]{2,1,0:T(8,128)S(1)}, u32[]{:S(2)}, u32[]{:S(2)}) collective-permute-start(f32[5,8,128]{2,1,0:T(8,128)S(1)} %get-tuple-element.49.refs_0_.after.own), channel_id=1, source_target_pairs={{0,4},{8,12},{16,20},{24,28},{4,0},{12,8},{20,16},{28,24},{1,5},{9... | collective-permute-start | bytes 61448 | tf_op jit(solution)/shard_map/ppermute | solution.py:894
  48.0 10.0 %collective-permute-start.11 = (f32[64,128]{1,0:T(8,128)S(1)}, f32[64,128]{1,0:T(8,128)S(1)}, u32[]{:S(2)}, u32[]{:S(2)}) collective-permute-start(f32[64,128]{1,0:T(8,128)S(1)} %get-tuple-element.57), channel_id=1, source_target_pairs={{4,8},{12,16},{20,24},{28,0},{8,4},{16,12},{24,20},{0,28},{5,9},{1... | collective-permute-start | bytes 98312 | tf_op jit(solution)/shard_map/ppermute | solution.py:894
  50.0 8.0 %collective-permute-start.10 = (f32[56,128]{1,0:T(8,128)S(1)}, f32[56,128]{1,0:T(8,128)S(1)}, u32[]{:S(2)}, u32[]{:S(2)}) collective-permute-start(f32[56,128]{1,0:T(8,128)S(1)} %get-tuple-element.56.after), channel_id=1, source_target_pairs={{0,4},{8,12},{16,20},{24,28},{4,0},{12,8},{20,16},{28,24},{1,5},{9... | collective-permute-start | bytes 86024 | tf_op jit(solution)/shard_map/ppermute | solution.py:894
  51.0 7.0 %collective-permute-start.12 = (f32[24,128]{1,0:T(8,128)S(1)}, f32[24,128]{1,0:T(8,128)S(1)}, u32[]{:S(2)}, u32[]{:S(2)}) collective-permute-start(f32[24,128]{1,0:T(8,128)S(1)} %get-tuple-element.58), channel_id=1, source_target_pairs={{0,1},{2,3},{1,0},{3,2},{4,5},{6,7},{5,4},{7,6},{8,9},{10,11},{9,8... | collective-permute-start | bytes 36872 | tf_op jit(solution)/shard_map/ppermute | solution.py:894
  52.8 5.2 %collective-permute-start.13 = (f32[24,128]{1,0:T(8,128)S(1)}, f32[24,128]{1,0:T(8,128)S(1)}, u32[]{:S(2)}, u32[]{:S(2)}) collective-permute-start(f32[24,128]{1,0:T(8,128)S(1)} %get-tuple-element.59), channel_id=1, source_target_pairs={{1,2},{2,1},{5,6},{6,5},{9,10},{10,9},{13,14},{14,13},{17,18},{18,... | collective-permute-start | bytes 36872 | tf_op jit(solution)/shard_map/ppermute | solution.py:894
  (1 other events, 3.0 us)

commit v8 on v7

--- a/solution.py
+++ b/solution.py
@@ -347,7 +347,7 @@
 
 
 def source_blocks(transfer, moved, comps, body):
-    block = block_rows(comps)
+    block = comps if moved.shape[1] <= 2 * LANES else block_rows(comps)
 
     for n in range(comps // block):
         rows = slice(n * block, (n + 1) * block)

time: 59.2 us -> 59.2 us (level)
  no operation moved by 1% of the time
where the time goes in v8:
time: 59.2 us; the launch traced here: 59.1 us
  Pallas kernels  32.7 us (55%)
  starting transfers between devices  23.9 us (40%)
  waiting for transfers between devices  1.23 us (2%)
  between operations  1.02 us (2%)
    ppermute x14, starting transfers between devices, swap(): got.append(lax.ppermute(value, axis, pairs + [(j, i) for i, j in pairs]))  23.9 us
    pallas_call x2, Pallas kernels, interior(): pl.pallas_call(functools.partial(interior_kernel, plan, step), out_shape=...  10.9 us
    pallas_call x2, Pallas kernels, advect(): pl.pallas_call(functools.partial(advect_kernel, plan, step), out_shape=ja...  5.93 us
    pallas_call x2, Pallas kernels, edges(): pl.pallas_call(functools.partial(edges_kernel, plan, step), out_shape=out...  3.36 us
    pallas_call x1, Pallas kernels, pack_lat(): pl.pallas_call(functools.partial(pack_lat_kernel, plan), out_shape=[jax.S...  2.8 us
    pallas_call x1, Pallas kernels, remap_rest(): pl.pallas_call(functools.partial(remap_kernel, False), out_shape=jax.Shap...  2.35 us
    pallas_call x1, Pallas kernels, remap_own(): pl.pallas_call(functools.partial(remap_kernel, True), out_shape=[jax.Shap...  2.19 us
    pallas_call x1, Pallas kernels, pack_lon(): pl.pallas_call(functools.partial(pack_lon_kernel, plan), out_shape=[jax.S...  1.39 us
  transfers between devices with their start and end apart: 14, of which 1 were waited for; matrix products, arithmetic and copies ran while one was open for 0% of the time, Pallas kernels for 45%

profile of v8, /device:TPU:1, one launch (start us, length us, event | category | flops | bytes accessed | tf_op | source)
XLA Modules:
  0.0 59.1 jit_solution(9173512337905335399)
XLA Ops:
  0.6 1.4 %pack_lon.1 = (f32[656,128]{1,0:T(8,128)S(1)}, f32[656,128]{1,0:T(8,128)S(1)}) custom-call(f32[1296,8,1,128]{3,2,1,0:T(1,128)} %bitcast.28, s32[8,128]{1,0:T(8,128)} %refs_5_.7), custom_call_target="tpu_custom_call" | custom-call | flops 1 | bytes 1 | tf_op jit(solution)/shard_map/pack_lon/pallas_call | solution.py:231
  2.1 2.1 %collective-permute-start.2 = (f32[656,128]{1,0:T(8,128)S(1)}, f32[656,128]{1,0:T(8,128)S(1)}, u32[]{:S(2)}, u32[]{:S(2)}) collective-permute-start(f32[656,128]{1,0:T(8,128)S(1)} %get-tuple-element.33.after), channel_id=1, source_target_pairs={{0,4},{8,12},{16,20},{24,28},{4,0},{12,8},{20,16},{28,24},{1,5},{9... | collective-permute-start | bytes 1007624 | tf_op jit(solution)/shard_map/ppermute | solution.py:894
  4.2 3.3 %collective-permute-start.3 = (f32[656,128]{1,0:T(8,128)S(1)}, f32[656,128]{1,0:T(8,128)S(1)}, u32[]{:S(2)}, u32[]{:S(2)}) collective-permute-start(f32[656,128]{1,0:T(8,128)S(1)} %get-tuple-element.38), channel_id=1, source_target_pairs={{4,8},{12,16},{20,24},{28,0},{8,4},{16,12},{24,20},{0,28},{5,9},{1... | collective-permute-start | bytes 1007624 | tf_op jit(solution)/shard_map/ppermute | solution.py:894
  7.5 2.8 %pack_lat.1 = (f32[200,128]{1,0:T(8,128)S(1)}, f32[200,128]{1,0:T(8,128)S(1)}) custom-call(f32[10368,128]{1,0:T(8,128)S(1)} %bitcast.29, s32[8,128]{1,0:T(8,128)S(1)} %copy-done.5, f32[8,24,384]{2,1,0:T(8,128)} %u.3, f32[8,24,384]{2,1,0:T(8,128)} %v.3, f32[656,128]{1,0:T(8,128)S(1)} %get-tuple-element.33.after), custom_call_target="tpu_custom_call" | custom-call | flops 1 | bytes 1 | tf_op jit(solution)/shard_map/pack_lat/pallas_call | solution.py:284
  10.3 1.3 %collective-permute-start = (f32[200,128]{1,0:T(8,128)S(1)}, f32[200,128]{1,0:T(8,128)S(1)}, u32[]{:S(2)}, u32[]{:S(2)}) collective-permute-start(f32[200,128]{1,0:T(8,128)S(1)} %get-tuple-element.34), channel_id=1, source_target_pairs={{0,1},{2,3},{1,0},{3,2},{4,5},{6,7},{5,4},{7,6},{8,9},{10,11},{9,8... | collective-permute-start | bytes 307208 | tf_op jit(solution)/shard_map/ppermute | solution.py:894
  11.6 3.0 %collective-permute-start.1 = (f32[200,128]{1,0:T(8,128)S(1)}, f32[200,128]{1,0:T(8,128)S(1)}, u32[]{:S(2)}, u32[]{:S(2)}) collective-permute-start(f32[200,128]{1,0:T(8,128)S(1)} %get-tuple-element.35), channel_id=1, source_target_pairs={{1,2},{2,1},{5,6},{6,5},{9,10},{10,9},{13,14},{14,13},{17,18},{18,... | collective-permute-start | bytes 307208 | tf_op jit(solution)/shard_map/ppermute | solution.py:894
  14.9 3.0 %advect.2.refs_0_ = f32[8,1296,128]{2,1,0:T(8,128)S(1)} custom-call(f32[10368,128]{1,0:T(8,128)S(1)} %bitcast.30, f32[1296,8]{1,0:T(8,128)S(1)} %columns.1.coefs.refs_4_, s32[8,128]{1,0:T(8,128)S(1)} %copy-done.5), custom_call_target="tpu_custom_call" | custom-call | flops 1 | bytes 1 | tf_op jit(solution)/shard_map/advect/pallas_call | solution.py:334
  17.9 4.5 %interior.2 = (f32[6,1296,128]{2,1,0:T(8,128)S(1)}, f32[2,1296,128]{2,1,0:T(8,128)S(1)}, f32[176,128]{1,0:T(8,128)S(1)}, f32[176,128]{1,0:T(8,128)S(1)}) custom-call(f32[8,1296,128]{2,1,0:T(8,128)S(1)} %advect.2.refs_0_, f32[200,128]{1,0:T(8,128)S(1)} %collective-permute-done.refs_1_.from_odd, f32[200,128]{1,0:T(8,128)S(1)} %collective-permute-done.1.refs_2_.from_even, ...), custom_call_target="tpu_custom_call" | custom-call | flops 1 | bytes 1 | tf_op jit(solution)/shard_map/interior/pallas_call | solution.py:460
  22.5 1.5 %edges.2 = (f32[2,1296,128]{2,1,0:T(8,128)S(1)}, f32[656,128]{1,0:T(8,128)S(1)}, f32[656,128]{1,0:T(8,128)S(1)}) custom-call(f32[2,1296,128]{2,1,0:T(8,128)S(1)} %get-tuple-element.37.refs_0_, f32[656,128]{1,0:T(8,128)S(1)} %collective-permute-done.2.refs_1_, f32[656,128]{1,0:T(8,128)S(1)} %collective-permute-done.3.refs_2_, bf16[1296,1296]{1,0:T(8,128)(2,1)S(1)} %copy-done, ...), custom_call_target="tpu_custom_call" | custom-call | flops 1 | bytes 1 | tf_op jit(solution)/shard_map/edges/pallas_call | solution.py:564
  24.1 1.3 %collective-permute-start.7 = (f32[656,128]{1,0:T(8,128)S(1)}, f32[656,128]{1,0:T(8,128)S(1)}, u32[]{:S(2)}, u32[]{:S(2)}) collective-permute-start(f32[656,128]{1,0:T(8,128)S(1)} %get-tuple-element.46), channel_id=1, source_target_pairs={{4,8},{12,16},{20,24},{28,0},{8,4},{16,12},{24,20},{0,28},{5,9},{1... | collective-permute-start | bytes 1007624 | tf_op jit(solution)/shard_map/ppermute | solution.py:894
  25.8 1.7 %collective-permute-start.4 = (f32[176,128]{1,0:T(8,128)S(1)}, f32[176,128]{1,0:T(8,128)S(1)}, u32[]{:S(2)}, u32[]{:S(2)}) collective-permute-start(f32[176,128]{1,0:T(8,128)S(1)} %get-tuple-element.42), channel_id=1, source_target_pairs={{0,1},{2,3},{1,0},{3,2},{4,5},{6,7},{5,4},{7,6},{8,9},{10,11},{9,8... | collective-permute-start | bytes 270344 | tf_op jit(solution)/shard_map/ppermute | solution.py:894
  27.6 3.2 %collective-permute-start.5 = (f32[176,128]{1,0:T(8,128)S(1)}, f32[176,128]{1,0:T(8,128)S(1)}, u32[]{:S(2)}, u32[]{:S(2)}) collective-permute-start(f32[176,128]{1,0:T(8,128)S(1)} %get-tuple-element.43), channel_id=1, source_target_pairs={{1,2},{2,1},{5,6},{6,5},{9,10},{10,9},{13,14},{14,13},{17,18},{18,... | collective-permute-start | bytes 270344 | tf_op jit(solution)/shard_map/ppermute | solution.py:894
  30.8 2.9 %advect.3.refs_0_ = f32[8,1296,128]{2,1,0:T(8,128)S(1)} custom-call(f32[6,1296,128]{2,1,0:T(8,128)S(1)} %get-tuple-element.36.state, f32[1296,8]{1,0:T(8,128)S(1)} %columns.1.coefs.refs_4_, f32[2,1296,128]{2,1,0:T(8,128)S(1)} %get-tuple-element.39.more.state), custom_call_target="tpu_custom_call" | custom-call | flops 1 | bytes 1 | tf_op jit(solution)/shard_map/advect/pallas_call | solution.py:334
  33.8 6.3 %interior.3 = (f32[1296,8,1,128]{3,2,1,0:T(1,128)}, f32[2,1296,128]{2,1,0:T(8,128)S(1)}, f32[5,8,128]{2,1,0:T(8,128)S(1)}, f32[5,1296,128]{2,1,0:T(8,128)S(1)}) custom-call(f32[8,1296,128]{2,1,0:T(8,128)S(1)} %advect.3.refs_0_, f32[176,128]{1,0:T(8,128)S(1)} %collective-permute-done.4.refs_1_, f32[176,128]{1,0:T(8,128)S(1)} %collective-permute-done.5.refs_2_, ...), custom_call_target="tpu_custom_call" | custom-call | flops 1 | bytes 1 | tf_op jit(solution)/shard_map/interior/pallas_call | solution.py:460
  40.2 1.9 %edges.3 = (f32[2,1296,128]{2,1,0:T(8,128)S(1)}, f32[5,8,128]{2,1,0:T(8,128)S(1)}, f32[6,8,128]{2,1,0:T(8,128)S(1)}) custom-call(f32[2,1296,128]{2,1,0:T(8,128)S(1)} %get-tuple-element.44.refs_0_, f32[656,128]{1,0:T(8,128)S(1)} %collective-permute-done.6.refs_1_, f32[656,128]{1,0:T(8,128)S(1)} %collective-permute-done.7.refs_2_, ...), custom_call_target="tpu_custom_call" | custom-call | flops 1 | bytes 1 | tf_op jit(solution)/shard_map/edges/pallas_call | solution.py:564
  42.1 1.3 %collective-permute-start.9 = (f32[6,8,128]{2,1,0:T(8,128)S(1)}, f32[6,8,128]{2,1,0:T(8,128)S(1)}, u32[]{:S(2)}, u32[]{:S(2)}) collective-permute-start(f32[6,8,128]{2,1,0:T(8,128)S(1)} %get-tuple-element.53), channel_id=1, source_target_pairs={{4,8},{12,16},{20,24},{28,0},{8,4},{16,12},{24,20},{0,28},{5,9},{1... | collective-permute-start | bytes 73736 | tf_op jit(solution)/shard_map/ppermute | solution.py:894
  43.5 2.2 %remap_own.1 = (f32[5,24,384]{2,1,0:T(8,128)S(1)}, f32[1296,8,1,128]{3,2,1,0:T(1,128)}) custom-call(f32[5,8,128]{2,1,0:T(8,128)S(1)} %get-tuple-element.49.refs_0_.after.own, s32[4,24,384]{2,1,0:T(8,128)S(1)} %get-tuple-element.64.refs_1_.refs_2_.cell, s32[4,24,384]{2,1,0:T(8,128)S(1)} %get-tuple-element.63.refs_2_.refs_3_.offset, ...), custom_call_target="tpu_custom_call", output_to_operand_aliasing={{1}: (5, {})} | custom-call | flops 1 | bytes 1 | tf_op jit(solution)/shard_map/remap_own/pallas_call | solution.py:797
  46.3 1.2 %collective-permute-done.9.refs_1_.from_even = f32[6,8,128]{2,1,0:T(8,128)S(1)} collective-permute-done((f32[6,8,128]{2,1,0:T(8,128)S(1)}, f32[6,8,128]{2,1,0:T(8,128)S(1)}, u32[]{:S(2)}, u32[]{:S(2)}) %collective-permute-start.9) | collective-permute-done | bytes 24608 | tf_op jit(solution)/shard_map/ppermute | solution.py:894
  48.1 2.0 %collective-permute-start.11 = (f32[64,128]{1,0:T(8,128)S(1)}, f32[64,128]{1,0:T(8,128)S(1)}, u32[]{:S(2)}, u32[]{:S(2)}) collective-permute-start(f32[64,128]{1,0:T(8,128)S(1)} %get-tuple-element.57), channel_id=1, source_target_pairs={{4,8},{12,16},{20,24},{28,0},{8,4},{16,12},{24,20},{0,28},{5,9},{1... | collective-permute-start | bytes 98312 | tf_op jit(solution)/shard_map/ppermute | solution.py:894
  50.1 1.0 %remap_lat.1 = (f32[24,128]{1,0:T(8,128)S(1)}, f32[24,128]{1,0:T(8,128)S(1)}) custom-call(f32[5,8,128]{2,1,0:T(8,128)S(1)} %get-tuple-element.49.refs_0_.after.own, f32[5,8,128]{2,1,0:T(8,128)S(1)} %collective-permute-done.8.refs_0_.from_odd, f32[6,8,128]{2,1,0:T(8,128)S(1)} %collective-permute-done.9.refs_1_.from_even, ...), custom_call_target="tpu_custom_call" | custom-call | flops 1 | bytes 1 | tf_op jit(solution)/shard_map/remap_lat/pallas_call | solution.py:738
  51.1 1.8 %collective-permute-start.12 = (f32[24,128]{1,0:T(8,128)S(1)}, f32[24,128]{1,0:T(8,128)S(1)}, u32[]{:S(2)}, u32[]{:S(2)}) collective-permute-start(f32[24,128]{1,0:T(8,128)S(1)} %get-tuple-element.58), channel_id=1, source_target_pairs={{0,1},{2,3},{1,0},{3,2},{4,5},{6,7},{5,4},{7,6},{8,9},{10,11},{9,8... | collective-permute-start | bytes 36872 | tf_op jit(solution)/shard_map/ppermute | solution.py:894
  52.8 2.8 %collective-permute-start.13 = (f32[24,128]{1,0:T(8,128)S(1)}, f32[24,128]{1,0:T(8,128)S(1)}, u32[]{:S(2)}, u32[]{:S(2)}) collective-permute-start(f32[24,128]{1,0:T(8,128)S(1)} %get-tuple-element.59), channel_id=1, source_target_pairs={{1,2},{2,1},{5,6},{6,5},{9,10},{10,9},{13,14},{14,13},{17,18},{18,... | collective-permute-start | bytes 36872 | tf_op jit(solution)/shard_map/ppermute | solution.py:894
  55.7 2.4 %remap_rest.1.forcing = f32[5,24,384]{2,1,0:T(8,128)S(1)} custom-call(f32[5,8,128]{2,1,0:T(8,128)S(1)} %collective-permute-done.8.refs_0_.from_odd, f32[6,8,128]{2,1,0:T(8,128)S(1)} %collective-permute-done.9.refs_1_.from_even, s32[4,24,384]{2,1,0:T(8,128)S(1)} %get-tuple-element.64.refs_1_.refs_2_.cell, ...), custom_call_target="tpu_custom_call" | custom-call | flops 1 | bytes 1 | tf_op jit(solution)/shard_map/remap_rest/pallas_call | solution.py:812
  58.1 1.0 %ocean_final.1 = (f32[8,24,384]{2,1,0:T(8,128)}, f32[8,24,384]{2,1,0:T(8,128)}) custom-call(f32[5,24,384]{2,1,0:T(8,128)S(1)} %remap_rest.1.forcing, f32[56,128]{1,0:T(8,128)S(1)} %collective-permute-done.10.lon_odd, f32[64,128]{1,0:T(8,128)S(1)} %collective-permute-done.11.lon_even, f32[24,128]{1,0:T(8,128)S(1)} %collective-permute-done.12.lat_odd, ...), custom_call_target="tpu_custom_call" | custom-call | flops 1 | bytes 1 | tf_op jit(solution)/shard_map/ocean_final/pallas_call | solution.py:877
  (45 shorter events, 2.1 us)
Async XLA Ops:
  0.6 6.8 %copy-start.5 = (s32[8,128]{1,0:T(8,128)S(1)}, s32[8,128]{1,0:T(8,128)}, u32[]{:S(2)}) copy-start(s32[8,128]{1,0:T(8,128)} %refs_5_.7) | copy-start | bytes 12292
  0.6 6.8 %copy-start.1 = (f32[1296,8,128]{2,1,0:T(8,128)S(1)}, f32[1296,8,128]{2,1,0:T(8,128)}, u32[]{:S(2)}) copy-start(f32[1296,8,128]{2,1,0:T(8,128)} %param.11) | copy-start | bytes 15925252
  2.0 12.6 %copy-start.4 = (f32[1296,8]{1,0:T(8,128)S(1)}, f32[1296,8]{1,0:T(8,128)}, u32[]{:S(2)}) copy-start(f32[1296,8]{1,0:T(8,128)} %constant.32.clone.coef) | copy-start | bytes 124420
  2.1 12.6 %copy-start.7 = (f32[5,1296]{1,0:T(8,128)S(1)}, f32[5,1296]{1,0:T(8,128)}, u32[]{:S(2)}) copy-start(f32[5,1296]{1,0:T(8,128)} %bulk_weight.1) | copy-start | bytes 77764
  2.1 20.4 %collective-permute-start.2 = (f32[656,128]{1,0:T(8,128)S(1)}, f32[656,128]{1,0:T(8,128)S(1)}, u32[]{:S(2)}, u32[]{:S(2)}) collective-permute-start(f32[656,128]{1,0:T(8,128)S(1)} %get-tuple-element.33.after), channel_id=1, source_target_pairs={{0,4},{8,12},{16,20},{24,28},{4,0},{12,8},{20,16},{28,24},{1,5},{9... | collective-permute-start | bytes 1007624 | tf_op jit(solution)/shard_map/ppermute | solution.py:894
  4.2 18.3 %collective-permute-start.3 = (f32[656,128]{1,0:T(8,128)S(1)}, f32[656,128]{1,0:T(8,128)S(1)}, u32[]{:S(2)}, u32[]{:S(2)}) collective-permute-start(f32[656,128]{1,0:T(8,128)S(1)} %get-tuple-element.38), channel_id=1, source_target_pairs={{4,8},{12,16},{20,24},{28,0},{8,4},{16,12},{24,20},{0,28},{5,9},{1... | collective-permute-start | bytes 1007624 | tf_op jit(solution)/shard_map/ppermute | solution.py:894
  10.3 7.6 %collective-permute-start = (f32[200,128]{1,0:T(8,128)S(1)}, f32[200,128]{1,0:T(8,128)S(1)}, u32[]{:S(2)}, u32[]{:S(2)}) collective-permute-start(f32[200,128]{1,0:T(8,128)S(1)} %get-tuple-element.34), channel_id=1, source_target_pairs={{0,1},{2,3},{1,0},{3,2},{4,5},{6,7},{5,4},{7,6},{8,9},{10,11},{9,8... | collective-permute-start | bytes 307208 | tf_op jit(solution)/shard_map/ppermute | solution.py:894
  11.6 6.3 %collective-permute-start.1 = (f32[200,128]{1,0:T(8,128)S(1)}, f32[200,128]{1,0:T(8,128)S(1)}, u32[]{:S(2)}, u32[]{:S(2)}) collective-permute-start(f32[200,128]{1,0:T(8,128)S(1)} %get-tuple-element.35), channel_id=1, source_target_pairs={{1,2},{2,1},{5,6},{6,5},{9,10},{10,9},{13,14},{14,13},{17,18},{18,... | collective-permute-start | bytes 307208 | tf_op jit(solution)/shard_map/ppermute | solution.py:894
  24.0 16.1 %collective-permute-start.6 = (f32[656,128]{1,0:T(8,128)S(1)}, f32[656,128]{1,0:T(8,128)S(1)}, u32[]{:S(2)}, u32[]{:S(2)}) collective-permute-start(f32[656,128]{1,0:T(8,128)S(1)} %get-tuple-element.45), channel_id=1, source_target_pairs={{0,4},{8,12},{16,20},{24,28},{4,0},{12,8},{20,16},{28,24},{1,5},{9... | collective-permute-start | bytes 1007624 | tf_op jit(solution)/shard_map/ppermute | solution.py:894
  24.1 16.0 %collective-permute-start.7 = (f32[656,128]{1,0:T(8,128)S(1)}, f32[656,128]{1,0:T(8,128)S(1)}, u32[]{:S(2)}, u32[]{:S(2)}) collective-permute-start(f32[656,128]{1,0:T(8,128)S(1)} %get-tuple-element.46), channel_id=1, source_target_pairs={{4,8},{12,16},{20,24},{28,0},{8,4},{16,12},{24,20},{0,28},{5,9},{1... | collective-permute-start | bytes 1007624 | tf_op jit(solution)/shard_map/ppermute | solution.py:894
  25.8 7.9 %collective-permute-start.4 = (f32[176,128]{1,0:T(8,128)S(1)}, f32[176,128]{1,0:T(8,128)S(1)}, u32[]{:S(2)}, u32[]{:S(2)}) collective-permute-start(f32[176,128]{1,0:T(8,128)S(1)} %get-tuple-element.42), channel_id=1, source_target_pairs={{0,1},{2,3},{1,0},{3,2},{4,5},{6,7},{5,4},{7,6},{8,9},{10,11},{9,8... | collective-permute-start | bytes 270344 | tf_op jit(solution)/shard_map/ppermute | solution.py:894
  27.6 6.2 %collective-permute-start.5 = (f32[176,128]{1,0:T(8,128)S(1)}, f32[176,128]{1,0:T(8,128)S(1)}, u32[]{:S(2)}, u32[]{:S(2)}) collective-permute-start(f32[176,128]{1,0:T(8,128)S(1)} %get-tuple-element.43), channel_id=1, source_target_pairs={{1,2},{2,1},{5,6},{6,5},{9,10},{10,9},{13,14},{14,13},{17,18},{18,... | collective-permute-start | bytes 270344 | tf_op jit(solution)/shard_map/ppermute | solution.py:894
  40.1 3.2 %copy-start.8 = (s32[24,384,4]{1,2,0:T(4,128)S(1)}, s32[24,384,4]{1,2,0:T(4,128)}, u32[]{:S(2)}) copy-start(s32[24,384,4]{1,2,0:T(4,128)} %param.15) | copy-start | bytes 442372
  40.1 3.3 %copy-start.9 = (f32[24,384,4]{1,2,0:T(4,128)S(1)}, f32[24,384,4]{1,2,0:T(4,128)}, u32[]{:S(2)}) copy-start(f32[24,384,4]{1,2,0:T(4,128)} %param.16) | copy-start | bytes 442372
  40.2 3.3 %copy-start.10 = (f32[384]{0:T(512)S(1)}, f32[384]{0:T(512)}, u32[]{:S(2)}) copy-start(f32[384]{0:T(512)} %param.20) | copy-start | bytes 4612
  42.0 3.7 %copy-start.2 = (f32[8,24,384]{2,1,0:T(8,128)S(1)}, f32[8,24,384]{2,1,0:T(8,128)}, u32[]{:S(2)}) copy-start(f32[8,24,384]{2,1,0:T(8,128)} %u.3) | copy-start | bytes 884740
  42.1 3.7 %copy-start.3 = (f32[8,24,384]{2,1,0:T(8,128)S(1)}, f32[8,24,384]{2,1,0:T(8,128)}, u32[]{:S(2)}) copy-start(f32[8,24,384]{2,1,0:T(8,128)} %v.3) | copy-start | bytes 884740
  42.1 3.7 %copy-start.6 = (s32[24,384]{1,0:T(8,128)S(1)}, s32[24,384]{1,0:T(8,128)}, u32[]{:S(2)}) copy-start(s32[24,384]{1,0:T(8,128)} %mask.7) | copy-start | bytes 110596
  42.1 5.4 %collective-permute-start.9 = (f32[6,8,128]{2,1,0:T(8,128)S(1)}, f32[6,8,128]{2,1,0:T(8,128)S(1)}, u32[]{:S(2)}, u32[]{:S(2)}) collective-permute-start(f32[6,8,128]{2,1,0:T(8,128)S(1)} %get-tuple-element.53), channel_id=1, source_target_pairs={{4,8},{12,16},{20,24},{28,0},{8,4},{16,12},{24,20},{0,28},{5,9},{1... | collective-permute-start | bytes 73736 | tf_op jit(solution)/shard_map/ppermute | solution.py:894
  43.3 3.0 %collective-permute-start.8 = (f32[5,8,128]{2,1,0:T(8,128)S(1)}, f32[5,8,128]{2,1,0:T(8,128)S(1)}, u32[]{:S(2)}, u32[]{:S(2)}) collective-permute-start(f32[5,8,128]{2,1,0:T(8,128)S(1)} %get-tuple-element.49.refs_0_.after.own), channel_id=1, source_target_pairs={{0,4},{8,12},{16,20},{24,28},{4,0},{12,8},{20,16},{28,24},{1,5},{9... | collective-permute-start | bytes 61448 | tf_op jit(solution)/shard_map/ppermute | solution.py:894
  48.1 10.0 %collective-permute-start.11 = (f32[64,128]{1,0:T(8,128)S(1)}, f32[64,128]{1,0:T(8,128)S(1)}, u32[]{:S(2)}, u32[]{:S(2)}) collective-permute-start(f32[64,128]{1,0:T(8,128)S(1)} %get-tuple-element.57), channel_id=1, source_target_pairs={{4,8},{12,16},{20,24},{28,0},{8,4},{16,12},{24,20},{0,28},{5,9},{1... | collective-permute-start | bytes 98312 | tf_op jit(solution)/shard_map/ppermute | solution.py:894
  50.1 8.0 %collective-permute-start.10 = (f32[56,128]{1,0:T(8,128)S(1)}, f32[56,128]{1,0:T(8,128)S(1)}, u32[]{:S(2)}, u32[]{:S(2)}) collective-permute-start(f32[56,128]{1,0:T(8,128)S(1)} %get-tuple-element.56.after), channel_id=1, source_target_pairs={{0,4},{8,12},{16,20},{24,28},{4,0},{12,8},{20,16},{28,24},{1,5},{9... | collective-permute-start | bytes 86024 | tf_op jit(solution)/shard_map/ppermute | solution.py:894
  51.1 7.0 %collective-permute-start.12 = (f32[24,128]{1,0:T(8,128)S(1)}, f32[24,128]{1,0:T(8,128)S(1)}, u32[]{:S(2)}, u32[]{:S(2)}) collective-permute-start(f32[24,128]{1,0:T(8,128)S(1)} %get-tuple-element.58), channel_id=1, source_target_pairs={{0,1},{2,3},{1,0},{3,2},{4,5},{6,7},{5,4},{7,6},{8,9},{10,11},{9,8... | collective-permute-start | bytes 36872 | tf_op jit(solution)/shard_map/ppermute | solution.py:894
  52.8 5.2 %collective-permute-start.13 = (f32[24,128]{1,0:T(8,128)S(1)}, f32[24,128]{1,0:T(8,128)S(1)}, u32[]{:S(2)}, u32[]{:S(2)}) collective-permute-start(f32[24,128]{1,0:T(8,128)S(1)} %get-tuple-element.59), channel_id=1, source_target_pairs={{1,2},{2,1},{5,6},{6,5},{9,10},{10,9},{13,14},{14,13},{17,18},{18,... | collective-permute-start | bytes 36872 | tf_op jit(solution)/shard_map/ppermute | solution.py:894
  (1 other events, 3.0 us)
